TPU v7x, 256 devices: a whole 4x4x8 slice. The times are simulated.
256 devices in a mesh: tm: 64 (over z, x, core), space: 4 (over y).
Axes of the slice: x: 4, y: 4, z: 8, core: 2. Of those that a mesh axis runs over, the one named last changes fastest.
Arguments:
- forcing: float32 [2, 64, 125, 8, 128], P(None, 'tm', None, 'space'), may hold values from -6 to 6
- init_state: float32 [125, 8, 128], P(None, 'space'), may hold values from -6 to 6
- elem_scale: float32 [8, 128], P('space'), may hold values from 0.5 to 2
- vol_op: float32 [125, 125], replicated, may hold values from -0.5 to 8, as said below
- face_ops: float32 [4, 125, 125], replicated, may hold values from -0.25 to 0.25
Outputs:
- solution: float32 [2, 64, 125, 8, 128], P(None, 'tm', None, 'space')
Inputs may be any that keep to these rules, and one draw needn't show every extreme that they name: `vol_op`: its diagonal entries lie between 4 and 8.
All inputs are finite; a program needn't handle non-finite values.
Results may differ from a plain program's by a relative error of at most 0.0003.
Values sent between devices are 32-bit elements; how exact they have to be, the bound alone decides.
No kernel may reach another device: no remote copies, remote signals or barrier semaphores. Data moves between devices by JAX's collectives and lax.ppermute only.
A program may use at most 64 MiB of HBM per device.

v0:
```python
import math

import jax
import jax.numpy as jnp
from jax import lax
from jax.sharding import PartitionSpec as P

SWEEPS = 8
SECTIONS = 2


circ_alpha = 0.01
damping = 0.7


def padded(block, sides, width):
    for axis, dim in sides:
        count = lax.axis_size(axis)
        forward = [(i, i + 1) for i in range(count - 1)]
        forward.append((count - 1, 0))
        backward = [(target, source) for source, target in forward]
        low = lax.ppermute(
            lax.slice_in_dim(block, block.shape[dim] - width, None, axis=dim), axis, forward
        )
        high = lax.ppermute(lax.slice_in_dim(block, 0, width, axis=dim), axis, backward)
        block = jnp.concatenate([low, block, high], axis=dim)
    return block


def swapped(shard, axis, bit):
    return lax.ppermute(shard, axis, [(i, i ^ 1 << bit) for i in range(lax.axis_size(axis))])


def from_root(block, axis, holder):
    block = jnp.where(lax.axis_index(axis) == holder, block, jnp.zeros_like(block))
    return lax.psum(block, axis)


def product(left, right):
    return jnp.dot(left, right, precision=lax.Precision.HIGHEST, preferred_element_type=jnp.float32)


def apply_rows(matrix, field):
    flat = field.reshape(field.shape[0], -1)
    return product(matrix, flat).reshape((matrix.shape[0],) + field.shape[1:])


def couple(field, elem_scale, stacked):
    count = field.shape[0]
    widened = padded(field, (("space", 2),), 1)
    local = apply_rows(stacked[: 3 * count], field).reshape((3, count) + field.shape[1:])
    south = apply_rows(stacked[3 * count : 4 * count], widened[:, :, :-2])
    north = apply_rows(stacked[4 * count :], widened[:, :, 2:])
    zero_col = jnp.zeros(field.shape[:-1] + (1,), jnp.float32)
    west = jnp.concatenate([zero_col, local[1][..., :-1]], axis=-1)
    east = jnp.concatenate([local[2][..., 1:], zero_col], axis=-1)
    return elem_scale * local[0] + west + east + south + north


def rotate(base_re, base_im, angle):
    cosine = jnp.cos(angle)
    sine = jnp.sin(angle)
    return (base_re * cosine - base_im * sine, base_re * sine + base_im * cosine)


def bit_reverse(index, bits):
    total = jnp.zeros((), jnp.int32)
    for bit in range(bits):
        total = total + (index >> bit & 1) * (1 << bits - 1 - bit)
    return total


def forward_butterfly(scaled, index, bits):
    paired = None
    for segment in range(bits):
        bit = bits - 1 - segment
        half = 1 << bit
        upper = index >> bit & 1 == 1
        within = (index & half - 1).astype(jnp.float32)
        angle = jnp.where(upper, -math.pi * within / half, 0.0)
        if segment == 0:
            partner = swapped(scaled, "tm", bit)
            base = jnp.where(upper, partner - scaled, partner + scaled)
            part_re = base * jnp.cos(angle)
            part_im = base * jnp.sin(angle)
        else:
            partner = swapped(paired, "tm", bit)
            base = jnp.where(upper, partner - paired, partner + paired)
            part_re, part_im = rotate(base[:, 0], base[:, 1], angle)
        paired = jnp.stack((part_re, part_im), 1)
    return paired


def inverse_butterfly(paired, index, bits):
    for bit in range(bits):
        half = 1 << bit
        upper = index >> bit & 1 == 1
        within = (index & half - 1).astype(jnp.float32)
        angle = jnp.where(upper, math.pi * within / half, 0.0)
        send_re, send_im = rotate(paired[:, 0], paired[:, 1], angle)
        if bit == bits - 1:
            partner = swapped(send_re, "tm", bit)
            return jnp.where(upper, partner - send_re, send_re + partner)
        outgoing = jnp.stack((send_re, send_im), 1)
        partner = swapped(outgoing, "tm", bit)
        paired = jnp.where(upper, partner - outgoing, outgoing + partner)
    return paired[:, 0]


def per_device(forcing, init_state, elem_scale, vol_op, face_ops):
    steps = lax.axis_size("tm")
    bits = steps.bit_length() - 1
    index = lax.axis_index("tm")
    count = vol_op.shape[0]
    log_alpha = math.log(circ_alpha)
    place = index.astype(jnp.float32)
    grow = jnp.exp(place * (log_alpha / steps))
    shrink = jnp.exp(place * (-log_alpha / steps))
    frequency = bit_reverse(index, bits)
    root = math.exp(log_alpha / steps)
    theta = 2.0 * math.pi / steps * frequency.astype(jnp.float32)
    shift_re = 1.0 - root * jnp.cos(theta)
    shift_im = root * jnp.sin(theta)
    stacked = jnp.concatenate((vol_op[None], face_ops), 0).reshape(5 * count, count)
    vol_diag = jnp.diagonal(vol_op)[:, None, None]
    state = init_state
    results = []
    for section in range(SECTIONS):
        rhs = forcing[section, 0] + 0.5 * state
        rhs = rhs + jnp.where(index == 0, state, 0.0)
        scaled = grow * rhs
        spectrum = forward_butterfly(scaled, index, bits)
        divisor_re = shift_re + elem_scale * vol_diag
        modulus = divisor_re * divisor_re + shift_im * shift_im
        spectrum_re = spectrum[:, 0]
        spectrum_im = spectrum[:, 1]
        iterate_re = damping * (spectrum_re * divisor_re + spectrum_im * shift_im) / modulus
        iterate_im = damping * (spectrum_im * divisor_re - spectrum_re * shift_im) / modulus
        for sweep in range(SWEEPS - 1):
            joined = jnp.stack((iterate_re, iterate_im), 1)
            coupled = couple(joined, elem_scale, stacked)
            residual_re = spectrum_re - (
                shift_re * iterate_re - shift_im * iterate_im + coupled[:, 0]
            )
            residual_im = spectrum_im - (
                shift_re * iterate_im + shift_im * iterate_re + coupled[:, 1]
            )
            iterate_re, iterate_im = (
                iterate_re
                + damping * (residual_re * divisor_re + residual_im * shift_im) / modulus,
                iterate_im
                + damping * (residual_im * divisor_re - residual_re * shift_im) / modulus,
            )
        real = inverse_butterfly(jnp.stack((iterate_re, iterate_im), 1), index, bits)
        result = real * shrink / steps
        results.append(result)
        if section + 1 < SECTIONS:
            state = from_root(result, "tm", steps - 1)
    return jnp.stack(results, 0)[:, None]


def solution(mesh):
    return jax.shard_map(
        per_device,
        mesh=mesh,
        in_specs=(
            P(None, "tm", None, "space", None),
            P(None, "space", None),
            P("space", None),
            P(),
            P(),
        ),
        out_specs=P(None, "tm", None, "space", None),
        check_vma=False,
    )
```

profile of v0, /device:TPU:1, one launch (start us, length us, event | category | flops | bytes accessed | tf_op | source)
XLA Modules:
  0.0 522.5 jit_solution(2422275741622749817)
XLA Ops:
  8.6 7.8 %collective-permute-start = (f32[125,2,128]{0,2,1:T(8,128)S(1)}, f32[125,2,128]{0,2,1:T(8,128)S(1)}, u32[]{:S(2)}, u32[]{:S(2)}) collective-permute-start(f32[125,2,128]{0,2,1:T(8,128)S(1)} %fusion.71), channel_id=1, source_target_pairs={{0,128},{4,132},{8,136},{12,140},{16,144},{20,148},{24,152},{28,15... | collective-permute-start | bytes 384008 | tf_op jit(solution)/shard_map/ppermute | solution.py:31
  16.6 2.5 collective-permute-done
  19.2 5.0 collective-permute-start.1
  24.3 10.6 %collective-permute-done.1 = f32[125,2,2,128]{0,3,2,1:T(8,128)S(1)} collective-permute-done((f32[125,2,2,128]{0,3,2,1:T(8,128)S(1)}, f32[125,2,2,128]{0,3,2,1:T(8,128)S(1)}, u32[]{:S(2)}, u32[]{:S(2)}) %collective-permute-start.1) | collective-permute-done | bytes 256032 | tf_op jit(solution)/shard_map/ppermute | solution.py:31
  35.3 7.1 %collective-permute-done.2 = f32[125,2,2,128]{0,3,2,1:T(8,128)S(1)} collective-permute-done((f32[125,2,2,128]{0,3,2,1:T(8,128)S(1)}, f32[125,2,2,128]{0,3,2,1:T(8,128)S(1)}, u32[]{:S(2)}, u32[]{:S(2)}) %collective-permute-start.2) | collective-permute-done | bytes 256032 | tf_op jit(solution)/shard_map/ppermute | solution.py:31
  42.5 2.8 collective-permute-start.3
  45.5 5.0 collective-permute-done.3
  52.3 3.6 collective-permute-done.4
  56.0 3.6 collective-permute-start.5
  67.0 2.3 collective-permute-done.6
  74.1 2.1 collective-permute-done.8
  81.9 2.4 collective-permute-done.10
  89.6 2.3 collective-permute-done.12
  95.3 2.4 collective-permute-start.15
  105.4 2.3 collective-permute-done.16
  113.1 2.6 collective-permute-done.18
  118.6 9.2 %collective-permute-start.20 = (f32[125,2,2,128]{0,3,2,1:T(8,128)S(1)}, f32[125,2,2,128]{0,3,2,1:T(8,128)S(1)}, u32[]{:S(2)}, u32[]{:S(2)}) collective-permute-start(f32[125,2,2,128]{0,3,2,1:T(8,128)S(1)} %pad_maximum_fusion.77), channel_id=1, source_target_pairs={{0,4},{4,0},{8,12},{12,8},{16,20},{20,16},{24,28},{28,24},{32,36},... | collective-permute-start | bytes 768008 | tf_op jit(solution)/shard_map/ppermute | solution.py:31
  130.6 6.1 %collective-permute-done.21 = f32[125,2,2,128]{0,3,2,1:T(8,128)S(1)} collective-permute-done((f32[125,2,2,128]{0,3,2,1:T(8,128)S(1)}, f32[125,2,2,128]{0,3,2,1:T(8,128)S(1)}, u32[]{:S(2)}, u32[]{:S(2)}) %collective-permute-start.21) | collective-permute-done | bytes 256032 | tf_op jit(solution)/shard_map/ppermute | solution.py:31
  136.8 2.8 collective-permute-start.22
  139.8 5.2 collective-permute-done.22
  146.1 4.9 collective-permute-done.23
  151.9 13.4 %collective-permute-done.24 = f32[125,2,2,128]{0,3,2,1:T(8,128)S(1)} collective-permute-done((f32[125,2,2,128]{0,3,2,1:T(8,128)S(1)}, f32[125,2,2,128]{0,3,2,1:T(8,128)S(1)}, u32[]{:S(2)}, u32[]{:S(2)}) %collective-permute-start.24) | collective-permute-done | bytes 256032 | tf_op jit(solution)/shard_map/ppermute | solution.py:31
  165.4 6.2 %collective-permute-start.25 = (f32[125,2,128]{0,2,1:T(8,128)S(1)}, f32[125,2,128]{0,2,1:T(8,128)S(1)}, u32[]{:S(2)}, u32[]{:S(2)}) collective-permute-start(f32[125,2,128]{0,2,1:T(8,128)S(1)} %fusion.53), channel_id=1, source_target_pairs={{0,128},{4,132},{8,136},{12,140},{16,144},{20,148},{24,152},{28,15... | collective-permute-start | bytes 384008 | tf_op jit(solution)/shard_map/ppermute | solution.py:31
  171.7 2.3 collective-permute-done.25
  174.8 176.8 %all-reduce.30.cloned.1.call-done = f32[125,2,128]{0,2,1:T(8,128)} async-done(((f32[125,2,128]{0,2,1:T(8,128)}), f32[125,2,128]{0,2,1:T(8,128)}) %all-reduce.30.cloned.1.call-update) | async-done | bytes 128016 | tf_op jit(solution)/shard_map/psum | solution.py:36
  353.0 10.7 %collective-permute-done.26 = f32[125,2,128]{0,2,1:T(8,128)S(1)} collective-permute-done((f32[125,2,128]{0,2,1:T(8,128)S(1)}, f32[125,2,128]{0,2,1:T(8,128)S(1)}, u32[]{:S(2)}, u32[]{:S(2)}) %collective-permute-start.26) | collective-permute-done | bytes 128032 | tf_op jit(solution)/shard_map/ppermute | solution.py:31
  363.8 12.4 %collective-permute-done.27 = f32[125,2,2,128]{0,3,2,1:T(8,128)S(1)} collective-permute-done((f32[125,2,2,128]{0,3,2,1:T(8,128)S(1)}, f32[125,2,2,128]{0,3,2,1:T(8,128)S(1)}, u32[]{:S(2)}, u32[]{:S(2)}) %collective-permute-start.27) | collective-permute-done | bytes 256032 | tf_op jit(solution)/shard_map/ppermute | solution.py:31
  376.4 7.2 %collective-permute-done.28 = f32[125,2,2,128]{0,3,2,1:T(8,128)S(1)} collective-permute-done((f32[125,2,2,128]{0,3,2,1:T(8,128)S(1)}, f32[125,2,2,128]{0,3,2,1:T(8,128)S(1)}, u32[]{:S(2)}, u32[]{:S(2)}) %collective-permute-start.28) | collective-permute-done | bytes 256032 | tf_op jit(solution)/shard_map/ppermute | solution.py:31
  383.7 4.0 collective-permute-start.29
  387.7 5.3 %collective-permute-done.29 = f32[125,2,2,128]{0,3,2,1:T(8,128)S(1)} collective-permute-done((f32[125,2,2,128]{0,3,2,1:T(8,128)S(1)}, f32[125,2,2,128]{0,3,2,1:T(8,128)S(1)}, u32[]{:S(2)}, u32[]{:S(2)}) %collective-permute-start.29) | collective-permute-done | bytes 256032 | tf_op jit(solution)/shard_map/ppermute | solution.py:31
  394.1 4.9 collective-permute-done.30
  399.1 3.0 collective-permute-start.31
  406.3 3.2 collective-permute-done.32
  413.1 2.0 collective-permute-start.35
  415.1 2.2 collective-permute-done.34
  422.8 2.3 collective-permute-done.36
  430.5 2.3 collective-permute-done.38
  436.3 2.1 collective-permute-start.41
  438.4 2.0 collective-permute-done.40
  446.1 2.3 collective-permute-done.42
  453.8 3.0 collective-permute-done.44
  459.7 9.2 %collective-permute-start.46 = (f32[125,2,2,128]{0,3,2,1:T(8,128)S(1)}, f32[125,2,2,128]{0,3,2,1:T(8,128)S(1)}, u32[]{:S(2)}, u32[]{:S(2)}) collective-permute-start(f32[125,2,2,128]{0,3,2,1:T(8,128)S(1)} %pad_maximum_fusion.87), channel_id=1, source_target_pairs={{0,4},{4,0},{8,12},{12,8},{16,20},{20,16},{24,28},{28,24},{32,36},... | collective-permute-start | bytes 768008 | tf_op jit(solution)/shard_map/ppermute | solution.py:31
  471.6 6.3 %collective-permute-done.47 = f32[125,2,2,128]{0,3,2,1:T(8,128)S(1)} collective-permute-done((f32[125,2,2,128]{0,3,2,1:T(8,128)S(1)}, f32[125,2,2,128]{0,3,2,1:T(8,128)S(1)}, u32[]{:S(2)}, u32[]{:S(2)}) %collective-permute-start.47) | collective-permute-done | bytes 256032 | tf_op jit(solution)/shard_map/ppermute | solution.py:31
  477.9 2.8 collective-permute-start.48
  480.7 5.4 %collective-permute-done.48 = f32[125,2,2,128]{0,3,2,1:T(8,128)S(1)} collective-permute-done((f32[125,2,2,128]{0,3,2,1:T(8,128)S(1)}, f32[125,2,2,128]{0,3,2,1:T(8,128)S(1)}, u32[]{:S(2)}, u32[]{:S(2)}) %collective-permute-start.48) | collective-permute-done | bytes 256032 | tf_op jit(solution)/shard_map/ppermute | solution.py:31
  487.0 5.0 collective-permute-done.49
  492.5 13.8 %collective-permute-done.50 = f32[125,2,2,128]{0,3,2,1:T(8,128)S(1)} collective-permute-done((f32[125,2,2,128]{0,3,2,1:T(8,128)S(1)}, f32[125,2,2,128]{0,3,2,1:T(8,128)S(1)}, u32[]{:S(2)}, u32[]{:S(2)}) %collective-permute-start.50) | collective-permute-done | bytes 256032 | tf_op jit(solution)/shard_map/ppermute | solution.py:31
  506.6 7.7 %collective-permute-done.51 = f32[125,2,128]{0,2,1:T(8,128)S(1)} collective-permute-done((f32[125,2,128]{0,2,1:T(8,128)S(1)}, f32[125,2,128]{0,2,1:T(8,128)S(1)}, u32[]{:S(2)}, u32[]{:S(2)}) %collective-permute-start.51) | collective-permute-done | bytes 128032 | tf_op jit(solution)/shard_map/ppermute | solution.py:31
  (317 shorter events, 94.6 us)
Async XLA Ops:
  6.5 345.1 %all-reduce.30.cloned.1.call-start = ((), (), s32[]{:S(2)}) async-start(), calls=%async_computation | async-start | bytes 262144 | tf_op jit(solution)/shard_map/psum | solution.py:36
  8.6 10.5 %collective-permute-start = (f32[125,2,128]{0,2,1:T(8,128)S(1)}, f32[125,2,128]{0,2,1:T(8,128)S(1)}, u32[]{:S(2)}, u32[]{:S(2)}) collective-permute-start(f32[125,2,128]{0,2,1:T(8,128)S(1)} %fusion.71), channel_id=1, source_target_pairs={{0,128},{4,132},{8,136},{12,140},{16,144},{20,148},{24,152},{28,15... | collective-permute-start | bytes 384008 | tf_op jit(solution)/shard_map/ppermute | solution.py:31
  19.2 15.7 %collective-permute-start.1 = (f32[125,2,2,128]{0,3,2,1:T(8,128)S(1)}, f32[125,2,2,128]{0,3,2,1:T(8,128)S(1)}, u32[]{:S(2)}, u32[]{:S(2)}) collective-permute-start(f32[125,2,2,128]{0,3,2,1:T(8,128)S(1)} %pad_maximum_fusion.72), channel_id=1, source_target_pairs={{0,64},{4,68},{8,72},{12,76},{16,80},{20,84},{24,88},{28,92},{32,9... | collective-permute-start | bytes 768008 | tf_op jit(solution)/shard_map/ppermute | solution.py:31
  35.0 7.4 %collective-permute-start.2 = (f32[125,2,2,128]{0,3,2,1:T(8,128)S(1)}, f32[125,2,2,128]{0,3,2,1:T(8,128)S(1)}, u32[]{:S(2)}, u32[]{:S(2)}) collective-permute-start(f32[125,2,2,128]{0,3,2,1:T(8,128)S(1)} %pad_maximum_fusion.73), channel_id=1, source_target_pairs={{0,32},{4,36},{8,40},{12,44},{16,48},{20,52},{24,56},{28,60},{32,0... | collective-permute-start | bytes 768008 | tf_op jit(solution)/shard_map/ppermute | solution.py:31
  42.5 7.9 %collective-permute-start.3 = (f32[125,2,2,128]{0,3,2,1:T(8,128)S(1)}, f32[125,2,2,128]{0,3,2,1:T(8,128)S(1)}, u32[]{:S(2)}, u32[]{:S(2)}) collective-permute-start(f32[125,2,2,128]{0,3,2,1:T(8,128)S(1)} %pad_maximum_fusion.74), channel_id=1, source_target_pairs={{0,16},{4,20},{8,24},{12,28},{16,0},{20,4},{24,8},{28,12},{32,48},... | collective-permute-start | bytes 768008 | tf_op jit(solution)/shard_map/ppermute | solution.py:31
  50.6 5.3 %collective-permute-start.4 = (f32[125,2,2,128]{0,3,2,1:T(8,128)S(1)}, f32[125,2,2,128]{0,3,2,1:T(8,128)S(1)}, u32[]{:S(2)}, u32[]{:S(2)}) collective-permute-start(f32[125,2,2,128]{0,3,2,1:T(8,128)S(1)} %pad_maximum_fusion.75), channel_id=1, source_target_pairs={{0,8},{4,12},{8,0},{12,4},{16,24},{20,28},{24,16},{28,20},{32,40},... | collective-permute-start | bytes 768008 | tf_op jit(solution)/shard_map/ppermute | solution.py:31
  56.0 5.8 %collective-permute-start.5 = (f32[125,2,2,128]{0,3,2,1:T(8,128)S(1)}, f32[125,2,2,128]{0,3,2,1:T(8,128)S(1)}, u32[]{:S(2)}, u32[]{:S(2)}) collective-permute-start(f32[125,2,2,128]{0,3,2,1:T(8,128)S(1)} %pad_maximum_fusion.76), channel_id=1, source_target_pairs={{0,4},{4,0},{8,12},{12,8},{16,20},{20,16},{24,28},{28,24},{32,36},... | collective-permute-start | bytes 768008 | tf_op jit(solution)/shard_map/ppermute | solution.py:31
  62.8 6.5 %collective-permute-start.6 = (f32[125,2,1,128]{0,3,2,1:T(8,128)S(1)}, f32[125,2,1,128]{0,3,2,1:T(8,128)S(1)}, u32[]{:S(2)}, u32[]{:S(2)}) collective-permute-start(f32[125,2,1,128]{0,3,2,1:T(8,128)S(1)} %get-tuple-element.177), channel_id=1, source_target_pairs={{0,1},{1,2},{2,3},{3,0},{4,5},{5,6},{6,7},{7,4},{8,9},{9,10},{10,1... | collective-permute-start | bytes 384008 | tf_op jit(solution)/shard_map/ppermute | solution.py:22
  65.5 4.8 collective-permute-start.7
  71.0 5.2 collective-permute-start.8
  72.4 4.3 collective-permute-start.9
  79.2 5.1 collective-permute-start.10
  86.8 5.1 collective-permute-start.12
  94.4 5.2 collective-permute-start.14
  95.3 4.3 collective-permute-start.15
  102.1 5.5 %collective-permute-start.16 = (f32[125,2,1,128]{0,3,2,1:T(8,128)S(1)}, f32[125,2,1,128]{0,3,2,1:T(8,128)S(1)}, u32[]{:S(2)}, u32[]{:S(2)}) collective-permute-start(f32[125,2,1,128]{0,3,2,1:T(8,128)S(1)} %get-tuple-element.154), channel_id=1, source_target_pairs={{0,1},{1,2},{2,3},{3,0},{4,5},{5,6},{6,7},{7,4},{8,9},{9,10},{10,1... | collective-permute-start | bytes 384008 | tf_op jit(solution)/shard_map/ppermute | solution.py:22
  103.5 4.1 collective-permute-start.17
  110.1 5.5 %collective-permute-start.18 = (f32[125,2,1,128]{0,3,2,1:T(8,128)S(1)}, f32[125,2,1,128]{0,3,2,1:T(8,128)S(1)}, u32[]{:S(2)}, u32[]{:S(2)}) collective-permute-start(f32[125,2,1,128]{0,3,2,1:T(8,128)S(1)} %get-tuple-element.149), channel_id=1, source_target_pairs={{0,1},{1,2},{2,3},{3,0},{4,5},{5,6},{6,7},{7,4},{8,9},{9,10},{10,1... | collective-permute-start | bytes 384008 | tf_op jit(solution)/shard_map/ppermute | solution.py:22
  111.2 4.8 collective-permute-start.19
  118.6 10.4 %collective-permute-start.20 = (f32[125,2,2,128]{0,3,2,1:T(8,128)S(1)}, f32[125,2,2,128]{0,3,2,1:T(8,128)S(1)}, u32[]{:S(2)}, u32[]{:S(2)}) collective-permute-start(f32[125,2,2,128]{0,3,2,1:T(8,128)S(1)} %pad_maximum_fusion.77), channel_id=1, source_target_pairs={{0,4},{4,0},{8,12},{12,8},{16,20},{20,16},{24,28},{28,24},{32,36},... | collective-permute-start | bytes 768008 | tf_op jit(solution)/shard_map/ppermute | solution.py:31
  129.1 7.6 %collective-permute-start.21 = (f32[125,2,2,128]{0,3,2,1:T(8,128)S(1)}, f32[125,2,2,128]{0,3,2,1:T(8,128)S(1)}, u32[]{:S(2)}, u32[]{:S(2)}) collective-permute-start(f32[125,2,2,128]{0,3,2,1:T(8,128)S(1)} %pad_maximum_fusion.78), channel_id=1, source_target_pairs={{0,8},{4,12},{8,0},{12,4},{16,24},{20,28},{24,16},{28,20},{32,40},... | collective-permute-start | bytes 768008 | tf_op jit(solution)/shard_map/ppermute | solution.py:31
  136.8 8.2 %collective-permute-start.22 = (f32[125,2,2,128]{0,3,2,1:T(8,128)S(1)}, f32[125,2,2,128]{0,3,2,1:T(8,128)S(1)}, u32[]{:S(2)}, u32[]{:S(2)}) collective-permute-start(f32[125,2,2,128]{0,3,2,1:T(8,128)S(1)} %pad_maximum_fusion.79), channel_id=1, source_target_pairs={{0,16},{4,20},{8,24},{12,28},{16,0},{20,4},{24,8},{28,12},{32,48},... | collective-permute-start | bytes 768008 | tf_op jit(solution)/shard_map/ppermute | solution.py:31
  145.1 5.9 %collective-permute-start.23 = (f32[125,2,2,128]{0,3,2,1:T(8,128)S(1)}, f32[125,2,2,128]{0,3,2,1:T(8,128)S(1)}, u32[]{:S(2)}, u32[]{:S(2)}) collective-permute-start(f32[125,2,2,128]{0,3,2,1:T(8,128)S(1)} %pad_maximum_fusion.80), channel_id=1, source_target_pairs={{0,32},{4,36},{8,40},{12,44},{16,48},{20,52},{24,56},{28,60},{32,0... | collective-permute-start | bytes 768008 | tf_op jit(solution)/shard_map/ppermute | solution.py:31
  151.2 14.2 %collective-permute-start.24 = (f32[125,2,2,128]{0,3,2,1:T(8,128)S(1)}, f32[125,2,2,128]{0,3,2,1:T(8,128)S(1)}, u32[]{:S(2)}, u32[]{:S(2)}) collective-permute-start(f32[125,2,2,128]{0,3,2,1:T(8,128)S(1)} %pad_maximum_fusion.81), channel_id=1, source_target_pairs={{0,64},{4,68},{8,72},{12,76},{16,80},{20,84},{24,88},{28,92},{32,9... | collective-permute-start | bytes 768008 | tf_op jit(solution)/shard_map/ppermute | solution.py:31
  165.4 8.6 %collective-permute-start.25 = (f32[125,2,128]{0,2,1:T(8,128)S(1)}, f32[125,2,128]{0,2,1:T(8,128)S(1)}, u32[]{:S(2)}, u32[]{:S(2)}) collective-permute-start(f32[125,2,128]{0,2,1:T(8,128)S(1)} %fusion.53), channel_id=1, source_target_pairs={{0,128},{4,132},{8,136},{12,140},{16,144},{20,148},{24,152},{28,15... | collective-permute-start | bytes 384008 | tf_op jit(solution)/shard_map/ppermute | solution.py:31
  352.6 11.1 %collective-permute-start.26 = (f32[125,2,128]{0,2,1:T(8,128)S(1)}, f32[125,2,128]{0,2,1:T(8,128)S(1)}, u32[]{:S(2)}, u32[]{:S(2)}) collective-permute-start(f32[125,2,128]{0,2,1:T(8,128)S(1)} %fusion.69), channel_id=1, source_target_pairs={{0,128},{4,132},{8,136},{12,140},{16,144},{20,148},{24,152},{28,15... | collective-permute-start | bytes 384008 | tf_op jit(solution)/shard_map/ppermute | solution.py:31
  363.7 12.5 %collective-permute-start.27 = (f32[125,2,2,128]{0,3,2,1:T(8,128)S(1)}, f32[125,2,2,128]{0,3,2,1:T(8,128)S(1)}, u32[]{:S(2)}, u32[]{:S(2)}) collective-permute-start(f32[125,2,2,128]{0,3,2,1:T(8,128)S(1)} %pad_maximum_fusion.82), channel_id=1, source_target_pairs={{0,64},{4,68},{8,72},{12,76},{16,80},{20,84},{24,88},{28,92},{32,9... | collective-permute-start | bytes 768008 | tf_op jit(solution)/shard_map/ppermute | solution.py:31
  376.3 7.3 %collective-permute-start.28 = (f32[125,2,2,128]{0,3,2,1:T(8,128)S(1)}, f32[125,2,2,128]{0,3,2,1:T(8,128)S(1)}, u32[]{:S(2)}, u32[]{:S(2)}) collective-permute-start(f32[125,2,2,128]{0,3,2,1:T(8,128)S(1)} %pad_maximum_fusion.83), channel_id=1, source_target_pairs={{0,32},{4,36},{8,40},{12,44},{16,48},{20,52},{24,56},{28,60},{32,0... | collective-permute-start | bytes 768008 | tf_op jit(solution)/shard_map/ppermute | solution.py:31
  383.7 9.3 %collective-permute-start.29 = (f32[125,2,2,128]{0,3,2,1:T(8,128)S(1)}, f32[125,2,2,128]{0,3,2,1:T(8,128)S(1)}, u32[]{:S(2)}, u32[]{:S(2)}) collective-permute-start(f32[125,2,2,128]{0,3,2,1:T(8,128)S(1)} %pad_maximum_fusion.84), channel_id=1, source_target_pairs={{0,16},{4,20},{8,24},{12,28},{16,0},{20,4},{24,8},{28,12},{32,48},... | collective-permute-start | bytes 768008 | tf_op jit(solution)/shard_map/ppermute | solution.py:31
  393.1 5.9 %collective-permute-start.30 = (f32[125,2,2,128]{0,3,2,1:T(8,128)S(1)}, f32[125,2,2,128]{0,3,2,1:T(8,128)S(1)}, u32[]{:S(2)}, u32[]{:S(2)}) collective-permute-start(f32[125,2,2,128]{0,3,2,1:T(8,128)S(1)} %pad_maximum_fusion.85), channel_id=1, source_target_pairs={{0,8},{4,12},{8,0},{12,4},{16,24},{20,28},{24,16},{28,20},{32,40},... | collective-permute-start | bytes 768008 | tf_op jit(solution)/shard_map/ppermute | solution.py:31
  399.1 4.1 collective-permute-start.31
  403.6 6.0 %collective-permute-start.32 = (f32[125,2,1,128]{0,3,2,1:T(8,128)S(1)}, f32[125,2,1,128]{0,3,2,1:T(8,128)S(1)}, u32[]{:S(2)}, u32[]{:S(2)}) collective-permute-start(f32[125,2,1,128]{0,3,2,1:T(8,128)S(1)} %get-tuple-element.126), channel_id=1, source_target_pairs={{0,1},{1,2},{2,3},{3,0},{4,5},{5,6},{6,7},{7,4},{8,9},{9,10},{10,1... | collective-permute-start | bytes 384008 | tf_op jit(solution)/shard_map/ppermute | solution.py:22
  404.9 4.7 collective-permute-start.33
  412.2 5.1 collective-permute-start.34
  413.1 4.2 collective-permute-start.35
  419.8 5.3 %collective-permute-start.36 = (f32[125,2,1,128]{0,3,2,1:T(8,128)S(1)}, f32[125,2,1,128]{0,3,2,1:T(8,128)S(1)}, u32[]{:S(2)}, u32[]{:S(2)}) collective-permute-start(f32[125,2,1,128]{0,3,2,1:T(8,128)S(1)} %get-tuple-element.116), channel_id=1, source_target_pairs={{0,1},{1,2},{2,3},{3,0},{4,5},{5,6},{6,7},{7,4},{8,9},{9,10},{10,1... | collective-permute-start | bytes 384008 | tf_op jit(solution)/shard_map/ppermute | solution.py:22
  420.9 4.2 collective-permute-start.37
  427.6 5.2 collective-permute-start.38
  435.2 5.2 collective-permute-start.40
  442.9 5.4 %collective-permute-start.42 = (f32[125,2,1,128]{0,3,2,1:T(8,128)S(1)}, f32[125,2,1,128]{0,3,2,1:T(8,128)S(1)}, u32[]{:S(2)}, u32[]{:S(2)}) collective-permute-start(f32[125,2,1,128]{0,3,2,1:T(8,128)S(1)} %get-tuple-element.101), channel_id=1, source_target_pairs={{0,1},{1,2},{2,3},{3,0},{4,5},{5,6},{6,7},{7,4},{8,9},{9,10},{10,1... | collective-permute-start | bytes 384008 | tf_op jit(solution)/shard_map/ppermute | solution.py:22
  450.9 5.9 %collective-permute-start.44 = (f32[125,2,1,128]{0,3,2,1:T(8,128)S(1)}, f32[125,2,1,128]{0,3,2,1:T(8,128)S(1)}, u32[]{:S(2)}, u32[]{:S(2)}) collective-permute-start(f32[125,2,1,128]{0,3,2,1:T(8,128)S(1)} %get-tuple-element.96), channel_id=1, source_target_pairs={{0,1},{1,2},{2,3},{3,0},{4,5},{5,6},{6,7},{7,4},{8,9},{9,10},{10,1... | collective-permute-start | bytes 384008 | tf_op jit(solution)/shard_map/ppermute | solution.py:22
  451.9 5.3 %collective-permute-start.45 = (f32[125,2,1,128]{0,3,2,1:T(8,128)S(1)}, f32[125,2,1,128]{0,3,2,1:T(8,128)S(1)}, u32[]{:S(2)}, u32[]{:S(2)}) collective-permute-start(f32[125,2,1,128]{0,3,2,1:T(8,128)S(1)} %get-tuple-element.97), channel_id=1, source_target_pairs={{1,0},{2,1},{3,2},{0,3},{5,4},{6,5},{7,6},{4,7},{9,8},{10,9},{11,1... | collective-permute-start | bytes 384008 | tf_op jit(solution)/shard_map/ppermute | solution.py:25
  459.7 10.4 %collective-permute-start.46 = (f32[125,2,2,128]{0,3,2,1:T(8,128)S(1)}, f32[125,2,2,128]{0,3,2,1:T(8,128)S(1)}, u32[]{:S(2)}, u32[]{:S(2)}) collective-permute-start(f32[125,2,2,128]{0,3,2,1:T(8,128)S(1)} %pad_maximum_fusion.87), channel_id=1, source_target_pairs={{0,4},{4,0},{8,12},{12,8},{16,20},{20,16},{24,28},{28,24},{32,36},... | collective-permute-start | bytes 768008 | tf_op jit(solution)/shard_map/ppermute | solution.py:31
  470.2 7.6 %collective-permute-start.47 = (f32[125,2,2,128]{0,3,2,1:T(8,128)S(1)}, f32[125,2,2,128]{0,3,2,1:T(8,128)S(1)}, u32[]{:S(2)}, u32[]{:S(2)}) collective-permute-start(f32[125,2,2,128]{0,3,2,1:T(8,128)S(1)} %pad_maximum_fusion.88), channel_id=1, source_target_pairs={{0,8},{4,12},{8,0},{12,4},{16,24},{20,28},{24,16},{28,20},{32,40},... | collective-permute-start | bytes 768008 | tf_op jit(solution)/shard_map/ppermute | solution.py:31
  477.9 8.2 %collective-permute-start.48 = (f32[125,2,2,128]{0,3,2,1:T(8,128)S(1)}, f32[125,2,2,128]{0,3,2,1:T(8,128)S(1)}, u32[]{:S(2)}, u32[]{:S(2)}) collective-permute-start(f32[125,2,2,128]{0,3,2,1:T(8,128)S(1)} %pad_maximum_fusion.89), channel_id=1, source_target_pairs={{0,16},{4,20},{8,24},{12,28},{16,0},{20,4},{24,8},{28,12},{32,48},... | collective-permute-start | bytes 768008 | tf_op jit(solution)/shard_map/ppermute | solution.py:31
  486.2 5.8 %collective-permute-start.49 = (f32[125,2,2,128]{0,3,2,1:T(8,128)S(1)}, f32[125,2,2,128]{0,3,2,1:T(8,128)S(1)}, u32[]{:S(2)}, u32[]{:S(2)}) collective-permute-start(f32[125,2,2,128]{0,3,2,1:T(8,128)S(1)} %pad_maximum_fusion.90), channel_id=1, source_target_pairs={{0,32},{4,36},{8,40},{12,44},{16,48},{20,52},{24,56},{28,60},{32,0... | collective-permute-start | bytes 768008 | tf_op jit(solution)/shard_map/ppermute | solution.py:31
  492.1 14.2 %collective-permute-start.50 = (f32[125,2,2,128]{0,3,2,1:T(8,128)S(1)}, f32[125,2,2,128]{0,3,2,1:T(8,128)S(1)}, u32[]{:S(2)}, u32[]{:S(2)}) collective-permute-start(f32[125,2,2,128]{0,3,2,1:T(8,128)S(1)} %pad_maximum_fusion.91), channel_id=1, source_target_pairs={{0,64},{4,68},{8,72},{12,76},{16,80},{20,84},{24,88},{28,92},{32,9... | collective-permute-start | bytes 768008 | tf_op jit(solution)/shard_map/ppermute | solution.py:31
  506.4 7.9 %collective-permute-start.51 = (f32[125,2,128]{0,2,1:T(8,128)S(1)}, f32[125,2,128]{0,2,1:T(8,128)S(1)}, u32[]{:S(2)}, u32[]{:S(2)}) collective-permute-start(f32[125,2,128]{0,2,1:T(8,128)S(1)} %fusion.37), channel_id=1, source_target_pairs={{0,128},{4,132},{8,136},{12,140},{16,144},{20,148},{24,152},{28,15... | collective-permute-start | bytes 384008 | tf_op jit(solution)/shard_map/ppermute | solution.py:31
  (9 other events, 24.9 us)
Sparse Core Ops, SparseCore 0:
  174.8 176.7 all-reduce.29
where the time goes:
time: 531 us; the launch traced here: 522 us
  waiting for transfers between devices  354 us (67%)
  starting transfers between devices  107 us (20%)
  matrix products  21.5 us (4%)
  between operations  17.8 us (3%)
  local copies, waits for them, and re-layouts  12.4 us (2%)
  other arithmetic  9.4 us (2%)
    psum x1, waiting for transfers between devices, from_root(): return lax.psum(block, axis)  177 us
    ppermute x24, waiting for transfers between devices, swapped(): lax.ppermute(shard, axis, [(i, i ^ 1 << bit) for i in range(lax.axis_size...  143 us
    ppermute x24, starting transfers between devices, swapped(): lax.ppermute(shard, axis, [(i, i ^ 1 << bit) for i in range(lax.axis_size...  65 us
    ppermute x14, waiting for transfers between devices, padded(): lax.ppermute(lax.slice_in_dim(block, block.shape[dim] - width, None, axis...  32.9 us
    ppermute x14, starting transfers between devices, padded(): lax.ppermute(lax.slice_in_dim(block, 0, width, axis=dim), axis, backward)  25.6 us
    dot_general x42, matrix products, product(): jnp.dot(left, right, precision=lax.Precision.HIGHEST, preferred_element_t...  21.5 us
    ppermute x14, starting transfers between devices, padded(): lax.ppermute(lax.slice_in_dim(block, block.shape[dim] - width, None, axis...  16.4 us
  transfers between devices with their start and end apart: 53, of which 43 were waited for; matrix products, arithmetic and copies ran while one was open for 1% of the time, Pallas kernels for 0%

commit v1 on v0

v1 whole, which is shorter than its diff:
```python
import math

import jax
import jax.numpy as jnp
import numpy as np
from jax import lax
from jax.experimental import pallas as pl
from jax.experimental.pallas import tpu as pltpu
from jax.sharding import Mesh
from jax.sharding import PartitionSpec as P

NB = 125
SWEEPS = 8
STEPS = 64
LANES = 128
FREQS = STEPS // 2
CHUNK = 16
WINDOW = 32
HALO = 8
ES_LANE = NB

circ_alpha = 0.01
damping = 0.7

TIME = ("z", "x", "core")
PLANE = ("x", "core", "y")


def tables():
    n = np.arange(STEPS)
    log_alpha = math.log(circ_alpha)
    grow = np.exp(n * (log_alpha / STEPS))
    forward = np.zeros((STEPS, STEPS))
    backward = np.zeros((STEPS, STEPS))
    shifts = np.zeros((FREQS, 4))
    root = math.exp(log_alpha / STEPS)
    forward[0] = 1.0
    forward[1] = (-1.0) ** n
    backward[:, 0] = 1.0
    backward[:, 1] = (-1.0) ** n
    shifts[0] = (1.0 - root, 1.0 + root, 0.0, 0.0)
    for k in range(1, FREQS):
        angle = 2.0 * math.pi * ((k * n) % STEPS) / STEPS
        forward[2 * k] = np.cos(angle)
        forward[2 * k + 1] = -np.sin(angle)
        backward[:, 2 * k] = 2.0 * np.cos(angle)
        backward[:, 2 * k + 1] = -2.0 * np.sin(angle)
        theta = 2.0 * math.pi * k / STEPS
        shifts[k, :3] = (1.0 - root * math.cos(theta), 1.0 - root * math.cos(theta), root * math.sin(theta))
    forward = forward * grow[None, :]
    backward = backward / grow[:, None] / STEPS
    carry = 0.5 * forward.sum(1) + forward[:, 0]
    last = backward[STEPS - 1]
    return tuple(a.astype(np.float32) for a in (forward, backward, shifts, carry, last))


FORWARD, BACKWARD, SHIFTS, CARRY, LAST = tables()
LAST_ROWS = np.repeat(LAST.reshape(FREQS, 2, 1), 4, axis=1).reshape(FREQS, 8, 1)

VMEM = pl.BlockSpec(memory_space=pltpu.VMEM)
SMEM = pl.BlockSpec(memory_space=pltpu.SMEM)
PARAMS = pltpu.CompilerParams(vmem_limit_bytes=32 * 1024 * 1024)


def exact(left, right):
    return jnp.dot(left, right, precision=lax.Precision.HIGHEST, preferred_element_type=jnp.float32)


def pack_kernel(forcing, init, scale, out, rows, flip):
    step = lax.axis_index("z") * 8 + lax.axis_index("x") * 2 + lax.axis_index("core")
    weight = jnp.where(step == 0, 1.5, 0.5).astype(jnp.float32)
    rows[NB:, :] = jnp.zeros((LANES - NB, LANES), jnp.float32)
    for s in range(2):
        for r in range(2):
            value = forcing[s, 0, :, r, :]
            if s == 0:
                value = value + weight * init[:, r, :]
            rows[:NB, :] = value
            rows[ES_LANE : ES_LANE + 1, :] = scale[r : r + 1, :]
            flip[...] = rows[...].T
            for c in range(2):
                out[pl.ds(s * 8 + c * 2 + r, STEPS, stride=16), :] = flip[pl.ds(c, STEPS, stride=2), :]
    blank = jnp.zeros((4, LANES), jnp.float32)
    for m in range(STEPS):
        source = m - 4 if m % 8 < 4 else m + 4
        for s in range(2):
            at = m * 16 + s * 8 + 4
            if 0 <= source < STEPS:
                out[at : at + 4, :] = out[source * 16 + s * 8 : source * 16 + s * 8 + 4, :]
            else:
                out[at : at + 4, :] = blank


def forward_kernel(table, got, out0, out1):
    lane = lax.broadcasted_iota(jnp.int32, (STEPS, LANES), 1)
    for s, out in enumerate((out0, out1)):
        parts = [got[pl.ds(s * 8 + p, STEPS, stride=16), :] for p in range(8)]
        waves = exact(table[...], jnp.concatenate(parts, axis=1))
        for p in range(8):
            wave = waves[:, p * LANES : (p + 1) * LANES]
            wave = jnp.where(lane == ES_LANE, jnp.broadcast_to(parts[p][:1, :], wave.shape), wave)
            out[pl.ds(p, STEPS, stride=8), :] = wave


def operator_kernel(vol, faces, out, diag, square):
    square[...] = jnp.zeros((LANES, LANES), jnp.float32)
    row = lax.broadcasted_iota(jnp.int32, (LANES, LANES), 0)
    col = lax.broadcasted_iota(jnp.int32, (LANES, LANES), 1)
    for op in range(5):
        square[:NB, :NB] = vol[...] if op == 0 else faces[op - 1]
        value = square[...]
        if op == 0:
            on = jnp.where(row == col, value, 0.0)
            diag[...] = jnp.broadcast_to(jnp.sum(on, axis=0, keepdims=True), (8, LANES))
            value = value - on
        value = value.T
        high = value.astype(jnp.bfloat16)
        low = (value - high.astype(jnp.float32)).astype(jnp.bfloat16)
        at = op * LANES
        out[:LANES, at : at + LANES] = high
        out[LANES : 2 * LANES, at : at + LANES] = high
        out[2 * LANES :, at : at + LANES] = low


def solve_kernel(shifts, ops, diag, got, out, iterate, source, inverse):
    kappa = lax.axis_index("x") * 8 + lax.axis_index("core") * 4 + lax.axis_index("y")
    for xc in range(8):
        for yd in range(4):
            for c in range(2):
                for col in range(4):
                    w = HALO + 2 * xc + col
                    if col >= 2:
                        w = (2 * xc if xc < 4 else 16 + 2 * xc) + col - 2
                    at = c * 8 + col * 2
                    iterate[c, w, 2 * yd : 2 * yd + 2, :] = got[xc * 4 + yd, at : at + 2, :]
    shape = (WINDOW, 8, LANES)
    scale = jnp.broadcast_to(iterate[0, :, :, ES_LANE : ES_LANE + 1], shape)
    lane = lax.broadcasted_iota(jnp.int32, shape, 2)
    place = lax.axis_index("z") * CHUNK - HALO + lax.broadcasted_iota(jnp.int32, shape, 0)
    inside = jnp.logical_and(place >= 0, place < 8 * CHUNK)
    scaled = scale * diag[...][None]
    im = shifts[kappa, 2]
    re0 = shifts[kappa, 0] + scaled
    re1 = shifts[kappa, 1] + scaled
    mod0 = jnp.where(inside, damping / (re0 * re0 + im * im), 0.0)
    mod1 = jnp.where(inside, damping / (re1 * re1 + im * im), 0.0)
    inverse[0] = re0 * mod0
    inverse[1] = re1 * mod1
    inverse[2] = im * mod0
    inverse[3] = scale
    g0 = jnp.where(lane < NB, iterate[0], 0.0)
    g1 = jnp.where(lane < NB, iterate[1], 0.0)
    source[0] = inverse[0] * g0 + inverse[2] * g1
    source[1] = inverse[1] * g1 - inverse[2] * g0
    iterate[0] = source[0]
    iterate[1] = source[1]
    for sweep in range(1, SWEEPS):
        lo, hi = sweep, WINDOW - sweep
        wide = hi - lo + 2
        coupled = []
        for c in range(2):
            field = iterate[c, lo - 1 : hi + 1].reshape(wide * 8, LANES)
            high = field.astype(jnp.bfloat16)
            low = (field - high.astype(jnp.float32)).astype(jnp.bfloat16)
            sums = jnp.dot(
                jnp.concatenate((high, low, high), axis=1), ops[...], preferred_element_type=jnp.float32
            )
            part = [sums[:, i * LANES : (i + 1) * LANES].reshape(wide, 8, LANES) for i in range(5)]
            coupled.append(
                inverse[3, lo:hi] * part[0][1:-1]
                + part[1][:-2]
                + part[2][2:]
                + pltpu.roll(part[3][1:-1], 1, 1)
                + pltpu.roll(part[4][1:-1], 7, 1)
            )
        cross = inverse[2, lo:hi]
        new0 = (1.0 - damping) * iterate[0, lo:hi] + source[0, lo:hi] - inverse[0, lo:hi] * coupled[0] - cross * coupled[1]
        new1 = (1.0 - damping) * iterate[1, lo:hi] + source[1, lo:hi] - inverse[1, lo:hi] * coupled[1] + cross * coupled[0]
        iterate[0, lo:hi] = new0
        iterate[1, lo:hi] = new1
    for xc in range(8):
        for yd in range(4):
            for c in range(2):
                for col in range(2):
                    at = c * 4 + col * 2
                    out[xc * 4 + yd, at : at + 2, :] = iterate[c, HALO + 2 * xc + col, 2 * yd : 2 * yd + 2, :]


def state_kernel(last, got, out):
    total = jnp.sum(got[...] * last[...], axis=0)
    out[...] = total + pltpu.roll(total, 4, 0)


def carry_kernel(carry, waves, own, near, out):
    row = lax.broadcasted_iota(jnp.int32, (8, LANES), 0)
    state = jnp.where(row < 4, own[...], near[...])
    for k in range(STEPS):
        out[k * 8 : k * 8 + 8, :] = waves[k * 8 : k * 8 + 8, :] + carry[k] * state


def backward_kernel(table, got0, got1, out):
    for s, got in enumerate((got0, got1)):
        parts = [got[pl.ds(p, STEPS, stride=4), :] for p in range(4)]
        slices = exact(table[...], jnp.concatenate(parts, axis=1))
        for p in range(4):
            out[pl.ds(s * 4 + p, STEPS, stride=8), :] = slices[:, p * LANES : (p + 1) * LANES]


def unpack_kernel(got, out, flip):
    for s in range(2):
        for r in range(2):
            for c in range(2):
                flip[pl.ds(c, STEPS, stride=2), :] = got[pl.ds(s * 4 + c * 2 + r, STEPS, stride=8), :]
            out[s, 0, :, r, :] = flip[...].T[:NB, :]


def call(kernel, outs, ins, scratch=(), specs=None, name=None):
    return pl.pallas_call(
        kernel,
        out_shape=outs,
        in_specs=specs or [VMEM] * len(ins),
        out_specs=jax.tree.map(lambda _: VMEM, outs),
        scratch_shapes=scratch,
        compiler_params=PARAMS,
        name=name,
    )(*ins)


def f32(*shape):
    return jax.ShapeDtypeStruct(shape, jnp.float32)


def exchange(rows, axes, count):
    blocks = rows.reshape(count, -1, LANES)
    return lax.all_to_all(blocks, axes, 0, 0, tiled=True)


def per_device(forcing, init_state, elem_scale, vol_op, face_ops):
    square = pltpu.VMEM((LANES, LANES), jnp.float32)
    ops, diag = call(
        operator_kernel,
        (jax.ShapeDtypeStruct((3 * LANES, 5 * LANES), jnp.bfloat16), f32(8, LANES)),
        (vol_op, face_ops),
        (square,),
        name="operators",
    )
    packed = call(pack_kernel, f32(STEPS * 16, LANES), (forcing, init_state, elem_scale), (square, square), name="pack")
    by_point = exchange(packed, TIME, STEPS).reshape(STEPS * 16, LANES)
    waves0, waves1 = call(
        forward_kernel, (f32(STEPS * 8, LANES), f32(STEPS * 8, LANES)), (FORWARD, by_point), name="forward"
    )

    def solve(waves):
        got = exchange(waves, PLANE, FREQS)
        cube = (WINDOW, 8, LANES)
        done = call(
            solve_kernel,
            f32(FREQS, 8, LANES),
            (SHIFTS, ops, diag, got),
            (
                pltpu.VMEM((2,) + cube, jnp.float32),
                pltpu.VMEM((2,) + cube, jnp.float32),
                pltpu.VMEM((4,) + cube, jnp.float32),
            ),
            [SMEM, VMEM, VMEM, VMEM],
            name="solve",
        )
        return exchange(done, PLANE, FREQS)

    solved0 = solve(waves0)
    own = call(state_kernel, f32(8, LANES), (LAST_ROWS, solved0), name="state")
    moves = []
    for m in range(STEPS):
        target = m + 4 if m % 8 >= 4 else m - 4
        moves.append((m, target % STEPS))
    near = lax.ppermute(own, TIME, moves)
    waves1 = call(
        carry_kernel, f32(STEPS * 8, LANES), (CARRY, waves1, own, near), (), [SMEM, VMEM, VMEM, VMEM], name="carry"
    )
    solved1 = solve(waves1)
    slices = call(
        backward_kernel,
        f32(STEPS * 8, LANES),
        (BACKWARD, solved0.reshape(-1, LANES), solved1.reshape(-1, LANES)),
        name="backward",
    )
    by_column = exchange(slices, TIME, STEPS).reshape(STEPS * 8, LANES)
    return call(unpack_kernel, f32(2, 1, NB, 2, LANES), (by_column,), (square,), name="unpack")


def solution(mesh):
    grid = Mesh(mesh.devices.reshape(8, 4, 2, 4), ("z", "x", "core", "y"))
    return jax.shard_map(
        per_device,
        mesh=grid,
        in_specs=(
            P(None, TIME, None, "y", None),
            P(None, "y", None),
            P("y", None),
            P(),
            P(),
        ),
        out_specs=P(None, TIME, None, "y", None),
        check_vma=False,
    )
```

time: 531 us -> 122 us (0.23); the launches traced: 522 us -> 121 us
  waiting for transfers between devices: 354 us -> 13.8 us
  starting transfers between devices: 107 us -> 7.66 us
  blocking collectives: 0 us -> 84.2 us
  matrix products: 21.5 us -> 0 us
  between operations: 17.8 us -> 0.13 us
  Pallas kernels: 0 us -> 11.8 us
  other arithmetic: 9.4 us -> 0 us
  local copies, waits for them, and re-layouts: 12.4 us -> 3.39 us
    psum x1 -> x0, waiting for transfers between devices: 177 us -> none  [from_root(): return lax.psum(block, axis)]
    ppermute x52 -> x1, waiting for transfers between devices: 178 us -> 6.06 us  [per_device(): near = lax.ppermute(own, TIME, moves)]
    ppermute x52 -> x1, starting transfers between devices: 107 us -> 0.09 us  [per_device(): near = lax.ppermute(own, TIME, moves)]
    all_to_all x0 -> x5, blocking collectives: none -> 84.2 us  [exchange(): return lax.all_to_all(blocks, axes, 0, 0, tiled=True)]
    dot_general x42 -> x0, matrix products: 21.5 us -> none  [product(): jnp.dot(left, right, precision=lax.Precision.HIGHEST, preferred_element_t...]
    pallas_call x0 -> x9, Pallas kernels: none -> 11.8 us  [call(): pl.pallas_call(kernel, out_shape=outs, in_specs=specs or [VMEM] * len(ins...]
    all_to_all x0 -> x1, waiting for transfers between devices: none -> 7.76 us  [exchange(): return lax.all_to_all(blocks, axes, 0, 0, tiled=True)]
    slice x71 -> x0, local copies, waits for them, and re-layouts: 7.65 us -> none  [the longest x27 2.81 us: couple(): return elem_scale * local[0] + west + east + south + north]
  transfers between devices with their start and end apart: 53 -> 2, of which waited for: 43 -> 2; matrix products, arithmetic and copies ran while one was open for 1% -> 0% of each run, Pallas kernels for 0% -> 0%
where the time goes in v1:
time: 122 us; the launch traced here: 121 us
  blocking collectives  84.2 us (69%)
  waiting for transfers between devices  13.8 us (11%)
  Pallas kernels  11.8 us (10%)
  starting transfers between devices  7.66 us (6%)
  local copies, waits for them, and re-layouts  3.39 us (3%)
    all_to_all x5, blocking collectives, exchange(): return lax.all_to_all(blocks, axes, 0, 0, tiled=True)  84.2 us
    pallas_call x9, Pallas kernels, call(): pl.pallas_call(kernel, out_shape=outs, in_specs=specs or [VMEM] * len(ins...  11.8 us
    all_to_all x1, waiting for transfers between devices, exchange(): return lax.all_to_all(blocks, axes, 0, 0, tiled=True)  7.76 us
    all_to_all x1, starting transfers between devices, exchange(): return lax.all_to_all(blocks, axes, 0, 0, tiled=True)  7.57 us
    ppermute x1, waiting for transfers between devices, per_device(): near = lax.ppermute(own, TIME, moves)  6.06 us
    unnamed x21, local copies, waits for them, and re-layouts  3.39 us
  transfers between devices with their start and end apart: 2, of which 2 were waited for; matrix products, arithmetic and copies ran while one was open for 0% of the time, Pallas kernels for 0%

profile of v1, /device:TPU:1, one launch (start us, length us, event | category | flops | bytes accessed | tf_op | source)
XLA Modules:
  0.0 121.0 jit_solution(11216911866920698868)
XLA Ops:
  0.0 0.0 copy-start
  0.0 0.9 copy-done
  0.9 0.0 copy-start.2
  1.0 0.9 copy-done.2
  1.9 0.0 copy-start.7
  1.9 0.7 copy-done.7
  2.5 0.4 pack.1
  2.9 0.0 copy-start.6
  2.9 30.5 %all_to_all.30 = f32[64,16,128]{2,1,0:T(8,128)S(1)} all-to-all(f32[64,16,128]{2,1,0:T(8,128)S(1)} %bitcast.8), channel_id=1, replica_groups=mesh['z'=8,'x'=4,'core'=2,'y'=4] {'z','x','core'}, dimensions={0} | all-to-all | bytes 1048576 | tf_op jit(solution)/shard_map/all_to_all | solution.py:235
  33.4 0.0 copy-done.6
  33.4 1.1 forward.1
  34.5 0.0 copy-start.9
  34.6 7.6 %all-to-all-start.1 = ((f32[32,16,128]{2,1,0:T(8,128)}), f32[32,16,128]{2,1,0:T(8,128)S(1)}, u32[]{:S(2)}, u32[]{:S(2)}) async-start(f32[32,16,128]{2,1,0:T(8,128)} %bitcast.2), calls=%async_computation.1 | async-start | bytes 524288 | tf_op jit(solution)/shard_map/all_to_all | solution.py:235
  42.1 0.0 copy-done.9
  42.1 0.0 copy-start.4
  42.2 0.8 copy-done.4
  43.0 0.0 copy-start.3
  43.0 0.2 operators.1
  43.2 7.8 %all-to-all-done.1.got = f32[32,16,128]{2,1,0:T(8,128)S(1)} async-done(((f32[32,16,128]{2,1,0:T(8,128)}), f32[32,16,128]{2,1,0:T(8,128)S(1)}, u32[]{:S(2)}, u32[]{:S(2)}) %all-to-all-start.1) | async-done | bytes 262176 | tf_op jit(solution)/shard_map/all_to_all | solution.py:235
  50.9 0.0 copy-done.3
  50.9 4.1 %solve.2 = f32[32,8,128]{2,1,0:T(8,128)S(1)} custom-call(f32[32,4]{1,0:T(8,128)S(1)} %copy-done.3, bf16[384,640]{1,0:T(8,128)(2,1)S(1)} %get-tuple-element.9.ops, f32[8,128]{1,0:T(8,128)S(1)} %get-tuple-element.10.diag, f32[32,16,128]{2,1,0:T(8,128)S(1)} %all-to-all-done.1.got), custom_call_target="tpu_custom_call" | custom-call | tf_op jit(solution)/shard_map/solve/pallas_call | solution.py:218
  55.0 0.0 copy-start.1
  55.0 11.6 %all_to_all.31.got = f32[32,8,128]{2,1,0:T(8,128)S(1)} all-to-all(f32[32,8,128]{2,1,0:T(8,128)S(1)} %solve.2), channel_id=1, replica_groups=mesh['z'=8,'x'=4,'core'=2,'y'=4] {'x','core','y'}, dimensions={0} | all-to-all | bytes 262144 | tf_op jit(solution)/shard_map/all_to_all | solution.py:235
  66.6 0.0 copy-done.1
  66.6 0.1 state.1.own
  66.8 0.0 copy-start.8
  66.8 0.1 collective-permute-start
  66.9 6.1 %collective-permute-done.near = f32[8,128]{1,0:T(8,128)S(1)} collective-permute-done((f32[8,128]{1,0:T(8,128)S(1)}, f32[8,128]{1,0:T(8,128)S(1)}, u32[]{:S(2)}, u32[]{:S(2)}) %collective-permute-start) | collective-permute-done | bytes 4128 | tf_op jit(solution)/shard_map/ppermute | solution.py:276
  72.9 0.0 copy-done.8
  72.9 0.6 carry.2
  73.5 13.2 %all_to_all.32.got = f32[32,16,128]{2,1,0:T(8,128)S(1)} all-to-all(f32[32,16,128]{2,1,0:T(8,128)S(1)} %bitcast.11), channel_id=1, replica_groups=mesh['z'=8,'x'=4,'core'=2,'y'=4] {'x','core','y'}, dimensions={0} | all-to-all | bytes 524288 | tf_op jit(solution)/shard_map/all_to_all | solution.py:235
  86.7 4.1 %solve.3 = f32[32,8,128]{2,1,0:T(8,128)S(1)} custom-call(f32[32,4]{1,0:T(8,128)S(1)} %copy-done.3, bf16[384,640]{1,0:T(8,128)(2,1)S(1)} %get-tuple-element.9.ops, f32[8,128]{1,0:T(8,128)S(1)} %get-tuple-element.10.diag, f32[32,16,128]{2,1,0:T(8,128)S(1)} %all_to_all.32.got), custom_call_target="tpu_custom_call" | custom-call | tf_op jit(solution)/shard_map/solve/pallas_call | solution.py:218
  90.8 0.0 copy-start.5
  90.8 11.5 %all_to_all.33 = f32[32,8,128]{2,1,0:T(8,128)S(1)} all-to-all(f32[32,8,128]{2,1,0:T(8,128)S(1)} %solve.3), channel_id=1, replica_groups=mesh['z'=8,'x'=4,'core'=2,'y'=4] {'x','core','y'}, dimensions={0} | all-to-all | bytes 262144 | tf_op jit(solution)/shard_map/all_to_all | solution.py:235
  102.3 0.0 copy-done.5
  102.3 0.4 backward.1
  102.7 17.4 %all_to_all.34 = f32[64,8,128]{2,1,0:T(8,128)S(1)} all-to-all(f32[64,8,128]{2,1,0:T(8,128)S(1)} %bitcast.12), channel_id=1, replica_groups=mesh['z'=8,'x'=4,'core'=2,'y'=4] {'z','x','core'}, dimensions={0} | all-to-all | bytes 524288 | tf_op jit(solution)/shard_map/all_to_all | solution.py:235
  120.1 0.9 unpack.1
  (1 shorter events, 0.0 us)
Async XLA Ops:
  0.0 0.9 copy-start
  0.9 0.9 copy-start.2
  1.9 0.7 copy-start.7
  2.9 30.5 %copy-start.6 = (f32[64,64]{1,0:T(8,128)S(1)}, f32[64,64]{1,0:T(8,128)}, u32[]{:S(2)}) copy-start(f32[64,64]{1,0:T(8,128)} %constant.10.clone.table) | copy-start | bytes 49156
  34.5 7.6 %copy-start.9 = (f32[4,125,125]{2,0,1:T(4,128)S(1)}, f32[4,125,125]{2,0,1:T(4,128)}, u32[]{:S(2)}) copy-start(f32[4,125,125]{2,0,1:T(4,128)} %param.14) | copy-start | bytes 750004
  34.6 16.4 %all-to-all-start.1 = ((f32[32,16,128]{2,1,0:T(8,128)}), f32[32,16,128]{2,1,0:T(8,128)S(1)}, u32[]{:S(2)}, u32[]{:S(2)}) async-start(f32[32,16,128]{2,1,0:T(8,128)} %bitcast.2), calls=%async_computation.1 | async-start | bytes 524288 | tf_op jit(solution)/shard_map/all_to_all | solution.py:235
  42.1 0.8 copy-start.4
  43.0 8.0 %copy-start.3 = (f32[32,4]{1,0:T(8,128)S(1)}, f32[32,4]{1,0:T(8,128)}, u32[]{:S(2)}) copy-start(f32[32,4]{1,0:T(8,128)} %constant.11.clone.shifts) | copy-start | bytes 1540
  55.0 11.6 %copy-start.1 = (f32[32,8,1]{2,1,0:T(8,128)S(1)}, f32[32,8,1]{2,1,0:T(8,128)}, u32[]{:S(2)}) copy-start(f32[32,8,1]{2,1,0:T(8,128)} %constant.12.clone.last) | copy-start | bytes 3076
  66.8 6.2 %copy-start.8 = (f32[64]{0:T(128)S(1)}, f32[64]{0:T(128)}, u32[]{:S(2)}) copy-start(f32[64]{0:T(128)} %constant.13.clone.carry) | copy-start | bytes 772
  66.8 6.2 %collective-permute-start = (f32[8,128]{1,0:T(8,128)S(1)}, f32[8,128]{1,0:T(8,128)S(1)}, u32[]{:S(2)}, u32[]{:S(2)}) collective-permute-start(f32[8,128]{1,0:T(8,128)S(1)} %state.1.own), channel_id=1, source_target_pairs={{0,240},{4,244},{8,248},{12,252},{16,32},{20,36},{24,40},{28,44},{... | collective-permute-start | bytes 12296 | tf_op jit(solution)/shard_map/ppermute | solution.py:276
  90.8 11.5 %copy-start.5 = (f32[64,64]{1,0:T(8,128)S(1)}, f32[64,64]{1,0:T(8,128)}, u32[]{:S(2)}) copy-start(f32[64,64]{1,0:T(8,128)} %constant.14.clone.table) | copy-start | bytes 49156

commit v2 on v1

v2 whole, which is shorter than its diff:
```python
import math

import jax
import jax.numpy as jnp
import numpy as np
from jax import lax
from jax.experimental import pallas as pl
from jax.experimental.pallas import tpu as pltpu
from jax.sharding import Mesh
from jax.sharding import PartitionSpec as P

NB = 125
SWEEPS = 8
STEPS = 64
LANES = 128
FREQS = STEPS // 2
CHUNK = 16
WINDOW = 32
HALO = 8
ES_LANE = NB

circ_alpha = 0.01
damping = 0.7

TIME = ("z", "x", "core")
PLANE = ("x", "core", "y")


def tables():
    n = np.arange(STEPS)
    log_alpha = math.log(circ_alpha)
    grow = np.exp(n * (log_alpha / STEPS))
    forward = np.zeros((STEPS, STEPS))
    backward = np.zeros((STEPS, STEPS))
    shifts = np.zeros((FREQS, 4))
    root = math.exp(log_alpha / STEPS)
    forward[0] = 1.0
    forward[1] = (-1.0) ** n
    backward[:, 0] = 1.0
    backward[:, 1] = (-1.0) ** n
    shifts[0] = (1.0 - root, 1.0 + root, 0.0, 0.0)
    for k in range(1, FREQS):
        angle = 2.0 * math.pi * ((k * n) % STEPS) / STEPS
        forward[2 * k] = np.cos(angle)
        forward[2 * k + 1] = -np.sin(angle)
        backward[:, 2 * k] = 2.0 * np.cos(angle)
        backward[:, 2 * k + 1] = -2.0 * np.sin(angle)
        theta = 2.0 * math.pi * k / STEPS
        shifts[k, :3] = (1.0 - root * math.cos(theta), 1.0 - root * math.cos(theta), root * math.sin(theta))
    forward = forward * grow[None, :]
    backward = backward / grow[:, None] / STEPS
    carry = 0.5 * forward.sum(1) + forward[:, 0]
    last = backward[STEPS - 1]
    return tuple(a.astype(np.float32) for a in (forward, backward, shifts, carry, last))


FORWARD, BACKWARD, SHIFTS, CARRY, LAST = tables()
BY_PART = np.concatenate((np.arange(0, STEPS, 2), np.arange(1, STEPS, 2)))
FORWARD = FORWARD[BY_PART]
BACKWARD = BACKWARD[:, BY_PART]
SLOTS = np.concatenate((SHIFTS[:, :3], LAST.reshape(FREQS, 2), CARRY.reshape(FREQS, 2), SHIFTS[:, :1]), axis=1)

VMEM = pl.BlockSpec(memory_space=pltpu.VMEM)
SMEM = pl.BlockSpec(memory_space=pltpu.SMEM)
HBM = pl.BlockSpec(memory_space=pltpu.HBM)
PARAMS = pltpu.CompilerParams(vmem_limit_bytes=32 * 1024 * 1024)


def exact(left, right):
    return jnp.dot(left, right, precision=lax.Precision.HIGHEST, preferred_element_type=jnp.float32)


def pack_kernel(forcing, init, scale, out, value, state, elems, rows, flip, sems):
    copies = [
        pltpu.make_async_copy(ref, into, sems.at[i])
        for i, (ref, into) in enumerate(((forcing, value), (init, state), (scale, elems)))
    ]
    for copy in copies:
        copy.start()
    step = lax.axis_index("z") * 8 + lax.axis_index("x") * 2 + lax.axis_index("core")
    weight = jnp.where(step == 0, 1.5, 0.5).astype(jnp.float32)
    rows[NB:, :] = jnp.zeros((LANES - NB, LANES), jnp.float32)
    for copy in copies:
        copy.wait()
    for s in (1, 0):
        for r in range(2):
            if s == 0:
                rows[:NB, :] = value[s, 0, :, r, :] + weight * state[:, r, :]
                rows[ES_LANE : ES_LANE + 1, :] = elems[r : r + 1, :]
            else:
                rows[:NB, :] = value[s, 0, :, r, :]
            flip[...] = rows[...].T
            for c in range(2):
                out[pl.ds(s * 8 + c * 2 + r, STEPS, stride=12), :] = flip[pl.ds(c, STEPS, stride=2), :]
    blank = jnp.zeros((4, LANES), jnp.float32)
    for m in range(STEPS):
        source = m - 4 if m % 8 < 4 else m + 4
        at = m * 12 + 4
        if 0 <= source < STEPS:
            out[at : at + 4, :] = out[source * 12 : source * 12 + 4, :]
        else:
            out[at : at + 4, :] = blank


def forward_kernel(table, got, out):
    lane = lax.broadcasted_iota(jnp.int32, (STEPS, LANES), 1)
    parts = [got[pl.ds(p, STEPS, stride=12), :] for p in range(12)]
    waves = exact(table[...], jnp.concatenate(parts, axis=1))
    for p in range(12):
        wave = waves[:, p * LANES : (p + 1) * LANES]
        if p < 8:
            wave = jnp.where(lane == ES_LANE, jnp.broadcast_to(parts[p][:1, :], wave.shape), wave)
        for c in range(2):
            at = c * 8 + p if p < 8 else 16 + c * 4 + p - 8
            out[pl.ds(at, FREQS, stride=24), :] = wave[c * FREQS : (c + 1) * FREQS]


def operator_kernel(vol, faces, out, diag, square):
    square[...] = jnp.zeros((LANES, LANES), jnp.float32)
    row = lax.broadcasted_iota(jnp.int32, (LANES, LANES), 0)
    col = lax.broadcasted_iota(jnp.int32, (LANES, LANES), 1)
    for op in range(5):
        square[:NB, :NB] = vol[...] if op == 0 else faces[op - 1]
        value = square[...]
        if op == 0:
            on = jnp.where(row == col, value, 0.0)
            diag[...] = jnp.broadcast_to(jnp.sum(on, axis=0, keepdims=True), (8, LANES))
            value = value - on
        value = value.T
        high = value.astype(jnp.bfloat16)
        low = (value - high.astype(jnp.float32)).astype(jnp.bfloat16)
        at = op * LANES
        out[:LANES, at : at + LANES] = high
        out[LANES : 2 * LANES, at : at + LANES] = high
        out[2 * LANES :, at : at + LANES] = low


def slot():
    return lax.axis_index("x") * 8 + lax.axis_index("core") * 4 + lax.axis_index("y")


def relax(slots, ops, diag, scale, iterate, source, inverse):
    kappa = slot()
    shape = (WINDOW, 8, LANES)
    lane = lax.broadcasted_iota(jnp.int32, shape, 2)
    place = lax.axis_index("z") * CHUNK - HALO + lax.broadcasted_iota(jnp.int32, shape, 0)
    inside = jnp.logical_and(place >= 0, place < 8 * CHUNK)
    scaled = scale[...] * diag[...][None]
    im = slots[kappa, 2]
    re0 = slots[kappa, 0] + scaled
    re1 = slots[kappa, 1] + scaled
    mod0 = jnp.where(inside, damping / (re0 * re0 + im * im), 0.0)
    mod1 = jnp.where(inside, damping / (re1 * re1 + im * im), 0.0)
    inverse[0] = re0 * mod0
    inverse[1] = re1 * mod1
    inverse[2] = im * mod0
    g0 = jnp.where(lane < NB, iterate[0], 0.0)
    g1 = jnp.where(lane < NB, iterate[1], 0.0)
    source[0] = inverse[0] * g0 + inverse[2] * g1
    source[1] = inverse[1] * g1 - inverse[2] * g0
    iterate[0] = source[0]
    iterate[1] = source[1]
    for sweep in range(1, SWEEPS):
        lo, hi = sweep, WINDOW - sweep
        wide = hi - lo + 2
        coupled = []
        for c in range(2):
            field = iterate[c, lo - 1 : hi + 1].reshape(wide * 8, LANES)
            high = field.astype(jnp.bfloat16)
            low = (field - high.astype(jnp.float32)).astype(jnp.bfloat16)
            sums = jnp.dot(
                jnp.concatenate((high, low, high), axis=1), ops[...], preferred_element_type=jnp.float32
            )
            part = [sums[:, i * LANES : (i + 1) * LANES].reshape(wide, 8, LANES) for i in range(5)]
            coupled.append(
                scale[lo:hi] * part[0][1:-1]
                + part[1][:-2]
                + part[2][2:]
                + pltpu.roll(part[3][1:-1], 1, 1)
                + pltpu.roll(part[4][1:-1], 7, 1)
            )
        cross = inverse[2, lo:hi]
        new0 = (1.0 - damping) * iterate[0, lo:hi] + source[0, lo:hi] - inverse[0, lo:hi] * coupled[0] - cross * coupled[1]
        new1 = (1.0 - damping) * iterate[1, lo:hi] + source[1, lo:hi] - inverse[1, lo:hi] * coupled[1] + cross * coupled[0]
        iterate[0, lo:hi] = new0
        iterate[1, lo:hi] = new1


def hand_out(iterate, out, first):
    for xc in range(8):
        for yd in range(4):
            for c in range(2):
                for col in range(2):
                    at = first + c * 4 + col * 2
                    out[xc * 4 + yd, at : at + 2, :] = iterate[c, HALO + 2 * xc + col, 2 * yd : 2 * yd + 2, :]


def first_kernel(slots, ops, diag, got, out, state, scale, iterate, source, inverse):
    for xc in range(8):
        for yd in range(4):
            for c in range(2):
                for col in range(4):
                    w = HALO + 2 * xc + col
                    if col >= 2:
                        w = (2 * xc if xc < 4 else 16 + 2 * xc) + col - 2
                    at = c * 8 + col * 2
                    iterate[c, w, 2 * yd : 2 * yd + 2, :] = got[xc * 4 + yd, at : at + 2, :]
    scale[...] = jnp.broadcast_to(iterate[0, :, :, ES_LANE : ES_LANE + 1], scale.shape)
    relax(slots, ops, diag, scale, iterate, source, inverse)
    kappa = slot()
    middle = slice(HALO, HALO + CHUNK)
    state[...] = slots[kappa, 3] * iterate[0, middle] + slots[kappa, 4] * iterate[1, middle]
    hand_out(iterate, out, 0)


def carry_kernel(slots, got, state0, state1, state2, state3, left, right):
    state = (state0[...] + state1[...]) + (state2[...] + state3[...])
    kappa = slot()
    for c in range(2):
        part = slots[kappa, 5 + c] * state
        left[c] = part[: CHUNK // 2]
        right[c] = part[CHUNK // 2 :]
        for xc in range(8):
            side = left if xc < 4 else right
            for yd in range(4):
                for col in range(2):
                    at = 16 + c * 4 + col * 2
                    here = (c, 2 * (xc % 4) + col, slice(2 * yd, 2 * yd + 2))
                    side[here] = side[here] + got[xc * 4 + yd, at : at + 2, :]


def second_kernel(slots, ops, diag, scale, west, left, right, east, before, out, iterate, source, inverse):
    for i, part in enumerate((west, left, right, east)):
        iterate[:, i * HALO : (i + 1) * HALO] = part[...]
    out[:, :8, :] = before[...]
    relax(slots, ops, diag, scale, iterate, source, inverse)
    hand_out(iterate, out, 8)


def backward_kernel(table, got, out):
    parts = []
    for p in range(8):
        at = (p // 4) * 8 + p % 4
        halves = [got[pl.ds(at + 4 * c, FREQS, stride=16), :] for c in range(2)]
        parts.append(jnp.concatenate(halves, axis=0))
    slices = exact(table[...], jnp.concatenate(parts, axis=1))
    for p in range(8):
        out[pl.ds(p, STEPS, stride=8), :] = slices[:, p * LANES : (p + 1) * LANES]


def unpack_kernel(got, out, flip):
    for s in range(2):
        for r in range(2):
            for c in range(2):
                flip[pl.ds(c, STEPS, stride=2), :] = got[pl.ds(s * 4 + c * 2 + r, STEPS, stride=8), :]
            out[s, 0, :, r, :] = flip[...].T[:NB, :]


def call(kernel, outs, ins, scratch=(), specs=None, name=None, params=PARAMS):
    return pl.pallas_call(
        kernel,
        out_shape=outs,
        in_specs=specs or [VMEM] * len(ins),
        out_specs=jax.tree.map(lambda _: VMEM, outs),
        scratch_shapes=scratch,
        compiler_params=params,
        name=name,
    )(*ins)


def f32(*shape):
    return jax.ShapeDtypeStruct(shape, jnp.float32)


def exchange(blocks, axes):
    return lax.all_to_all(blocks, axes, 0, 0, tiled=True)


def moved(block, axis, by):
    count = lax.axis_size(axis)
    return lax.ppermute(block, axis, [(i, (i + by) % count) for i in range(count)])


def per_device(forcing, init_state, elem_scale, vol_op, face_ops):
    square = pltpu.VMEM((LANES, LANES), jnp.float32)
    window = (WINDOW, 8, LANES)
    work = [pltpu.VMEM((count,) + window, jnp.float32) for count in (2, 2, 3)]
    ops, diag = call(
        operator_kernel,
        (jax.ShapeDtypeStruct((3 * LANES, 5 * LANES), jnp.bfloat16), f32(8, LANES)),
        (vol_op, face_ops),
        (square,),
        name="operators",
    )
    packed = call(
        pack_kernel,
        f32(STEPS * 12, LANES),
        (forcing, init_state, elem_scale),
        (
            pltpu.VMEM(forcing.shape, jnp.float32),
            pltpu.VMEM(init_state.shape, jnp.float32),
            pltpu.VMEM(elem_scale.shape, jnp.float32),
            square,
            square,
            pltpu.SemaphoreType.DMA((3,)),
        ),
        [HBM] * 3,
        name="pack",
        params=pltpu.CompilerParams(vmem_limit_bytes=60 * 1024 * 1024),
    )
    by_point = exchange(packed.reshape(STEPS, 3, 4, LANES), TIME).reshape(STEPS * 12, LANES)
    waves = call(forward_kernel, f32(FREQS * 24, LANES), (FORWARD, by_point), name="forward")
    got = exchange(waves.reshape(FREQS, 24, LANES), PLANE)
    done, state, scale = call(
        first_kernel,
        (f32(FREQS, 8, LANES), f32(CHUNK, 8, LANES), f32(*window)),
        (SLOTS, ops, diag, got),
        work,
        [SMEM, VMEM, VMEM, VMEM],
        name="first",
    )
    state = state + moved(state, "core", 1)
    state = state + moved(state, "y", 1) + moved(state, "y", 2) + moved(state, "y", 3)
    states = [state] + [moved(state, "x", by) for by in (1, 2, 3)]
    half = f32(2, CHUNK // 2, 8, LANES)
    left, right = call(carry_kernel, (half, half), (SLOTS, got, *states), (), [SMEM] + [VMEM] * 5, name="carry")
    west = moved(right, "z", 1)
    east = moved(left, "z", -1)
    done = call(
        second_kernel,
        f32(FREQS, 16, LANES),
        (SLOTS, ops, diag, scale, west, left, right, east, done),
        work,
        [SMEM] + [VMEM] * 8,
        name="second",
    )
    got = exchange(done, PLANE).reshape(FREQS * 16, LANES)
    slices = call(backward_kernel, f32(STEPS * 8, LANES), (BACKWARD, got), name="backward")
    by_column = exchange(slices.reshape(STEPS, 8, LANES), TIME).reshape(STEPS * 8, LANES)
    return call(unpack_kernel, f32(2, 1, NB, 2, LANES), (by_column,), (square,), name="unpack")


def solution(mesh):
    grid = Mesh(mesh.devices.reshape(8, 4, 2, 4), ("z", "x", "core", "y"))
    return jax.shard_map(
        per_device,
        mesh=grid,
        in_specs=(
            P(None, TIME, None, "y", None),
            P(None, "y", None),
            P("y", None),
            P(),
            P(),
        ),
        out_specs=P(None, TIME, None, "y", None),
        check_vma=False,
    )
```

time: 122 us -> 115 us (0.943)
  blocking collectives: 84.2 us -> 63.2 us
  starting transfers between devices: 7.66 us -> 15.1 us
  waiting for transfers between devices: 13.8 us -> 21 us
  local copies, waits for them, and re-layouts: 3.39 us -> 0.85 us
  Pallas kernels: 11.8 us -> 13.8 us
    all_to_all x5 -> x3, blocking collectives: 84.2 us -> 63.2 us  [exchange(): return lax.all_to_all(blocks, axes, 0, 0, tiled=True)]
    ppermute x1 -> x9, starting transfers between devices: 0.09 us -> 7.74 us  [moved(): lax.ppermute(block, axis, [(i, (i + by) % count) for i in range(count)])]
    ppermute x1 -> x9, waiting for transfers between devices: 6.06 us -> 12 us  [moved(): lax.ppermute(block, axis, [(i, (i + by) % count) for i in range(count)])]
    unnamed x21 -> x11, local copies, waits for them, and re-layouts: 3.39 us -> 0.85 us
    pallas_call x9 -> x8, Pallas kernels: 11.8 us -> 13.8 us  [call(): pl.pallas_call(kernel, out_shape=outs, in_specs=specs or [VMEM] * len(ins...]
    all_to_all x1, waiting for transfers between devices: 7.76 us -> 8.99 us  [exchange(): return lax.all_to_all(blocks, axes, 0, 0, tiled=True)]
  transfers between devices with their start and end apart: 2 -> 10, of which waited for: 2 -> 9; matrix products, arithmetic and copies ran while one was open for 0% -> 0% of each run, Pallas kernels for 0% -> 0%
where the time goes in v2:
time: 115 us; the launch traced here: 114 us
  blocking collectives  63.2 us (55%)
  waiting for transfers between devices  21 us (18%)
  starting transfers between devices  15.1 us (13%)
  Pallas kernels  13.8 us (12%)
    all_to_all x3, blocking collectives, exchange(): return lax.all_to_all(blocks, axes, 0, 0, tiled=True)  63.2 us
    pallas_call x8, Pallas kernels, call(): pl.pallas_call(kernel, out_shape=outs, in_specs=specs or [VMEM] * len(ins...  13.8 us
    ppermute x9, waiting for transfers between devices, moved(): lax.ppermute(block, axis, [(i, (i + by) % count) for i in range(count)])  12 us
    all_to_all x1, waiting for transfers between devices, exchange(): return lax.all_to_all(blocks, axes, 0, 0, tiled=True)  8.99 us
    ppermute x9, starting transfers between devices, moved(): lax.ppermute(block, axis, [(i, (i + by) % count) for i in range(count)])  7.74 us
    all_to_all x1, starting transfers between devices, exchange(): return lax.all_to_all(blocks, axes, 0, 0, tiled=True)  7.41 us
  transfers between devices with their start and end apart: 10, of which 9 were waited for; matrix products, arithmetic and copies ran while one was open for 0% of the time, Pallas kernels for 0%

profile of v2, /device:TPU:1, one launch (start us, length us, event | category | flops | bytes accessed | tf_op | source)
XLA Modules:
  0.0 114.2 jit_solution(12097058392865702878)
XLA Ops:
  0.0 2.1 %pack.1 = f32[768,128]{1,0:T(8,128)} custom-call(f32[2,1,125,2,128]{4,3,2,1,0:T(2,128)} %forcing.1, f32[125,2,128]{2,1,0:T(2,128)} %init.1, f32[2,128]{1,0:T(2,128)} %scale.1), custom_call_target="tpu_custom_call" | custom-call | tf_op jit(solution)/shard_map/pack/pallas_call | solution.py:260
  2.1 0.0 copy-start.3
  2.1 28.1 %all_to_all.20 = f32[64,3,4,128]{3,2,1,0:T(4,128)S(1)} all-to-all(f32[64,3,4,128]{3,2,1,0:T(4,128)} %bitcast.10), channel_id=1, replica_groups=mesh['z'=8,'x'=4,'core'=2,'y'=4] {'z','x','core'}, dimensions={0} | all-to-all | bytes 786432 | tf_op jit(solution)/shard_map/all_to_all | solution.py:276
  30.2 0.0 copy-done.3
  30.2 1.2 %forward.1 = f32[768,128]{1,0:T(8,128)} custom-call(f32[64,64]{1,0:T(8,128)S(1)} %copy-done.3, f32[768,128]{1,0:T(8,128)S(1)} %bitcast.6), custom_call_target="tpu_custom_call" | custom-call | tf_op jit(solution)/shard_map/forward/pallas_call | solution.py:260
  31.4 0.0 copy-start.4
  31.4 7.4 %all-to-all-start.1 = ((f32[32,24,128]{2,1,0:T(8,128)}), f32[32,24,128]{2,1,0:T(8,128)S(1)}, u32[]{:S(2)}, u32[]{:S(2)}) async-start(f32[32,24,128]{2,1,0:T(8,128)} %bitcast.2), calls=%async_computation.1 | async-start | bytes 786432 | tf_op jit(solution)/shard_map/all_to_all | solution.py:276
  38.8 0.0 copy-done.4
  38.9 0.0 copy-start.1
  38.9 0.8 copy-done.1
  39.7 0.0 copy-start
  39.7 0.2 operators.1
  39.9 9.0 %all-to-all-done.1.got = f32[32,24,128]{2,1,0:T(8,128)S(1)} async-done(((f32[32,24,128]{2,1,0:T(8,128)}), f32[32,24,128]{2,1,0:T(8,128)S(1)}, u32[]{:S(2)}, u32[]{:S(2)}) %all-to-all-start.1) | async-done | bytes 393248 | tf_op jit(solution)/shard_map/all_to_all | solution.py:276
  48.9 0.0 copy-done
  48.9 4.1 %first.1 = (f32[32,8,128]{2,1,0:T(8,128)S(1)}, f32[16,8,128]{2,1,0:T(8,128)S(1)}, f32[32,8,128]{2,1,0:T(8,128)S(1)}) custom-call(f32[32,8]{1,0:T(8,128)S(1)} %copy-done, bf16[384,640]{1,0:T(8,128)(2,1)S(1)} %get-tuple-element.12.ops, f32[8,128]{1,0:T(8,128)S(1)} %get-tuple-element.13.diag, f32[32,24,128]{2,1,0:T(8,128)S(1)} %all-to-all-done.1.got), custom_call_target="tpu_custom_call" | custom-call | tf_op jit(solution)/shard_map/first/pallas_call | solution.py:260
  53.0 0.8 collective-permute-start
  53.8 0.9 collective-permute-done
  54.7 0.9 collective-permute-start.3
  55.6 1.0 collective-permute-start.2
  56.6 0.0 collective-permute-start.1
  56.6 1.3 %collective-permute-done.3 = f32[16,8,128]{2,1,0:T(8,128)S(1)} collective-permute-done((f32[16,8,128]{2,1,0:T(8,128)S(1)}, f32[16,8,128]{2,1,0:T(8,128)S(1)}, u32[]{:S(2)}, u32[]{:S(2)}) %collective-permute-start.3) | collective-permute-done | bytes 65568 | tf_op jit(solution)/shard_map/ppermute | solution.py:281
  57.9 2.3 %collective-permute-done.2 = f32[16,8,128]{2,1,0:T(8,128)S(1)} collective-permute-done((f32[16,8,128]{2,1,0:T(8,128)S(1)}, f32[16,8,128]{2,1,0:T(8,128)S(1)}, u32[]{:S(2)}, u32[]{:S(2)}) %collective-permute-start.2) | collective-permute-done | bytes 65568 | tf_op jit(solution)/shard_map/ppermute | solution.py:281
  60.2 1.5 %collective-permute-done.1 = f32[16,8,128]{2,1,0:T(8,128)S(1)} collective-permute-done((f32[16,8,128]{2,1,0:T(8,128)S(1)}, f32[16,8,128]{2,1,0:T(8,128)S(1)}, u32[]{:S(2)}, u32[]{:S(2)}) %collective-permute-start.1) | collective-permute-done | bytes 65568 | tf_op jit(solution)/shard_map/ppermute | solution.py:281
  61.8 1.0 collective-permute-start.6
  62.8 1.2 %collective-permute-start.5 = (f32[16,8,128]{2,1,0:T(8,128)S(1)}, f32[16,8,128]{2,1,0:T(8,128)S(1)}, u32[]{:S(2)}, u32[]{:S(2)}) collective-permute-start(f32[16,8,128]{2,1,0:T(8,128)S(1)} %add_add_fusion.state0), channel_id=1, source_target_pairs={{0,16},{8,24},{16,0},{24,8},{1,17},{9,25},{17,1},{25,9},{2,18},{10... | collective-permute-start | bytes 196616 | tf_op jit(solution)/shard_map/ppermute | solution.py:281
  64.0 0.0 collective-permute-start.4
  64.0 0.9 collective-permute-done.6.state3
  65.0 2.4 %collective-permute-done.5.state2 = f32[16,8,128]{2,1,0:T(8,128)S(1)} collective-permute-done((f32[16,8,128]{2,1,0:T(8,128)S(1)}, f32[16,8,128]{2,1,0:T(8,128)S(1)}, u32[]{:S(2)}, u32[]{:S(2)}) %collective-permute-start.5) | collective-permute-done | bytes 65568 | tf_op jit(solution)/shard_map/ppermute | solution.py:281
  67.4 0.9 collective-permute-done.4.state1
  68.4 0.9 carry.1
  69.3 0.6 collective-permute-start.7
  69.9 2.1 %collective-permute-start.8 = (f32[2,8,8,128]{3,2,1,0:T(8,128)S(1)}, f32[2,8,8,128]{3,2,1,0:T(8,128)S(1)}, u32[]{:S(2)}, u32[]{:S(2)}) collective-permute-start(f32[2,8,8,128]{3,2,1,0:T(8,128)S(1)} %get-tuple-element.17.left), channel_id=1, source_target_pairs={{0,224},{32,0},{64,32},{96,64},{128,96},{160,128},{192,160},{224,1... | collective-permute-start | bytes 196616 | tf_op jit(solution)/shard_map/ppermute | solution.py:281
  72.0 1.6 %collective-permute-done.7.west = f32[2,8,8,128]{3,2,1,0:T(8,128)S(1)} collective-permute-done((f32[2,8,8,128]{3,2,1,0:T(8,128)S(1)}, f32[2,8,8,128]{3,2,1,0:T(8,128)S(1)}, u32[]{:S(2)}, u32[]{:S(2)}) %collective-permute-start.7) | collective-permute-done | bytes 65568 | tf_op jit(solution)/shard_map/ppermute | solution.py:281
  73.7 0.0 collective-permute-done.8.east
  73.7 4.0 %second.1 = f32[32,16,128]{2,1,0:T(8,128)S(1)} custom-call(f32[32,8]{1,0:T(8,128)S(1)} %copy-done, bf16[384,640]{1,0:T(8,128)(2,1)S(1)} %get-tuple-element.12.ops, f32[8,128]{1,0:T(8,128)S(1)} %get-tuple-element.13.diag, f32[32,8,128]{2,1,0:T(8,128)S(1)} %get-tuple-element.14.scale, f32[2,8,8,128]{3,2,1,0:T(8,128)S(1)} %collective-permute-done.7.west, ...), custom_call_target="tpu_custom_call" | custom-call | tf_op jit(solution)/shard_map/second/pallas_call | solution.py:260
  77.7 0.0 copy-start.2
  77.7 15.8 %all_to_all.21 = f32[32,16,128]{2,1,0:T(8,128)S(1)} all-to-all(f32[32,16,128]{2,1,0:T(8,128)S(1)} %second.1), channel_id=1, replica_groups=mesh['z'=8,'x'=4,'core'=2,'y'=4] {'x','core','y'}, dimensions={0} | all-to-all | bytes 524288 | tf_op jit(solution)/shard_map/all_to_all | solution.py:276
  93.5 0.0 copy-done.2
  93.5 0.4 backward.1
  93.9 19.3 %all_to_all.22 = f32[64,8,128]{2,1,0:T(8,128)S(1)} all-to-all(f32[64,8,128]{2,1,0:T(8,128)S(1)} %bitcast.8), channel_id=1, replica_groups=mesh['z'=8,'x'=4,'core'=2,'y'=4] {'z','x','core'}, dimensions={0} | all-to-all | bytes 524288 | tf_op jit(solution)/shard_map/all_to_all | solution.py:276
  113.2 0.9 unpack.1
  (3 shorter events, 0.0 us)
Async XLA Ops:
  2.1 28.1 %copy-start.3 = (f32[64,64]{1,0:T(8,128)S(1)}, f32[64,64]{1,0:T(8,128)}, u32[]{:S(2)}) copy-start(f32[64,64]{1,0:T(8,128)} %constant.6.clone.table) | copy-start | bytes 49156
  31.4 7.4 %copy-start.4 = (f32[4,125,125]{2,0,1:T(4,128)S(1)}, f32[4,125,125]{2,0,1:T(4,128)}, u32[]{:S(2)}) copy-start(f32[4,125,125]{2,0,1:T(4,128)} %param.12) | copy-start | bytes 750004
  31.4 17.5 %all-to-all-start.1 = ((f32[32,24,128]{2,1,0:T(8,128)}), f32[32,24,128]{2,1,0:T(8,128)S(1)}, u32[]{:S(2)}, u32[]{:S(2)}) async-start(f32[32,24,128]{2,1,0:T(8,128)} %bitcast.2), calls=%async_computation.1 | async-start | bytes 786432 | tf_op jit(solution)/shard_map/all_to_all | solution.py:276
  38.9 0.8 copy-start.1
  39.7 9.2 %copy-start = (f32[32,8]{1,0:T(8,128)S(1)}, f32[32,8]{1,0:T(8,128)}, u32[]{:S(2)}) copy-start(f32[32,8]{1,0:T(8,128)} %constant.7.clone.slots) | copy-start | bytes 3076
  53.0 1.7 %collective-permute-start = (f32[16,8,128]{2,1,0:T(8,128)S(1)}, f32[16,8,128]{2,1,0:T(8,128)S(1)}, u32[]{:S(2)}, u32[]{:S(2)}) collective-permute-start(f32[16,8,128]{2,1,0:T(8,128)S(1)} %get-tuple-element.15), channel_id=1, source_target_pairs={{0,4},{4,0},{1,5},{5,1},{2,6},{6,2},{3,7},{7,3},{8,12},{12,8},{9,1... | collective-permute-start | bytes 196616 | tf_op jit(solution)/shard_map/ppermute | solution.py:281
  54.7 3.2 %collective-permute-start.3 = (f32[16,8,128]{2,1,0:T(8,128)S(1)}, f32[16,8,128]{2,1,0:T(8,128)S(1)}, u32[]{:S(2)}, u32[]{:S(2)}) collective-permute-start(f32[16,8,128]{2,1,0:T(8,128)S(1)} %add.12), channel_id=1, source_target_pairs={{0,3},{1,0},{2,1},{3,2},{4,7},{5,4},{6,5},{7,6},{8,11},{9,8},{10,9... | collective-permute-start | bytes 196616 | tf_op jit(solution)/shard_map/ppermute | solution.py:281
  55.6 4.6 %collective-permute-start.2 = (f32[16,8,128]{2,1,0:T(8,128)S(1)}, f32[16,8,128]{2,1,0:T(8,128)S(1)}, u32[]{:S(2)}, u32[]{:S(2)}) collective-permute-start(f32[16,8,128]{2,1,0:T(8,128)S(1)} %add.12), channel_id=1, source_target_pairs={{0,2},{1,3},{2,0},{3,1},{4,6},{5,7},{6,4},{7,5},{8,10},{9,11},{10,... | collective-permute-start | bytes 196616 | tf_op jit(solution)/shard_map/ppermute | solution.py:281
  56.6 5.1 %collective-permute-start.1 = (f32[16,8,128]{2,1,0:T(8,128)S(1)}, f32[16,8,128]{2,1,0:T(8,128)S(1)}, u32[]{:S(2)}, u32[]{:S(2)}) collective-permute-start(f32[16,8,128]{2,1,0:T(8,128)S(1)} %add.12), channel_id=1, source_target_pairs={{0,1},{1,2},{2,3},{3,0},{4,5},{5,6},{6,7},{7,4},{8,9},{9,10},{10,1... | collective-permute-start | bytes 196616 | tf_op jit(solution)/shard_map/ppermute | solution.py:281
  61.8 3.2 %collective-permute-start.6 = (f32[16,8,128]{2,1,0:T(8,128)S(1)}, f32[16,8,128]{2,1,0:T(8,128)S(1)}, u32[]{:S(2)}, u32[]{:S(2)}) collective-permute-start(f32[16,8,128]{2,1,0:T(8,128)S(1)} %add_add_fusion.state0), channel_id=1, source_target_pairs={{0,24},{8,0},{16,8},{24,16},{1,25},{9,1},{17,9},{25,17},{2,26},{10... | collective-permute-start | bytes 196616 | tf_op jit(solution)/shard_map/ppermute | solution.py:281
  62.8 4.6 %collective-permute-start.5 = (f32[16,8,128]{2,1,0:T(8,128)S(1)}, f32[16,8,128]{2,1,0:T(8,128)S(1)}, u32[]{:S(2)}, u32[]{:S(2)}) collective-permute-start(f32[16,8,128]{2,1,0:T(8,128)S(1)} %add_add_fusion.state0), channel_id=1, source_target_pairs={{0,16},{8,24},{16,0},{24,8},{1,17},{9,25},{17,1},{25,9},{2,18},{10... | collective-permute-start | bytes 196616 | tf_op jit(solution)/shard_map/ppermute | solution.py:281
  64.0 4.3 %collective-permute-start.4 = (f32[16,8,128]{2,1,0:T(8,128)S(1)}, f32[16,8,128]{2,1,0:T(8,128)S(1)}, u32[]{:S(2)}, u32[]{:S(2)}) collective-permute-start(f32[16,8,128]{2,1,0:T(8,128)S(1)} %add_add_fusion.state0), channel_id=1, source_target_pairs={{0,8},{8,16},{16,24},{24,0},{1,9},{9,17},{17,25},{25,1},{2,10},{10... | collective-permute-start | bytes 196616 | tf_op jit(solution)/shard_map/ppermute | solution.py:281
  69.3 4.4 %collective-permute-start.7 = (f32[2,8,8,128]{3,2,1,0:T(8,128)S(1)}, f32[2,8,8,128]{3,2,1,0:T(8,128)S(1)}, u32[]{:S(2)}, u32[]{:S(2)}) collective-permute-start(f32[2,8,8,128]{3,2,1,0:T(8,128)S(1)} %get-tuple-element.16.right), channel_id=1, source_target_pairs={{0,32},{32,64},{64,96},{96,128},{128,160},{160,192},{192,224},{224... | collective-permute-start | bytes 196616 | tf_op jit(solution)/shard_map/ppermute | solution.py:281
  69.9 3.8 %collective-permute-start.8 = (f32[2,8,8,128]{3,2,1,0:T(8,128)S(1)}, f32[2,8,8,128]{3,2,1,0:T(8,128)S(1)}, u32[]{:S(2)}, u32[]{:S(2)}) collective-permute-start(f32[2,8,8,128]{3,2,1,0:T(8,128)S(1)} %get-tuple-element.17.left), channel_id=1, source_target_pairs={{0,224},{32,0},{64,32},{96,64},{128,96},{160,128},{192,160},{224,1... | collective-permute-start | bytes 196616 | tf_op jit(solution)/shard_map/ppermute | solution.py:281
  77.7 15.8 %copy-start.2 = (f32[64,64]{1,0:T(8,128)S(1)}, f32[64,64]{1,0:T(8,128)}, u32[]{:S(2)}) copy-start(f32[64,64]{1,0:T(8,128)} %constant.8.clone.table) | copy-start | bytes 49156

commit v3 on v2

--- a/solution.py
+++ b/solution.py
@@ -59,10 +59,11 @@
 FORWARD = FORWARD[BY_PART]
 BACKWARD = BACKWARD[:, BY_PART]
 SLOTS = np.concatenate((SHIFTS[:, :3], LAST.reshape(FREQS, 2), CARRY.reshape(FREQS, 2), SHIFTS[:, :1]), axis=1)
+SLOTS = np.repeat(SLOTS[:, :, None], LANES, axis=2)
 
 VMEM = pl.BlockSpec(memory_space=pltpu.VMEM)
-SMEM = pl.BlockSpec(memory_space=pltpu.SMEM)
 HBM = pl.BlockSpec(memory_space=pltpu.HBM)
+ANY = pl.BlockSpec(memory_space=pl.ANY)
 PARAMS = pltpu.CompilerParams(vmem_limit_bytes=32 * 1024 * 1024)
 
 
@@ -70,17 +71,40 @@
     return jnp.dot(left, right, precision=lax.Precision.HIGHEST, preferred_element_type=jnp.float32)
 
 
-def pack_kernel(forcing, init, scale, out, value, state, elems, rows, flip, sems):
+def pack_kernel(
+    forcing, init, scale, vol, faces, out, ops, diag, value, state, elems, volume, sides, rows, flip, sems
+):
     copies = [
         pltpu.make_async_copy(ref, into, sems.at[i])
-        for i, (ref, into) in enumerate(((forcing, value), (init, state), (scale, elems)))
+        for i, (ref, into) in enumerate(
+            ((vol, volume), (faces, sides), (forcing, value), (init, state), (scale, elems))
+        )
     ]
     for copy in copies:
         copy.start()
     step = lax.axis_index("z") * 8 + lax.axis_index("x") * 2 + lax.axis_index("core")
     weight = jnp.where(step == 0, 1.5, 0.5).astype(jnp.float32)
+    flip[...] = jnp.zeros((LANES, LANES), jnp.float32)
     rows[NB:, :] = jnp.zeros((LANES - NB, LANES), jnp.float32)
-    for copy in copies:
+    for copy in copies[:2]:
+        copy.wait()
+    row = lax.broadcasted_iota(jnp.int32, (LANES, LANES), 0)
+    col = lax.broadcasted_iota(jnp.int32, (LANES, LANES), 1)
+    for op in range(5):
+        flip[:NB, :NB] = volume[...] if op == 0 else sides[:, op - 1, :]
+        square = flip[...]
+        if op == 0:
+            on = jnp.where(row == col, square, 0.0)
+            diag[...] = jnp.broadcast_to(jnp.sum(on, axis=0, keepdims=True), (8, LANES))
+            square = square - on
+        square = square.T
+        high = square.astype(jnp.bfloat16)
+        low = (square - high.astype(jnp.float32)).astype(jnp.bfloat16)
+        at = op * LANES
+        ops[:LANES, at : at + LANES] = high
+        ops[LANES : 2 * LANES, at : at + LANES] = high
+        ops[2 * LANES :, at : at + LANES] = low
+    for copy in copies[2:]:
         copy.wait()
     for s in (1, 0):
         for r in range(2):
@@ -115,45 +139,28 @@
             out[pl.ds(at, FREQS, stride=24), :] = wave[c * FREQS : (c + 1) * FREQS]
 
 
-def operator_kernel(vol, faces, out, diag, square):
-    square[...] = jnp.zeros((LANES, LANES), jnp.float32)
-    row = lax.broadcasted_iota(jnp.int32, (LANES, LANES), 0)
-    col = lax.broadcasted_iota(jnp.int32, (LANES, LANES), 1)
-    for op in range(5):
-        square[:NB, :NB] = vol[...] if op == 0 else faces[op - 1]
-        value = square[...]
-        if op == 0:
-            on = jnp.where(row == col, value, 0.0)
-            diag[...] = jnp.broadcast_to(jnp.sum(on, axis=0, keepdims=True), (8, LANES))
-            value = value - on
-        value = value.T
-        high = value.astype(jnp.bfloat16)
-        low = (value - high.astype(jnp.float32)).astype(jnp.bfloat16)
-        at = op * LANES
-        out[:LANES, at : at + LANES] = high
-        out[LANES : 2 * LANES, at : at + LANES] = high
-        out[2 * LANES :, at : at + LANES] = low
-
-
 def slot():
     return lax.axis_index("x") * 8 + lax.axis_index("core") * 4 + lax.axis_index("y")
 
 
-def relax(slots, ops, diag, scale, iterate, source, inverse):
-    kappa = slot()
+def invert(slots, diag, scale, inverse):
+    mine = slots[slot()]
     shape = (WINDOW, 8, LANES)
-    lane = lax.broadcasted_iota(jnp.int32, shape, 2)
     place = lax.axis_index("z") * CHUNK - HALO + lax.broadcasted_iota(jnp.int32, shape, 0)
     inside = jnp.logical_and(place >= 0, place < 8 * CHUNK)
     scaled = scale[...] * diag[...][None]
-    im = slots[kappa, 2]
-    re0 = slots[kappa, 0] + scaled
-    re1 = slots[kappa, 1] + scaled
+    im = mine[2:3][None]
+    re0 = mine[0:1][None] + scaled
+    re1 = mine[1:2][None] + scaled
     mod0 = jnp.where(inside, damping / (re0 * re0 + im * im), 0.0)
     mod1 = jnp.where(inside, damping / (re1 * re1 + im * im), 0.0)
     inverse[0] = re0 * mod0
     inverse[1] = re1 * mod1
     inverse[2] = im * mod0
+
+
+def relax(ops, scale, inverse, iterate, source):
+    lane = lax.broadcasted_iota(jnp.int32, (WINDOW, 8, LANES), 2)
     g0 = jnp.where(lane < NB, iterate[0], 0.0)
     g1 = jnp.where(lane < NB, iterate[1], 0.0)
     source[0] = inverse[0] * g0 + inverse[2] * g1
@@ -161,7 +168,7 @@
     iterate[0] = source[0]
     iterate[1] = source[1]
     for sweep in range(1, SWEEPS):
-        lo, hi = sweep, WINDOW - sweep
+        lo, hi = sweep + 1, WINDOW - sweep - 1
         wide = hi - lo + 2
         coupled = []
         for c in range(2):
@@ -186,16 +193,7 @@
         iterate[1, lo:hi] = new1
 
 
-def hand_out(iterate, out, first):
-    for xc in range(8):
-        for yd in range(4):
-            for c in range(2):
-                for col in range(2):
-                    at = first + c * 4 + col * 2
-                    out[xc * 4 + yd, at : at + 2, :] = iterate[c, HALO + 2 * xc + col, 2 * yd : 2 * yd + 2, :]
-
-
-def first_kernel(slots, ops, diag, got, out, state, scale, iterate, source, inverse):
+def first_kernel(slots, ops, diag, got, solved, state, scale, inverse, iterate, source):
     for xc in range(8):
         for yd in range(4):
             for c in range(2):
@@ -206,35 +204,47 @@
                     at = c * 8 + col * 2
                     iterate[c, w, 2 * yd : 2 * yd + 2, :] = got[xc * 4 + yd, at : at + 2, :]
     scale[...] = jnp.broadcast_to(iterate[0, :, :, ES_LANE : ES_LANE + 1], scale.shape)
-    relax(slots, ops, diag, scale, iterate, source, inverse)
-    kappa = slot()
-    middle = slice(HALO, HALO + CHUNK)
-    state[...] = slots[kappa, 3] * iterate[0, middle] + slots[kappa, 4] * iterate[1, middle]
-    hand_out(iterate, out, 0)
-
-
-def carry_kernel(slots, got, state0, state1, state2, state3, left, right):
-    state = (state0[...] + state1[...]) + (state2[...] + state3[...])
-    kappa = slot()
+    invert(slots, diag, scale, inverse)
+    relax(ops, scale, inverse, iterate, source)
+    mine = slots[slot()]
+    middle = iterate[:, HALO : HALO + CHUNK]
+    solved[...] = middle
+    state[...] = mine[3:4][None] * middle[0] + mine[4:5][None] * middle[1]
+
+
+def between_kernel(got, solved, after, done, left, right):
+    del after
     for c in range(2):
-        part = slots[kappa, 5 + c] * state
-        left[c] = part[: CHUNK // 2]
-        right[c] = part[CHUNK // 2 :]
         for xc in range(8):
             side = left if xc < 4 else right
             for yd in range(4):
                 for col in range(2):
-                    at = 16 + c * 4 + col * 2
-                    here = (c, 2 * (xc % 4) + col, slice(2 * yd, 2 * yd + 2))
-                    side[here] = side[here] + got[xc * 4 + yd, at : at + 2, :]
-
-
-def second_kernel(slots, ops, diag, scale, west, left, right, east, before, out, iterate, source, inverse):
+                    rows = slice(2 * yd, 2 * yd + 2)
+                    at = c * 4 + col * 2
+                    done[xc * 4 + yd, at : at + 2, :] = solved[c, 2 * xc + col, rows, :]
+                    side[c, 2 * (xc % 4) + col, rows, :] = got[xc * 4 + yd, 16 + at : 18 + at, :]
+
+
+def carry_kernel(slots, left, right, state0, state1, state2, state3, out_left, out_right):
+    state = (state0[...] + state1[...]) + (state2[...] + state3[...])
+    mine = slots[slot()]
+    for c in range(2):
+        part = mine[5 + c : 6 + c][None] * state
+        out_left[c] = left[c] + part[: CHUNK // 2]
+        out_right[c] = right[c] + part[CHUNK // 2 :]
+
+
+def second_kernel(ops, scale, inverse, west, left, right, east, before, out, iterate, source):
     for i, part in enumerate((west, left, right, east)):
         iterate[:, i * HALO : (i + 1) * HALO] = part[...]
     out[:, :8, :] = before[...]
-    relax(slots, ops, diag, scale, iterate, source, inverse)
-    hand_out(iterate, out, 8)
+    relax(ops, scale, inverse, iterate, source)
+    for xc in range(8):
+        for yd in range(4):
+            for c in range(2):
+                for col in range(2):
+                    at = 8 + c * 4 + col * 2
+                    out[xc * 4 + yd, at : at + 2, :] = iterate[c, HALO + 2 * xc + col, 2 * yd : 2 * yd + 2, :]
 
 
 def backward_kernel(table, got, out):
@@ -284,54 +294,43 @@
 def per_device(forcing, init_state, elem_scale, vol_op, face_ops):
     square = pltpu.VMEM((LANES, LANES), jnp.float32)
     window = (WINDOW, 8, LANES)
-    work = [pltpu.VMEM((count,) + window, jnp.float32) for count in (2, 2, 3)]
-    ops, diag = call(
-        operator_kernel,
-        (jax.ShapeDtypeStruct((3 * LANES, 5 * LANES), jnp.bfloat16), f32(8, LANES)),
-        (vol_op, face_ops),
-        (square,),
-        name="operators",
-    )
-    packed = call(
+    inputs = (forcing, init_state, elem_scale, vol_op, jnp.transpose(face_ops, (1, 0, 2)))
+    packed, ops, diag = call(
         pack_kernel,
-        f32(STEPS * 12, LANES),
-        (forcing, init_state, elem_scale),
-        (
-            pltpu.VMEM(forcing.shape, jnp.float32),
-            pltpu.VMEM(init_state.shape, jnp.float32),
-            pltpu.VMEM(elem_scale.shape, jnp.float32),
-            square,
-            square,
-            pltpu.SemaphoreType.DMA((3,)),
-        ),
-        [HBM] * 3,
+        (f32(STEPS * 12, LANES), jax.ShapeDtypeStruct((3 * LANES, 5 * LANES), jnp.bfloat16), f32(8, LANES)),
+        inputs,
+        [pltpu.VMEM(value.shape, jnp.float32) for value in inputs]
+        + [square, square, pltpu.SemaphoreType.DMA((len(inputs),))],
+        [HBM] * len(inputs),
         name="pack",
         params=pltpu.CompilerParams(vmem_limit_bytes=60 * 1024 * 1024),
     )
     by_point = exchange(packed.reshape(STEPS, 3, 4, LANES), TIME).reshape(STEPS * 12, LANES)
     waves = call(forward_kernel, f32(FREQS * 24, LANES), (FORWARD, by_point), name="forward")
     got = exchange(waves.reshape(FREQS, 24, LANES), PLANE)
-    done, state, scale = call(
+    both = pltpu.VMEM((2,) + window, jnp.float32)
+    solved, state, scale, inverse = call(
         first_kernel,
-        (f32(FREQS, 8, LANES), f32(CHUNK, 8, LANES), f32(*window)),
+        (f32(2, CHUNK, 8, LANES), f32(CHUNK, 8, LANES), f32(*window), f32(3, *window)),
         (SLOTS, ops, diag, got),
-        work,
-        [SMEM, VMEM, VMEM, VMEM],
+        (both, both),
         name="first",
     )
+    half = f32(2, CHUNK // 2, 8, LANES)
     state = state + moved(state, "core", 1)
+    done, left, right = call(
+        between_kernel, (f32(FREQS, 8, LANES), half, half), (got, solved, state), (), [VMEM, VMEM, ANY], name="between"
+    )
     state = state + moved(state, "y", 1) + moved(state, "y", 2) + moved(state, "y", 3)
     states = [state] + [moved(state, "x", by) for by in (1, 2, 3)]
-    half = f32(2, CHUNK // 2, 8, LANES)
-    left, right = call(carry_kernel, (half, half), (SLOTS, got, *states), (), [SMEM] + [VMEM] * 5, name="carry")
+    left, right = call(carry_kernel, (half, half), (SLOTS, left, right, *states), name="carry")
     west = moved(right, "z", 1)
     east = moved(left, "z", -1)
     done = call(
         second_kernel,
         f32(FREQS, 16, LANES),
-        (SLOTS, ops, diag, scale, west, left, right, east, done),
-        work,
-        [SMEM] + [VMEM] * 8,
+        (ops, scale, inverse, west, left, right, east, done),
+        (both, both),
         name="second",
     )
     got = exchange(done, PLANE).reshape(FREQS * 16, LANES)

time: 115 us -> 111 us (0.965)
  blocking collectives: 63.2 us -> 80.5 us
  waiting for transfers between devices: 21 us -> 11.9 us
  starting transfers between devices: 15.1 us -> 7.74 us
  Pallas kernels: 13.8 us -> 10.6 us
    all_to_all x3 -> x4, blocking collectives: 63.2 us -> 80.5 us  [exchange(): return lax.all_to_all(blocks, axes, 0, 0, tiled=True)]
    all_to_all x1 -> x0, waiting for transfers between devices: 8.99 us -> none  [exchange(): return lax.all_to_all(blocks, axes, 0, 0, tiled=True)]
    all_to_all x1 -> x0, starting transfers between devices: 7.41 us -> none  [exchange(): return lax.all_to_all(blocks, axes, 0, 0, tiled=True)]
    pallas_call x8, Pallas kernels: 13.8 us -> 10.6 us  [call(): pl.pallas_call(kernel, out_shape=outs, in_specs=specs or [VMEM] * len(ins...]
  transfers between devices with their start and end apart: 10 -> 9, of which waited for: 9 -> 8; matrix products, arithmetic and copies ran while one was open for 0% -> 0% of each run, Pallas kernels for 0% -> 0%
where the time goes in v3:
time: 111 us
  blocking collectives  80.5 us (73%)
  waiting for transfers between devices  11.9 us (11%)
  Pallas kernels  10.6 us (10%)
  starting transfers between devices  7.74 us (7%)
    all_to_all x4, blocking collectives, exchange(): return lax.all_to_all(blocks, axes, 0, 0, tiled=True)  80.5 us
    ppermute x9, waiting for transfers between devices, moved(): lax.ppermute(block, axis, [(i, (i + by) % count) for i in range(count)])  11.9 us
    pallas_call x8, Pallas kernels, call(): pl.pallas_call(kernel, out_shape=outs, in_specs=specs or [VMEM] * len(ins...  10.6 us
    ppermute x9, starting transfers between devices, moved(): lax.ppermute(block, axis, [(i, (i + by) % count) for i in range(count)])  7.74 us
  transfers between devices with their start and end apart: 9, of which 8 were waited for; matrix products, arithmetic and copies ran while one was open for 0% of the time, Pallas kernels for 0%

profile of v3, /device:TPU:1, one launch (start us, length us, event | category | flops | bytes accessed | tf_op | source)
XLA Modules:
  0.0 110.8 jit_solution(4572755735091878072)
XLA Ops:
  0.0 2.4 %pack.1 = (f32[768,128]{1,0:T(8,128)}, bf16[384,640]{1,0:T(8,128)(2,1)}, f32[8,128]{1,0:T(8,128)}) custom-call(f32[2,1,125,2,128]{4,3,2,1,0:T(2,128)} %forcing.1, f32[125,2,128]{2,1,0:T(2,128)} %init.1, f32[2,128]{1,0:T(2,128)} %scale.1, f32[125,125]{1,0:T(8,128)} %vol.1, f32[125,4,125]{2,1,0:T(4,128)} %bitcast.13), custom_call_target="tpu_custom_call" | custom-call | tf_op jit(solution)/shard_map/pack/pallas_call | solution.py:270
  2.4 0.0 copy-start.3
  2.4 28.1 %all_to_all.20 = f32[64,3,4,128]{3,2,1,0:T(4,128)S(1)} all-to-all(f32[64,3,4,128]{3,2,1,0:T(4,128)} %bitcast.12), channel_id=1, replica_groups=mesh['z'=8,'x'=4,'core'=2,'y'=4] {'z','x','core'}, dimensions={0} | all-to-all | bytes 786432 | tf_op jit(solution)/shard_map/all_to_all | solution.py:286
  30.5 0.0 copy-done.3
  30.5 0.5 forward.1
  31.0 0.0 copy-start
  31.0 0.0 copy-start.1
  31.0 0.0 copy-start.4
  31.0 17.3 %all_to_all.21.got = f32[32,24,128]{2,1,0:T(8,128)S(1)} all-to-all(f32[32,24,128]{2,1,0:T(8,128)S(1)} %bitcast.8), channel_id=1, replica_groups=mesh['z'=8,'x'=4,'core'=2,'y'=4] {'x','core','y'}, dimensions={0} | all-to-all | bytes 786432 | tf_op jit(solution)/shard_map/all_to_all | solution.py:286
  48.3 0.0 copy-done
  48.3 0.0 copy-done.1
  48.3 0.0 copy-done.4
  48.3 3.1 %first.1 = (f32[2,16,8,128]{3,2,1,0:T(8,128)S(1)}, f32[16,8,128]{2,1,0:T(8,128)S(1)}, f32[32,8,128]{2,1,0:T(8,128)S(1)}, f32[3,32,8,128]{3,2,1,0:T(8,128)S(1)}) custom-call(f32[32,8,128]{2,1,0:T(8,128)S(1)} %copy-done.1, bf16[384,640]{1,0:T(8,128)(2,1)S(1)} %copy-done, f32[8,128]{1,0:T(8,128)S(1)} %copy-done.4, f32[32,24,128]{2,1,0:T(8,128)S(1)} %all_to_all.21.got), custom_call_target="tpu_custom_call" | custom-call | tf_op jit(solution)/shard_map/first/pallas_call | solution.py:270
  51.4 0.8 collective-permute-start
  52.2 0.9 collective-permute-done
  53.2 0.9 collective-permute-start.3
  54.0 1.0 collective-permute-start.2
  55.1 0.0 collective-permute-start.1
  55.1 1.3 %collective-permute-done.3 = f32[16,8,128]{2,1,0:T(8,128)S(1)} collective-permute-done((f32[16,8,128]{2,1,0:T(8,128)S(1)}, f32[16,8,128]{2,1,0:T(8,128)S(1)}, u32[]{:S(2)}, u32[]{:S(2)}) %collective-permute-start.3) | collective-permute-done | bytes 65568 | tf_op jit(solution)/shard_map/ppermute | solution.py:291
  56.3 2.3 %collective-permute-done.2 = f32[16,8,128]{2,1,0:T(8,128)S(1)} collective-permute-done((f32[16,8,128]{2,1,0:T(8,128)S(1)}, f32[16,8,128]{2,1,0:T(8,128)S(1)}, u32[]{:S(2)}, u32[]{:S(2)}) %collective-permute-start.2) | collective-permute-done | bytes 65568 | tf_op jit(solution)/shard_map/ppermute | solution.py:291
  58.7 1.5 %collective-permute-done.1 = f32[16,8,128]{2,1,0:T(8,128)S(1)} collective-permute-done((f32[16,8,128]{2,1,0:T(8,128)S(1)}, f32[16,8,128]{2,1,0:T(8,128)S(1)}, u32[]{:S(2)}, u32[]{:S(2)}) %collective-permute-start.1) | collective-permute-done | bytes 65568 | tf_op jit(solution)/shard_map/ppermute | solution.py:291
  60.2 1.0 collective-permute-start.6
  61.2 1.2 %collective-permute-start.5 = (f32[16,8,128]{2,1,0:T(8,128)S(1)}, f32[16,8,128]{2,1,0:T(8,128)S(1)}, u32[]{:S(2)}, u32[]{:S(2)}) collective-permute-start(f32[16,8,128]{2,1,0:T(8,128)S(1)} %add_add_fusion.state0), channel_id=1, source_target_pairs={{0,16},{8,24},{16,0},{24,8},{1,17},{9,25},{17,1},{25,9},{2,18},{10... | collective-permute-start | bytes 196616 | tf_op jit(solution)/shard_map/ppermute | solution.py:291
  62.5 0.0 collective-permute-start.4
  62.5 0.1 between.1
  62.6 0.8 collective-permute-done.6.state3
  63.4 2.5 %collective-permute-done.5.state2 = f32[16,8,128]{2,1,0:T(8,128)S(1)} collective-permute-done((f32[16,8,128]{2,1,0:T(8,128)S(1)}, f32[16,8,128]{2,1,0:T(8,128)S(1)}, u32[]{:S(2)}, u32[]{:S(2)}) %collective-permute-start.5) | collective-permute-done | bytes 65568 | tf_op jit(solution)/shard_map/ppermute | solution.py:291
  65.9 0.9 collective-permute-done.4.state1
  66.8 0.6 collective-permute-start.7
  67.5 2.1 %collective-permute-start.8 = (f32[2,8,8,128]{3,2,1,0:T(8,128)S(1)}, f32[2,8,8,128]{3,2,1,0:T(8,128)S(1)}, u32[]{:S(2)}, u32[]{:S(2)}) collective-permute-start(f32[2,8,8,128]{3,2,1,0:T(8,128)S(1)} %get-tuple-element.27.left), channel_id=1, source_target_pairs={{0,224},{32,0},{64,32},{96,64},{128,96},{160,128},{192,160},{224,1... | collective-permute-start | bytes 196616 | tf_op jit(solution)/shard_map/ppermute | solution.py:291
  69.6 1.6 %collective-permute-done.7.west = f32[2,8,8,128]{3,2,1,0:T(8,128)S(1)} collective-permute-done((f32[2,8,8,128]{3,2,1,0:T(8,128)S(1)}, f32[2,8,8,128]{3,2,1,0:T(8,128)S(1)}, u32[]{:S(2)}, u32[]{:S(2)}) %collective-permute-start.7) | collective-permute-done | bytes 65568 | tf_op jit(solution)/shard_map/ppermute | solution.py:291
  71.2 0.0 collective-permute-done.8.east
  71.2 3.1 %second.1 = f32[32,16,128]{2,1,0:T(8,128)S(1)} custom-call(bf16[384,640]{1,0:T(8,128)(2,1)S(1)} %copy-done, f32[32,8,128]{2,1,0:T(8,128)S(1)} %get-tuple-element.20.scale, f32[3,32,8,128]{3,2,1,0:T(8,128)S(1)} %get-tuple-element.21.inverse, f32[2,8,8,128]{3,2,1,0:T(8,128)S(1)} %collective-permute-done.7.west, f32[2,8,8,128]{3,2,1,0:T(8,128)S(1)} %get-tuple-element.27.left, ...), custom_call_target="tpu_custom_call" | custom-call | tf_op jit(solution)/shard_map/second/pallas_call | solution.py:270
  74.3 0.0 copy-start.2
  74.3 15.8 %all_to_all.22 = f32[32,16,128]{2,1,0:T(8,128)S(1)} all-to-all(f32[32,16,128]{2,1,0:T(8,128)S(1)} %second.1), channel_id=1, replica_groups=mesh['z'=8,'x'=4,'core'=2,'y'=4] {'x','core','y'}, dimensions={0} | all-to-all | bytes 524288 | tf_op jit(solution)/shard_map/all_to_all | solution.py:286
  90.1 0.0 copy-done.2
  90.1 0.4 backward.1
  90.5 19.4 %all_to_all.23 = f32[64,8,128]{2,1,0:T(8,128)S(1)} all-to-all(f32[64,8,128]{2,1,0:T(8,128)S(1)} %bitcast.10), channel_id=1, replica_groups=mesh['z'=8,'x'=4,'core'=2,'y'=4] {'z','x','core'}, dimensions={0} | all-to-all | bytes 524288 | tf_op jit(solution)/shard_map/all_to_all | solution.py:286
  109.9 0.9 unpack.1
  (3 shorter events, 0.1 us)
Async XLA Ops:
  2.4 28.1 %copy-start.3 = (f32[64,64]{1,0:T(8,128)S(1)}, f32[64,64]{1,0:T(8,128)}, u32[]{:S(2)}) copy-start(f32[64,64]{1,0:T(8,128)} %constant.6.clone.table) | copy-start | bytes 49156
  31.0 17.3 %copy-start = (bf16[384,640]{1,0:T(8,128)(2,1)S(1)}, bf16[384,640]{1,0:T(8,128)(2,1)}, u32[]{:S(2)}) copy-start(bf16[384,640]{1,0:T(8,128)(2,1)} %get-tuple-element.17.ops) | copy-start | bytes 1474564
  31.0 17.3 %copy-start.1 = (f32[32,8,128]{2,1,0:T(8,128)S(1)}, f32[32,8,128]{2,1,0:T(8,128)}, u32[]{:S(2)}) copy-start(f32[32,8,128]{2,1,0:T(8,128)} %constant.7.clone.slots) | copy-start | bytes 393220
  31.0 17.3 %copy-start.4 = (f32[8,128]{1,0:T(8,128)S(1)}, f32[8,128]{1,0:T(8,128)}, u32[]{:S(2)}) copy-start(f32[8,128]{1,0:T(8,128)} %get-tuple-element.18.diag) | copy-start | bytes 12292
  51.4 1.7 %collective-permute-start = (f32[16,8,128]{2,1,0:T(8,128)S(1)}, f32[16,8,128]{2,1,0:T(8,128)S(1)}, u32[]{:S(2)}, u32[]{:S(2)}) collective-permute-start(f32[16,8,128]{2,1,0:T(8,128)S(1)} %get-tuple-element.23), channel_id=1, source_target_pairs={{0,4},{4,0},{1,5},{5,1},{2,6},{6,2},{3,7},{7,3},{8,12},{12,8},{9,1... | collective-permute-start | bytes 196616 | tf_op jit(solution)/shard_map/ppermute | solution.py:291
  53.2 3.2 %collective-permute-start.3 = (f32[16,8,128]{2,1,0:T(8,128)S(1)}, f32[16,8,128]{2,1,0:T(8,128)S(1)}, u32[]{:S(2)}, u32[]{:S(2)}) collective-permute-start(f32[16,8,128]{2,1,0:T(8,128)S(1)} %add.12.after), channel_id=1, source_target_pairs={{0,3},{1,0},{2,1},{3,2},{4,7},{5,4},{6,5},{7,6},{8,11},{9,8},{10,9... | collective-permute-start | bytes 196616 | tf_op jit(solution)/shard_map/ppermute | solution.py:291
  54.0 4.6 %collective-permute-start.2 = (f32[16,8,128]{2,1,0:T(8,128)S(1)}, f32[16,8,128]{2,1,0:T(8,128)S(1)}, u32[]{:S(2)}, u32[]{:S(2)}) collective-permute-start(f32[16,8,128]{2,1,0:T(8,128)S(1)} %add.12.after), channel_id=1, source_target_pairs={{0,2},{1,3},{2,0},{3,1},{4,6},{5,7},{6,4},{7,5},{8,10},{9,11},{10,... | collective-permute-start | bytes 196616 | tf_op jit(solution)/shard_map/ppermute | solution.py:291
  55.1 5.1 %collective-permute-start.1 = (f32[16,8,128]{2,1,0:T(8,128)S(1)}, f32[16,8,128]{2,1,0:T(8,128)S(1)}, u32[]{:S(2)}, u32[]{:S(2)}) collective-permute-start(f32[16,8,128]{2,1,0:T(8,128)S(1)} %add.12.after), channel_id=1, source_target_pairs={{0,1},{1,2},{2,3},{3,0},{4,5},{5,6},{6,7},{7,4},{8,9},{9,10},{10,1... | collective-permute-start | bytes 196616 | tf_op jit(solution)/shard_map/ppermute | solution.py:291
  60.2 3.2 %collective-permute-start.6 = (f32[16,8,128]{2,1,0:T(8,128)S(1)}, f32[16,8,128]{2,1,0:T(8,128)S(1)}, u32[]{:S(2)}, u32[]{:S(2)}) collective-permute-start(f32[16,8,128]{2,1,0:T(8,128)S(1)} %add_add_fusion.state0), channel_id=1, source_target_pairs={{0,24},{8,0},{16,8},{24,16},{1,25},{9,1},{17,9},{25,17},{2,26},{10... | collective-permute-start | bytes 196616 | tf_op jit(solution)/shard_map/ppermute | solution.py:291
  61.2 4.6 %collective-permute-start.5 = (f32[16,8,128]{2,1,0:T(8,128)S(1)}, f32[16,8,128]{2,1,0:T(8,128)S(1)}, u32[]{:S(2)}, u32[]{:S(2)}) collective-permute-start(f32[16,8,128]{2,1,0:T(8,128)S(1)} %add_add_fusion.state0), channel_id=1, source_target_pairs={{0,16},{8,24},{16,0},{24,8},{1,17},{9,25},{17,1},{25,9},{2,18},{10... | collective-permute-start | bytes 196616 | tf_op jit(solution)/shard_map/ppermute | solution.py:291
  62.5 4.3 %collective-permute-start.4 = (f32[16,8,128]{2,1,0:T(8,128)S(1)}, f32[16,8,128]{2,1,0:T(8,128)S(1)}, u32[]{:S(2)}, u32[]{:S(2)}) collective-permute-start(f32[16,8,128]{2,1,0:T(8,128)S(1)} %add_add_fusion.state0), channel_id=1, source_target_pairs={{0,8},{8,16},{16,24},{24,0},{1,9},{9,17},{17,25},{25,1},{2,10},{10... | collective-permute-start | bytes 196616 | tf_op jit(solution)/shard_map/ppermute | solution.py:291
  66.8 4.4 %collective-permute-start.7 = (f32[2,8,8,128]{3,2,1,0:T(8,128)S(1)}, f32[2,8,8,128]{3,2,1,0:T(8,128)S(1)}, u32[]{:S(2)}, u32[]{:S(2)}) collective-permute-start(f32[2,8,8,128]{3,2,1,0:T(8,128)S(1)} %get-tuple-element.26.right), channel_id=1, source_target_pairs={{0,32},{32,64},{64,96},{96,128},{128,160},{160,192},{192,224},{224... | collective-permute-start | bytes 196616 | tf_op jit(solution)/shard_map/ppermute | solution.py:291
  67.5 3.8 %collective-permute-start.8 = (f32[2,8,8,128]{3,2,1,0:T(8,128)S(1)}, f32[2,8,8,128]{3,2,1,0:T(8,128)S(1)}, u32[]{:S(2)}, u32[]{:S(2)}) collective-permute-start(f32[2,8,8,128]{3,2,1,0:T(8,128)S(1)} %get-tuple-element.27.left), channel_id=1, source_target_pairs={{0,224},{32,0},{64,32},{96,64},{128,96},{160,128},{192,160},{224,1... | collective-permute-start | bytes 196616 | tf_op jit(solution)/shard_map/ppermute | solution.py:291
  74.3 15.8 %copy-start.2 = (f32[64,64]{1,0:T(8,128)S(1)}, f32[64,64]{1,0:T(8,128)}, u32[]{:S(2)}) copy-start(f32[64,64]{1,0:T(8,128)} %constant.8.clone.table) | copy-start | bytes 49156

commit v4 on v3

--- a/solution.py
+++ b/solution.py
@@ -2,6 +2,7 @@
 
 import jax
 import jax.numpy as jnp
+import ml_dtypes
 import numpy as np
 from jax import lax
 from jax.experimental import pallas as pl
@@ -54,10 +55,16 @@
     return tuple(a.astype(np.float32) for a in (forward, backward, shifts, carry, last))
 
 
+def in_parts(table):
+    high = table.astype(ml_dtypes.bfloat16)
+    low = (table - high.astype(np.float32)).astype(ml_dtypes.bfloat16)
+    return np.concatenate((high, high, low), axis=1)
+
+
 FORWARD, BACKWARD, SHIFTS, CARRY, LAST = tables()
 BY_PART = np.concatenate((np.arange(0, STEPS, 2), np.arange(1, STEPS, 2)))
-FORWARD = FORWARD[BY_PART]
-BACKWARD = BACKWARD[:, BY_PART]
+FORWARD = in_parts(FORWARD[BY_PART])
+BACKWARD = in_parts(BACKWARD[:, BY_PART])
 SLOTS = np.concatenate((SHIFTS[:, :3], LAST.reshape(FREQS, 2), CARRY.reshape(FREQS, 2), SHIFTS[:, :1]), axis=1)
 SLOTS = np.repeat(SLOTS[:, :, None], LANES, axis=2)
 
@@ -67,12 +74,18 @@
 PARAMS = pltpu.CompilerParams(vmem_limit_bytes=32 * 1024 * 1024)
 
 
-def exact(left, right):
-    return jnp.dot(left, right, precision=lax.Precision.HIGHEST, preferred_element_type=jnp.float32)
+def split(value):
+    high = value.astype(jnp.bfloat16)
+    return high, (value - high.astype(jnp.float32)).astype(jnp.bfloat16)
+
+
+def transform(table, parts):
+    high, low = split(jnp.concatenate(parts, axis=1))
+    return jnp.dot(table[...], jnp.concatenate((high, low, high), axis=0), preferred_element_type=jnp.float32)
 
 
 def pack_kernel(
-    forcing, init, scale, vol, faces, out, ops, diag, value, state, elems, volume, sides, rows, flip, sems
+    forcing, init, scale, vol, faces, out, ops, lows, diag, value, state, elems, volume, sides, rows, flip, sems
 ):
     copies = [
         pltpu.make_async_copy(ref, into, sems.at[i])
@@ -91,28 +104,32 @@
     row = lax.broadcasted_iota(jnp.int32, (LANES, LANES), 0)
     col = lax.broadcasted_iota(jnp.int32, (LANES, LANES), 1)
     for op in range(5):
-        flip[:NB, :NB] = volume[...] if op == 0 else sides[:, op - 1, :]
+        flip[:NB, :NB] = volume[0] if op == 0 else sides[:, op - 1, :]
         square = flip[...]
         if op == 0:
             on = jnp.where(row == col, square, 0.0)
             diag[...] = jnp.broadcast_to(jnp.sum(on, axis=0, keepdims=True), (8, LANES))
             square = square - on
         square = square.T
-        high = square.astype(jnp.bfloat16)
-        low = (square - high.astype(jnp.float32)).astype(jnp.bfloat16)
-        at = op * LANES
-        ops[:LANES, at : at + LANES] = high
-        ops[LANES : 2 * LANES, at : at + LANES] = high
-        ops[2 * LANES :, at : at + LANES] = low
+        high, low = split(square)
+        if op == 0:
+            here, rest = 4 * LANES, ops.at[:LANES, 5 * LANES :]
+        else:
+            here = (op - 1) * LANES
+            rest = lows.at[:, here : here + LANES]
+        ops[:LANES, here : here + LANES] = high
+        ops[LANES:, here : here + LANES] = high
+        rest[...] = low
+    ops[LANES:, 5 * LANES :] = jnp.zeros((LANES, LANES), jnp.bfloat16)
     for copy in copies[2:]:
         copy.wait()
     for s in (1, 0):
         for r in range(2):
             if s == 0:
-                rows[:NB, :] = value[s, 0, :, r, :] + weight * state[:, r, :]
-                rows[ES_LANE : ES_LANE + 1, :] = elems[r : r + 1, :]
+                rows[:NB, :] = value[s * NB : (s + 1) * NB, r, :] + weight * state[0, :, r, :]
+                rows[ES_LANE : ES_LANE + 1, :] = elems[0, r : r + 1, :]
             else:
-                rows[:NB, :] = value[s, 0, :, r, :]
+                rows[:NB, :] = value[s * NB : (s + 1) * NB, r, :]
             flip[...] = rows[...].T
             for c in range(2):
                 out[pl.ds(s * 8 + c * 2 + r, STEPS, stride=12), :] = flip[pl.ds(c, STEPS, stride=2), :]
@@ -129,7 +146,7 @@
 def forward_kernel(table, got, out):
     lane = lax.broadcasted_iota(jnp.int32, (STEPS, LANES), 1)
     parts = [got[pl.ds(p, STEPS, stride=12), :] for p in range(12)]
-    waves = exact(table[...], jnp.concatenate(parts, axis=1))
+    waves = transform(table, parts)
     for p in range(12):
         wave = waves[:, p * LANES : (p + 1) * LANES]
         if p < 8:
@@ -159,7 +176,7 @@
     inverse[2] = im * mod0
 
 
-def relax(ops, scale, inverse, iterate, source):
+def relax(ops, lows, scale, inverse, iterate, source):
     lane = lax.broadcasted_iota(jnp.int32, (WINDOW, 8, LANES), 2)
     g0 = jnp.where(lane < NB, iterate[0], 0.0)
     g1 = jnp.where(lane < NB, iterate[1], 0.0)
@@ -173,18 +190,21 @@
         coupled = []
         for c in range(2):
             field = iterate[c, lo - 1 : hi + 1].reshape(wide * 8, LANES)
-            high = field.astype(jnp.bfloat16)
-            low = (field - high.astype(jnp.float32)).astype(jnp.bfloat16)
+            high, low = split(field)
             sums = jnp.dot(
-                jnp.concatenate((high, low, high), axis=1), ops[...], preferred_element_type=jnp.float32
+                jnp.concatenate((high, low), axis=1), ops[...], preferred_element_type=jnp.float32
             )
-            part = [sums[:, i * LANES : (i + 1) * LANES].reshape(wide, 8, LANES) for i in range(5)]
+            rest = jnp.dot(high, lows[...], preferred_element_type=jnp.float32)
+            part = [sums[:, i * LANES : (i + 1) * LANES].reshape(wide, 8, LANES) for i in range(6)]
+            face = [
+                part[i] + rest[:, i * LANES : (i + 1) * LANES].reshape(wide, 8, LANES) for i in range(4)
+            ]
             coupled.append(
-                scale[lo:hi] * part[0][1:-1]
-                + part[1][:-2]
-                + part[2][2:]
-                + pltpu.roll(part[3][1:-1], 1, 1)
-                + pltpu.roll(part[4][1:-1], 7, 1)
+                scale[lo:hi] * (part[4] + part[5])[1:-1]
+                + face[0][:-2]
+                + face[1][2:]
+                + pltpu.roll(face[2][1:-1], 1, 1)
+                + pltpu.roll(face[3][1:-1], 7, 1)
             )
         cross = inverse[2, lo:hi]
         new0 = (1.0 - damping) * iterate[0, lo:hi] + source[0, lo:hi] - inverse[0, lo:hi] * coupled[0] - cross * coupled[1]
@@ -193,7 +213,7 @@
         iterate[1, lo:hi] = new1
 
 
-def first_kernel(slots, ops, diag, got, solved, state, scale, inverse, iterate, source):
+def first_kernel(slots, ops, lows, diag, got, solved, state, scale, inverse, iterate, source):
     for xc in range(8):
         for yd in range(4):
             for c in range(2):
@@ -205,7 +225,7 @@
                     iterate[c, w, 2 * yd : 2 * yd + 2, :] = got[xc * 4 + yd, at : at + 2, :]
     scale[...] = jnp.broadcast_to(iterate[0, :, :, ES_LANE : ES_LANE + 1], scale.shape)
     invert(slots, diag, scale, inverse)
-    relax(ops, scale, inverse, iterate, source)
+    relax(ops, lows, scale, inverse, iterate, source)
     mine = slots[slot()]
     middle = iterate[:, HALO : HALO + CHUNK]
     solved[...] = middle
@@ -234,11 +254,11 @@
         out_right[c] = right[c] + part[CHUNK // 2 :]
 
 
-def second_kernel(ops, scale, inverse, west, left, right, east, before, out, iterate, source):
+def second_kernel(ops, lows, scale, inverse, west, left, right, east, before, out, iterate, source):
     for i, part in enumerate((west, left, right, east)):
         iterate[:, i * HALO : (i + 1) * HALO] = part[...]
     out[:, :8, :] = before[...]
-    relax(ops, scale, inverse, iterate, source)
+    relax(ops, lows, scale, inverse, iterate, source)
     for xc in range(8):
         for yd in range(4):
             for c in range(2):
@@ -253,25 +273,30 @@
         at = (p // 4) * 8 + p % 4
         halves = [got[pl.ds(at + 4 * c, FREQS, stride=16), :] for c in range(2)]
         parts.append(jnp.concatenate(halves, axis=0))
-    slices = exact(table[...], jnp.concatenate(parts, axis=1))
+    slices = transform(table, parts)
     for p in range(8):
         out[pl.ds(p, STEPS, stride=8), :] = slices[:, p * LANES : (p + 1) * LANES]
 
 
-def unpack_kernel(got, out, flip):
+def unpack_kernel(got, out, flip, held, sems):
+    copies = []
     for s in range(2):
         for r in range(2):
             for c in range(2):
                 flip[pl.ds(c, STEPS, stride=2), :] = got[pl.ds(s * 4 + c * 2 + r, STEPS, stride=8), :]
-            out[s, 0, :, r, :] = flip[...].T[:NB, :]
-
-
-def call(kernel, outs, ins, scratch=(), specs=None, name=None, params=PARAMS):
+            held[s, 0, :, r, :] = flip[...].T[:NB, :]
+        copies.append(pltpu.make_async_copy(held.at[s], out.at[s], sems.at[s]))
+        copies[s].start()
+    for copy in copies:
+        copy.wait()
+
+
+def call(kernel, outs, ins, scratch=(), specs=None, name=None, params=PARAMS, out=VMEM):
     return pl.pallas_call(
         kernel,
         out_shape=outs,
         in_specs=specs or [VMEM] * len(ins),
-        out_specs=jax.tree.map(lambda _: VMEM, outs),
+        out_specs=jax.tree.map(lambda _: out, outs),
         scratch_shapes=scratch,
         compiler_params=params,
         name=name,
@@ -294,10 +319,21 @@
 def per_device(forcing, init_state, elem_scale, vol_op, face_ops):
     square = pltpu.VMEM((LANES, LANES), jnp.float32)
     window = (WINDOW, 8, LANES)
-    inputs = (forcing, init_state, elem_scale, vol_op, jnp.transpose(face_ops, (1, 0, 2)))
-    packed, ops, diag = call(
+    inputs = (
+        forcing.reshape(2 * NB, 2, LANES),
+        init_state.reshape(1, NB, 2, LANES),
+        elem_scale.reshape(1, 2, LANES),
+        vol_op.reshape(1, NB, NB),
+        jnp.transpose(face_ops, (1, 0, 2)),
+    )
+    packed, ops, lows, diag = call(
         pack_kernel,
-        (f32(STEPS * 12, LANES), jax.ShapeDtypeStruct((3 * LANES, 5 * LANES), jnp.bfloat16), f32(8, LANES)),
+        (
+            pltpu.VMEM((STEPS * 12, LANES), jnp.float32),
+            pltpu.VMEM((2 * LANES, 6 * LANES), jnp.bfloat16),
+            pltpu.VMEM((LANES, 4 * LANES), jnp.bfloat16),
+            pltpu.VMEM((8, LANES), jnp.float32),
+        ),
         inputs,
         [pltpu.VMEM(value.shape, jnp.float32) for value in inputs]
         + [square, square, pltpu.SemaphoreType.DMA((len(inputs),))],
@@ -312,7 +348,7 @@
     solved, state, scale, inverse = call(
         first_kernel,
         (f32(2, CHUNK, 8, LANES), f32(CHUNK, 8, LANES), f32(*window), f32(3, *window)),
-        (SLOTS, ops, diag, got),
+        (SLOTS, ops, lows, diag, got),
         (both, both),
         name="first",
     )
@@ -329,14 +365,22 @@
     done = call(
         second_kernel,
         f32(FREQS, 16, LANES),
-        (ops, scale, inverse, west, left, right, east, done),
+        (ops, lows, scale, inverse, west, left, right, east, done),
         (both, both),
         name="second",
     )
     got = exchange(done, PLANE).reshape(FREQS * 16, LANES)
     slices = call(backward_kernel, f32(STEPS * 8, LANES), (BACKWARD, got), name="backward")
     by_column = exchange(slices.reshape(STEPS, 8, LANES), TIME).reshape(STEPS * 8, LANES)
-    return call(unpack_kernel, f32(2, 1, NB, 2, LANES), (by_column,), (square,), name="unpack")
+    result = f32(2, 1, NB, 2, LANES)
+    return call(
+        unpack_kernel,
+        result,
+        (by_column,),
+        (square, pltpu.VMEM(result.shape, jnp.float32), pltpu.SemaphoreType.DMA((2,))),
+        name="unpack",
+        out=ANY,
+    )
 
 
 def solution(mesh):

time: 111 us -> 109 us (0.982)
  Pallas kernels: 10.6 us -> 8.66 us
    pallas_call x8, Pallas kernels: 10.6 us -> 8.66 us  [call(): pl.pallas_call(kernel, out_shape=outs, in_specs=specs or [VMEM] * len(ins...]
where the time goes in v4:
time: 109 us
  blocking collectives  80.2 us (74%)
  waiting for transfers between devices  11.9 us (11%)
  Pallas kernels  8.66 us (8%)
  starting transfers between devices  7.75 us (7%)
    all_to_all x4, blocking collectives, exchange(): return lax.all_to_all(blocks, axes, 0, 0, tiled=True)  80.2 us
    ppermute x9, waiting for transfers between devices, moved(): lax.ppermute(block, axis, [(i, (i + by) % count) for i in range(count)])  11.9 us
    pallas_call x8, Pallas kernels, call(): pl.pallas_call(kernel, out_shape=outs, in_specs=specs or [VMEM] * len(ins...  8.66 us
    ppermute x9, starting transfers between devices, moved(): lax.ppermute(block, axis, [(i, (i + by) % count) for i in range(count)])  7.75 us
  transfers between devices with their start and end apart: 9, of which 8 were waited for; matrix products, arithmetic and copies ran while one was open for 0% of the time, Pallas kernels for 0%

profile of v4, /device:TPU:1, one launch (start us, length us, event | category | flops | bytes accessed | tf_op | source)
XLA Modules:
  0.0 108.8 jit_solution(12994369349635881976)
XLA Ops:
  0.0 1.6 %pack.1 = (f32[768,128]{1,0:T(8,128)S(1)}, bf16[256,768]{1,0:T(8,128)(2,1)S(1)}, bf16[128,512]{1,0:T(8,128)(2,1)S(1)}, f32[8,128]{1,0:T(8,128)S(1)}) custom-call(f32[250,2,128]{2,1,0:T(2,128)} %bitcast.17, f32[1,125,2,128]{3,2,1,0:T(2,128)} %bitcast.19, f32[1,2,128]{2,1,0:T(2,128)} %bitcast.21, f32[1,125,125]{2,1,0:T(8,128)} %bitcast.20, f32[125,4,125]{2,1,0:T(4,128)} %bitcast.18), custom_call_target="tpu_custom_call" | custom-call | tf_op jit(solution)/shard_map/pack/pallas_call | solution.py:295
  1.6 0.0 copy-start.2
  1.6 27.8 %all_to_all.20 = f32[64,3,4,128]{3,2,1,0:T(4,128)S(1)} all-to-all(f32[64,3,4,128]{3,2,1,0:T(4,128)S(1)} %bitcast.16), channel_id=1, replica_groups=mesh['z'=8,'x'=4,'core'=2,'y'=4] {'z','x','core'}, dimensions={0} | all-to-all | bytes 786432 | tf_op jit(solution)/shard_map/all_to_all | solution.py:311
  29.5 0.0 copy-done.2
  29.5 0.2 forward.1
  29.7 0.0 copy-start
  29.7 17.3 %all_to_all.21.got = f32[32,24,128]{2,1,0:T(8,128)S(1)} all-to-all(f32[32,24,128]{2,1,0:T(8,128)S(1)} %bitcast.12), channel_id=1, replica_groups=mesh['z'=8,'x'=4,'core'=2,'y'=4] {'x','core','y'}, dimensions={0} | all-to-all | bytes 786432 | tf_op jit(solution)/shard_map/all_to_all | solution.py:311
  47.0 0.0 copy-done
  47.0 2.8 %first.1 = (f32[2,16,8,128]{3,2,1,0:T(8,128)S(1)}, f32[16,8,128]{2,1,0:T(8,128)S(1)}, f32[32,8,128]{2,1,0:T(8,128)S(1)}, f32[3,32,8,128]{3,2,1,0:T(8,128)S(1)}) custom-call(f32[32,8,128]{2,1,0:T(8,128)S(1)} %copy-done, bf16[256,768]{1,0:T(8,128)(2,1)S(1)} %get-tuple-element.18.ops, bf16[128,512]{1,0:T(8,128)(2,1)S(1)} %get-tuple-element.19.lows, ...), custom_call_target="tpu_custom_call" | custom-call | tf_op jit(solution)/shard_map/first/pallas_call | solution.py:295
  49.8 0.8 collective-permute-start
  50.6 0.9 collective-permute-done
  51.6 0.9 collective-permute-start.3
  52.5 1.0 collective-permute-start.2
  53.5 0.0 collective-permute-start.1
  53.5 1.3 %collective-permute-done.3 = f32[16,8,128]{2,1,0:T(8,128)S(1)} collective-permute-done((f32[16,8,128]{2,1,0:T(8,128)S(1)}, f32[16,8,128]{2,1,0:T(8,128)S(1)}, u32[]{:S(2)}, u32[]{:S(2)}) %collective-permute-start.3) | collective-permute-done | bytes 65568 | tf_op jit(solution)/shard_map/ppermute | solution.py:316
  54.8 2.3 %collective-permute-done.2 = f32[16,8,128]{2,1,0:T(8,128)S(1)} collective-permute-done((f32[16,8,128]{2,1,0:T(8,128)S(1)}, f32[16,8,128]{2,1,0:T(8,128)S(1)}, u32[]{:S(2)}, u32[]{:S(2)}) %collective-permute-start.2) | collective-permute-done | bytes 65568 | tf_op jit(solution)/shard_map/ppermute | solution.py:316
  57.1 1.5 %collective-permute-done.1 = f32[16,8,128]{2,1,0:T(8,128)S(1)} collective-permute-done((f32[16,8,128]{2,1,0:T(8,128)S(1)}, f32[16,8,128]{2,1,0:T(8,128)S(1)}, u32[]{:S(2)}, u32[]{:S(2)}) %collective-permute-start.1) | collective-permute-done | bytes 65568 | tf_op jit(solution)/shard_map/ppermute | solution.py:316
  58.6 1.0 collective-permute-start.6
  59.6 1.2 %collective-permute-start.5 = (f32[16,8,128]{2,1,0:T(8,128)S(1)}, f32[16,8,128]{2,1,0:T(8,128)S(1)}, u32[]{:S(2)}, u32[]{:S(2)}) collective-permute-start(f32[16,8,128]{2,1,0:T(8,128)S(1)} %add_add_fusion.state0), channel_id=1, source_target_pairs={{0,16},{8,24},{16,0},{24,8},{1,17},{9,25},{17,1},{25,9},{2,18},{10... | collective-permute-start | bytes 196616 | tf_op jit(solution)/shard_map/ppermute | solution.py:316
  60.9 0.0 collective-permute-start.4
  60.9 0.1 between.1
  61.0 0.8 collective-permute-done.6.state3
  61.8 2.4 %collective-permute-done.5.state2 = f32[16,8,128]{2,1,0:T(8,128)S(1)} collective-permute-done((f32[16,8,128]{2,1,0:T(8,128)S(1)}, f32[16,8,128]{2,1,0:T(8,128)S(1)}, u32[]{:S(2)}, u32[]{:S(2)}) %collective-permute-start.5) | collective-permute-done | bytes 65568 | tf_op jit(solution)/shard_map/ppermute | solution.py:316
  64.3 1.0 collective-permute-done.4.state1
  65.3 0.6 collective-permute-start.7
  65.9 2.1 %collective-permute-start.8 = (f32[2,8,8,128]{3,2,1,0:T(8,128)S(1)}, f32[2,8,8,128]{3,2,1,0:T(8,128)S(1)}, u32[]{:S(2)}, u32[]{:S(2)}) collective-permute-start(f32[2,8,8,128]{3,2,1,0:T(8,128)S(1)} %get-tuple-element.29.left), channel_id=1, source_target_pairs={{0,224},{32,0},{64,32},{96,64},{128,96},{160,128},{192,160},{224,1... | collective-permute-start | bytes 196616 | tf_op jit(solution)/shard_map/ppermute | solution.py:316
  68.0 1.6 %collective-permute-done.7.west = f32[2,8,8,128]{3,2,1,0:T(8,128)S(1)} collective-permute-done((f32[2,8,8,128]{3,2,1,0:T(8,128)S(1)}, f32[2,8,8,128]{3,2,1,0:T(8,128)S(1)}, u32[]{:S(2)}, u32[]{:S(2)}) %collective-permute-start.7) | collective-permute-done | bytes 65568 | tf_op jit(solution)/shard_map/ppermute | solution.py:316
  69.7 0.0 collective-permute-done.8.east
  69.7 2.7 %second.1 = f32[32,16,128]{2,1,0:T(8,128)S(1)} custom-call(bf16[256,768]{1,0:T(8,128)(2,1)S(1)} %get-tuple-element.18.ops, bf16[128,512]{1,0:T(8,128)(2,1)S(1)} %get-tuple-element.19.lows, f32[32,8,128]{2,1,0:T(8,128)S(1)} %get-tuple-element.22.scale, f32[3,32,8,128]{3,2,1,0:T(8,128)S(1)} %get-tuple-element.23.inverse, ...), custom_call_target="tpu_custom_call" | custom-call | tf_op jit(solution)/shard_map/second/pallas_call | solution.py:295
  72.4 0.0 copy-start.1
  72.4 15.8 %all_to_all.22 = f32[32,16,128]{2,1,0:T(8,128)S(1)} all-to-all(f32[32,16,128]{2,1,0:T(8,128)S(1)} %second.1), channel_id=1, replica_groups=mesh['z'=8,'x'=4,'core'=2,'y'=4] {'x','core','y'}, dimensions={0} | all-to-all | bytes 524288 | tf_op jit(solution)/shard_map/all_to_all | solution.py:311
  88.2 0.0 copy-done.1
  88.2 0.2 backward.1
  88.4 19.3 %all_to_all.23 = f32[64,8,128]{2,1,0:T(8,128)S(1)} all-to-all(f32[64,8,128]{2,1,0:T(8,128)S(1)} %bitcast.14), channel_id=1, replica_groups=mesh['z'=8,'x'=4,'core'=2,'y'=4] {'z','x','core'}, dimensions={0} | all-to-all | bytes 524288 | tf_op jit(solution)/shard_map/all_to_all | solution.py:311
  107.8 0.9 unpack.1
  (3 shorter events, 0.1 us)
Async XLA Ops:
  1.6 27.9 %copy-start.2 = (bf16[64,192]{1,0:T(8,128)(2,1)S(1)}, bf16[64,192]{1,0:T(8,128)(2,1)}, u32[]{:S(2)}) copy-start(bf16[64,192]{1,0:T(8,128)(2,1)} %constant.6.clone.table) | copy-start | bytes 73732
  29.7 17.3 %copy-start = (f32[32,8,128]{2,1,0:T(8,128)S(1)}, f32[32,8,128]{2,1,0:T(8,128)}, u32[]{:S(2)}) copy-start(f32[32,8,128]{2,1,0:T(8,128)} %constant.7.clone.slots) | copy-start | bytes 393220
  49.8 1.7 %collective-permute-start = (f32[16,8,128]{2,1,0:T(8,128)S(1)}, f32[16,8,128]{2,1,0:T(8,128)S(1)}, u32[]{:S(2)}, u32[]{:S(2)}) collective-permute-start(f32[16,8,128]{2,1,0:T(8,128)S(1)} %get-tuple-element.25), channel_id=1, source_target_pairs={{0,4},{4,0},{1,5},{5,1},{2,6},{6,2},{3,7},{7,3},{8,12},{12,8},{9,1... | collective-permute-start | bytes 196616 | tf_op jit(solution)/shard_map/ppermute | solution.py:316
  51.6 3.2 %collective-permute-start.3 = (f32[16,8,128]{2,1,0:T(8,128)S(1)}, f32[16,8,128]{2,1,0:T(8,128)S(1)}, u32[]{:S(2)}, u32[]{:S(2)}) collective-permute-start(f32[16,8,128]{2,1,0:T(8,128)S(1)} %add.12.after), channel_id=1, source_target_pairs={{0,3},{1,0},{2,1},{3,2},{4,7},{5,4},{6,5},{7,6},{8,11},{9,8},{10,9... | collective-permute-start | bytes 196616 | tf_op jit(solution)/shard_map/ppermute | solution.py:316
  52.5 4.6 %collective-permute-start.2 = (f32[16,8,128]{2,1,0:T(8,128)S(1)}, f32[16,8,128]{2,1,0:T(8,128)S(1)}, u32[]{:S(2)}, u32[]{:S(2)}) collective-permute-start(f32[16,8,128]{2,1,0:T(8,128)S(1)} %add.12.after), channel_id=1, source_target_pairs={{0,2},{1,3},{2,0},{3,1},{4,6},{5,7},{6,4},{7,5},{8,10},{9,11},{10,... | collective-permute-start | bytes 196616 | tf_op jit(solution)/shard_map/ppermute | solution.py:316
  53.5 5.1 %collective-permute-start.1 = (f32[16,8,128]{2,1,0:T(8,128)S(1)}, f32[16,8,128]{2,1,0:T(8,128)S(1)}, u32[]{:S(2)}, u32[]{:S(2)}) collective-permute-start(f32[16,8,128]{2,1,0:T(8,128)S(1)} %add.12.after), channel_id=1, source_target_pairs={{0,1},{1,2},{2,3},{3,0},{4,5},{5,6},{6,7},{7,4},{8,9},{9,10},{10,1... | collective-permute-start | bytes 196616 | tf_op jit(solution)/shard_map/ppermute | solution.py:316
  58.6 3.2 %collective-permute-start.6 = (f32[16,8,128]{2,1,0:T(8,128)S(1)}, f32[16,8,128]{2,1,0:T(8,128)S(1)}, u32[]{:S(2)}, u32[]{:S(2)}) collective-permute-start(f32[16,8,128]{2,1,0:T(8,128)S(1)} %add_add_fusion.state0), channel_id=1, source_target_pairs={{0,24},{8,0},{16,8},{24,16},{1,25},{9,1},{17,9},{25,17},{2,26},{10... | collective-permute-start | bytes 196616 | tf_op jit(solution)/shard_map/ppermute | solution.py:316
  59.6 4.6 %collective-permute-start.5 = (f32[16,8,128]{2,1,0:T(8,128)S(1)}, f32[16,8,128]{2,1,0:T(8,128)S(1)}, u32[]{:S(2)}, u32[]{:S(2)}) collective-permute-start(f32[16,8,128]{2,1,0:T(8,128)S(1)} %add_add_fusion.state0), channel_id=1, source_target_pairs={{0,16},{8,24},{16,0},{24,8},{1,17},{9,25},{17,1},{25,9},{2,18},{10... | collective-permute-start | bytes 196616 | tf_op jit(solution)/shard_map/ppermute | solution.py:316
  60.9 4.3 %collective-permute-start.4 = (f32[16,8,128]{2,1,0:T(8,128)S(1)}, f32[16,8,128]{2,1,0:T(8,128)S(1)}, u32[]{:S(2)}, u32[]{:S(2)}) collective-permute-start(f32[16,8,128]{2,1,0:T(8,128)S(1)} %add_add_fusion.state0), channel_id=1, source_target_pairs={{0,8},{8,16},{16,24},{24,0},{1,9},{9,17},{17,25},{25,1},{2,10},{10... | collective-permute-start | bytes 196616 | tf_op jit(solution)/shard_map/ppermute | solution.py:316
  65.3 4.4 %collective-permute-start.7 = (f32[2,8,8,128]{3,2,1,0:T(8,128)S(1)}, f32[2,8,8,128]{3,2,1,0:T(8,128)S(1)}, u32[]{:S(2)}, u32[]{:S(2)}) collective-permute-start(f32[2,8,8,128]{3,2,1,0:T(8,128)S(1)} %get-tuple-element.28.right), channel_id=1, source_target_pairs={{0,32},{32,64},{64,96},{96,128},{128,160},{160,192},{192,224},{224... | collective-permute-start | bytes 196616 | tf_op jit(solution)/shard_map/ppermute | solution.py:316
  65.9 3.8 %collective-permute-start.8 = (f32[2,8,8,128]{3,2,1,0:T(8,128)S(1)}, f32[2,8,8,128]{3,2,1,0:T(8,128)S(1)}, u32[]{:S(2)}, u32[]{:S(2)}) collective-permute-start(f32[2,8,8,128]{3,2,1,0:T(8,128)S(1)} %get-tuple-element.29.left), channel_id=1, source_target_pairs={{0,224},{32,0},{64,32},{96,64},{128,96},{160,128},{192,160},{224,1... | collective-permute-start | bytes 196616 | tf_op jit(solution)/shard_map/ppermute | solution.py:316
  72.4 15.8 %copy-start.1 = (bf16[64,192]{1,0:T(8,128)(2,1)S(1)}, bf16[64,192]{1,0:T(8,128)(2,1)}, u32[]{:S(2)}) copy-start(bf16[64,192]{1,0:T(8,128)(2,1)} %constant.8.clone.table) | copy-start | bytes 73732

commit v5 on v4

--- a/solution.py
+++ b/solution.py
@@ -57,8 +57,10 @@
 
 def in_parts(table):
     high = table.astype(ml_dtypes.bfloat16)
-    low = (table - high.astype(np.float32)).astype(ml_dtypes.bfloat16)
-    return np.concatenate((high, high, low), axis=1)
+    rest = table - high.astype(np.float32)
+    middle = rest.astype(ml_dtypes.bfloat16)
+    low = (rest - middle.astype(np.float32)).astype(ml_dtypes.bfloat16)
+    return np.concatenate((high, high, middle, high, middle, low), axis=1)
 
 
 FORWARD, BACKWARD, SHIFTS, CARRY, LAST = tables()
@@ -80,8 +82,11 @@
 
 
 def transform(table, parts):
-    high, low = split(jnp.concatenate(parts, axis=1))
-    return jnp.dot(table[...], jnp.concatenate((high, low, high), axis=0), preferred_element_type=jnp.float32)
+    whole = jnp.concatenate(parts, axis=1)
+    high = whole.astype(jnp.bfloat16)
+    middle, low = split(whole - high.astype(jnp.float32))
+    stack = jnp.concatenate((high, middle, high, low, middle, high), axis=0)
+    return jnp.dot(table[...], stack, preferred_element_type=jnp.float32)
 
 
 def pack_kernel(
@@ -176,41 +181,55 @@
     inverse[2] = im * mod0
 
 
+def start(inverse, field, source, at):
+    lane = lax.broadcasted_iota(jnp.int32, field.shape[1:], 2)
+    g0 = jnp.where(lane < NB, field[0], 0.0)
+    g1 = jnp.where(lane < NB, field[1], 0.0)
+    source[0, at] = inverse[0, at] * g0 + inverse[2, at] * g1
+    source[1, at] = inverse[1, at] * g1 - inverse[2, at] * g0
+
+
+def couple(ops, lows, scale, field):
+    wide = field.shape[0]
+    inner = (wide - 2, 8, LANES)
+    high, low = split(field.reshape(wide * 8, LANES))
+    both = jnp.concatenate((high, low), axis=1)
+
+    def product(left, right):
+        return jnp.dot(left, right, preferred_element_type=jnp.float32)
+
+    def columns(sums, i):
+        return sums[:, i * LANES : (i + 1) * LANES].reshape(-1, 8, LANES)
+
+    own = product(both[8:-8], ops[:, 4 * LANES :])
+    along = product(both, ops[:, : 2 * LANES]) + product(high, lows[:, : 2 * LANES])
+    across = product(both[8:-8], ops[:, 2 * LANES : 4 * LANES]) + product(high[8:-8], lows[:, 2 * LANES :])
+    return (
+        scale * (columns(own, 0) + columns(own, 1))
+        + columns(along, 0)[:-2]
+        + columns(along, 1)[2:]
+        + pltpu.roll(columns(across, 0), 1, 1)
+        + pltpu.roll(columns(across, 1), 7, 1)
+    )
+
+
+def damped(field, source, inverse, coupled):
+    keep = 1.0 - damping
+    return (
+        keep * field[0] + source[0] - inverse[0] * coupled[0] - inverse[2] * coupled[1],
+        keep * field[1] + source[1] - inverse[1] * coupled[1] + inverse[2] * coupled[0],
+    )
+
+
 def relax(ops, lows, scale, inverse, iterate, source):
-    lane = lax.broadcasted_iota(jnp.int32, (WINDOW, 8, LANES), 2)
-    g0 = jnp.where(lane < NB, iterate[0], 0.0)
-    g1 = jnp.where(lane < NB, iterate[1], 0.0)
-    source[0] = inverse[0] * g0 + inverse[2] * g1
-    source[1] = inverse[1] * g1 - inverse[2] * g0
-    iterate[0] = source[0]
-    iterate[1] = source[1]
+    start(inverse, iterate[...], source, slice(0, WINDOW))
+    iterate[...] = source[...]
     for sweep in range(1, SWEEPS):
-        lo, hi = sweep + 1, WINDOW - sweep - 1
-        wide = hi - lo + 2
-        coupled = []
-        for c in range(2):
-            field = iterate[c, lo - 1 : hi + 1].reshape(wide * 8, LANES)
-            high, low = split(field)
-            sums = jnp.dot(
-                jnp.concatenate((high, low), axis=1), ops[...], preferred_element_type=jnp.float32
-            )
-            rest = jnp.dot(high, lows[...], preferred_element_type=jnp.float32)
-            part = [sums[:, i * LANES : (i + 1) * LANES].reshape(wide, 8, LANES) for i in range(6)]
-            face = [
-                part[i] + rest[:, i * LANES : (i + 1) * LANES].reshape(wide, 8, LANES) for i in range(4)
-            ]
-            coupled.append(
-                scale[lo:hi] * (part[4] + part[5])[1:-1]
-                + face[0][:-2]
-                + face[1][2:]
-                + pltpu.roll(face[2][1:-1], 1, 1)
-                + pltpu.roll(face[3][1:-1], 7, 1)
-            )
-        cross = inverse[2, lo:hi]
-        new0 = (1.0 - damping) * iterate[0, lo:hi] + source[0, lo:hi] - inverse[0, lo:hi] * coupled[0] - cross * coupled[1]
-        new1 = (1.0 - damping) * iterate[1, lo:hi] + source[1, lo:hi] - inverse[1, lo:hi] * coupled[1] + cross * coupled[0]
-        iterate[0, lo:hi] = new0
-        iterate[1, lo:hi] = new1
+        here = slice(sweep + 1, WINDOW - sweep - 1)
+        coupled = [couple(ops, lows, scale[here], iterate[c, sweep : WINDOW - sweep]) for c in range(2)]
+        fresh = damped(iterate[:, here], source[:, here], inverse[:, here], coupled)
+        iterate[0, here] = fresh[0]
+        iterate[1, here] = fresh[1]
 
 
 def first_kernel(slots, ops, lows, diag, got, solved, state, scale, inverse, iterate, source):
@@ -254,17 +273,57 @@
         out_right[c] = right[c] + part[CHUNK // 2 :]
 
 
-def second_kernel(ops, lows, scale, inverse, west, left, right, east, before, out, iterate, source):
+def inner_kernel(ops, lows, scale, inverse, left, right, edges, iterate, source):
+    middle = slice(HALO, HALO + CHUNK)
+    for i, part in enumerate((left, right)):
+        start(inverse, part[...], source, slice((i + 1) * HALO, (i + 2) * HALO))
+    iterate[...] = source[:, middle]
+    for sweep in range(SWEEPS):
+        lo, hi = sweep, CHUNK - sweep
+        if sweep:
+            here = slice(HALO + lo, HALO + hi)
+            coupled = [couple(ops, lows, scale[here], iterate[c, lo - 1 : hi + 1]) for c in range(2)]
+            fresh = damped(iterate[:, lo:hi], source[:, here], inverse[:, here], coupled)
+            iterate[0, lo:hi] = fresh[0]
+            iterate[1, lo:hi] = fresh[1]
+        edges[sweep, :, :2] = iterate[:, lo : lo + 2]
+        edges[sweep, :, 2:] = iterate[:, hi - 2 : hi]
+
+
+def outer_kernel(ops, lows, scale, inverse, west, left, right, east, edges, before, out, iterate, source):
     for i, part in enumerate((west, left, right, east)):
-        iterate[:, i * HALO : (i + 1) * HALO] = part[...]
+        start(inverse, part[...], source, slice(i * HALO, (i + 1) * HALO))
     out[:, :8, :] = before[...]
-    relax(ops, lows, scale, inverse, iterate, source)
+    reach = SWEEPS - 1
+    iterate[:, :reach] = source[:, 1:HALO]
+    iterate[:, reach + 4 :] = source[:, HALO + CHUNK : WINDOW - 1]
+    for sweep in range(1, SWEEPS):
+        iterate[:, reach : reach + 4] = edges[sweep - 1]
+        one = slice(sweep + 1, HALO + sweep)
+        two = slice(WINDOW - HALO - sweep, WINDOW - 1 - sweep)
+        sides = [
+            jnp.concatenate((ref[one], ref[HALO : HALO + 2], ref[two]), axis=0)
+            for ref in [scale] + [inverse.at[i] for i in range(3)] + [source.at[i] for i in range(2)]
+        ]
+        coupled = [couple(ops, lows, sides[0], iterate[c]) for c in range(2)]
+        fresh = damped(iterate[:, 1:-1], sides[4:], sides[1:4], coupled)
+        for c in range(2):
+            iterate[c, :reach] = fresh[c][:reach]
+            iterate[c, reach + 4 :] = fresh[c][reach + 2 :]
+    last = edges.at[SWEEPS - 1]
     for xc in range(8):
-        for yd in range(4):
+        for col in range(2):
+            x = 2 * xc + col
             for c in range(2):
-                for col in range(2):
-                    at = 8 + c * 4 + col * 2
-                    out[xc * 4 + yd, at : at + 2, :] = iterate[c, HALO + 2 * xc + col, 2 * yd : 2 * yd + 2, :]
+                if x < reach:
+                    tile = iterate.at[c, x]
+                elif x < reach + 2:
+                    tile = last.at[c, x - reach]
+                else:
+                    tile = iterate.at[c, x + 2]
+                at = 8 + c * 4 + col * 2
+                for yd in range(4):
+                    out[xc * 4 + yd, at : at + 2, :] = tile[2 * yd : 2 * yd + 2, :]
 
 
 def backward_kernel(table, got, out):
@@ -291,7 +350,7 @@
         copy.wait()
 
 
-def call(kernel, outs, ins, scratch=(), specs=None, name=None, params=PARAMS, out=VMEM):
+def call(kernel, outs, ins, scratch=(), specs=None, name=None, params=PARAMS, out=VMEM, cost=None):
     return pl.pallas_call(
         kernel,
         out_shape=outs,
@@ -299,6 +358,7 @@
         out_specs=jax.tree.map(lambda _: out, outs),
         scratch_shapes=scratch,
         compiler_params=params,
+        cost_estimate=cost,
         name=name,
     )(*ins)
 
@@ -362,12 +422,20 @@
     left, right = call(carry_kernel, (half, half), (SLOTS, left, right, *states), name="carry")
     west = moved(right, "z", 1)
     east = moved(left, "z", -1)
+    edges = call(
+        inner_kernel,
+        f32(SWEEPS, 2, 4, 8, LANES),
+        (ops, lows, scale, inverse, left, right),
+        (pltpu.VMEM((2, CHUNK, 8, LANES), jnp.float32), both),
+        name="inner",
+        cost=pl.CostEstimate(flops=2_000_000_000, bytes_accessed=1_000_000, transcendentals=0),
+    )
     done = call(
-        second_kernel,
+        outer_kernel,
         f32(FREQS, 16, LANES),
-        (ops, lows, scale, inverse, west, left, right, east, done),
-        (both, both),
-        name="second",
+        (ops, lows, scale, inverse, west, left, right, east, edges, done),
+        (pltpu.VMEM((2, 2 * SWEEPS + 2, 8, LANES), jnp.float32), both),
+        name="outer",
     )
     got = exchange(done, PLANE).reshape(FREQS * 16, LANES)
     slices = call(backward_kernel, f32(STEPS * 8, LANES), (BACKWARD, got), name="backward")

time: 109 us -> 109 us (level)
  waiting for transfers between devices: 11.9 us -> 10.2 us
  Pallas kernels: 8.66 us -> 9.98 us
    ppermute x9, waiting for transfers between devices: 11.9 us -> 10.2 us  [moved(): lax.ppermute(block, axis, [(i, (i + by) % count) for i in range(count)])]
    pallas_call x8 -> x9, Pallas kernels: 8.66 us -> 9.98 us  [call(): pl.pallas_call(kernel, out_shape=outs, in_specs=specs or [VMEM] * len(ins...]
  transfers between devices with their start and end apart: 9 -> 9, of which waited for: 8 -> 7; matrix products, arithmetic and copies ran while one was open for 0% -> 0% of each run, Pallas kernels for 0% -> 2%
where the time goes in v5:
time: 109 us
  blocking collectives  80.3 us (74%)
  waiting for transfers between devices  10.2 us (9%)
  Pallas kernels  9.98 us (9%)
  starting transfers between devices  7.74 us (7%)
    all_to_all x4, blocking collectives, exchange(): return lax.all_to_all(blocks, axes, 0, 0, tiled=True)  80.3 us
    ppermute x9, waiting for transfers between devices, moved(): lax.ppermute(block, axis, [(i, (i + by) % count) for i in range(count)])  10.2 us
    pallas_call x9, Pallas kernels, call(): pl.pallas_call(kernel, out_shape=outs, in_specs=specs or [VMEM] * len(ins...  9.98 us
    ppermute x9, starting transfers between devices, moved(): lax.ppermute(block, axis, [(i, (i + by) % count) for i in range(count)])  7.74 us
  transfers between devices with their start and end apart: 9, of which 7 were waited for; matrix products, arithmetic and copies ran while one was open for 0% of the time, Pallas kernels for 2%

profile of v5, /device:TPU:1, one launch (start us, length us, event | category | flops | bytes accessed | tf_op | source)
XLA Modules:
  0.0 108.5 jit_solution(10170689942893460699)
XLA Ops:
  0.0 1.6 %pack.1 = (f32[768,128]{1,0:T(8,128)S(1)}, bf16[256,768]{1,0:T(8,128)(2,1)S(1)}, bf16[128,512]{1,0:T(8,128)(2,1)S(1)}, f32[8,128]{1,0:T(8,128)S(1)}) custom-call(f32[250,2,128]{2,1,0:T(2,128)} %bitcast.17, f32[1,125,2,128]{3,2,1,0:T(2,128)} %bitcast.19, f32[1,2,128]{2,1,0:T(2,128)} %bitcast.21, f32[1,125,125]{2,1,0:T(8,128)} %bitcast.20, f32[125,4,125]{2,1,0:T(4,128)} %bitcast.18), custom_call_target="tpu_custom_call" | custom-call | tf_op jit(solution)/shard_map/pack/pallas_call | solution.py:354
  1.6 0.0 copy-start.2
  1.6 28.0 %all_to_all.20 = f32[64,3,4,128]{3,2,1,0:T(4,128)S(1)} all-to-all(f32[64,3,4,128]{3,2,1,0:T(4,128)S(1)} %bitcast.16), channel_id=1, replica_groups=mesh['z'=8,'x'=4,'core'=2,'y'=4] {'z','x','core'}, dimensions={0} | all-to-all | bytes 786432 | tf_op jit(solution)/shard_map/all_to_all | solution.py:371
  29.6 0.0 copy-done.2
  29.6 0.3 forward.1
  30.0 0.0 copy-start
  30.0 17.3 %all_to_all.21.got = f32[32,24,128]{2,1,0:T(8,128)S(1)} all-to-all(f32[32,24,128]{2,1,0:T(8,128)S(1)} %bitcast.12), channel_id=1, replica_groups=mesh['z'=8,'x'=4,'core'=2,'y'=4] {'x','core','y'}, dimensions={0} | all-to-all | bytes 786432 | tf_op jit(solution)/shard_map/all_to_all | solution.py:371
  47.2 0.0 copy-done
  47.2 2.7 %first.1 = (f32[2,16,8,128]{3,2,1,0:T(8,128)S(1)}, f32[16,8,128]{2,1,0:T(8,128)S(1)}, f32[32,8,128]{2,1,0:T(8,128)S(1)}, f32[3,32,8,128]{3,2,1,0:T(8,128)S(1)}) custom-call(f32[32,8,128]{2,1,0:T(8,128)S(1)} %copy-done, bf16[256,768]{1,0:T(8,128)(2,1)S(1)} %get-tuple-element.18.ops, bf16[128,512]{1,0:T(8,128)(2,1)S(1)} %get-tuple-element.19.lows, ...), custom_call_target="tpu_custom_call" | custom-call | tf_op jit(solution)/shard_map/first/pallas_call | solution.py:354
  49.9 0.8 collective-permute-start
  50.7 0.9 collective-permute-done
  51.6 0.9 collective-permute-start.3
  52.5 1.0 collective-permute-start.2
  53.6 0.0 collective-permute-start.1
  53.6 1.3 %collective-permute-done.3 = f32[16,8,128]{2,1,0:T(8,128)S(1)} collective-permute-done((f32[16,8,128]{2,1,0:T(8,128)S(1)}, f32[16,8,128]{2,1,0:T(8,128)S(1)}, u32[]{:S(2)}, u32[]{:S(2)}) %collective-permute-start.3) | collective-permute-done | bytes 65568 | tf_op jit(solution)/shard_map/ppermute | solution.py:376
  54.8 2.3 %collective-permute-done.2 = f32[16,8,128]{2,1,0:T(8,128)S(1)} collective-permute-done((f32[16,8,128]{2,1,0:T(8,128)S(1)}, f32[16,8,128]{2,1,0:T(8,128)S(1)}, u32[]{:S(2)}, u32[]{:S(2)}) %collective-permute-start.2) | collective-permute-done | bytes 65568 | tf_op jit(solution)/shard_map/ppermute | solution.py:376
  57.2 1.5 %collective-permute-done.1 = f32[16,8,128]{2,1,0:T(8,128)S(1)} collective-permute-done((f32[16,8,128]{2,1,0:T(8,128)S(1)}, f32[16,8,128]{2,1,0:T(8,128)S(1)}, u32[]{:S(2)}, u32[]{:S(2)}) %collective-permute-start.1) | collective-permute-done | bytes 65568 | tf_op jit(solution)/shard_map/ppermute | solution.py:376
  58.7 1.0 collective-permute-start.6
  59.7 1.2 %collective-permute-start.5 = (f32[16,8,128]{2,1,0:T(8,128)S(1)}, f32[16,8,128]{2,1,0:T(8,128)S(1)}, u32[]{:S(2)}, u32[]{:S(2)}) collective-permute-start(f32[16,8,128]{2,1,0:T(8,128)S(1)} %add_add_fusion.state0), channel_id=1, source_target_pairs={{0,16},{8,24},{16,0},{24,8},{1,17},{9,25},{17,1},{25,9},{2,18},{10... | collective-permute-start | bytes 196616 | tf_op jit(solution)/shard_map/ppermute | solution.py:376
  61.0 0.0 collective-permute-start.4
  61.0 0.1 between.1
  61.1 0.8 collective-permute-done.6.state3
  61.9 2.5 %collective-permute-done.5.state2 = f32[16,8,128]{2,1,0:T(8,128)S(1)} collective-permute-done((f32[16,8,128]{2,1,0:T(8,128)S(1)}, f32[16,8,128]{2,1,0:T(8,128)S(1)}, u32[]{:S(2)}, u32[]{:S(2)}) %collective-permute-start.5) | collective-permute-done | bytes 65568 | tf_op jit(solution)/shard_map/ppermute | solution.py:376
  64.3 0.9 collective-permute-done.4.state1
  65.3 0.6 collective-permute-start.7
  66.0 2.1 %collective-permute-start.8 = (f32[2,8,8,128]{3,2,1,0:T(8,128)S(1)}, f32[2,8,8,128]{3,2,1,0:T(8,128)S(1)}, u32[]{:S(2)}, u32[]{:S(2)}) collective-permute-start(f32[2,8,8,128]{3,2,1,0:T(8,128)S(1)} %get-tuple-element.29.left), channel_id=1, source_target_pairs={{0,224},{32,0},{64,32},{96,64},{128,96},{160,128},{192,160},{224,1... | collective-permute-start | bytes 196616 | tf_op jit(solution)/shard_map/ppermute | solution.py:376
  68.1 1.9 %inner.1.edges = f32[8,2,4,8,128]{4,3,2,1,0:T(8,128)S(1)} custom-call(bf16[256,768]{1,0:T(8,128)(2,1)S(1)} %get-tuple-element.18.ops, bf16[128,512]{1,0:T(8,128)(2,1)S(1)} %get-tuple-element.19.lows, f32[32,8,128]{2,1,0:T(8,128)S(1)} %get-tuple-element.22.scale, f32[3,32,8,128]{3,2,1,0:T(8,128)S(1)} %get-tuple-element.23.inverse, ...), custom_call_target="tpu_custom_call" | custom-call | flops 2000000000 | bytes 1000000 | tf_op jit(solution)/shard_map/inner/pallas_call | solution.py:354
  69.9 0.0 collective-permute-done.7.west
  70.0 0.0 collective-permute-done.8.east
  70.0 2.2 %outer.1 = f32[32,16,128]{2,1,0:T(8,128)S(1)} custom-call(bf16[256,768]{1,0:T(8,128)(2,1)S(1)} %get-tuple-element.18.ops, bf16[128,512]{1,0:T(8,128)(2,1)S(1)} %get-tuple-element.19.lows, f32[32,8,128]{2,1,0:T(8,128)S(1)} %get-tuple-element.22.scale, f32[3,32,8,128]{3,2,1,0:T(8,128)S(1)} %get-tuple-element.23.inverse, ...), custom_call_target="tpu_custom_call" | custom-call | tf_op jit(solution)/shard_map/outer/pallas_call | solution.py:354
  72.1 0.0 copy-start.1
  72.2 15.7 %all_to_all.22 = f32[32,16,128]{2,1,0:T(8,128)S(1)} all-to-all(f32[32,16,128]{2,1,0:T(8,128)S(1)} %outer.1), channel_id=1, replica_groups=mesh['z'=8,'x'=4,'core'=2,'y'=4] {'x','core','y'}, dimensions={0} | all-to-all | bytes 524288 | tf_op jit(solution)/shard_map/all_to_all | solution.py:371
  87.8 0.0 copy-done.1
  87.8 0.3 backward.1
  88.1 19.3 %all_to_all.23 = f32[64,8,128]{2,1,0:T(8,128)S(1)} all-to-all(f32[64,8,128]{2,1,0:T(8,128)S(1)} %bitcast.14), channel_id=1, replica_groups=mesh['z'=8,'x'=4,'core'=2,'y'=4] {'z','x','core'}, dimensions={0} | all-to-all | bytes 524288 | tf_op jit(solution)/shard_map/all_to_all | solution.py:371
  107.5 0.9 unpack.1
  (3 shorter events, 0.1 us)
Async XLA Ops:
  1.6 28.0 %copy-start.2 = (bf16[64,384]{1,0:T(8,128)(2,1)S(1)}, bf16[64,384]{1,0:T(8,128)(2,1)}, u32[]{:S(2)}) copy-start(bf16[64,384]{1,0:T(8,128)(2,1)} %constant.6.clone.table) | copy-start | bytes 147460
  30.0 17.3 %copy-start = (f32[32,8,128]{2,1,0:T(8,128)S(1)}, f32[32,8,128]{2,1,0:T(8,128)}, u32[]{:S(2)}) copy-start(f32[32,8,128]{2,1,0:T(8,128)} %constant.7.clone.slots) | copy-start | bytes 393220
  49.9 1.7 %collective-permute-start = (f32[16,8,128]{2,1,0:T(8,128)S(1)}, f32[16,8,128]{2,1,0:T(8,128)S(1)}, u32[]{:S(2)}, u32[]{:S(2)}) collective-permute-start(f32[16,8,128]{2,1,0:T(8,128)S(1)} %get-tuple-element.25), channel_id=1, source_target_pairs={{0,4},{4,0},{1,5},{5,1},{2,6},{6,2},{3,7},{7,3},{8,12},{12,8},{9,1... | collective-permute-start | bytes 196616 | tf_op jit(solution)/shard_map/ppermute | solution.py:376
  51.6 3.2 %collective-permute-start.3 = (f32[16,8,128]{2,1,0:T(8,128)S(1)}, f32[16,8,128]{2,1,0:T(8,128)S(1)}, u32[]{:S(2)}, u32[]{:S(2)}) collective-permute-start(f32[16,8,128]{2,1,0:T(8,128)S(1)} %add.12.after), channel_id=1, source_target_pairs={{0,3},{1,0},{2,1},{3,2},{4,7},{5,4},{6,5},{7,6},{8,11},{9,8},{10,9... | collective-permute-start | bytes 196616 | tf_op jit(solution)/shard_map/ppermute | solution.py:376
  52.5 4.6 %collective-permute-start.2 = (f32[16,8,128]{2,1,0:T(8,128)S(1)}, f32[16,8,128]{2,1,0:T(8,128)S(1)}, u32[]{:S(2)}, u32[]{:S(2)}) collective-permute-start(f32[16,8,128]{2,1,0:T(8,128)S(1)} %add.12.after), channel_id=1, source_target_pairs={{0,2},{1,3},{2,0},{3,1},{4,6},{5,7},{6,4},{7,5},{8,10},{9,11},{10,... | collective-permute-start | bytes 196616 | tf_op jit(solution)/shard_map/ppermute | solution.py:376
  53.6 5.1 %collective-permute-start.1 = (f32[16,8,128]{2,1,0:T(8,128)S(1)}, f32[16,8,128]{2,1,0:T(8,128)S(1)}, u32[]{:S(2)}, u32[]{:S(2)}) collective-permute-start(f32[16,8,128]{2,1,0:T(8,128)S(1)} %add.12.after), channel_id=1, source_target_pairs={{0,1},{1,2},{2,3},{3,0},{4,5},{5,6},{6,7},{7,4},{8,9},{9,10},{10,1... | collective-permute-start | bytes 196616 | tf_op jit(solution)/shard_map/ppermute | solution.py:376
  58.7 3.2 %collective-permute-start.6 = (f32[16,8,128]{2,1,0:T(8,128)S(1)}, f32[16,8,128]{2,1,0:T(8,128)S(1)}, u32[]{:S(2)}, u32[]{:S(2)}) collective-permute-start(f32[16,8,128]{2,1,0:T(8,128)S(1)} %add_add_fusion.state0), channel_id=1, source_target_pairs={{0,24},{8,0},{16,8},{24,16},{1,25},{9,1},{17,9},{25,17},{2,26},{10... | collective-permute-start | bytes 196616 | tf_op jit(solution)/shard_map/ppermute | solution.py:376
  59.7 4.6 %collective-permute-start.5 = (f32[16,8,128]{2,1,0:T(8,128)S(1)}, f32[16,8,128]{2,1,0:T(8,128)S(1)}, u32[]{:S(2)}, u32[]{:S(2)}) collective-permute-start(f32[16,8,128]{2,1,0:T(8,128)S(1)} %add_add_fusion.state0), channel_id=1, source_target_pairs={{0,16},{8,24},{16,0},{24,8},{1,17},{9,25},{17,1},{25,9},{2,18},{10... | collective-permute-start | bytes 196616 | tf_op jit(solution)/shard_map/ppermute | solution.py:376
  61.0 4.3 %collective-permute-start.4 = (f32[16,8,128]{2,1,0:T(8,128)S(1)}, f32[16,8,128]{2,1,0:T(8,128)S(1)}, u32[]{:S(2)}, u32[]{:S(2)}) collective-permute-start(f32[16,8,128]{2,1,0:T(8,128)S(1)} %add_add_fusion.state0), channel_id=1, source_target_pairs={{0,8},{8,16},{16,24},{24,0},{1,9},{9,17},{17,25},{25,1},{2,10},{10... | collective-permute-start | bytes 196616 | tf_op jit(solution)/shard_map/ppermute | solution.py:376
  65.3 4.6 %collective-permute-start.7 = (f32[2,8,8,128]{3,2,1,0:T(8,128)S(1)}, f32[2,8,8,128]{3,2,1,0:T(8,128)S(1)}, u32[]{:S(2)}, u32[]{:S(2)}) collective-permute-start(f32[2,8,8,128]{3,2,1,0:T(8,128)S(1)} %get-tuple-element.28.right), channel_id=1, source_target_pairs={{0,32},{32,64},{64,96},{96,128},{128,160},{160,192},{192,224},{224... | collective-permute-start | bytes 196616 | tf_op jit(solution)/shard_map/ppermute | solution.py:376
  66.0 4.0 %collective-permute-start.8 = (f32[2,8,8,128]{3,2,1,0:T(8,128)S(1)}, f32[2,8,8,128]{3,2,1,0:T(8,128)S(1)}, u32[]{:S(2)}, u32[]{:S(2)}) collective-permute-start(f32[2,8,8,128]{3,2,1,0:T(8,128)S(1)} %get-tuple-element.29.left), channel_id=1, source_target_pairs={{0,224},{32,0},{64,32},{96,64},{128,96},{160,128},{192,160},{224,1... | collective-permute-start | bytes 196616 | tf_op jit(solution)/shard_map/ppermute | solution.py:376
  72.1 15.7 %copy-start.1 = (bf16[64,384]{1,0:T(8,128)(2,1)S(1)}, bf16[64,384]{1,0:T(8,128)(2,1)}, u32[]{:S(2)}) copy-start(bf16[64,384]{1,0:T(8,128)(2,1)} %constant.8.clone.table) | copy-start | bytes 147460

commit v6 on v5

--- a/solution.py
+++ b/solution.py
@@ -24,7 +24,7 @@
 damping = 0.7
 
 TIME = ("z", "x", "core")
-PLANE = ("x", "core", "y")
+PLANE = ("core", "y", "x")
 
 
 def tables():
@@ -162,7 +162,11 @@
 
 
 def slot():
-    return lax.axis_index("x") * 8 + lax.axis_index("core") * 4 + lax.axis_index("y")
+    return lax.axis_index("core") * 16 + lax.axis_index("y") * 4 + lax.axis_index("x")
+
+
+def seat(xc, yd):
+    return xc % 2 * 16 + yd * 4 + xc // 2
 
 
 def invert(slots, diag, scale, inverse):
@@ -241,7 +245,7 @@
                     if col >= 2:
                         w = (2 * xc if xc < 4 else 16 + 2 * xc) + col - 2
                     at = c * 8 + col * 2
-                    iterate[c, w, 2 * yd : 2 * yd + 2, :] = got[xc * 4 + yd, at : at + 2, :]
+                    iterate[c, w, 2 * yd : 2 * yd + 2, :] = got[seat(xc, yd), at : at + 2, :]
     scale[...] = jnp.broadcast_to(iterate[0, :, :, ES_LANE : ES_LANE + 1], scale.shape)
     invert(slots, diag, scale, inverse)
     relax(ops, lows, scale, inverse, iterate, source)
@@ -260,8 +264,8 @@
                 for col in range(2):
                     rows = slice(2 * yd, 2 * yd + 2)
                     at = c * 4 + col * 2
-                    done[xc * 4 + yd, at : at + 2, :] = solved[c, 2 * xc + col, rows, :]
-                    side[c, 2 * (xc % 4) + col, rows, :] = got[xc * 4 + yd, 16 + at : 18 + at, :]
+                    done[seat(xc, yd), at : at + 2, :] = solved[c, 2 * xc + col, rows, :]
+                    side[c, 2 * (xc % 4) + col, rows, :] = got[seat(xc, yd), 16 + at : 18 + at, :]
 
 
 def carry_kernel(slots, left, right, state0, state1, state2, state3, out_left, out_right):
@@ -323,7 +327,7 @@
                     tile = iterate.at[c, x + 2]
                 at = 8 + c * 4 + col * 2
                 for yd in range(4):
-                    out[xc * 4 + yd, at : at + 2, :] = tile[2 * yd : 2 * yd + 2, :]
+                    out[seat(xc, yd), at : at + 2, :] = tile[2 * yd : 2 * yd + 2, :]
 
 
 def backward_kernel(table, got, out):
@@ -374,6 +378,10 @@
 def moved(block, axis, by):
     count = lax.axis_size(axis)
     return lax.ppermute(block, axis, [(i, (i + by) % count) for i in range(count)])
+
+
+def swapped(block, axis, bits):
+    return lax.ppermute(block, axis, [(i, i ^ bits) for i in range(lax.axis_size(axis))])
 
 
 def per_device(forcing, init_state, elem_scale, vol_op, face_ops):
@@ -413,12 +421,13 @@
         name="first",
     )
     half = f32(2, CHUNK // 2, 8, LANES)
-    state = state + moved(state, "core", 1)
+    state = state + swapped(state, "core", 1)
     done, left, right = call(
         between_kernel, (f32(FREQS, 8, LANES), half, half), (got, solved, state), (), [VMEM, VMEM, ANY], name="between"
     )
-    state = state + moved(state, "y", 1) + moved(state, "y", 2) + moved(state, "y", 3)
-    states = [state] + [moved(state, "x", by) for by in (1, 2, 3)]
+    near, far, across = (swapped(state, "y", bits) for bits in (1, 3, 2))
+    state = ((state + near) + far) + across
+    states = [state] + [swapped(state, "x", bits) for bits in (1, 3, 2)]
     left, right = call(carry_kernel, (half, half), (SLOTS, left, right, *states), name="carry")
     west = moved(right, "z", 1)
     east = moved(left, "z", -1)

time: 109 us -> 109 us (level)
  waiting for transfers between devices: 10.2 us -> 8.15 us
  starting transfers between devices: 7.74 us -> 9.61 us
    ppermute x9 -> x2, waiting for transfers between devices: 10.2 us -> 0.01 us  [moved(): lax.ppermute(block, axis, [(i, (i + by) % count) for i in range(count)])]
    ppermute x0 -> x7, waiting for transfers between devices: none -> 8.14 us  [swapped(): lax.ppermute(block, axis, [(i, i ^ bits) for i in range(lax.axis_size(axi...]
    ppermute x0 -> x7, starting transfers between devices: none -> 6.85 us  [swapped(): lax.ppermute(block, axis, [(i, i ^ bits) for i in range(lax.axis_size(axi...]
    ppermute x9 -> x2, starting transfers between devices: 7.74 us -> 2.75 us  [moved(): lax.ppermute(block, axis, [(i, (i + by) % count) for i in range(count)])]
  transfers between devices with their start and end apart: 9 -> 9, of which waited for: 7 -> 6; matrix products, arithmetic and copies ran while one was open for 0% -> 0% of each run, Pallas kernels for 2% -> 2%
where the time goes in v6:
time: 109 us; the launch traced here: 108 us
  blocking collectives  80.3 us (74%)
  Pallas kernels  9.99 us (9%)
  starting transfers between devices  9.61 us (9%)
  waiting for transfers between devices  8.15 us (7%)
    all_to_all x4, blocking collectives, exchange(): return lax.all_to_all(blocks, axes, 0, 0, tiled=True)  80.3 us
    pallas_call x9, Pallas kernels, call(): pl.pallas_call(kernel, out_shape=outs, in_specs=specs or [VMEM] * len(ins...  9.99 us
    ppermute x7, waiting for transfers between devices, swapped(): lax.ppermute(block, axis, [(i, i ^ bits) for i in range(lax.axis_size(axi...  8.14 us
    ppermute x7, starting transfers between devices, swapped(): lax.ppermute(block, axis, [(i, i ^ bits) for i in range(lax.axis_size(axi...  6.85 us
    ppermute x2, starting transfers between devices, moved(): lax.ppermute(block, axis, [(i, (i + by) % count) for i in range(count)])  2.75 us
  transfers between devices with their start and end apart: 9, of which 6 were waited for; matrix products, arithmetic and copies ran while one was open for 0% of the time, Pallas kernels for 2%

profile of v6, /device:TPU:1, one launch (start us, length us, event | category | flops | bytes accessed | tf_op | source)
XLA Modules:
  0.0 108.3 jit_solution(13027181517107415272)
XLA Ops:
  0.0 1.6 %pack.1 = (f32[768,128]{1,0:T(8,128)S(1)}, bf16[256,768]{1,0:T(8,128)(2,1)S(1)}, bf16[128,512]{1,0:T(8,128)(2,1)S(1)}, f32[8,128]{1,0:T(8,128)S(1)}) custom-call(f32[250,2,128]{2,1,0:T(2,128)} %bitcast.17, f32[1,125,2,128]{3,2,1,0:T(2,128)} %bitcast.19, f32[1,2,128]{2,1,0:T(2,128)} %bitcast.21, f32[1,125,125]{2,1,0:T(8,128)} %bitcast.20, f32[125,4,125]{2,1,0:T(4,128)} %bitcast.18), custom_call_target="tpu_custom_call" | custom-call | tf_op jit(solution)/shard_map/pack/pallas_call | solution.py:358
  1.6 0.0 copy-start.2
  1.6 28.0 %all_to_all.20 = f32[64,3,4,128]{3,2,1,0:T(4,128)S(1)} all-to-all(f32[64,3,4,128]{3,2,1,0:T(4,128)S(1)} %bitcast.16), channel_id=1, replica_groups=mesh['z'=8,'x'=4,'core'=2,'y'=4] {'z','x','core'}, dimensions={0} | all-to-all | bytes 786432 | tf_op jit(solution)/shard_map/all_to_all | solution.py:375
  29.6 0.0 copy-done.2
  29.6 0.3 forward.1
  30.0 0.0 copy-start
  30.0 16.8 %all_to_all.21.got = f32[32,24,128]{2,1,0:T(8,128)S(1)} all-to-all(f32[32,24,128]{2,1,0:T(8,128)S(1)} %bitcast.12), channel_id=1, replica_groups=mesh['z'=8,'x'=4,'core'=2,'y'=4] {'core','y','x'}, dimensions={0} | all-to-all | bytes 786432 | tf_op jit(solution)/shard_map/all_to_all | solution.py:375
  46.7 0.0 copy-done
  46.7 2.7 %first.1 = (f32[2,16,8,128]{3,2,1,0:T(8,128)S(1)}, f32[16,8,128]{2,1,0:T(8,128)S(1)}, f32[32,8,128]{2,1,0:T(8,128)S(1)}, f32[3,32,8,128]{3,2,1,0:T(8,128)S(1)}) custom-call(f32[32,8,128]{2,1,0:T(8,128)S(1)} %copy-done, bf16[256,768]{1,0:T(8,128)(2,1)S(1)} %get-tuple-element.18.ops, bf16[128,512]{1,0:T(8,128)(2,1)S(1)} %get-tuple-element.19.lows, ...), custom_call_target="tpu_custom_call" | custom-call | tf_op jit(solution)/shard_map/first/pallas_call | solution.py:358
  49.4 1.3 %collective-permute-start = (f32[16,8,128]{2,1,0:T(8,128)S(1)}, f32[16,8,128]{2,1,0:T(8,128)S(1)}, u32[]{:S(2)}, u32[]{:S(2)}) collective-permute-start(f32[16,8,128]{2,1,0:T(8,128)S(1)} %get-tuple-element.25), channel_id=1, source_target_pairs={{0,4},{4,0},{1,5},{5,1},{2,6},{6,2},{3,7},{7,3},{8,12},{12,8},{9,1... | collective-permute-start | bytes 196616 | tf_op jit(solution)/shard_map/ppermute | solution.py:384
  50.7 0.9 collective-permute-done
  51.6 1.4 %collective-permute-start.3 = (f32[16,8,128]{2,1,0:T(8,128)S(1)}, f32[16,8,128]{2,1,0:T(8,128)S(1)}, u32[]{:S(2)}, u32[]{:S(2)}) collective-permute-start(f32[16,8,128]{2,1,0:T(8,128)S(1)} %add.12.after), channel_id=1, source_target_pairs={{0,2},{1,3},{2,0},{3,1},{4,6},{5,7},{6,4},{7,5},{8,10},{9,11},{10,... | collective-permute-start | bytes 196616 | tf_op jit(solution)/shard_map/ppermute | solution.py:384
  53.0 1.4 %collective-permute-start.2 = (f32[16,8,128]{2,1,0:T(8,128)S(1)}, f32[16,8,128]{2,1,0:T(8,128)S(1)}, u32[]{:S(2)}, u32[]{:S(2)}) collective-permute-start(f32[16,8,128]{2,1,0:T(8,128)S(1)} %add.12.after), channel_id=1, source_target_pairs={{0,3},{1,2},{2,1},{3,0},{4,7},{5,6},{6,5},{7,4},{8,11},{9,10},{10,... | collective-permute-start | bytes 196616 | tf_op jit(solution)/shard_map/ppermute | solution.py:384
  54.5 0.0 collective-permute-start.1
  54.5 1.9 %collective-permute-done.3 = f32[16,8,128]{2,1,0:T(8,128)S(1)} collective-permute-done((f32[16,8,128]{2,1,0:T(8,128)S(1)}, f32[16,8,128]{2,1,0:T(8,128)S(1)}, u32[]{:S(2)}, u32[]{:S(2)}) %collective-permute-start.3) | collective-permute-done | bytes 65568 | tf_op jit(solution)/shard_map/ppermute | solution.py:384
  56.4 1.9 %collective-permute-done.2 = f32[16,8,128]{2,1,0:T(8,128)S(1)} collective-permute-done((f32[16,8,128]{2,1,0:T(8,128)S(1)}, f32[16,8,128]{2,1,0:T(8,128)S(1)}, u32[]{:S(2)}, u32[]{:S(2)}) %collective-permute-start.2) | collective-permute-done | bytes 65568 | tf_op jit(solution)/shard_map/ppermute | solution.py:384
  58.3 0.0 collective-permute-done.1
  58.3 1.4 %collective-permute-start.6 = (f32[16,8,128]{2,1,0:T(8,128)S(1)}, f32[16,8,128]{2,1,0:T(8,128)S(1)}, u32[]{:S(2)}, u32[]{:S(2)}) collective-permute-start(f32[16,8,128]{2,1,0:T(8,128)S(1)} %add_add_fusion.state0), channel_id=1, source_target_pairs={{0,16},{8,24},{16,0},{24,8},{1,17},{9,25},{17,1},{25,9},{2,18},{10... | collective-permute-start | bytes 196616 | tf_op jit(solution)/shard_map/ppermute | solution.py:384
  59.7 0.8 collective-permute-start.5
  60.5 0.5 collective-permute-start.4
  61.0 0.1 between.1
  61.1 1.9 %collective-permute-done.6.state3 = f32[16,8,128]{2,1,0:T(8,128)S(1)} collective-permute-done((f32[16,8,128]{2,1,0:T(8,128)S(1)}, f32[16,8,128]{2,1,0:T(8,128)S(1)}, u32[]{:S(2)}, u32[]{:S(2)}) %collective-permute-start.6) | collective-permute-done | bytes 65568 | tf_op jit(solution)/shard_map/ppermute | solution.py:384
  63.0 1.0 collective-permute-done.5.state2
  64.0 0.6 collective-permute-done.4.state1
  64.6 0.6 collective-permute-start.7
  65.2 2.1 %collective-permute-start.8 = (f32[2,8,8,128]{3,2,1,0:T(8,128)S(1)}, f32[2,8,8,128]{3,2,1,0:T(8,128)S(1)}, u32[]{:S(2)}, u32[]{:S(2)}) collective-permute-start(f32[2,8,8,128]{3,2,1,0:T(8,128)S(1)} %get-tuple-element.29.left), channel_id=1, source_target_pairs={{0,224},{32,0},{64,32},{96,64},{128,96},{160,128},{192,160},{224,1... | collective-permute-start | bytes 196616 | tf_op jit(solution)/shard_map/ppermute | solution.py:380
  67.4 1.9 %inner.1.edges = f32[8,2,4,8,128]{4,3,2,1,0:T(8,128)S(1)} custom-call(bf16[256,768]{1,0:T(8,128)(2,1)S(1)} %get-tuple-element.18.ops, bf16[128,512]{1,0:T(8,128)(2,1)S(1)} %get-tuple-element.19.lows, f32[32,8,128]{2,1,0:T(8,128)S(1)} %get-tuple-element.22.scale, f32[3,32,8,128]{3,2,1,0:T(8,128)S(1)} %get-tuple-element.23.inverse, ...), custom_call_target="tpu_custom_call" | custom-call | flops 2000000000 | bytes 1000000 | tf_op jit(solution)/shard_map/inner/pallas_call | solution.py:358
  69.2 0.0 collective-permute-done.7.west
  69.2 0.0 collective-permute-done.8.east
  69.3 2.2 %outer.1 = f32[32,16,128]{2,1,0:T(8,128)S(1)} custom-call(bf16[256,768]{1,0:T(8,128)(2,1)S(1)} %get-tuple-element.18.ops, bf16[128,512]{1,0:T(8,128)(2,1)S(1)} %get-tuple-element.19.lows, f32[32,8,128]{2,1,0:T(8,128)S(1)} %get-tuple-element.22.scale, f32[3,32,8,128]{3,2,1,0:T(8,128)S(1)} %get-tuple-element.23.inverse, ...), custom_call_target="tpu_custom_call" | custom-call | tf_op jit(solution)/shard_map/outer/pallas_call | solution.py:358
  71.4 0.0 copy-start.1
  71.4 15.4 %all_to_all.22 = f32[32,16,128]{2,1,0:T(8,128)S(1)} all-to-all(f32[32,16,128]{2,1,0:T(8,128)S(1)} %outer.1), channel_id=1, replica_groups=mesh['z'=8,'x'=4,'core'=2,'y'=4] {'core','y','x'}, dimensions={0} | all-to-all | bytes 524288 | tf_op jit(solution)/shard_map/all_to_all | solution.py:375
  86.9 0.0 copy-done.1
  86.9 0.3 backward.1
  87.2 20.1 %all_to_all.23 = f32[64,8,128]{2,1,0:T(8,128)S(1)} all-to-all(f32[64,8,128]{2,1,0:T(8,128)S(1)} %bitcast.14), channel_id=1, replica_groups=mesh['z'=8,'x'=4,'core'=2,'y'=4] {'z','x','core'}, dimensions={0} | all-to-all | bytes 524288 | tf_op jit(solution)/shard_map/all_to_all | solution.py:375
  107.3 0.9 unpack.1
  (3 shorter events, 0.1 us)
Async XLA Ops:
  1.6 28.0 %copy-start.2 = (bf16[64,384]{1,0:T(8,128)(2,1)S(1)}, bf16[64,384]{1,0:T(8,128)(2,1)}, u32[]{:S(2)}) copy-start(bf16[64,384]{1,0:T(8,128)(2,1)} %constant.6.clone.table) | copy-start | bytes 147460
  30.0 16.8 %copy-start = (f32[32,8,128]{2,1,0:T(8,128)S(1)}, f32[32,8,128]{2,1,0:T(8,128)}, u32[]{:S(2)}) copy-start(f32[32,8,128]{2,1,0:T(8,128)} %constant.7.clone.slots) | copy-start | bytes 393220
  49.4 2.2 %collective-permute-start = (f32[16,8,128]{2,1,0:T(8,128)S(1)}, f32[16,8,128]{2,1,0:T(8,128)S(1)}, u32[]{:S(2)}, u32[]{:S(2)}) collective-permute-start(f32[16,8,128]{2,1,0:T(8,128)S(1)} %get-tuple-element.25), channel_id=1, source_target_pairs={{0,4},{4,0},{1,5},{5,1},{2,6},{6,2},{3,7},{7,3},{8,12},{12,8},{9,1... | collective-permute-start | bytes 196616 | tf_op jit(solution)/shard_map/ppermute | solution.py:384
  51.6 4.7 %collective-permute-start.3 = (f32[16,8,128]{2,1,0:T(8,128)S(1)}, f32[16,8,128]{2,1,0:T(8,128)S(1)}, u32[]{:S(2)}, u32[]{:S(2)}) collective-permute-start(f32[16,8,128]{2,1,0:T(8,128)S(1)} %add.12.after), channel_id=1, source_target_pairs={{0,2},{1,3},{2,0},{3,1},{4,6},{5,7},{6,4},{7,5},{8,10},{9,11},{10,... | collective-permute-start | bytes 196616 | tf_op jit(solution)/shard_map/ppermute | solution.py:384
  53.0 5.2 %collective-permute-start.2 = (f32[16,8,128]{2,1,0:T(8,128)S(1)}, f32[16,8,128]{2,1,0:T(8,128)S(1)}, u32[]{:S(2)}, u32[]{:S(2)}) collective-permute-start(f32[16,8,128]{2,1,0:T(8,128)S(1)} %add.12.after), channel_id=1, source_target_pairs={{0,3},{1,2},{2,1},{3,0},{4,7},{5,6},{6,5},{7,4},{8,11},{9,10},{10,... | collective-permute-start | bytes 196616 | tf_op jit(solution)/shard_map/ppermute | solution.py:384
  54.5 3.8 %collective-permute-start.1 = (f32[16,8,128]{2,1,0:T(8,128)S(1)}, f32[16,8,128]{2,1,0:T(8,128)S(1)}, u32[]{:S(2)}, u32[]{:S(2)}) collective-permute-start(f32[16,8,128]{2,1,0:T(8,128)S(1)} %add.12.after), channel_id=1, source_target_pairs={{0,1},{1,0},{2,3},{3,2},{4,5},{5,4},{6,7},{7,6},{8,9},{9,8},{10,11... | collective-permute-start | bytes 196616 | tf_op jit(solution)/shard_map/ppermute | solution.py:384
  58.3 4.7 %collective-permute-start.6 = (f32[16,8,128]{2,1,0:T(8,128)S(1)}, f32[16,8,128]{2,1,0:T(8,128)S(1)}, u32[]{:S(2)}, u32[]{:S(2)}) collective-permute-start(f32[16,8,128]{2,1,0:T(8,128)S(1)} %add_add_fusion.state0), channel_id=1, source_target_pairs={{0,16},{8,24},{16,0},{24,8},{1,17},{9,25},{17,1},{25,9},{2,18},{10... | collective-permute-start | bytes 196616 | tf_op jit(solution)/shard_map/ppermute | solution.py:384
  59.7 4.3 %collective-permute-start.5 = (f32[16,8,128]{2,1,0:T(8,128)S(1)}, f32[16,8,128]{2,1,0:T(8,128)S(1)}, u32[]{:S(2)}, u32[]{:S(2)}) collective-permute-start(f32[16,8,128]{2,1,0:T(8,128)S(1)} %add_add_fusion.state0), channel_id=1, source_target_pairs={{0,24},{8,16},{16,8},{24,0},{1,25},{9,17},{17,9},{25,1},{2,26},{10... | collective-permute-start | bytes 196616 | tf_op jit(solution)/shard_map/ppermute | solution.py:384
  60.5 4.1 %collective-permute-start.4 = (f32[16,8,128]{2,1,0:T(8,128)S(1)}, f32[16,8,128]{2,1,0:T(8,128)S(1)}, u32[]{:S(2)}, u32[]{:S(2)}) collective-permute-start(f32[16,8,128]{2,1,0:T(8,128)S(1)} %add_add_fusion.state0), channel_id=1, source_target_pairs={{0,8},{8,0},{16,24},{24,16},{1,9},{9,1},{17,25},{25,17},{2,10},{10... | collective-permute-start | bytes 196616 | tf_op jit(solution)/shard_map/ppermute | solution.py:384
  64.6 4.6 %collective-permute-start.7 = (f32[2,8,8,128]{3,2,1,0:T(8,128)S(1)}, f32[2,8,8,128]{3,2,1,0:T(8,128)S(1)}, u32[]{:S(2)}, u32[]{:S(2)}) collective-permute-start(f32[2,8,8,128]{3,2,1,0:T(8,128)S(1)} %get-tuple-element.28.right), channel_id=1, source_target_pairs={{0,32},{32,64},{64,96},{96,128},{128,160},{160,192},{192,224},{224... | collective-permute-start | bytes 196616 | tf_op jit(solution)/shard_map/ppermute | solution.py:380
  65.2 4.0 %collective-permute-start.8 = (f32[2,8,8,128]{3,2,1,0:T(8,128)S(1)}, f32[2,8,8,128]{3,2,1,0:T(8,128)S(1)}, u32[]{:S(2)}, u32[]{:S(2)}) collective-permute-start(f32[2,8,8,128]{3,2,1,0:T(8,128)S(1)} %get-tuple-element.29.left), channel_id=1, source_target_pairs={{0,224},{32,0},{64,32},{96,64},{128,96},{160,128},{192,160},{224,1... | collective-permute-start | bytes 196616 | tf_op jit(solution)/shard_map/ppermute | solution.py:380
  71.4 15.4 %copy-start.1 = (bf16[64,384]{1,0:T(8,128)(2,1)S(1)}, bf16[64,384]{1,0:T(8,128)(2,1)}, u32[]{:S(2)}) copy-start(bf16[64,384]{1,0:T(8,128)(2,1)} %constant.8.clone.table) | copy-start | bytes 147460

commit v7 on v6

--- a/solution.py
+++ b/solution.py
@@ -268,19 +268,23 @@
                     side[c, 2 * (xc % 4) + col, rows, :] = got[seat(xc, yd), 16 + at : 18 + at, :]
 
 
-def carry_kernel(slots, left, right, state0, state1, state2, state3, out_left, out_right):
+def by_side(one, two):
+    even = lax.rem(lax.axis_index("z"), 2) == 0
+    return jnp.where(even, two, one), jnp.where(even, one, two)
+
+
+def carry_kernel(slots, left, right, state0, state1, state2, state3, near, far):
     state = (state0[...] + state1[...]) + (state2[...] + state3[...])
     mine = slots[slot()]
     for c in range(2):
         part = mine[5 + c : 6 + c][None] * state
-        out_left[c] = left[c] + part[: CHUNK // 2]
-        out_right[c] = right[c] + part[CHUNK // 2 :]
-
-
-def inner_kernel(ops, lows, scale, inverse, left, right, edges, iterate, source):
+        far[c], near[c] = by_side(right[c] + part[CHUNK // 2 :], left[c] + part[: CHUNK // 2])
+
+
+def inner_kernel(ops, lows, scale, inverse, near, far, edges, iterate, source):
     middle = slice(HALO, HALO + CHUNK)
-    for i, part in enumerate((left, right)):
-        start(inverse, part[...], source, slice((i + 1) * HALO, (i + 2) * HALO))
+    for i, part in enumerate(by_side(near[...], far[...])):
+        start(inverse, part, source, slice((i + 1) * HALO, (i + 2) * HALO))
     iterate[...] = source[:, middle]
     for sweep in range(SWEEPS):
         lo, hi = sweep, CHUNK - sweep
@@ -294,9 +298,11 @@
         edges[sweep, :, 2:] = iterate[:, hi - 2 : hi]
 
 
-def outer_kernel(ops, lows, scale, inverse, west, left, right, east, edges, before, out, iterate, source):
+def outer_kernel(ops, lows, scale, inverse, near, far, beyond_near, beyond_far, edges, before, out, iterate, source):
+    left, right = by_side(near[...], far[...])
+    west, east = by_side(beyond_near[...], beyond_far[...])
     for i, part in enumerate((west, left, right, east)):
-        start(inverse, part[...], source, slice(i * HALO, (i + 1) * HALO))
+        start(inverse, part, source, slice(i * HALO, (i + 1) * HALO))
     out[:, :8, :] = before[...]
     reach = SWEEPS - 1
     iterate[:, :reach] = source[:, 1:HALO]
@@ -375,11 +381,6 @@
     return lax.all_to_all(blocks, axes, 0, 0, tiled=True)
 
 
-def moved(block, axis, by):
-    count = lax.axis_size(axis)
-    return lax.ppermute(block, axis, [(i, (i + by) % count) for i in range(count)])
-
-
 def swapped(block, axis, bits):
     return lax.ppermute(block, axis, [(i, i ^ bits) for i in range(lax.axis_size(axis))])
 
@@ -428,13 +429,15 @@
     near, far, across = (swapped(state, "y", bits) for bits in (1, 3, 2))
     state = ((state + near) + far) + across
     states = [state] + [swapped(state, "x", bits) for bits in (1, 3, 2)]
-    left, right = call(carry_kernel, (half, half), (SLOTS, left, right, *states), name="carry")
-    west = moved(right, "z", 1)
-    east = moved(left, "z", -1)
+    near, far = call(carry_kernel, (half, half), (SLOTS, left, right, *states), name="carry")
+    beyond_near = swapped(near, "z", 1)
+    planes = lax.axis_size("z")
+    other = [(z, (z + 1 if z % 2 else z - 1) % planes) for z in range(planes)]
+    beyond_far = lax.ppermute(far, "z", other)
     edges = call(
         inner_kernel,
         f32(SWEEPS, 2, 4, 8, LANES),
-        (ops, lows, scale, inverse, left, right),
+        (ops, lows, scale, inverse, near, far),
         (pltpu.VMEM((2, CHUNK, 8, LANES), jnp.float32), both),
         name="inner",
         cost=pl.CostEstimate(flops=2_000_000_000, bytes_accessed=1_000_000, transcendentals=0),
@@ -442,7 +445,7 @@
     done = call(
         outer_kernel,
         f32(FREQS, 16, LANES),
-        (ops, lows, scale, inverse, west, left, right, east, edges, done),
+        (ops, lows, scale, inverse, near, far, beyond_near, beyond_far, edges, done),
         (pltpu.VMEM((2, 2 * SWEEPS + 2, 8, LANES), jnp.float32), both),
         name="outer",
     )

time: 109 us -> 108 us (level)
  waiting for transfers between devices: 8.15 us -> 10.6 us
  starting transfers between devices: 9.61 us -> 7.51 us
    ppermute x2 -> x1, starting transfers between devices: 2.75 us -> 0.01 us  [per_device(): beyond_far = lax.ppermute(far, 'z', other)]
    ppermute x2 -> x1, waiting for transfers between devices: 0.01 us -> 1.77 us  [per_device(): beyond_far = lax.ppermute(far, 'z', other)]
    ppermute x7 -> x8, waiting for transfers between devices: 8.14 us -> 8.83 us  [swapped(): lax.ppermute(block, axis, [(i, i ^ bits) for i in range(lax.axis_size(axi...]
    ppermute x7 -> x8, starting transfers between devices: 6.85 us -> 7.51 us  [swapped(): lax.ppermute(block, axis, [(i, i ^ bits) for i in range(lax.axis_size(axi...]
  transfers between devices with their start and end apart: 9 -> 9, of which waited for: 6 -> 8; matrix products, arithmetic and copies ran while one was open for 0% -> 0% of each run, Pallas kernels for 2% -> 2%
where the time goes in v7:
time: 108 us
  blocking collectives  79.3 us (73%)
  waiting for transfers between devices  10.6 us (10%)
  Pallas kernels  9.97 us (9%)
  starting transfers between devices  7.51 us (7%)
    all_to_all x4, blocking collectives, exchange(): return lax.all_to_all(blocks, axes, 0, 0, tiled=True)  79.3 us
    pallas_call x9, Pallas kernels, call(): pl.pallas_call(kernel, out_shape=outs, in_specs=specs or [VMEM] * len(ins...  9.97 us
    ppermute x8, waiting for transfers between devices, swapped(): lax.ppermute(block, axis, [(i, i ^ bits) for i in range(lax.axis_size(axi...  8.83 us
    ppermute x8, starting transfers between devices, swapped(): lax.ppermute(block, axis, [(i, i ^ bits) for i in range(lax.axis_size(axi...  7.51 us
  transfers between devices with their start and end apart: 9, of which 8 were waited for; matrix products, arithmetic and copies ran while one was open for 0% of the time, Pallas kernels for 2%

profile of v7, /device:TPU:1, one launch (start us, length us, event | category | flops | bytes accessed | tf_op | source)
XLA Modules:
  0.0 107.7 jit_solution(17396161820638502241)
XLA Ops:
  0.0 1.6 %pack.1 = (f32[768,128]{1,0:T(8,128)S(1)}, bf16[256,768]{1,0:T(8,128)(2,1)S(1)}, bf16[128,512]{1,0:T(8,128)(2,1)S(1)}, f32[8,128]{1,0:T(8,128)S(1)}) custom-call(f32[250,2,128]{2,1,0:T(2,128)} %bitcast.17, f32[1,125,2,128]{3,2,1,0:T(2,128)} %bitcast.19, f32[1,2,128]{2,1,0:T(2,128)} %bitcast.21, f32[1,125,125]{2,1,0:T(8,128)} %bitcast.20, f32[125,4,125]{2,1,0:T(4,128)} %bitcast.18), custom_call_target="tpu_custom_call" | custom-call | tf_op jit(solution)/shard_map/pack/pallas_call | solution.py:364
  1.6 0.0 copy-start.2
  1.6 28.0 %all_to_all.20 = f32[64,3,4,128]{3,2,1,0:T(4,128)S(1)} all-to-all(f32[64,3,4,128]{3,2,1,0:T(4,128)S(1)} %bitcast.16), channel_id=1, replica_groups=mesh['z'=8,'x'=4,'core'=2,'y'=4] {'z','x','core'}, dimensions={0} | all-to-all | bytes 786432 | tf_op jit(solution)/shard_map/all_to_all | solution.py:381
  29.6 0.0 copy-done.2
  29.6 0.3 forward.1
  30.0 0.0 copy-start
  30.0 16.8 %all_to_all.21.got = f32[32,24,128]{2,1,0:T(8,128)S(1)} all-to-all(f32[32,24,128]{2,1,0:T(8,128)S(1)} %bitcast.12), channel_id=1, replica_groups=mesh['z'=8,'x'=4,'core'=2,'y'=4] {'core','y','x'}, dimensions={0} | all-to-all | bytes 786432 | tf_op jit(solution)/shard_map/all_to_all | solution.py:381
  46.7 0.0 copy-done
  46.7 2.7 %first.1 = (f32[2,16,8,128]{3,2,1,0:T(8,128)S(1)}, f32[16,8,128]{2,1,0:T(8,128)S(1)}, f32[32,8,128]{2,1,0:T(8,128)S(1)}, f32[3,32,8,128]{3,2,1,0:T(8,128)S(1)}) custom-call(f32[32,8,128]{2,1,0:T(8,128)S(1)} %copy-done, bf16[256,768]{1,0:T(8,128)(2,1)S(1)} %get-tuple-element.18.ops, bf16[128,512]{1,0:T(8,128)(2,1)S(1)} %get-tuple-element.19.lows, ...), custom_call_target="tpu_custom_call" | custom-call | tf_op jit(solution)/shard_map/first/pallas_call | solution.py:364
  49.4 1.3 %collective-permute-start = (f32[16,8,128]{2,1,0:T(8,128)S(1)}, f32[16,8,128]{2,1,0:T(8,128)S(1)}, u32[]{:S(2)}, u32[]{:S(2)}) collective-permute-start(f32[16,8,128]{2,1,0:T(8,128)S(1)} %get-tuple-element.25), channel_id=1, source_target_pairs={{0,4},{4,0},{1,5},{5,1},{2,6},{6,2},{3,7},{7,3},{8,12},{12,8},{9,1... | collective-permute-start | bytes 196616 | tf_op jit(solution)/shard_map/ppermute | solution.py:385
  50.7 0.9 collective-permute-done
  51.6 1.4 %collective-permute-start.3 = (f32[16,8,128]{2,1,0:T(8,128)S(1)}, f32[16,8,128]{2,1,0:T(8,128)S(1)}, u32[]{:S(2)}, u32[]{:S(2)}) collective-permute-start(f32[16,8,128]{2,1,0:T(8,128)S(1)} %add.12.after), channel_id=1, source_target_pairs={{0,2},{1,3},{2,0},{3,1},{4,6},{5,7},{6,4},{7,5},{8,10},{9,11},{10,... | collective-permute-start | bytes 196616 | tf_op jit(solution)/shard_map/ppermute | solution.py:385
  53.0 1.4 %collective-permute-start.2 = (f32[16,8,128]{2,1,0:T(8,128)S(1)}, f32[16,8,128]{2,1,0:T(8,128)S(1)}, u32[]{:S(2)}, u32[]{:S(2)}) collective-permute-start(f32[16,8,128]{2,1,0:T(8,128)S(1)} %add.12.after), channel_id=1, source_target_pairs={{0,3},{1,2},{2,1},{3,0},{4,7},{5,6},{6,5},{7,4},{8,11},{9,10},{10,... | collective-permute-start | bytes 196616 | tf_op jit(solution)/shard_map/ppermute | solution.py:385
  54.5 0.0 collective-permute-start.1
  54.5 1.9 %collective-permute-done.3 = f32[16,8,128]{2,1,0:T(8,128)S(1)} collective-permute-done((f32[16,8,128]{2,1,0:T(8,128)S(1)}, f32[16,8,128]{2,1,0:T(8,128)S(1)}, u32[]{:S(2)}, u32[]{:S(2)}) %collective-permute-start.3) | collective-permute-done | bytes 65568 | tf_op jit(solution)/shard_map/ppermute | solution.py:385
  56.4 1.9 %collective-permute-done.2 = f32[16,8,128]{2,1,0:T(8,128)S(1)} collective-permute-done((f32[16,8,128]{2,1,0:T(8,128)S(1)}, f32[16,8,128]{2,1,0:T(8,128)S(1)}, u32[]{:S(2)}, u32[]{:S(2)}) %collective-permute-start.2) | collective-permute-done | bytes 65568 | tf_op jit(solution)/shard_map/ppermute | solution.py:385
  58.3 0.0 collective-permute-done.1
  58.3 1.4 %collective-permute-start.6 = (f32[16,8,128]{2,1,0:T(8,128)S(1)}, f32[16,8,128]{2,1,0:T(8,128)S(1)}, u32[]{:S(2)}, u32[]{:S(2)}) collective-permute-start(f32[16,8,128]{2,1,0:T(8,128)S(1)} %add_add_fusion.state0), channel_id=1, source_target_pairs={{0,16},{8,24},{16,0},{24,8},{1,17},{9,25},{17,1},{25,9},{2,18},{10... | collective-permute-start | bytes 196616 | tf_op jit(solution)/shard_map/ppermute | solution.py:385
  59.7 0.8 collective-permute-start.5
  60.5 0.5 collective-permute-start.4
  61.0 0.1 between.1
  61.1 1.9 %collective-permute-done.6.state3 = f32[16,8,128]{2,1,0:T(8,128)S(1)} collective-permute-done((f32[16,8,128]{2,1,0:T(8,128)S(1)}, f32[16,8,128]{2,1,0:T(8,128)S(1)}, u32[]{:S(2)}, u32[]{:S(2)}) %collective-permute-start.6) | collective-permute-done | bytes 65568 | tf_op jit(solution)/shard_map/ppermute | solution.py:385
  63.0 1.0 collective-permute-done.5.state2
  64.0 0.6 collective-permute-done.4.state1
  64.6 0.7 collective-permute-start.7
  65.3 0.0 collective-permute-start.8
  65.3 1.9 %inner.1.edges = f32[8,2,4,8,128]{4,3,2,1,0:T(8,128)S(1)} custom-call(bf16[256,768]{1,0:T(8,128)(2,1)S(1)} %get-tuple-element.18.ops, bf16[128,512]{1,0:T(8,128)(2,1)S(1)} %get-tuple-element.19.lows, f32[32,8,128]{2,1,0:T(8,128)S(1)} %get-tuple-element.22.scale, f32[3,32,8,128]{3,2,1,0:T(8,128)S(1)} %get-tuple-element.23.inverse, ...), custom_call_target="tpu_custom_call" | custom-call | flops 2000000000 | bytes 1000000 | tf_op jit(solution)/shard_map/inner/pallas_call | solution.py:364
  67.1 0.7 collective-permute-done.7.beyond_near
  67.8 1.8 %collective-permute-done.8.beyond_far = f32[2,8,8,128]{3,2,1,0:T(8,128)S(1)} collective-permute-done((f32[2,8,8,128]{3,2,1,0:T(8,128)S(1)}, f32[2,8,8,128]{3,2,1,0:T(8,128)S(1)}, u32[]{:S(2)}, u32[]{:S(2)}) %collective-permute-start.8) | collective-permute-done | bytes 65568 | tf_op jit(solution)/shard_map/ppermute | solution.py:436
  69.6 2.1 %outer.1 = f32[32,16,128]{2,1,0:T(8,128)S(1)} custom-call(bf16[256,768]{1,0:T(8,128)(2,1)S(1)} %get-tuple-element.18.ops, bf16[128,512]{1,0:T(8,128)(2,1)S(1)} %get-tuple-element.19.lows, f32[32,8,128]{2,1,0:T(8,128)S(1)} %get-tuple-element.22.scale, f32[3,32,8,128]{3,2,1,0:T(8,128)S(1)} %get-tuple-element.23.inverse, ...), custom_call_target="tpu_custom_call" | custom-call | tf_op jit(solution)/shard_map/outer/pallas_call | solution.py:364
  71.7 0.0 copy-start.1
  71.7 15.9 %all_to_all.22 = f32[32,16,128]{2,1,0:T(8,128)S(1)} all-to-all(f32[32,16,128]{2,1,0:T(8,128)S(1)} %outer.1), channel_id=1, replica_groups=mesh['z'=8,'x'=4,'core'=2,'y'=4] {'core','y','x'}, dimensions={0} | all-to-all | bytes 524288 | tf_op jit(solution)/shard_map/all_to_all | solution.py:381
  87.7 0.0 copy-done.1
  87.7 0.3 backward.1
  88.0 18.6 %all_to_all.23 = f32[64,8,128]{2,1,0:T(8,128)S(1)} all-to-all(f32[64,8,128]{2,1,0:T(8,128)S(1)} %bitcast.14), channel_id=1, replica_groups=mesh['z'=8,'x'=4,'core'=2,'y'=4] {'z','x','core'}, dimensions={0} | all-to-all | bytes 524288 | tf_op jit(solution)/shard_map/all_to_all | solution.py:381
  106.6 0.9 unpack.1
  (3 shorter events, 0.1 us)
Async XLA Ops:
  1.6 28.0 %copy-start.2 = (bf16[64,384]{1,0:T(8,128)(2,1)S(1)}, bf16[64,384]{1,0:T(8,128)(2,1)}, u32[]{:S(2)}) copy-start(bf16[64,384]{1,0:T(8,128)(2,1)} %constant.6.clone.table) | copy-start | bytes 147460
  30.0 16.8 %copy-start = (f32[32,8,128]{2,1,0:T(8,128)S(1)}, f32[32,8,128]{2,1,0:T(8,128)}, u32[]{:S(2)}) copy-start(f32[32,8,128]{2,1,0:T(8,128)} %constant.7.clone.slots) | copy-start | bytes 393220
  49.4 2.2 %collective-permute-start = (f32[16,8,128]{2,1,0:T(8,128)S(1)}, f32[16,8,128]{2,1,0:T(8,128)S(1)}, u32[]{:S(2)}, u32[]{:S(2)}) collective-permute-start(f32[16,8,128]{2,1,0:T(8,128)S(1)} %get-tuple-element.25), channel_id=1, source_target_pairs={{0,4},{4,0},{1,5},{5,1},{2,6},{6,2},{3,7},{7,3},{8,12},{12,8},{9,1... | collective-permute-start | bytes 196616 | tf_op jit(solution)/shard_map/ppermute | solution.py:385
  51.6 4.7 %collective-permute-start.3 = (f32[16,8,128]{2,1,0:T(8,128)S(1)}, f32[16,8,128]{2,1,0:T(8,128)S(1)}, u32[]{:S(2)}, u32[]{:S(2)}) collective-permute-start(f32[16,8,128]{2,1,0:T(8,128)S(1)} %add.12.after), channel_id=1, source_target_pairs={{0,2},{1,3},{2,0},{3,1},{4,6},{5,7},{6,4},{7,5},{8,10},{9,11},{10,... | collective-permute-start | bytes 196616 | tf_op jit(solution)/shard_map/ppermute | solution.py:385
  53.0 5.2 %collective-permute-start.2 = (f32[16,8,128]{2,1,0:T(8,128)S(1)}, f32[16,8,128]{2,1,0:T(8,128)S(1)}, u32[]{:S(2)}, u32[]{:S(2)}) collective-permute-start(f32[16,8,128]{2,1,0:T(8,128)S(1)} %add.12.after), channel_id=1, source_target_pairs={{0,3},{1,2},{2,1},{3,0},{4,7},{5,6},{6,5},{7,4},{8,11},{9,10},{10,... | collective-permute-start | bytes 196616 | tf_op jit(solution)/shard_map/ppermute | solution.py:385
  54.5 3.8 %collective-permute-start.1 = (f32[16,8,128]{2,1,0:T(8,128)S(1)}, f32[16,8,128]{2,1,0:T(8,128)S(1)}, u32[]{:S(2)}, u32[]{:S(2)}) collective-permute-start(f32[16,8,128]{2,1,0:T(8,128)S(1)} %add.12.after), channel_id=1, source_target_pairs={{0,1},{1,0},{2,3},{3,2},{4,5},{5,4},{6,7},{7,6},{8,9},{9,8},{10,11... | collective-permute-start | bytes 196616 | tf_op jit(solution)/shard_map/ppermute | solution.py:385
  58.3 4.7 %collective-permute-start.6 = (f32[16,8,128]{2,1,0:T(8,128)S(1)}, f32[16,8,128]{2,1,0:T(8,128)S(1)}, u32[]{:S(2)}, u32[]{:S(2)}) collective-permute-start(f32[16,8,128]{2,1,0:T(8,128)S(1)} %add_add_fusion.state0), channel_id=1, source_target_pairs={{0,16},{8,24},{16,0},{24,8},{1,17},{9,25},{17,1},{25,9},{2,18},{10... | collective-permute-start | bytes 196616 | tf_op jit(solution)/shard_map/ppermute | solution.py:385
  59.7 4.3 %collective-permute-start.5 = (f32[16,8,128]{2,1,0:T(8,128)S(1)}, f32[16,8,128]{2,1,0:T(8,128)S(1)}, u32[]{:S(2)}, u32[]{:S(2)}) collective-permute-start(f32[16,8,128]{2,1,0:T(8,128)S(1)} %add_add_fusion.state0), channel_id=1, source_target_pairs={{0,24},{8,16},{16,8},{24,0},{1,25},{9,17},{17,9},{25,1},{2,26},{10... | collective-permute-start | bytes 196616 | tf_op jit(solution)/shard_map/ppermute | solution.py:385
  60.5 4.1 %collective-permute-start.4 = (f32[16,8,128]{2,1,0:T(8,128)S(1)}, f32[16,8,128]{2,1,0:T(8,128)S(1)}, u32[]{:S(2)}, u32[]{:S(2)}) collective-permute-start(f32[16,8,128]{2,1,0:T(8,128)S(1)} %add_add_fusion.state0), channel_id=1, source_target_pairs={{0,8},{8,0},{16,24},{24,16},{1,9},{9,1},{17,25},{25,17},{2,10},{10... | collective-permute-start | bytes 196616 | tf_op jit(solution)/shard_map/ppermute | solution.py:385
  64.6 3.2 %collective-permute-start.7 = (f32[2,8,8,128]{3,2,1,0:T(8,128)S(1)}, f32[2,8,8,128]{3,2,1,0:T(8,128)S(1)}, u32[]{:S(2)}, u32[]{:S(2)}) collective-permute-start(f32[2,8,8,128]{3,2,1,0:T(8,128)S(1)} %get-tuple-element.28.near), channel_id=1, source_target_pairs={{0,32},{32,0},{64,96},{96,64},{128,160},{160,128},{192,224},{224,1... | collective-permute-start | bytes 196616 | tf_op jit(solution)/shard_map/ppermute | solution.py:385
  65.3 4.3 %collective-permute-start.8 = (f32[2,8,8,128]{3,2,1,0:T(8,128)S(1)}, f32[2,8,8,128]{3,2,1,0:T(8,128)S(1)}, u32[]{:S(2)}, u32[]{:S(2)}) collective-permute-start(f32[2,8,8,128]{3,2,1,0:T(8,128)S(1)} %get-tuple-element.29.far), channel_id=1, source_target_pairs={{0,224},{32,64},{64,32},{96,128},{128,96},{160,192},{192,160},{224... | collective-permute-start | bytes 196616 | tf_op jit(solution)/shard_map/ppermute | solution.py:436
  71.7 16.0 %copy-start.1 = (bf16[64,384]{1,0:T(8,128)(2,1)S(1)}, bf16[64,384]{1,0:T(8,128)(2,1)}, u32[]{:S(2)}) copy-start(bf16[64,384]{1,0:T(8,128)(2,1)} %constant.8.clone.table) | copy-start | bytes 147460

commit v8 on v7

--- a/solution.py
+++ b/solution.py
@@ -281,59 +281,19 @@
         far[c], near[c] = by_side(right[c] + part[CHUNK // 2 :], left[c] + part[: CHUNK // 2])
 
 
-def inner_kernel(ops, lows, scale, inverse, near, far, edges, iterate, source):
-    middle = slice(HALO, HALO + CHUNK)
-    for i, part in enumerate(by_side(near[...], far[...])):
-        start(inverse, part, source, slice((i + 1) * HALO, (i + 2) * HALO))
-    iterate[...] = source[:, middle]
-    for sweep in range(SWEEPS):
-        lo, hi = sweep, CHUNK - sweep
-        if sweep:
-            here = slice(HALO + lo, HALO + hi)
-            coupled = [couple(ops, lows, scale[here], iterate[c, lo - 1 : hi + 1]) for c in range(2)]
-            fresh = damped(iterate[:, lo:hi], source[:, here], inverse[:, here], coupled)
-            iterate[0, lo:hi] = fresh[0]
-            iterate[1, lo:hi] = fresh[1]
-        edges[sweep, :, :2] = iterate[:, lo : lo + 2]
-        edges[sweep, :, 2:] = iterate[:, hi - 2 : hi]
-
-
-def outer_kernel(ops, lows, scale, inverse, near, far, beyond_near, beyond_far, edges, before, out, iterate, source):
+def second_kernel(ops, lows, scale, inverse, near, far, beyond_near, beyond_far, before, out, iterate, source):
     left, right = by_side(near[...], far[...])
     west, east = by_side(beyond_near[...], beyond_far[...])
     for i, part in enumerate((west, left, right, east)):
-        start(inverse, part, source, slice(i * HALO, (i + 1) * HALO))
+        iterate[:, i * HALO : (i + 1) * HALO] = part
     out[:, :8, :] = before[...]
-    reach = SWEEPS - 1
-    iterate[:, :reach] = source[:, 1:HALO]
-    iterate[:, reach + 4 :] = source[:, HALO + CHUNK : WINDOW - 1]
-    for sweep in range(1, SWEEPS):
-        iterate[:, reach : reach + 4] = edges[sweep - 1]
-        one = slice(sweep + 1, HALO + sweep)
-        two = slice(WINDOW - HALO - sweep, WINDOW - 1 - sweep)
-        sides = [
-            jnp.concatenate((ref[one], ref[HALO : HALO + 2], ref[two]), axis=0)
-            for ref in [scale] + [inverse.at[i] for i in range(3)] + [source.at[i] for i in range(2)]
-        ]
-        coupled = [couple(ops, lows, sides[0], iterate[c]) for c in range(2)]
-        fresh = damped(iterate[:, 1:-1], sides[4:], sides[1:4], coupled)
-        for c in range(2):
-            iterate[c, :reach] = fresh[c][:reach]
-            iterate[c, reach + 4 :] = fresh[c][reach + 2 :]
-    last = edges.at[SWEEPS - 1]
+    relax(ops, lows, scale, inverse, iterate, source)
     for xc in range(8):
-        for col in range(2):
-            x = 2 * xc + col
+        for yd in range(4):
             for c in range(2):
-                if x < reach:
-                    tile = iterate.at[c, x]
-                elif x < reach + 2:
-                    tile = last.at[c, x - reach]
-                else:
-                    tile = iterate.at[c, x + 2]
-                at = 8 + c * 4 + col * 2
-                for yd in range(4):
-                    out[seat(xc, yd), at : at + 2, :] = tile[2 * yd : 2 * yd + 2, :]
+                for col in range(2):
+                    at = 8 + c * 4 + col * 2
+                    out[seat(xc, yd), at : at + 2, :] = iterate[c, HALO + 2 * xc + col, 2 * yd : 2 * yd + 2, :]
 
 
 def backward_kernel(table, got, out):
@@ -360,7 +320,7 @@
         copy.wait()
 
 
-def call(kernel, outs, ins, scratch=(), specs=None, name=None, params=PARAMS, out=VMEM, cost=None):
+def call(kernel, outs, ins, scratch=(), specs=None, name=None, params=PARAMS, out=VMEM):
     return pl.pallas_call(
         kernel,
         out_shape=outs,
@@ -368,7 +328,6 @@
         out_specs=jax.tree.map(lambda _: out, outs),
         scratch_shapes=scratch,
         compiler_params=params,
-        cost_estimate=cost,
         name=name,
     )(*ins)
 
@@ -434,20 +393,12 @@
     planes = lax.axis_size("z")
     other = [(z, (z + 1 if z % 2 else z - 1) % planes) for z in range(planes)]
     beyond_far = lax.ppermute(far, "z", other)
-    edges = call(
-        inner_kernel,
-        f32(SWEEPS, 2, 4, 8, LANES),
-        (ops, lows, scale, inverse, near, far),
-        (pltpu.VMEM((2, CHUNK, 8, LANES), jnp.float32), both),
-        name="inner",
-        cost=pl.CostEstimate(flops=2_000_000_000, bytes_accessed=1_000_000, transcendentals=0),
-    )
     done = call(
-        outer_kernel,
+        second_kernel,
         f32(FREQS, 16, LANES),
-        (ops, lows, scale, inverse, near, far, beyond_near, beyond_far, edges, done),
-        (pltpu.VMEM((2, 2 * SWEEPS + 2, 8, LANES), jnp.float32), both),
-        name="outer",
+        (ops, lows, scale, inverse, near, far, beyond_near, beyond_far, done),
+        (both, both),
+        name="second",
     )
     got = exchange(done, PLANE).reshape(FREQS * 16, LANES)
     slices = call(backward_kernel, f32(STEPS * 8, LANES), (BACKWARD, got), name="backward")

time: 108 us -> 108 us (level)
  waiting for transfers between devices: 10.6 us -> 12.5 us
  Pallas kernels: 9.97 us -> 8.52 us
    ppermute x8, waiting for transfers between devices: 8.83 us -> 10.7 us  [swapped(): lax.ppermute(block, axis, [(i, i ^ bits) for i in range(lax.axis_size(axi...]
    pallas_call x9 -> x8, Pallas kernels: 9.97 us -> 8.52 us  [call(): pl.pallas_call(kernel, out_shape=outs, in_specs=specs or [VMEM] * len(ins...]
  transfers between devices with their start and end apart: 9 -> 9, of which waited for: 8 -> 8; matrix products, arithmetic and copies ran while one was open for 0% -> 0% of each run, Pallas kernels for 2% -> 0%
where the time goes in v8:
time: 108 us
  blocking collectives  79.3 us (73%)
  waiting for transfers between devices  12.5 us (12%)
  Pallas kernels  8.52 us (8%)
  starting transfers between devices  7.49 us (7%)
    all_to_all x4, blocking collectives, exchange(): return lax.all_to_all(blocks, axes, 0, 0, tiled=True)  79.3 us
    ppermute x8, waiting for transfers between devices, swapped(): lax.ppermute(block, axis, [(i, i ^ bits) for i in range(lax.axis_size(axi...  10.7 us
    pallas_call x8, Pallas kernels, call(): pl.pallas_call(kernel, out_shape=outs, in_specs=specs or [VMEM] * len(ins...  8.52 us
    ppermute x8, starting transfers between devices, swapped(): lax.ppermute(block, axis, [(i, i ^ bits) for i in range(lax.axis_size(axi...  7.49 us
  transfers between devices with their start and end apart: 9, of which 8 were waited for; matrix products, arithmetic and copies ran while one was open for 0% of the time, Pallas kernels for 0%

profile of v8, /device:TPU:1, one launch (start us, length us, event | category | flops | bytes accessed | tf_op | source)
XLA Modules:
  0.0 108.1 jit_solution(1020860660838635764)
XLA Ops:
  0.0 1.6 %pack.1 = (f32[768,128]{1,0:T(8,128)S(1)}, bf16[256,768]{1,0:T(8,128)(2,1)S(1)}, bf16[128,512]{1,0:T(8,128)(2,1)S(1)}, f32[8,128]{1,0:T(8,128)S(1)}) custom-call(f32[250,2,128]{2,1,0:T(2,128)} %bitcast.17, f32[1,125,2,128]{3,2,1,0:T(2,128)} %bitcast.19, f32[1,2,128]{2,1,0:T(2,128)} %bitcast.21, f32[1,125,125]{2,1,0:T(8,128)} %bitcast.20, f32[125,4,125]{2,1,0:T(4,128)} %bitcast.18), custom_call_target="tpu_custom_call" | custom-call | tf_op jit(solution)/shard_map/pack/pallas_call | solution.py:324
  1.6 0.0 copy-start.2
  1.6 28.0 %all_to_all.20 = f32[64,3,4,128]{3,2,1,0:T(4,128)S(1)} all-to-all(f32[64,3,4,128]{3,2,1,0:T(4,128)S(1)} %bitcast.16), channel_id=1, replica_groups=mesh['z'=8,'x'=4,'core'=2,'y'=4] {'z','x','core'}, dimensions={0} | all-to-all | bytes 786432 | tf_op jit(solution)/shard_map/all_to_all | solution.py:340
  29.6 0.0 copy-done.2
  29.6 0.3 forward.1
  30.0 0.0 copy-start
  30.0 16.8 %all_to_all.21.got = f32[32,24,128]{2,1,0:T(8,128)S(1)} all-to-all(f32[32,24,128]{2,1,0:T(8,128)S(1)} %bitcast.12), channel_id=1, replica_groups=mesh['z'=8,'x'=4,'core'=2,'y'=4] {'core','y','x'}, dimensions={0} | all-to-all | bytes 786432 | tf_op jit(solution)/shard_map/all_to_all | solution.py:340
  46.7 0.0 copy-done
  46.7 2.7 %first.1 = (f32[2,16,8,128]{3,2,1,0:T(8,128)S(1)}, f32[16,8,128]{2,1,0:T(8,128)S(1)}, f32[32,8,128]{2,1,0:T(8,128)S(1)}, f32[3,32,8,128]{3,2,1,0:T(8,128)S(1)}) custom-call(f32[32,8,128]{2,1,0:T(8,128)S(1)} %copy-done, bf16[256,768]{1,0:T(8,128)(2,1)S(1)} %get-tuple-element.18.ops, bf16[128,512]{1,0:T(8,128)(2,1)S(1)} %get-tuple-element.19.lows, ...), custom_call_target="tpu_custom_call" | custom-call | tf_op jit(solution)/shard_map/first/pallas_call | solution.py:324
  49.4 1.3 %collective-permute-start = (f32[16,8,128]{2,1,0:T(8,128)S(1)}, f32[16,8,128]{2,1,0:T(8,128)S(1)}, u32[]{:S(2)}, u32[]{:S(2)}) collective-permute-start(f32[16,8,128]{2,1,0:T(8,128)S(1)} %get-tuple-element.25), channel_id=1, source_target_pairs={{0,4},{4,0},{1,5},{5,1},{2,6},{6,2},{3,7},{7,3},{8,12},{12,8},{9,1... | collective-permute-start | bytes 196616 | tf_op jit(solution)/shard_map/ppermute | solution.py:344
  50.7 0.9 collective-permute-done
  51.7 1.4 %collective-permute-start.3 = (f32[16,8,128]{2,1,0:T(8,128)S(1)}, f32[16,8,128]{2,1,0:T(8,128)S(1)}, u32[]{:S(2)}, u32[]{:S(2)}) collective-permute-start(f32[16,8,128]{2,1,0:T(8,128)S(1)} %add.12.after), channel_id=1, source_target_pairs={{0,2},{1,3},{2,0},{3,1},{4,6},{5,7},{6,4},{7,5},{8,10},{9,11},{10,... | collective-permute-start | bytes 196616 | tf_op jit(solution)/shard_map/ppermute | solution.py:344
  53.0 1.4 %collective-permute-start.2 = (f32[16,8,128]{2,1,0:T(8,128)S(1)}, f32[16,8,128]{2,1,0:T(8,128)S(1)}, u32[]{:S(2)}, u32[]{:S(2)}) collective-permute-start(f32[16,8,128]{2,1,0:T(8,128)S(1)} %add.12.after), channel_id=1, source_target_pairs={{0,3},{1,2},{2,1},{3,0},{4,7},{5,6},{6,5},{7,4},{8,11},{9,10},{10,... | collective-permute-start | bytes 196616 | tf_op jit(solution)/shard_map/ppermute | solution.py:344
  54.5 0.0 collective-permute-start.1
  54.5 1.9 %collective-permute-done.3 = f32[16,8,128]{2,1,0:T(8,128)S(1)} collective-permute-done((f32[16,8,128]{2,1,0:T(8,128)S(1)}, f32[16,8,128]{2,1,0:T(8,128)S(1)}, u32[]{:S(2)}, u32[]{:S(2)}) %collective-permute-start.3) | collective-permute-done | bytes 65568 | tf_op jit(solution)/shard_map/ppermute | solution.py:344
  56.4 1.9 %collective-permute-done.2 = f32[16,8,128]{2,1,0:T(8,128)S(1)} collective-permute-done((f32[16,8,128]{2,1,0:T(8,128)S(1)}, f32[16,8,128]{2,1,0:T(8,128)S(1)}, u32[]{:S(2)}, u32[]{:S(2)}) %collective-permute-start.2) | collective-permute-done | bytes 65568 | tf_op jit(solution)/shard_map/ppermute | solution.py:344
  58.3 0.0 collective-permute-done.1
  58.3 1.3 %collective-permute-start.6 = (f32[16,8,128]{2,1,0:T(8,128)S(1)}, f32[16,8,128]{2,1,0:T(8,128)S(1)}, u32[]{:S(2)}, u32[]{:S(2)}) collective-permute-start(f32[16,8,128]{2,1,0:T(8,128)S(1)} %add_add_fusion.state0), channel_id=1, source_target_pairs={{0,16},{8,24},{16,0},{24,8},{1,17},{9,25},{17,1},{25,9},{2,18},{10... | collective-permute-start | bytes 196616 | tf_op jit(solution)/shard_map/ppermute | solution.py:344
  59.7 0.9 collective-permute-start.5
  60.5 0.5 collective-permute-start.4
  61.1 0.1 between.1
  61.1 1.9 %collective-permute-done.6.state3 = f32[16,8,128]{2,1,0:T(8,128)S(1)} collective-permute-done((f32[16,8,128]{2,1,0:T(8,128)S(1)}, f32[16,8,128]{2,1,0:T(8,128)S(1)}, u32[]{:S(2)}, u32[]{:S(2)}) %collective-permute-start.6) | collective-permute-done | bytes 65568 | tf_op jit(solution)/shard_map/ppermute | solution.py:344
  63.0 1.0 collective-permute-done.5.state2
  64.0 0.6 collective-permute-done.4.state1
  64.6 0.6 collective-permute-start.7
  65.3 0.0 collective-permute-start.8
  65.3 2.6 %collective-permute-done.7.beyond_near = f32[2,8,8,128]{3,2,1,0:T(8,128)S(1)} collective-permute-done((f32[2,8,8,128]{3,2,1,0:T(8,128)S(1)}, f32[2,8,8,128]{3,2,1,0:T(8,128)S(1)}, u32[]{:S(2)}, u32[]{:S(2)}) %collective-permute-start.7) | collective-permute-done | bytes 65568 | tf_op jit(solution)/shard_map/ppermute | solution.py:344
  67.8 1.8 %collective-permute-done.8.beyond_far = f32[2,8,8,128]{3,2,1,0:T(8,128)S(1)} collective-permute-done((f32[2,8,8,128]{3,2,1,0:T(8,128)S(1)}, f32[2,8,8,128]{3,2,1,0:T(8,128)S(1)}, u32[]{:S(2)}, u32[]{:S(2)}) %collective-permute-start.8) | collective-permute-done | bytes 65568 | tf_op jit(solution)/shard_map/ppermute | solution.py:395
  69.6 2.6 %second.1 = f32[32,16,128]{2,1,0:T(8,128)S(1)} custom-call(bf16[256,768]{1,0:T(8,128)(2,1)S(1)} %get-tuple-element.18.ops, bf16[128,512]{1,0:T(8,128)(2,1)S(1)} %get-tuple-element.19.lows, f32[32,8,128]{2,1,0:T(8,128)S(1)} %get-tuple-element.22.scale, f32[3,32,8,128]{3,2,1,0:T(8,128)S(1)} %get-tuple-element.23.inverse, ...), custom_call_target="tpu_custom_call" | custom-call | tf_op jit(solution)/shard_map/second/pallas_call | solution.py:324
  72.1 0.0 copy-start.1
  72.2 15.9 %all_to_all.22 = f32[32,16,128]{2,1,0:T(8,128)S(1)} all-to-all(f32[32,16,128]{2,1,0:T(8,128)S(1)} %second.1), channel_id=1, replica_groups=mesh['z'=8,'x'=4,'core'=2,'y'=4] {'core','y','x'}, dimensions={0} | all-to-all | bytes 524288 | tf_op jit(solution)/shard_map/all_to_all | solution.py:340
  88.1 0.0 copy-done.1
  88.1 0.3 backward.1
  88.4 18.6 %all_to_all.23 = f32[64,8,128]{2,1,0:T(8,128)S(1)} all-to-all(f32[64,8,128]{2,1,0:T(8,128)S(1)} %bitcast.14), channel_id=1, replica_groups=mesh['z'=8,'x'=4,'core'=2,'y'=4] {'z','x','core'}, dimensions={0} | all-to-all | bytes 524288 | tf_op jit(solution)/shard_map/all_to_all | solution.py:340
  107.0 0.9 unpack.1
  (3 shorter events, 0.1 us)
Async XLA Ops:
  1.6 28.0 %copy-start.2 = (bf16[64,384]{1,0:T(8,128)(2,1)S(1)}, bf16[64,384]{1,0:T(8,128)(2,1)}, u32[]{:S(2)}) copy-start(bf16[64,384]{1,0:T(8,128)(2,1)} %constant.6.clone.table) | copy-start | bytes 147460
  30.0 16.8 %copy-start = (f32[32,8,128]{2,1,0:T(8,128)S(1)}, f32[32,8,128]{2,1,0:T(8,128)}, u32[]{:S(2)}) copy-start(f32[32,8,128]{2,1,0:T(8,128)} %constant.7.clone.slots) | copy-start | bytes 393220
  49.4 2.2 %collective-permute-start = (f32[16,8,128]{2,1,0:T(8,128)S(1)}, f32[16,8,128]{2,1,0:T(8,128)S(1)}, u32[]{:S(2)}, u32[]{:S(2)}) collective-permute-start(f32[16,8,128]{2,1,0:T(8,128)S(1)} %get-tuple-element.25), channel_id=1, source_target_pairs={{0,4},{4,0},{1,5},{5,1},{2,6},{6,2},{3,7},{7,3},{8,12},{12,8},{9,1... | collective-permute-start | bytes 196616 | tf_op jit(solution)/shard_map/ppermute | solution.py:344
  51.7 4.7 %collective-permute-start.3 = (f32[16,8,128]{2,1,0:T(8,128)S(1)}, f32[16,8,128]{2,1,0:T(8,128)S(1)}, u32[]{:S(2)}, u32[]{:S(2)}) collective-permute-start(f32[16,8,128]{2,1,0:T(8,128)S(1)} %add.12.after), channel_id=1, source_target_pairs={{0,2},{1,3},{2,0},{3,1},{4,6},{5,7},{6,4},{7,5},{8,10},{9,11},{10,... | collective-permute-start | bytes 196616 | tf_op jit(solution)/shard_map/ppermute | solution.py:344
  53.0 5.3 %collective-permute-start.2 = (f32[16,8,128]{2,1,0:T(8,128)S(1)}, f32[16,8,128]{2,1,0:T(8,128)S(1)}, u32[]{:S(2)}, u32[]{:S(2)}) collective-permute-start(f32[16,8,128]{2,1,0:T(8,128)S(1)} %add.12.after), channel_id=1, source_target_pairs={{0,3},{1,2},{2,1},{3,0},{4,7},{5,6},{6,5},{7,4},{8,11},{9,10},{10,... | collective-permute-start | bytes 196616 | tf_op jit(solution)/shard_map/ppermute | solution.py:344
  54.5 3.8 %collective-permute-start.1 = (f32[16,8,128]{2,1,0:T(8,128)S(1)}, f32[16,8,128]{2,1,0:T(8,128)S(1)}, u32[]{:S(2)}, u32[]{:S(2)}) collective-permute-start(f32[16,8,128]{2,1,0:T(8,128)S(1)} %add.12.after), channel_id=1, source_target_pairs={{0,1},{1,0},{2,3},{3,2},{4,5},{5,4},{6,7},{7,6},{8,9},{9,8},{10,11... | collective-permute-start | bytes 196616 | tf_op jit(solution)/shard_map/ppermute | solution.py:344
  58.3 4.7 %collective-permute-start.6 = (f32[16,8,128]{2,1,0:T(8,128)S(1)}, f32[16,8,128]{2,1,0:T(8,128)S(1)}, u32[]{:S(2)}, u32[]{:S(2)}) collective-permute-start(f32[16,8,128]{2,1,0:T(8,128)S(1)} %add_add_fusion.state0), channel_id=1, source_target_pairs={{0,16},{8,24},{16,0},{24,8},{1,17},{9,25},{17,1},{25,9},{2,18},{10... | collective-permute-start | bytes 196616 | tf_op jit(solution)/shard_map/ppermute | solution.py:344
  59.7 4.3 %collective-permute-start.5 = (f32[16,8,128]{2,1,0:T(8,128)S(1)}, f32[16,8,128]{2,1,0:T(8,128)S(1)}, u32[]{:S(2)}, u32[]{:S(2)}) collective-permute-start(f32[16,8,128]{2,1,0:T(8,128)S(1)} %add_add_fusion.state0), channel_id=1, source_target_pairs={{0,24},{8,16},{16,8},{24,0},{1,25},{9,17},{17,9},{25,1},{2,26},{10... | collective-permute-start | bytes 196616 | tf_op jit(solution)/shard_map/ppermute | solution.py:344
  60.5 4.1 %collective-permute-start.4 = (f32[16,8,128]{2,1,0:T(8,128)S(1)}, f32[16,8,128]{2,1,0:T(8,128)S(1)}, u32[]{:S(2)}, u32[]{:S(2)}) collective-permute-start(f32[16,8,128]{2,1,0:T(8,128)S(1)} %add_add_fusion.state0), channel_id=1, source_target_pairs={{0,8},{8,0},{16,24},{24,16},{1,9},{9,1},{17,25},{25,17},{2,10},{10... | collective-permute-start | bytes 196616 | tf_op jit(solution)/shard_map/ppermute | solution.py:344
  64.6 3.2 %collective-permute-start.7 = (f32[2,8,8,128]{3,2,1,0:T(8,128)S(1)}, f32[2,8,8,128]{3,2,1,0:T(8,128)S(1)}, u32[]{:S(2)}, u32[]{:S(2)}) collective-permute-start(f32[2,8,8,128]{3,2,1,0:T(8,128)S(1)} %get-tuple-element.28.near), channel_id=1, source_target_pairs={{0,32},{32,0},{64,96},{96,64},{128,160},{160,128},{192,224},{224,1... | collective-permute-start | bytes 196616 | tf_op jit(solution)/shard_map/ppermute | solution.py:344
  65.3 4.3 %collective-permute-start.8 = (f32[2,8,8,128]{3,2,1,0:T(8,128)S(1)}, f32[2,8,8,128]{3,2,1,0:T(8,128)S(1)}, u32[]{:S(2)}, u32[]{:S(2)}) collective-permute-start(f32[2,8,8,128]{3,2,1,0:T(8,128)S(1)} %get-tuple-element.29.far), channel_id=1, source_target_pairs={{0,224},{32,64},{64,32},{96,128},{128,96},{160,192},{192,160},{224... | collective-permute-start | bytes 196616 | tf_op jit(solution)/shard_map/ppermute | solution.py:395
  72.1 16.0 %copy-start.1 = (bf16[64,384]{1,0:T(8,128)(2,1)S(1)}, bf16[64,384]{1,0:T(8,128)(2,1)}, u32[]{:S(2)}) copy-start(bf16[64,384]{1,0:T(8,128)(2,1)} %constant.8.clone.table) | copy-start | bytes 147460

commit v9 on v7

--- a/solution.py
+++ b/solution.py
@@ -273,7 +273,7 @@
     return jnp.where(even, two, one), jnp.where(even, one, two)
 
 
-def carry_kernel(slots, left, right, state0, state1, state2, state3, near, far):
+def carry_kernel(slots, left, right, state0, state1, state2, state3, far, near):
     state = (state0[...] + state1[...]) + (state2[...] + state3[...])
     mine = slots[slot()]
     for c in range(2):
@@ -281,7 +281,7 @@
         far[c], near[c] = by_side(right[c] + part[CHUNK // 2 :], left[c] + part[: CHUNK // 2])
 
 
-def inner_kernel(ops, lows, scale, inverse, near, far, edges, iterate, source):
+def inner_kernel(ops, lows, scale, inverse, far, near, edges, iterate, source):
     middle = slice(HALO, HALO + CHUNK)
     for i, part in enumerate(by_side(near[...], far[...])):
         start(inverse, part, source, slice((i + 1) * HALO, (i + 2) * HALO))
@@ -298,7 +298,7 @@
         edges[sweep, :, 2:] = iterate[:, hi - 2 : hi]
 
 
-def outer_kernel(ops, lows, scale, inverse, near, far, beyond_near, beyond_far, edges, before, out, iterate, source):
+def outer_kernel(ops, lows, scale, inverse, far, near, beyond_far, beyond_near, edges, before, out, iterate, source):
     left, right = by_side(near[...], far[...])
     west, east = by_side(beyond_near[...], beyond_far[...])
     for i, part in enumerate((west, left, right, east)):
@@ -429,15 +429,15 @@
     near, far, across = (swapped(state, "y", bits) for bits in (1, 3, 2))
     state = ((state + near) + far) + across
     states = [state] + [swapped(state, "x", bits) for bits in (1, 3, 2)]
-    near, far = call(carry_kernel, (half, half), (SLOTS, left, right, *states), name="carry")
-    beyond_near = swapped(near, "z", 1)
+    far, near = call(carry_kernel, (half, half), (SLOTS, left, right, *states), name="carry")
     planes = lax.axis_size("z")
     other = [(z, (z + 1 if z % 2 else z - 1) % planes) for z in range(planes)]
     beyond_far = lax.ppermute(far, "z", other)
+    beyond_near = swapped(near, "z", 1)
     edges = call(
         inner_kernel,
         f32(SWEEPS, 2, 4, 8, LANES),
-        (ops, lows, scale, inverse, near, far),
+        (ops, lows, scale, inverse, far, near),
         (pltpu.VMEM((2, CHUNK, 8, LANES), jnp.float32), both),
         name="inner",
         cost=pl.CostEstimate(flops=2_000_000_000, bytes_accessed=1_000_000, transcendentals=0),
@@ -445,7 +445,7 @@
     done = call(
         outer_kernel,
         f32(FREQS, 16, LANES),
-        (ops, lows, scale, inverse, near, far, beyond_near, beyond_far, edges, done),
+        (ops, lows, scale, inverse, far, near, beyond_far, beyond_near, edges, done),
         (pltpu.VMEM((2, 2 * SWEEPS + 2, 8, LANES), jnp.float32), both),
         name="outer",
     )

time: 108 us -> 108 us (level)
  waiting for transfers between devices: 10.6 us -> 9.5 us
  transfers between devices with their start and end apart: 9 -> 9, of which waited for: 8 -> 7; matrix products, arithmetic and copies ran while one was open for 0% -> 0% of each run, Pallas kernels for 2% -> 2%
where the time goes in v9:
time: 108 us
  blocking collectives  79.7 us (74%)
  Pallas kernels  9.97 us (9%)
  waiting for transfers between devices  9.5 us (9%)
  starting transfers between devices  8.05 us (7%)
    all_to_all x4, blocking collectives, exchange(): return lax.all_to_all(blocks, axes, 0, 0, tiled=True)  79.7 us
    pallas_call x9, Pallas kernels, call(): pl.pallas_call(kernel, out_shape=outs, in_specs=specs or [VMEM] * len(ins...  9.97 us
    ppermute x8, waiting for transfers between devices, swapped(): lax.ppermute(block, axis, [(i, i ^ bits) for i in range(lax.axis_size(axi...  8.15 us
    ppermute x8, starting transfers between devices, swapped(): lax.ppermute(block, axis, [(i, i ^ bits) for i in range(lax.axis_size(axi...  7.95 us
  transfers between devices with their start and end apart: 9, of which 7 were waited for; matrix products, arithmetic and copies ran while one was open for 0% of the time, Pallas kernels for 2%

profile of v9, /device:TPU:1, one launch (start us, length us, event | category | flops | bytes accessed | tf_op | source)
XLA Modules:
  0.0 107.5 jit_solution(5214992098881376908)
XLA Ops:
  0.0 1.6 %pack.1 = (f32[768,128]{1,0:T(8,128)S(1)}, bf16[256,768]{1,0:T(8,128)(2,1)S(1)}, bf16[128,512]{1,0:T(8,128)(2,1)S(1)}, f32[8,128]{1,0:T(8,128)S(1)}) custom-call(f32[250,2,128]{2,1,0:T(2,128)} %bitcast.17, f32[1,125,2,128]{3,2,1,0:T(2,128)} %bitcast.19, f32[1,2,128]{2,1,0:T(2,128)} %bitcast.21, f32[1,125,125]{2,1,0:T(8,128)} %bitcast.20, f32[125,4,125]{2,1,0:T(4,128)} %bitcast.18), custom_call_target="tpu_custom_call" | custom-call | tf_op jit(solution)/shard_map/pack/pallas_call | solution.py:364
  1.6 0.0 copy-start.2
  1.6 28.0 %all_to_all.20 = f32[64,3,4,128]{3,2,1,0:T(4,128)S(1)} all-to-all(f32[64,3,4,128]{3,2,1,0:T(4,128)S(1)} %bitcast.16), channel_id=1, replica_groups=mesh['z'=8,'x'=4,'core'=2,'y'=4] {'z','x','core'}, dimensions={0} | all-to-all | bytes 786432 | tf_op jit(solution)/shard_map/all_to_all | solution.py:381
  29.6 0.0 copy-done.2
  29.6 0.3 forward.1
  30.0 0.0 copy-start
  30.0 16.8 %all_to_all.21.got = f32[32,24,128]{2,1,0:T(8,128)S(1)} all-to-all(f32[32,24,128]{2,1,0:T(8,128)S(1)} %bitcast.12), channel_id=1, replica_groups=mesh['z'=8,'x'=4,'core'=2,'y'=4] {'core','y','x'}, dimensions={0} | all-to-all | bytes 786432 | tf_op jit(solution)/shard_map/all_to_all | solution.py:381
  46.7 0.0 copy-done
  46.7 2.7 %first.1 = (f32[2,16,8,128]{3,2,1,0:T(8,128)S(1)}, f32[16,8,128]{2,1,0:T(8,128)S(1)}, f32[32,8,128]{2,1,0:T(8,128)S(1)}, f32[3,32,8,128]{3,2,1,0:T(8,128)S(1)}) custom-call(f32[32,8,128]{2,1,0:T(8,128)S(1)} %copy-done, bf16[256,768]{1,0:T(8,128)(2,1)S(1)} %get-tuple-element.18.ops, bf16[128,512]{1,0:T(8,128)(2,1)S(1)} %get-tuple-element.19.lows, ...), custom_call_target="tpu_custom_call" | custom-call | tf_op jit(solution)/shard_map/first/pallas_call | solution.py:364
  49.4 1.3 %collective-permute-start = (f32[16,8,128]{2,1,0:T(8,128)S(1)}, f32[16,8,128]{2,1,0:T(8,128)S(1)}, u32[]{:S(2)}, u32[]{:S(2)}) collective-permute-start(f32[16,8,128]{2,1,0:T(8,128)S(1)} %get-tuple-element.25), channel_id=1, source_target_pairs={{0,4},{4,0},{1,5},{5,1},{2,6},{6,2},{3,7},{7,3},{8,12},{12,8},{9,1... | collective-permute-start | bytes 196616 | tf_op jit(solution)/shard_map/ppermute | solution.py:385
  50.7 0.9 collective-permute-done
  51.6 1.4 %collective-permute-start.3 = (f32[16,8,128]{2,1,0:T(8,128)S(1)}, f32[16,8,128]{2,1,0:T(8,128)S(1)}, u32[]{:S(2)}, u32[]{:S(2)}) collective-permute-start(f32[16,8,128]{2,1,0:T(8,128)S(1)} %add.12.after), channel_id=1, source_target_pairs={{0,2},{1,3},{2,0},{3,1},{4,6},{5,7},{6,4},{7,5},{8,10},{9,11},{10,... | collective-permute-start | bytes 196616 | tf_op jit(solution)/shard_map/ppermute | solution.py:385
  53.0 1.4 %collective-permute-start.2 = (f32[16,8,128]{2,1,0:T(8,128)S(1)}, f32[16,8,128]{2,1,0:T(8,128)S(1)}, u32[]{:S(2)}, u32[]{:S(2)}) collective-permute-start(f32[16,8,128]{2,1,0:T(8,128)S(1)} %add.12.after), channel_id=1, source_target_pairs={{0,3},{1,2},{2,1},{3,0},{4,7},{5,6},{6,5},{7,4},{8,11},{9,10},{10,... | collective-permute-start | bytes 196616 | tf_op jit(solution)/shard_map/ppermute | solution.py:385
  54.5 0.0 collective-permute-start.1
  54.5 1.9 %collective-permute-done.3 = f32[16,8,128]{2,1,0:T(8,128)S(1)} collective-permute-done((f32[16,8,128]{2,1,0:T(8,128)S(1)}, f32[16,8,128]{2,1,0:T(8,128)S(1)}, u32[]{:S(2)}, u32[]{:S(2)}) %collective-permute-start.3) | collective-permute-done | bytes 65568 | tf_op jit(solution)/shard_map/ppermute | solution.py:385
  56.4 1.9 %collective-permute-done.2 = f32[16,8,128]{2,1,0:T(8,128)S(1)} collective-permute-done((f32[16,8,128]{2,1,0:T(8,128)S(1)}, f32[16,8,128]{2,1,0:T(8,128)S(1)}, u32[]{:S(2)}, u32[]{:S(2)}) %collective-permute-start.2) | collective-permute-done | bytes 65568 | tf_op jit(solution)/shard_map/ppermute | solution.py:385
  58.3 0.0 collective-permute-done.1
  58.3 1.4 %collective-permute-start.6 = (f32[16,8,128]{2,1,0:T(8,128)S(1)}, f32[16,8,128]{2,1,0:T(8,128)S(1)}, u32[]{:S(2)}, u32[]{:S(2)}) collective-permute-start(f32[16,8,128]{2,1,0:T(8,128)S(1)} %add_add_fusion.state0), channel_id=1, source_target_pairs={{0,16},{8,24},{16,0},{24,8},{1,17},{9,25},{17,1},{25,9},{2,18},{10... | collective-permute-start | bytes 196616 | tf_op jit(solution)/shard_map/ppermute | solution.py:385
  59.7 0.8 collective-permute-start.5
  60.5 0.5 collective-permute-start.4
  61.0 0.1 between.1
  61.1 1.9 %collective-permute-done.6.state3 = f32[16,8,128]{2,1,0:T(8,128)S(1)} collective-permute-done((f32[16,8,128]{2,1,0:T(8,128)S(1)}, f32[16,8,128]{2,1,0:T(8,128)S(1)}, u32[]{:S(2)}, u32[]{:S(2)}) %collective-permute-start.6) | collective-permute-done | bytes 65568 | tf_op jit(solution)/shard_map/ppermute | solution.py:385
  63.0 1.0 collective-permute-done.5.state2
  64.0 0.6 collective-permute-done.4.state1
  64.6 0.1 collective-permute-start.7
  64.7 1.1 %collective-permute-start.8 = (f32[2,8,8,128]{3,2,1,0:T(8,128)S(1)}, f32[2,8,8,128]{3,2,1,0:T(8,128)S(1)}, u32[]{:S(2)}, u32[]{:S(2)}) collective-permute-start(f32[2,8,8,128]{3,2,1,0:T(8,128)S(1)} %get-tuple-element.29.near), channel_id=1, source_target_pairs={{0,32},{32,0},{64,96},{96,64},{128,160},{160,128},{192,224},{224,1... | collective-permute-start | bytes 196616 | tf_op jit(solution)/shard_map/ppermute | solution.py:385
  65.8 1.9 %inner.1.edges = f32[8,2,4,8,128]{4,3,2,1,0:T(8,128)S(1)} custom-call(bf16[256,768]{1,0:T(8,128)(2,1)S(1)} %get-tuple-element.18.ops, bf16[128,512]{1,0:T(8,128)(2,1)S(1)} %get-tuple-element.19.lows, f32[32,8,128]{2,1,0:T(8,128)S(1)} %get-tuple-element.22.scale, f32[3,32,8,128]{3,2,1,0:T(8,128)S(1)} %get-tuple-element.23.inverse, ...), custom_call_target="tpu_custom_call" | custom-call | flops 2000000000 | bytes 1000000 | tf_op jit(solution)/shard_map/inner/pallas_call | solution.py:364
  67.7 1.4 %collective-permute-done.7.beyond_far = f32[2,8,8,128]{3,2,1,0:T(8,128)S(1)} collective-permute-done((f32[2,8,8,128]{3,2,1,0:T(8,128)S(1)}, f32[2,8,8,128]{3,2,1,0:T(8,128)S(1)}, u32[]{:S(2)}, u32[]{:S(2)}) %collective-permute-start.7) | collective-permute-done | bytes 65568 | tf_op jit(solution)/shard_map/ppermute | solution.py:435
  69.0 0.0 collective-permute-done.8.beyond_near
  69.0 2.2 %outer.1 = f32[32,16,128]{2,1,0:T(8,128)S(1)} custom-call(bf16[256,768]{1,0:T(8,128)(2,1)S(1)} %get-tuple-element.18.ops, bf16[128,512]{1,0:T(8,128)(2,1)S(1)} %get-tuple-element.19.lows, f32[32,8,128]{2,1,0:T(8,128)S(1)} %get-tuple-element.22.scale, f32[3,32,8,128]{3,2,1,0:T(8,128)S(1)} %get-tuple-element.23.inverse, ...), custom_call_target="tpu_custom_call" | custom-call | tf_op jit(solution)/shard_map/outer/pallas_call | solution.py:364
  71.2 0.0 copy-start.1
  71.2 15.7 %all_to_all.22 = f32[32,16,128]{2,1,0:T(8,128)S(1)} all-to-all(f32[32,16,128]{2,1,0:T(8,128)S(1)} %outer.1), channel_id=1, replica_groups=mesh['z'=8,'x'=4,'core'=2,'y'=4] {'core','y','x'}, dimensions={0} | all-to-all | bytes 524288 | tf_op jit(solution)/shard_map/all_to_all | solution.py:381
  86.9 0.0 copy-done.1
  86.9 0.3 backward.1
  87.2 19.3 %all_to_all.23 = f32[64,8,128]{2,1,0:T(8,128)S(1)} all-to-all(f32[64,8,128]{2,1,0:T(8,128)S(1)} %bitcast.14), channel_id=1, replica_groups=mesh['z'=8,'x'=4,'core'=2,'y'=4] {'z','x','core'}, dimensions={0} | all-to-all | bytes 524288 | tf_op jit(solution)/shard_map/all_to_all | solution.py:381
  106.5 0.9 unpack.1
  (3 shorter events, 0.1 us)
Async XLA Ops:
  1.6 28.0 %copy-start.2 = (bf16[64,384]{1,0:T(8,128)(2,1)S(1)}, bf16[64,384]{1,0:T(8,128)(2,1)}, u32[]{:S(2)}) copy-start(bf16[64,384]{1,0:T(8,128)(2,1)} %constant.6.clone.table) | copy-start | bytes 147460
  30.0 16.8 %copy-start = (f32[32,8,128]{2,1,0:T(8,128)S(1)}, f32[32,8,128]{2,1,0:T(8,128)}, u32[]{:S(2)}) copy-start(f32[32,8,128]{2,1,0:T(8,128)} %constant.7.clone.slots) | copy-start | bytes 393220
  49.4 2.2 %collective-permute-start = (f32[16,8,128]{2,1,0:T(8,128)S(1)}, f32[16,8,128]{2,1,0:T(8,128)S(1)}, u32[]{:S(2)}, u32[]{:S(2)}) collective-permute-start(f32[16,8,128]{2,1,0:T(8,128)S(1)} %get-tuple-element.25), channel_id=1, source_target_pairs={{0,4},{4,0},{1,5},{5,1},{2,6},{6,2},{3,7},{7,3},{8,12},{12,8},{9,1... | collective-permute-start | bytes 196616 | tf_op jit(solution)/shard_map/ppermute | solution.py:385
  51.6 4.7 %collective-permute-start.3 = (f32[16,8,128]{2,1,0:T(8,128)S(1)}, f32[16,8,128]{2,1,0:T(8,128)S(1)}, u32[]{:S(2)}, u32[]{:S(2)}) collective-permute-start(f32[16,8,128]{2,1,0:T(8,128)S(1)} %add.12.after), channel_id=1, source_target_pairs={{0,2},{1,3},{2,0},{3,1},{4,6},{5,7},{6,4},{7,5},{8,10},{9,11},{10,... | collective-permute-start | bytes 196616 | tf_op jit(solution)/shard_map/ppermute | solution.py:385
  53.0 5.2 %collective-permute-start.2 = (f32[16,8,128]{2,1,0:T(8,128)S(1)}, f32[16,8,128]{2,1,0:T(8,128)S(1)}, u32[]{:S(2)}, u32[]{:S(2)}) collective-permute-start(f32[16,8,128]{2,1,0:T(8,128)S(1)} %add.12.after), channel_id=1, source_target_pairs={{0,3},{1,2},{2,1},{3,0},{4,7},{5,6},{6,5},{7,4},{8,11},{9,10},{10,... | collective-permute-start | bytes 196616 | tf_op jit(solution)/shard_map/ppermute | solution.py:385
  54.5 3.8 %collective-permute-start.1 = (f32[16,8,128]{2,1,0:T(8,128)S(1)}, f32[16,8,128]{2,1,0:T(8,128)S(1)}, u32[]{:S(2)}, u32[]{:S(2)}) collective-permute-start(f32[16,8,128]{2,1,0:T(8,128)S(1)} %add.12.after), channel_id=1, source_target_pairs={{0,1},{1,0},{2,3},{3,2},{4,5},{5,4},{6,7},{7,6},{8,9},{9,8},{10,11... | collective-permute-start | bytes 196616 | tf_op jit(solution)/shard_map/ppermute | solution.py:385
  58.3 4.7 %collective-permute-start.6 = (f32[16,8,128]{2,1,0:T(8,128)S(1)}, f32[16,8,128]{2,1,0:T(8,128)S(1)}, u32[]{:S(2)}, u32[]{:S(2)}) collective-permute-start(f32[16,8,128]{2,1,0:T(8,128)S(1)} %add_add_fusion.state0), channel_id=1, source_target_pairs={{0,16},{8,24},{16,0},{24,8},{1,17},{9,25},{17,1},{25,9},{2,18},{10... | collective-permute-start | bytes 196616 | tf_op jit(solution)/shard_map/ppermute | solution.py:385
  59.7 4.3 %collective-permute-start.5 = (f32[16,8,128]{2,1,0:T(8,128)S(1)}, f32[16,8,128]{2,1,0:T(8,128)S(1)}, u32[]{:S(2)}, u32[]{:S(2)}) collective-permute-start(f32[16,8,128]{2,1,0:T(8,128)S(1)} %add_add_fusion.state0), channel_id=1, source_target_pairs={{0,24},{8,16},{16,8},{24,0},{1,25},{9,17},{17,9},{25,1},{2,26},{10... | collective-permute-start | bytes 196616 | tf_op jit(solution)/shard_map/ppermute | solution.py:385
  60.5 4.1 %collective-permute-start.4 = (f32[16,8,128]{2,1,0:T(8,128)S(1)}, f32[16,8,128]{2,1,0:T(8,128)S(1)}, u32[]{:S(2)}, u32[]{:S(2)}) collective-permute-start(f32[16,8,128]{2,1,0:T(8,128)S(1)} %add_add_fusion.state0), channel_id=1, source_target_pairs={{0,8},{8,0},{16,24},{24,16},{1,9},{9,1},{17,25},{25,17},{2,10},{10... | collective-permute-start | bytes 196616 | tf_op jit(solution)/shard_map/ppermute | solution.py:385
  64.6 4.4 %collective-permute-start.7 = (f32[2,8,8,128]{3,2,1,0:T(8,128)S(1)}, f32[2,8,8,128]{3,2,1,0:T(8,128)S(1)}, u32[]{:S(2)}, u32[]{:S(2)}) collective-permute-start(f32[2,8,8,128]{3,2,1,0:T(8,128)S(1)} %get-tuple-element.28.far), channel_id=1, source_target_pairs={{0,224},{32,64},{64,32},{96,128},{128,96},{160,192},{192,160},{224... | collective-permute-start | bytes 196616 | tf_op jit(solution)/shard_map/ppermute | solution.py:435
  64.7 4.3 %collective-permute-start.8 = (f32[2,8,8,128]{3,2,1,0:T(8,128)S(1)}, f32[2,8,8,128]{3,2,1,0:T(8,128)S(1)}, u32[]{:S(2)}, u32[]{:S(2)}) collective-permute-start(f32[2,8,8,128]{3,2,1,0:T(8,128)S(1)} %get-tuple-element.29.near), channel_id=1, source_target_pairs={{0,32},{32,0},{64,96},{96,64},{128,160},{160,128},{192,224},{224,1... | collective-permute-start | bytes 196616 | tf_op jit(solution)/shard_map/ppermute | solution.py:385
  71.2 15.7 %copy-start.1 = (bf16[64,384]{1,0:T(8,128)(2,1)S(1)}, bf16[64,384]{1,0:T(8,128)(2,1)}, u32[]{:S(2)}) copy-start(bf16[64,384]{1,0:T(8,128)(2,1)} %constant.8.clone.table) | copy-start | bytes 147460

commit v10 on v9

--- a/solution.py
+++ b/solution.py
@@ -18,6 +18,7 @@
 CHUNK = 16
 WINDOW = 32
 HALO = 8
+INNER = 4
 ES_LANE = NB
 
 circ_alpha = 0.01
@@ -225,10 +226,8 @@
     )
 
 
-def relax(ops, lows, scale, inverse, iterate, source):
-    start(inverse, iterate[...], source, slice(0, WINDOW))
-    iterate[...] = source[...]
-    for sweep in range(1, SWEEPS):
+def relax(ops, lows, scale, inverse, iterate, source, done):
+    for sweep in range(done, SWEEPS):
         here = slice(sweep + 1, WINDOW - sweep - 1)
         coupled = [couple(ops, lows, scale[here], iterate[c, sweep : WINDOW - sweep]) for c in range(2)]
         fresh = damped(iterate[:, here], source[:, here], inverse[:, here], coupled)
@@ -248,7 +247,9 @@
                     iterate[c, w, 2 * yd : 2 * yd + 2, :] = got[seat(xc, yd), at : at + 2, :]
     scale[...] = jnp.broadcast_to(iterate[0, :, :, ES_LANE : ES_LANE + 1], scale.shape)
     invert(slots, diag, scale, inverse)
-    relax(ops, lows, scale, inverse, iterate, source)
+    start(inverse, iterate[...], source, slice(0, WINDOW))
+    iterate[...] = source[...]
+    relax(ops, lows, scale, inverse, iterate, source, 1)
     mine = slots[slot()]
     middle = iterate[:, HALO : HALO + CHUNK]
     solved[...] = middle
@@ -281,12 +282,12 @@
         far[c], near[c] = by_side(right[c] + part[CHUNK // 2 :], left[c] + part[: CHUNK // 2])
 
 
-def inner_kernel(ops, lows, scale, inverse, far, near, edges, iterate, source):
+def inner_kernel(ops, lows, scale, inverse, far, near, edges, core, iterate, source):
     middle = slice(HALO, HALO + CHUNK)
     for i, part in enumerate(by_side(near[...], far[...])):
         start(inverse, part, source, slice((i + 1) * HALO, (i + 2) * HALO))
     iterate[...] = source[:, middle]
-    for sweep in range(SWEEPS):
+    for sweep in range(INNER + 1):
         lo, hi = sweep, CHUNK - sweep
         if sweep:
             here = slice(HALO + lo, HALO + hi)
@@ -294,46 +295,46 @@
             fresh = damped(iterate[:, lo:hi], source[:, here], inverse[:, here], coupled)
             iterate[0, lo:hi] = fresh[0]
             iterate[1, lo:hi] = fresh[1]
-        edges[sweep, :, :2] = iterate[:, lo : lo + 2]
-        edges[sweep, :, 2:] = iterate[:, hi - 2 : hi]
-
-
-def outer_kernel(ops, lows, scale, inverse, far, near, beyond_far, beyond_near, edges, before, out, iterate, source):
+        if sweep < INNER:
+            edges[sweep, :, :2] = iterate[:, lo : lo + 2]
+            edges[sweep, :, 2:] = iterate[:, hi - 2 : hi]
+    core[...] = iterate[:, INNER : CHUNK - INNER]
+
+
+def outer_kernel(
+    ops, lows, scale, inverse, far, near, beyond_far, beyond_near, edges, core, before, out, sides, iterate, source
+):
     left, right = by_side(near[...], far[...])
     west, east = by_side(beyond_near[...], beyond_far[...])
     for i, part in enumerate((west, left, right, east)):
         start(inverse, part, source, slice(i * HALO, (i + 1) * HALO))
     out[:, :8, :] = before[...]
-    reach = SWEEPS - 1
-    iterate[:, :reach] = source[:, 1:HALO]
-    iterate[:, reach + 4 :] = source[:, HALO + CHUNK : WINDOW - 1]
-    for sweep in range(1, SWEEPS):
-        iterate[:, reach : reach + 4] = edges[sweep - 1]
+    reach = HALO - 1
+    sides[:, :reach] = source[:, 1:HALO]
+    sides[:, reach + 4 :] = source[:, HALO + CHUNK : WINDOW - 1]
+    for sweep in range(1, INNER + 1):
+        sides[:, reach : reach + 4] = edges[sweep - 1]
         one = slice(sweep + 1, HALO + sweep)
         two = slice(WINDOW - HALO - sweep, WINDOW - 1 - sweep)
-        sides = [
+        given = [
             jnp.concatenate((ref[one], ref[HALO : HALO + 2], ref[two]), axis=0)
             for ref in [scale] + [inverse.at[i] for i in range(3)] + [source.at[i] for i in range(2)]
         ]
-        coupled = [couple(ops, lows, sides[0], iterate[c]) for c in range(2)]
-        fresh = damped(iterate[:, 1:-1], sides[4:], sides[1:4], coupled)
+        coupled = [couple(ops, lows, given[0], sides[c]) for c in range(2)]
+        fresh = damped(sides[:, 1:-1], given[4:], given[1:4], coupled)
         for c in range(2):
-            iterate[c, :reach] = fresh[c][:reach]
-            iterate[c, reach + 4 :] = fresh[c][reach + 2 :]
-    last = edges.at[SWEEPS - 1]
+            sides[c, :reach] = fresh[c][:reach]
+            sides[c, reach + 4 :] = fresh[c][reach + 2 :]
+    iterate[:, INNER + 1 : HALO + INNER] = sides[:, :reach]
+    iterate[:, HALO + INNER : WINDOW - HALO - INNER] = core[...]
+    iterate[:, WINDOW - HALO - INNER : WINDOW - 1 - INNER] = sides[:, reach + 4 :]
+    relax(ops, lows, scale, inverse, iterate, source, INNER + 1)
     for xc in range(8):
-        for col in range(2):
-            x = 2 * xc + col
+        for yd in range(4):
             for c in range(2):
-                if x < reach:
-                    tile = iterate.at[c, x]
-                elif x < reach + 2:
-                    tile = last.at[c, x - reach]
-                else:
-                    tile = iterate.at[c, x + 2]
-                at = 8 + c * 4 + col * 2
-                for yd in range(4):
-                    out[seat(xc, yd), at : at + 2, :] = tile[2 * yd : 2 * yd + 2, :]
+                for col in range(2):
+                    at = 8 + c * 4 + col * 2
+                    out[seat(xc, yd), at : at + 2, :] = iterate[c, HALO + 2 * xc + col, 2 * yd : 2 * yd + 2, :]
 
 
 def backward_kernel(table, got, out):
@@ -434,9 +435,9 @@
     other = [(z, (z + 1 if z % 2 else z - 1) % planes) for z in range(planes)]
     beyond_far = lax.ppermute(far, "z", other)
     beyond_near = swapped(near, "z", 1)
-    edges = call(
+    edges, core = call(
         inner_kernel,
-        f32(SWEEPS, 2, 4, 8, LANES),
+        (f32(INNER, 2, 4, 8, LANES), f32(2, CHUNK - 2 * INNER, 8, LANES)),
         (ops, lows, scale, inverse, far, near),
         (pltpu.VMEM((2, CHUNK, 8, LANES), jnp.float32), both),
         name="inner",
@@ -445,8 +446,8 @@
     done = call(
         outer_kernel,
         f32(FREQS, 16, LANES),
-        (ops, lows, scale, inverse, far, near, beyond_far, beyond_near, edges, done),
-        (pltpu.VMEM((2, 2 * SWEEPS + 2, 8, LANES), jnp.float32), both),
+        (ops, lows, scale, inverse, far, near, beyond_far, beyond_near, edges, core, done),
+        (pltpu.VMEM((2, 2 * HALO + 2, 8, LANES), jnp.float32), both, both),
         name="outer",
     )
     got = exchange(done, PLANE).reshape(FREQS * 16, LANES)

time: 108 us -> 108 us (level)
  transfers between devices with their start and end apart: 9 -> 9, of which waited for: 7 -> 7; matrix products, arithmetic and copies ran while one was open for 0% -> 0% of each run, Pallas kernels for 2% -> 1%
where the time goes in v10:
time: 108 us
  blocking collectives  79.7 us (74%)
  waiting for transfers between devices  10.3 us (10%)
  Pallas kernels  9.32 us (9%)
  starting transfers between devices  8.03 us (7%)
    all_to_all x4, blocking collectives, exchange(): return lax.all_to_all(blocks, axes, 0, 0, tiled=True)  79.7 us
    pallas_call x9, Pallas kernels, call(): pl.pallas_call(kernel, out_shape=outs, in_specs=specs or [VMEM] * len(ins...  9.32 us
    ppermute x8, waiting for transfers between devices, swapped(): lax.ppermute(block, axis, [(i, i ^ bits) for i in range(lax.axis_size(axi...  8.16 us
    ppermute x8, starting transfers between devices, swapped(): lax.ppermute(block, axis, [(i, i ^ bits) for i in range(lax.axis_size(axi...  7.94 us
  transfers between devices with their start and end apart: 9, of which 7 were waited for; matrix products, arithmetic and copies ran while one was open for 0% of the time, Pallas kernels for 1%

profile of v10, /device:TPU:1, one launch (start us, length us, event | category | flops | bytes accessed | tf_op | source)
XLA Modules:
  0.0 107.6 jit_solution(5075869511359892628)
XLA Ops:
  0.0 1.6 %pack.1 = (f32[768,128]{1,0:T(8,128)S(1)}, bf16[256,768]{1,0:T(8,128)(2,1)S(1)}, bf16[128,512]{1,0:T(8,128)(2,1)S(1)}, f32[8,128]{1,0:T(8,128)S(1)}) custom-call(f32[250,2,128]{2,1,0:T(2,128)} %bitcast.17, f32[1,125,2,128]{3,2,1,0:T(2,128)} %bitcast.19, f32[1,2,128]{2,1,0:T(2,128)} %bitcast.21, f32[1,125,125]{2,1,0:T(8,128)} %bitcast.20, f32[125,4,125]{2,1,0:T(4,128)} %bitcast.18), custom_call_target="tpu_custom_call" | custom-call | tf_op jit(solution)/shard_map/pack/pallas_call | solution.py:365
  1.6 0.0 copy-start.2
  1.6 28.0 %all_to_all.20 = f32[64,3,4,128]{3,2,1,0:T(4,128)S(1)} all-to-all(f32[64,3,4,128]{3,2,1,0:T(4,128)S(1)} %bitcast.16), channel_id=1, replica_groups=mesh['z'=8,'x'=4,'core'=2,'y'=4] {'z','x','core'}, dimensions={0} | all-to-all | bytes 786432 | tf_op jit(solution)/shard_map/all_to_all | solution.py:382
  29.6 0.0 copy-done.2
  29.6 0.3 forward.1
  30.0 0.0 copy-start
  30.0 16.8 %all_to_all.21.got = f32[32,24,128]{2,1,0:T(8,128)S(1)} all-to-all(f32[32,24,128]{2,1,0:T(8,128)S(1)} %bitcast.12), channel_id=1, replica_groups=mesh['z'=8,'x'=4,'core'=2,'y'=4] {'core','y','x'}, dimensions={0} | all-to-all | bytes 786432 | tf_op jit(solution)/shard_map/all_to_all | solution.py:382
  46.7 0.0 copy-done
  46.7 2.7 %first.1 = (f32[2,16,8,128]{3,2,1,0:T(8,128)S(1)}, f32[16,8,128]{2,1,0:T(8,128)S(1)}, f32[32,8,128]{2,1,0:T(8,128)S(1)}, f32[3,32,8,128]{3,2,1,0:T(8,128)S(1)}) custom-call(f32[32,8,128]{2,1,0:T(8,128)S(1)} %copy-done, bf16[256,768]{1,0:T(8,128)(2,1)S(1)} %get-tuple-element.20.ops, bf16[128,512]{1,0:T(8,128)(2,1)S(1)} %get-tuple-element.21.lows, ...), custom_call_target="tpu_custom_call" | custom-call | tf_op jit(solution)/shard_map/first/pallas_call | solution.py:365
  49.4 1.3 %collective-permute-start = (f32[16,8,128]{2,1,0:T(8,128)S(1)}, f32[16,8,128]{2,1,0:T(8,128)S(1)}, u32[]{:S(2)}, u32[]{:S(2)}) collective-permute-start(f32[16,8,128]{2,1,0:T(8,128)S(1)} %get-tuple-element.27), channel_id=1, source_target_pairs={{0,4},{4,0},{1,5},{5,1},{2,6},{6,2},{3,7},{7,3},{8,12},{12,8},{9,1... | collective-permute-start | bytes 196616 | tf_op jit(solution)/shard_map/ppermute | solution.py:386
  50.7 0.9 collective-permute-done
  51.7 1.4 %collective-permute-start.3 = (f32[16,8,128]{2,1,0:T(8,128)S(1)}, f32[16,8,128]{2,1,0:T(8,128)S(1)}, u32[]{:S(2)}, u32[]{:S(2)}) collective-permute-start(f32[16,8,128]{2,1,0:T(8,128)S(1)} %add.12.after), channel_id=1, source_target_pairs={{0,2},{1,3},{2,0},{3,1},{4,6},{5,7},{6,4},{7,5},{8,10},{9,11},{10,... | collective-permute-start | bytes 196616 | tf_op jit(solution)/shard_map/ppermute | solution.py:386
  53.0 1.4 %collective-permute-start.2 = (f32[16,8,128]{2,1,0:T(8,128)S(1)}, f32[16,8,128]{2,1,0:T(8,128)S(1)}, u32[]{:S(2)}, u32[]{:S(2)}) collective-permute-start(f32[16,8,128]{2,1,0:T(8,128)S(1)} %add.12.after), channel_id=1, source_target_pairs={{0,3},{1,2},{2,1},{3,0},{4,7},{5,6},{6,5},{7,4},{8,11},{9,10},{10,... | collective-permute-start | bytes 196616 | tf_op jit(solution)/shard_map/ppermute | solution.py:386
  54.5 0.0 collective-permute-start.1
  54.5 1.9 %collective-permute-done.3 = f32[16,8,128]{2,1,0:T(8,128)S(1)} collective-permute-done((f32[16,8,128]{2,1,0:T(8,128)S(1)}, f32[16,8,128]{2,1,0:T(8,128)S(1)}, u32[]{:S(2)}, u32[]{:S(2)}) %collective-permute-start.3) | collective-permute-done | bytes 65568 | tf_op jit(solution)/shard_map/ppermute | solution.py:386
  56.4 1.9 %collective-permute-done.2 = f32[16,8,128]{2,1,0:T(8,128)S(1)} collective-permute-done((f32[16,8,128]{2,1,0:T(8,128)S(1)}, f32[16,8,128]{2,1,0:T(8,128)S(1)}, u32[]{:S(2)}, u32[]{:S(2)}) %collective-permute-start.2) | collective-permute-done | bytes 65568 | tf_op jit(solution)/shard_map/ppermute | solution.py:386
  58.3 0.0 collective-permute-done.1
  58.3 1.3 %collective-permute-start.6 = (f32[16,8,128]{2,1,0:T(8,128)S(1)}, f32[16,8,128]{2,1,0:T(8,128)S(1)}, u32[]{:S(2)}, u32[]{:S(2)}) collective-permute-start(f32[16,8,128]{2,1,0:T(8,128)S(1)} %add_add_fusion.state0), channel_id=1, source_target_pairs={{0,16},{8,24},{16,0},{24,8},{1,17},{9,25},{17,1},{25,9},{2,18},{10... | collective-permute-start | bytes 196616 | tf_op jit(solution)/shard_map/ppermute | solution.py:386
  59.7 0.9 collective-permute-start.5
  60.5 0.5 collective-permute-start.4
  61.1 0.1 between.1
  61.1 1.9 %collective-permute-done.6.state3 = f32[16,8,128]{2,1,0:T(8,128)S(1)} collective-permute-done((f32[16,8,128]{2,1,0:T(8,128)S(1)}, f32[16,8,128]{2,1,0:T(8,128)S(1)}, u32[]{:S(2)}, u32[]{:S(2)}) %collective-permute-start.6) | collective-permute-done | bytes 65568 | tf_op jit(solution)/shard_map/ppermute | solution.py:386
  63.0 1.0 collective-permute-done.5.state2
  64.0 0.6 collective-permute-done.4.state1
  64.6 0.1 collective-permute-start.7
  64.7 1.1 %collective-permute-start.8 = (f32[2,8,8,128]{3,2,1,0:T(8,128)S(1)}, f32[2,8,8,128]{3,2,1,0:T(8,128)S(1)}, u32[]{:S(2)}, u32[]{:S(2)}) collective-permute-start(f32[2,8,8,128]{3,2,1,0:T(8,128)S(1)} %get-tuple-element.31.near), channel_id=1, source_target_pairs={{0,32},{32,0},{64,96},{96,64},{128,160},{160,128},{192,224},{224,1... | collective-permute-start | bytes 196616 | tf_op jit(solution)/shard_map/ppermute | solution.py:386
  65.8 1.1 %inner.1 = (f32[4,2,4,8,128]{4,3,2,1,0:T(8,128)S(1)}, f32[2,8,8,128]{3,2,1,0:T(8,128)S(1)}) custom-call(bf16[256,768]{1,0:T(8,128)(2,1)S(1)} %get-tuple-element.20.ops, bf16[128,512]{1,0:T(8,128)(2,1)S(1)} %get-tuple-element.21.lows, f32[32,8,128]{2,1,0:T(8,128)S(1)} %get-tuple-element.24.scale, f32[3,32,8,128]{3,2,1,0:T(8,128)S(1)} %get-tuple-element.25.inverse, ...), custom_call_target="tpu_custom_call" | custom-call | flops 2000000000 | bytes 1000000 | tf_op jit(solution)/shard_map/inner/pallas_call | solution.py:365
  66.9 2.1 %collective-permute-done.7.beyond_far = f32[2,8,8,128]{3,2,1,0:T(8,128)S(1)} collective-permute-done((f32[2,8,8,128]{3,2,1,0:T(8,128)S(1)}, f32[2,8,8,128]{3,2,1,0:T(8,128)S(1)}, u32[]{:S(2)}, u32[]{:S(2)}) %collective-permute-start.7) | collective-permute-done | bytes 65568 | tf_op jit(solution)/shard_map/ppermute | solution.py:436
  69.0 0.0 collective-permute-done.8.beyond_near
  69.0 2.2 %outer.1 = f32[32,16,128]{2,1,0:T(8,128)S(1)} custom-call(bf16[256,768]{1,0:T(8,128)(2,1)S(1)} %get-tuple-element.20.ops, bf16[128,512]{1,0:T(8,128)(2,1)S(1)} %get-tuple-element.21.lows, f32[32,8,128]{2,1,0:T(8,128)S(1)} %get-tuple-element.24.scale, f32[3,32,8,128]{3,2,1,0:T(8,128)S(1)} %get-tuple-element.25.inverse, ...), custom_call_target="tpu_custom_call" | custom-call | tf_op jit(solution)/shard_map/outer/pallas_call | solution.py:365
  71.3 0.0 copy-start.1
  71.3 15.7 %all_to_all.22 = f32[32,16,128]{2,1,0:T(8,128)S(1)} all-to-all(f32[32,16,128]{2,1,0:T(8,128)S(1)} %outer.1), channel_id=1, replica_groups=mesh['z'=8,'x'=4,'core'=2,'y'=4] {'core','y','x'}, dimensions={0} | all-to-all | bytes 524288 | tf_op jit(solution)/shard_map/all_to_all | solution.py:382
  86.9 0.0 copy-done.1
  86.9 0.3 backward.1
  87.3 19.3 %all_to_all.23 = f32[64,8,128]{2,1,0:T(8,128)S(1)} all-to-all(f32[64,8,128]{2,1,0:T(8,128)S(1)} %bitcast.14), channel_id=1, replica_groups=mesh['z'=8,'x'=4,'core'=2,'y'=4] {'z','x','core'}, dimensions={0} | all-to-all | bytes 524288 | tf_op jit(solution)/shard_map/all_to_all | solution.py:382
  106.5 0.9 unpack.1
  (3 shorter events, 0.1 us)
Async XLA Ops:
  1.6 28.0 %copy-start.2 = (bf16[64,384]{1,0:T(8,128)(2,1)S(1)}, bf16[64,384]{1,0:T(8,128)(2,1)}, u32[]{:S(2)}) copy-start(bf16[64,384]{1,0:T(8,128)(2,1)} %constant.6.clone.table) | copy-start | bytes 147460
  30.0 16.8 %copy-start = (f32[32,8,128]{2,1,0:T(8,128)S(1)}, f32[32,8,128]{2,1,0:T(8,128)}, u32[]{:S(2)}) copy-start(f32[32,8,128]{2,1,0:T(8,128)} %constant.7.clone.slots) | copy-start | bytes 393220
  49.4 2.2 %collective-permute-start = (f32[16,8,128]{2,1,0:T(8,128)S(1)}, f32[16,8,128]{2,1,0:T(8,128)S(1)}, u32[]{:S(2)}, u32[]{:S(2)}) collective-permute-start(f32[16,8,128]{2,1,0:T(8,128)S(1)} %get-tuple-element.27), channel_id=1, source_target_pairs={{0,4},{4,0},{1,5},{5,1},{2,6},{6,2},{3,7},{7,3},{8,12},{12,8},{9,1... | collective-permute-start | bytes 196616 | tf_op jit(solution)/shard_map/ppermute | solution.py:386
  51.7 4.7 %collective-permute-start.3 = (f32[16,8,128]{2,1,0:T(8,128)S(1)}, f32[16,8,128]{2,1,0:T(8,128)S(1)}, u32[]{:S(2)}, u32[]{:S(2)}) collective-permute-start(f32[16,8,128]{2,1,0:T(8,128)S(1)} %add.12.after), channel_id=1, source_target_pairs={{0,2},{1,3},{2,0},{3,1},{4,6},{5,7},{6,4},{7,5},{8,10},{9,11},{10,... | collective-permute-start | bytes 196616 | tf_op jit(solution)/shard_map/ppermute | solution.py:386
  53.0 5.3 %collective-permute-start.2 = (f32[16,8,128]{2,1,0:T(8,128)S(1)}, f32[16,8,128]{2,1,0:T(8,128)S(1)}, u32[]{:S(2)}, u32[]{:S(2)}) collective-permute-start(f32[16,8,128]{2,1,0:T(8,128)S(1)} %add.12.after), channel_id=1, source_target_pairs={{0,3},{1,2},{2,1},{3,0},{4,7},{5,6},{6,5},{7,4},{8,11},{9,10},{10,... | collective-permute-start | bytes 196616 | tf_op jit(solution)/shard_map/ppermute | solution.py:386
  54.5 3.8 %collective-permute-start.1 = (f32[16,8,128]{2,1,0:T(8,128)S(1)}, f32[16,8,128]{2,1,0:T(8,128)S(1)}, u32[]{:S(2)}, u32[]{:S(2)}) collective-permute-start(f32[16,8,128]{2,1,0:T(8,128)S(1)} %add.12.after), channel_id=1, source_target_pairs={{0,1},{1,0},{2,3},{3,2},{4,5},{5,4},{6,7},{7,6},{8,9},{9,8},{10,11... | collective-permute-start | bytes 196616 | tf_op jit(solution)/shard_map/ppermute | solution.py:386
  58.3 4.7 %collective-permute-start.6 = (f32[16,8,128]{2,1,0:T(8,128)S(1)}, f32[16,8,128]{2,1,0:T(8,128)S(1)}, u32[]{:S(2)}, u32[]{:S(2)}) collective-permute-start(f32[16,8,128]{2,1,0:T(8,128)S(1)} %add_add_fusion.state0), channel_id=1, source_target_pairs={{0,16},{8,24},{16,0},{24,8},{1,17},{9,25},{17,1},{25,9},{2,18},{10... | collective-permute-start | bytes 196616 | tf_op jit(solution)/shard_map/ppermute | solution.py:386
  59.7 4.3 %collective-permute-start.5 = (f32[16,8,128]{2,1,0:T(8,128)S(1)}, f32[16,8,128]{2,1,0:T(8,128)S(1)}, u32[]{:S(2)}, u32[]{:S(2)}) collective-permute-start(f32[16,8,128]{2,1,0:T(8,128)S(1)} %add_add_fusion.state0), channel_id=1, source_target_pairs={{0,24},{8,16},{16,8},{24,0},{1,25},{9,17},{17,9},{25,1},{2,26},{10... | collective-permute-start | bytes 196616 | tf_op jit(solution)/shard_map/ppermute | solution.py:386
  60.5 4.1 %collective-permute-start.4 = (f32[16,8,128]{2,1,0:T(8,128)S(1)}, f32[16,8,128]{2,1,0:T(8,128)S(1)}, u32[]{:S(2)}, u32[]{:S(2)}) collective-permute-start(f32[16,8,128]{2,1,0:T(8,128)S(1)} %add_add_fusion.state0), channel_id=1, source_target_pairs={{0,8},{8,0},{16,24},{24,16},{1,9},{9,1},{17,25},{25,17},{2,10},{10... | collective-permute-start | bytes 196616 | tf_op jit(solution)/shard_map/ppermute | solution.py:386
  64.6 4.4 %collective-permute-start.7 = (f32[2,8,8,128]{3,2,1,0:T(8,128)S(1)}, f32[2,8,8,128]{3,2,1,0:T(8,128)S(1)}, u32[]{:S(2)}, u32[]{:S(2)}) collective-permute-start(f32[2,8,8,128]{3,2,1,0:T(8,128)S(1)} %get-tuple-element.30.far), channel_id=1, source_target_pairs={{0,224},{32,64},{64,32},{96,128},{128,96},{160,192},{192,160},{224... | collective-permute-start | bytes 196616 | tf_op jit(solution)/shard_map/ppermute | solution.py:436
  64.7 4.3 %collective-permute-start.8 = (f32[2,8,8,128]{3,2,1,0:T(8,128)S(1)}, f32[2,8,8,128]{3,2,1,0:T(8,128)S(1)}, u32[]{:S(2)}, u32[]{:S(2)}) collective-permute-start(f32[2,8,8,128]{3,2,1,0:T(8,128)S(1)} %get-tuple-element.31.near), channel_id=1, source_target_pairs={{0,32},{32,0},{64,96},{96,64},{128,160},{160,128},{192,224},{224,1... | collective-permute-start | bytes 196616 | tf_op jit(solution)/shard_map/ppermute | solution.py:386
  71.3 15.7 %copy-start.1 = (bf16[64,384]{1,0:T(8,128)(2,1)S(1)}, bf16[64,384]{1,0:T(8,128)(2,1)}, u32[]{:S(2)}) copy-start(bf16[64,384]{1,0:T(8,128)(2,1)} %constant.8.clone.table) | copy-start | bytes 147460

commit v11 on v10

--- a/solution.py
+++ b/solution.py
@@ -270,7 +270,7 @@
 
 
 def by_side(one, two):
-    even = lax.rem(lax.axis_index("z"), 2) == 0
+    even = lax.rem(lax.axis_index("z") + lax.axis_index("core"), 2) == 0
     return jnp.where(even, two, one), jnp.where(even, one, two)
 
 
@@ -382,8 +382,20 @@
     return lax.all_to_all(blocks, axes, 0, 0, tiled=True)
 
 
-def swapped(block, axis, bits):
-    return lax.ppermute(block, axis, [(i, i ^ bits) for i in range(lax.axis_size(axis))])
+def routed(block, axis, partners):
+    count = lax.axis_size(axis)
+    axes = ("core", axis) if axis == "y" else (axis, "core")
+
+    def at(core, place):
+        return core * count + place if axis == "y" else place * 2 + core
+
+    pairs = [(at(core, i), at(core, partners[core](i))) for core in range(2) for i in range(count)]
+    return lax.ppermute(block, axes, pairs)
+
+
+def crossed(block, axis):
+    near, other, across = (lambda i: i ^ 1), (lambda i: i ^ 3), (lambda i: i ^ 2)
+    return [routed(block, axis, pair) for pair in ((near, other), (other, near), (across, across))]
 
 
 def per_device(forcing, init_state, elem_scale, vol_op, face_ops):
@@ -423,18 +435,24 @@
         name="first",
     )
     half = f32(2, CHUNK // 2, 8, LANES)
-    state = state + swapped(state, "core", 1)
+    state = state + lax.ppermute(state, "core", [(0, 1), (1, 0)])
     done, left, right = call(
         between_kernel, (f32(FREQS, 8, LANES), half, half), (got, solved, state), (), [VMEM, VMEM, ANY], name="between"
     )
-    near, far, across = (swapped(state, "y", bits) for bits in (1, 3, 2))
-    state = ((state + near) + far) + across
-    states = [state] + [swapped(state, "x", bits) for bits in (1, 3, 2)]
+    one, two, three = crossed(state, "y")
+    state = ((state + one) + two) + three
+    states = [state] + crossed(state, "x")
     far, near = call(carry_kernel, (half, half), (SLOTS, left, right, *states), name="carry")
     planes = lax.axis_size("z")
-    other = [(z, (z + 1 if z % 2 else z - 1) % planes) for z in range(planes)]
-    beyond_far = lax.ppermute(far, "z", other)
-    beyond_near = swapped(near, "z", 1)
+
+    def paired(z):
+        return z ^ 1
+
+    def other(z):
+        return (z + 1 if z % 2 else z - 1) % planes
+
+    beyond_far = routed(far, "z", (other, paired))
+    beyond_near = routed(near, "z", (paired, other))
     edges, core = call(
         inner_kernel,
         (f32(INNER, 2, 4, 8, LANES), f32(2, CHUNK - 2 * INNER, 8, LANES)),

time: 108 us -> 108 us (level)
  blocking collectives: 79.7 us -> 76.6 us
  waiting for transfers between devices: 10.3 us -> 12.7 us
    all_to_all x4, blocking collectives: 79.7 us -> 76.6 us  [exchange(): return lax.all_to_all(blocks, axes, 0, 0, tiled=True)]
    ppermute x9, waiting for transfers between devices: 10.3 us -> 12.7 us  [the longest x8 11.8 us: routed(): return lax.ppermute(block, axes, pairs)]
where the time goes in v11:
time: 108 us
  blocking collectives  76.6 us (71%)
  waiting for transfers between devices  12.7 us (12%)
  Pallas kernels  9.32 us (9%)
  starting transfers between devices  8.65 us (8%)
    all_to_all x4, blocking collectives, exchange(): return lax.all_to_all(blocks, axes, 0, 0, tiled=True)  76.6 us
    ppermute x8, waiting for transfers between devices, routed(): return lax.ppermute(block, axes, pairs)  11.8 us
    pallas_call x9, Pallas kernels, call(): pl.pallas_call(kernel, out_shape=outs, in_specs=specs or [VMEM] * len(ins...  9.32 us
    ppermute x8, starting transfers between devices, routed(): return lax.ppermute(block, axes, pairs)  7.35 us
  transfers between devices with their start and end apart: 9, of which 7 were waited for; matrix products, arithmetic and copies ran while one was open for 0% of the time, Pallas kernels for 1%

profile of v11, /device:TPU:1, one launch (start us, length us, event | category | flops | bytes accessed | tf_op | source)
XLA Modules:
  0.0 107.6 jit_solution(13427924288684178080)
XLA Ops:
  0.0 1.6 %pack.1 = (f32[768,128]{1,0:T(8,128)S(1)}, bf16[256,768]{1,0:T(8,128)(2,1)S(1)}, bf16[128,512]{1,0:T(8,128)(2,1)S(1)}, f32[8,128]{1,0:T(8,128)S(1)}) custom-call(f32[250,2,128]{2,1,0:T(2,128)} %bitcast.17, f32[1,125,2,128]{3,2,1,0:T(2,128)} %bitcast.19, f32[1,2,128]{2,1,0:T(2,128)} %bitcast.21, f32[1,125,125]{2,1,0:T(8,128)} %bitcast.20, f32[125,4,125]{2,1,0:T(4,128)} %bitcast.18), custom_call_target="tpu_custom_call" | custom-call | tf_op jit(solution)/shard_map/pack/pallas_call | solution.py:365
  1.6 0.0 copy-start.2
  1.6 28.0 %all_to_all.20 = f32[64,3,4,128]{3,2,1,0:T(4,128)S(1)} all-to-all(f32[64,3,4,128]{3,2,1,0:T(4,128)S(1)} %bitcast.16), channel_id=1, replica_groups=mesh['z'=8,'x'=4,'core'=2,'y'=4] {'z','x','core'}, dimensions={0} | all-to-all | bytes 786432 | tf_op jit(solution)/shard_map/all_to_all | solution.py:382
  29.6 0.0 copy-done.2
  29.6 0.3 forward.1
  30.0 0.0 copy-start
  30.0 16.8 %all_to_all.21.got = f32[32,24,128]{2,1,0:T(8,128)S(1)} all-to-all(f32[32,24,128]{2,1,0:T(8,128)S(1)} %bitcast.12), channel_id=1, replica_groups=mesh['z'=8,'x'=4,'core'=2,'y'=4] {'core','y','x'}, dimensions={0} | all-to-all | bytes 786432 | tf_op jit(solution)/shard_map/all_to_all | solution.py:382
  46.7 0.0 copy-done
  46.7 2.7 %first.1 = (f32[2,16,8,128]{3,2,1,0:T(8,128)S(1)}, f32[16,8,128]{2,1,0:T(8,128)S(1)}, f32[32,8,128]{2,1,0:T(8,128)S(1)}, f32[3,32,8,128]{3,2,1,0:T(8,128)S(1)}) custom-call(f32[32,8,128]{2,1,0:T(8,128)S(1)} %copy-done, bf16[256,768]{1,0:T(8,128)(2,1)S(1)} %get-tuple-element.20.ops, bf16[128,512]{1,0:T(8,128)(2,1)S(1)} %get-tuple-element.21.lows, ...), custom_call_target="tpu_custom_call" | custom-call | tf_op jit(solution)/shard_map/first/pallas_call | solution.py:365
  49.4 1.3 %collective-permute-start = (f32[16,8,128]{2,1,0:T(8,128)S(1)}, f32[16,8,128]{2,1,0:T(8,128)S(1)}, u32[]{:S(2)}, u32[]{:S(2)}) collective-permute-start(f32[16,8,128]{2,1,0:T(8,128)S(1)} %get-tuple-element.27), channel_id=1, source_target_pairs={{0,4},{4,0},{1,5},{5,1},{2,6},{6,2},{3,7},{7,3},{8,12},{12,8},{9,1... | collective-permute-start | bytes 196616 | tf_op jit(solution)/shard_map/ppermute | solution.py:438
  50.7 0.9 collective-permute-done
  51.7 1.4 %collective-permute-start.3 = (f32[16,8,128]{2,1,0:T(8,128)S(1)}, f32[16,8,128]{2,1,0:T(8,128)S(1)}, u32[]{:S(2)}, u32[]{:S(2)}) collective-permute-start(f32[16,8,128]{2,1,0:T(8,128)S(1)} %add.12.after), channel_id=1, source_target_pairs={{0,2},{1,3},{2,0},{3,1},{4,6},{5,7},{6,4},{7,5},{8,10},{9,11},{10,... | collective-permute-start | bytes 196616 | tf_op jit(solution)/shard_map/ppermute | solution.py:393
  53.0 0.0 collective-permute-start.2
  53.0 2.0 %collective-permute-start.1 = (f32[16,8,128]{2,1,0:T(8,128)S(1)}, f32[16,8,128]{2,1,0:T(8,128)S(1)}, u32[]{:S(2)}, u32[]{:S(2)}) collective-permute-start(f32[16,8,128]{2,1,0:T(8,128)S(1)} %add.12.after), channel_id=1, source_target_pairs={{0,1},{1,0},{2,3},{3,2},{4,7},{5,6},{6,5},{7,4},{8,9},{9,8},{10,11... | collective-permute-start | bytes 196616 | tf_op jit(solution)/shard_map/ppermute | solution.py:393
  55.0 1.3 %collective-permute-done.3 = f32[16,8,128]{2,1,0:T(8,128)S(1)} collective-permute-done((f32[16,8,128]{2,1,0:T(8,128)S(1)}, f32[16,8,128]{2,1,0:T(8,128)S(1)}, u32[]{:S(2)}, u32[]{:S(2)}) %collective-permute-start.3) | collective-permute-done | bytes 65568 | tf_op jit(solution)/shard_map/ppermute | solution.py:393
  56.4 0.0 collective-permute-done.2
  56.4 2.0 %collective-permute-done.1 = f32[16,8,128]{2,1,0:T(8,128)S(1)} collective-permute-done((f32[16,8,128]{2,1,0:T(8,128)S(1)}, f32[16,8,128]{2,1,0:T(8,128)S(1)}, u32[]{:S(2)}, u32[]{:S(2)}) %collective-permute-start.1) | collective-permute-done | bytes 65568 | tf_op jit(solution)/shard_map/ppermute | solution.py:393
  58.4 1.4 %collective-permute-start.6 = (f32[16,8,128]{2,1,0:T(8,128)S(1)}, f32[16,8,128]{2,1,0:T(8,128)S(1)}, u32[]{:S(2)}, u32[]{:S(2)}) collective-permute-start(f32[16,8,128]{2,1,0:T(8,128)S(1)} %add_add_fusion.state0), channel_id=1, source_target_pairs={{0,16},{8,24},{16,0},{24,8},{4,20},{12,28},{20,4},{28,12},{1,17},{... | collective-permute-start | bytes 196616 | tf_op jit(solution)/shard_map/ppermute | solution.py:393
  59.8 0.8 collective-permute-start.5
  60.6 1.1 %collective-permute-start.4 = (f32[16,8,128]{2,1,0:T(8,128)S(1)}, f32[16,8,128]{2,1,0:T(8,128)S(1)}, u32[]{:S(2)}, u32[]{:S(2)}) collective-permute-start(f32[16,8,128]{2,1,0:T(8,128)S(1)} %add_add_fusion.state0), channel_id=1, source_target_pairs={{0,8},{8,0},{16,24},{24,16},{4,28},{12,20},{20,12},{28,4},{1,9},{9... | collective-permute-start | bytes 196616 | tf_op jit(solution)/shard_map/ppermute | solution.py:393
  61.7 0.1 between.1
  61.8 1.3 %collective-permute-done.6.state3 = f32[16,8,128]{2,1,0:T(8,128)S(1)} collective-permute-done((f32[16,8,128]{2,1,0:T(8,128)S(1)}, f32[16,8,128]{2,1,0:T(8,128)S(1)}, u32[]{:S(2)}, u32[]{:S(2)}) %collective-permute-start.6) | collective-permute-done | bytes 65568 | tf_op jit(solution)/shard_map/ppermute | solution.py:393
  63.1 0.0 collective-permute-done.5.state2
  63.1 3.4 %collective-permute-done.4.state1 = f32[16,8,128]{2,1,0:T(8,128)S(1)} collective-permute-done((f32[16,8,128]{2,1,0:T(8,128)S(1)}, f32[16,8,128]{2,1,0:T(8,128)S(1)}, u32[]{:S(2)}, u32[]{:S(2)}) %collective-permute-start.4) | collective-permute-done | bytes 65568 | tf_op jit(solution)/shard_map/ppermute | solution.py:393
  66.5 0.6 collective-permute-start.7
  67.1 0.0 collective-permute-start.8
  67.1 1.1 %inner.1 = (f32[4,2,4,8,128]{4,3,2,1,0:T(8,128)S(1)}, f32[2,8,8,128]{3,2,1,0:T(8,128)S(1)}) custom-call(bf16[256,768]{1,0:T(8,128)(2,1)S(1)} %get-tuple-element.20.ops, bf16[128,512]{1,0:T(8,128)(2,1)S(1)} %get-tuple-element.21.lows, f32[32,8,128]{2,1,0:T(8,128)S(1)} %get-tuple-element.24.scale, f32[3,32,8,128]{3,2,1,0:T(8,128)S(1)} %get-tuple-element.25.inverse, ...), custom_call_target="tpu_custom_call" | custom-call | flops 2000000000 | bytes 1000000 | tf_op jit(solution)/shard_map/inner/pallas_call | solution.py:365
  68.3 1.4 %collective-permute-done.7.beyond_far = f32[2,8,8,128]{3,2,1,0:T(8,128)S(1)} collective-permute-done((f32[2,8,8,128]{3,2,1,0:T(8,128)S(1)}, f32[2,8,8,128]{3,2,1,0:T(8,128)S(1)}, u32[]{:S(2)}, u32[]{:S(2)}) %collective-permute-start.7) | collective-permute-done | bytes 65568 | tf_op jit(solution)/shard_map/ppermute | solution.py:393
  69.7 2.4 %collective-permute-done.8.beyond_near = f32[2,8,8,128]{3,2,1,0:T(8,128)S(1)} collective-permute-done((f32[2,8,8,128]{3,2,1,0:T(8,128)S(1)}, f32[2,8,8,128]{3,2,1,0:T(8,128)S(1)}, u32[]{:S(2)}, u32[]{:S(2)}) %collective-permute-start.8) | collective-permute-done | bytes 65568 | tf_op jit(solution)/shard_map/ppermute | solution.py:393
  72.1 2.2 %outer.1 = f32[32,16,128]{2,1,0:T(8,128)S(1)} custom-call(bf16[256,768]{1,0:T(8,128)(2,1)S(1)} %get-tuple-element.20.ops, bf16[128,512]{1,0:T(8,128)(2,1)S(1)} %get-tuple-element.21.lows, f32[32,8,128]{2,1,0:T(8,128)S(1)} %get-tuple-element.24.scale, f32[3,32,8,128]{3,2,1,0:T(8,128)S(1)} %get-tuple-element.25.inverse, ...), custom_call_target="tpu_custom_call" | custom-call | tf_op jit(solution)/shard_map/outer/pallas_call | solution.py:365
  74.4 0.0 copy-start.1
  74.4 12.6 %all_to_all.22 = f32[32,16,128]{2,1,0:T(8,128)S(1)} all-to-all(f32[32,16,128]{2,1,0:T(8,128)S(1)} %outer.1), channel_id=1, replica_groups=mesh['z'=8,'x'=4,'core'=2,'y'=4] {'core','y','x'}, dimensions={0} | all-to-all | bytes 524288 | tf_op jit(solution)/shard_map/all_to_all | solution.py:382
  86.9 0.0 copy-done.1
  86.9 0.3 backward.1
  87.2 19.3 %all_to_all.23 = f32[64,8,128]{2,1,0:T(8,128)S(1)} all-to-all(f32[64,8,128]{2,1,0:T(8,128)S(1)} %bitcast.14), channel_id=1, replica_groups=mesh['z'=8,'x'=4,'core'=2,'y'=4] {'z','x','core'}, dimensions={0} | all-to-all | bytes 524288 | tf_op jit(solution)/shard_map/all_to_all | solution.py:382
  106.5 0.9 unpack.1
  (3 shorter events, 0.1 us)
Async XLA Ops:
  1.6 28.0 %copy-start.2 = (bf16[64,384]{1,0:T(8,128)(2,1)S(1)}, bf16[64,384]{1,0:T(8,128)(2,1)}, u32[]{:S(2)}) copy-start(bf16[64,384]{1,0:T(8,128)(2,1)} %constant.6.clone.table) | copy-start | bytes 147460
  30.0 16.8 %copy-start = (f32[32,8,128]{2,1,0:T(8,128)S(1)}, f32[32,8,128]{2,1,0:T(8,128)}, u32[]{:S(2)}) copy-start(f32[32,8,128]{2,1,0:T(8,128)} %constant.7.clone.slots) | copy-start | bytes 393220
  49.4 2.2 %collective-permute-start = (f32[16,8,128]{2,1,0:T(8,128)S(1)}, f32[16,8,128]{2,1,0:T(8,128)S(1)}, u32[]{:S(2)}, u32[]{:S(2)}) collective-permute-start(f32[16,8,128]{2,1,0:T(8,128)S(1)} %get-tuple-element.27), channel_id=1, source_target_pairs={{0,4},{4,0},{1,5},{5,1},{2,6},{6,2},{3,7},{7,3},{8,12},{12,8},{9,1... | collective-permute-start | bytes 196616 | tf_op jit(solution)/shard_map/ppermute | solution.py:438
  51.7 4.7 %collective-permute-start.3 = (f32[16,8,128]{2,1,0:T(8,128)S(1)}, f32[16,8,128]{2,1,0:T(8,128)S(1)}, u32[]{:S(2)}, u32[]{:S(2)}) collective-permute-start(f32[16,8,128]{2,1,0:T(8,128)S(1)} %add.12.after), channel_id=1, source_target_pairs={{0,2},{1,3},{2,0},{3,1},{4,6},{5,7},{6,4},{7,5},{8,10},{9,11},{10,... | collective-permute-start | bytes 196616 | tf_op jit(solution)/shard_map/ppermute | solution.py:393
  53.0 3.3 %collective-permute-start.2 = (f32[16,8,128]{2,1,0:T(8,128)S(1)}, f32[16,8,128]{2,1,0:T(8,128)S(1)}, u32[]{:S(2)}, u32[]{:S(2)}) collective-permute-start(f32[16,8,128]{2,1,0:T(8,128)S(1)} %add.12.after), channel_id=1, source_target_pairs={{0,3},{1,2},{2,1},{3,0},{4,5},{5,4},{6,7},{7,6},{8,11},{9,10},{10,... | collective-permute-start | bytes 196616 | tf_op jit(solution)/shard_map/ppermute | solution.py:393
  53.0 5.3 %collective-permute-start.1 = (f32[16,8,128]{2,1,0:T(8,128)S(1)}, f32[16,8,128]{2,1,0:T(8,128)S(1)}, u32[]{:S(2)}, u32[]{:S(2)}) collective-permute-start(f32[16,8,128]{2,1,0:T(8,128)S(1)} %add.12.after), channel_id=1, source_target_pairs={{0,1},{1,0},{2,3},{3,2},{4,7},{5,6},{6,5},{7,4},{8,9},{9,8},{10,11... | collective-permute-start | bytes 196616 | tf_op jit(solution)/shard_map/ppermute | solution.py:393
  58.4 4.7 %collective-permute-start.6 = (f32[16,8,128]{2,1,0:T(8,128)S(1)}, f32[16,8,128]{2,1,0:T(8,128)S(1)}, u32[]{:S(2)}, u32[]{:S(2)}) collective-permute-start(f32[16,8,128]{2,1,0:T(8,128)S(1)} %add_add_fusion.state0), channel_id=1, source_target_pairs={{0,16},{8,24},{16,0},{24,8},{4,20},{12,28},{20,4},{28,12},{1,17},{... | collective-permute-start | bytes 196616 | tf_op jit(solution)/shard_map/ppermute | solution.py:393
  59.8 3.3 %collective-permute-start.5 = (f32[16,8,128]{2,1,0:T(8,128)S(1)}, f32[16,8,128]{2,1,0:T(8,128)S(1)}, u32[]{:S(2)}, u32[]{:S(2)}) collective-permute-start(f32[16,8,128]{2,1,0:T(8,128)S(1)} %add_add_fusion.state0), channel_id=1, source_target_pairs={{0,24},{8,16},{16,8},{24,0},{4,12},{12,4},{20,28},{28,20},{1,25},{... | collective-permute-start | bytes 196616 | tf_op jit(solution)/shard_map/ppermute | solution.py:393
  60.6 5.9 %collective-permute-start.4 = (f32[16,8,128]{2,1,0:T(8,128)S(1)}, f32[16,8,128]{2,1,0:T(8,128)S(1)}, u32[]{:S(2)}, u32[]{:S(2)}) collective-permute-start(f32[16,8,128]{2,1,0:T(8,128)S(1)} %add_add_fusion.state0), channel_id=1, source_target_pairs={{0,8},{8,0},{16,24},{24,16},{4,28},{12,20},{20,12},{28,4},{1,9},{9... | collective-permute-start | bytes 196616 | tf_op jit(solution)/shard_map/ppermute | solution.py:393
  66.5 3.2 %collective-permute-start.7 = (f32[2,8,8,128]{3,2,1,0:T(8,128)S(1)}, f32[2,8,8,128]{3,2,1,0:T(8,128)S(1)}, u32[]{:S(2)}, u32[]{:S(2)}) collective-permute-start(f32[2,8,8,128]{3,2,1,0:T(8,128)S(1)} %get-tuple-element.30.far), channel_id=1, source_target_pairs={{0,224},{32,64},{64,32},{96,128},{128,96},{160,192},{192,160},{224... | collective-permute-start | bytes 196616 | tf_op jit(solution)/shard_map/ppermute | solution.py:393
  67.1 5.0 %collective-permute-start.8 = (f32[2,8,8,128]{3,2,1,0:T(8,128)S(1)}, f32[2,8,8,128]{3,2,1,0:T(8,128)S(1)}, u32[]{:S(2)}, u32[]{:S(2)}) collective-permute-start(f32[2,8,8,128]{3,2,1,0:T(8,128)S(1)} %get-tuple-element.31.near), channel_id=1, source_target_pairs={{0,32},{32,0},{64,96},{96,64},{128,160},{160,128},{192,224},{224,1... | collective-permute-start | bytes 196616 | tf_op jit(solution)/shard_map/ppermute | solution.py:393
  74.4 12.6 %copy-start.1 = (bf16[64,384]{1,0:T(8,128)(2,1)S(1)}, bf16[64,384]{1,0:T(8,128)(2,1)}, u32[]{:S(2)}) copy-start(bf16[64,384]{1,0:T(8,128)(2,1)} %constant.8.clone.table) | copy-start | bytes 147460

commit v12 on v9

--- a/solution.py
+++ b/solution.py
@@ -255,7 +255,7 @@
     state[...] = mine[3:4][None] * middle[0] + mine[4:5][None] * middle[1]
 
 
-def between_kernel(got, solved, after, done, left, right):
+def between_kernel(got, solved, after, done, far, near, left, right):
     del after
     for c in range(2):
         for xc in range(8):
@@ -266,6 +266,7 @@
                     at = c * 4 + col * 2
                     done[seat(xc, yd), at : at + 2, :] = solved[c, 2 * xc + col, rows, :]
                     side[c, 2 * (xc % 4) + col, rows, :] = got[seat(xc, yd), 16 + at : 18 + at, :]
+    far[...], near[...] = by_side(right[...], left[...])
 
 
 def by_side(one, two):
@@ -273,12 +274,13 @@
     return jnp.where(even, two, one), jnp.where(even, one, two)
 
 
-def carry_kernel(slots, left, right, state0, state1, state2, state3, far, near):
+def carry_kernel(slots, wave_far, wave_near, state0, state1, state2, state3, far, near, state_far, state_near):
     state = (state0[...] + state1[...]) + (state2[...] + state3[...])
     mine = slots[slot()]
+    state_far[...], state_near[...] = by_side(state[CHUNK // 2 :], state[: CHUNK // 2])
     for c in range(2):
-        part = mine[5 + c : 6 + c][None] * state
-        far[c], near[c] = by_side(right[c] + part[CHUNK // 2 :], left[c] + part[: CHUNK // 2])
+        far[c] = wave_far[c] + mine[5 + c : 6 + c][None] * state_far[...]
+        near[c] = wave_near[c] + mine[5 + c : 6 + c][None] * state_near[...]
 
 
 def inner_kernel(ops, lows, scale, inverse, far, near, edges, iterate, source):
@@ -298,9 +300,17 @@
         edges[sweep, :, 2:] = iterate[:, hi - 2 : hi]
 
 
-def outer_kernel(ops, lows, scale, inverse, far, near, beyond_far, beyond_near, edges, before, out, iterate, source):
+def outer_kernel(
+    slots, ops, lows, scale, inverse, far, near, wave_far, state_far, wave_near, state_near, edges, before,
+    out, iterate, source,
+):
+    mine = slots[slot()]
+
+    def sides(wave, state):
+        return jnp.stack([wave[c] + mine[5 + c : 6 + c][None] * state[...] for c in range(2)])
+
     left, right = by_side(near[...], far[...])
-    west, east = by_side(beyond_near[...], beyond_far[...])
+    west, east = by_side(sides(wave_near, state_near), sides(wave_far, state_far))
     for i, part in enumerate((west, left, right, east)):
         start(inverse, part, source, slice(i * HALO, (i + 1) * HALO))
     out[:, :8, :] = before[...]
@@ -423,17 +433,27 @@
     )
     half = f32(2, CHUNK // 2, 8, LANES)
     state = state + swapped(state, "core", 1)
-    done, left, right = call(
-        between_kernel, (f32(FREQS, 8, LANES), half, half), (got, solved, state), (), [VMEM, VMEM, ANY], name="between"
-    )
-    near, far, across = (swapped(state, "y", bits) for bits in (1, 3, 2))
-    state = ((state + near) + far) + across
-    states = [state] + [swapped(state, "x", bits) for bits in (1, 3, 2)]
-    far, near = call(carry_kernel, (half, half), (SLOTS, left, right, *states), name="carry")
     planes = lax.axis_size("z")
     other = [(z, (z + 1 if z % 2 else z - 1) % planes) for z in range(planes)]
-    beyond_far = lax.ppermute(far, "z", other)
-    beyond_near = swapped(near, "z", 1)
+    done, wave_far, wave_near = call(
+        between_kernel,
+        (f32(FREQS, 8, LANES), half, half),
+        (got, solved, state),
+        (pltpu.VMEM(half.shape, jnp.float32), pltpu.VMEM(half.shape, jnp.float32)),
+        [VMEM, VMEM, ANY],
+        name="between",
+    )
+    beyond_wave_far = lax.ppermute(wave_far, "z", other)
+    beyond_wave_near = swapped(wave_near, "z", 1)
+    one, three, two = (swapped(state, "y", bits) for bits in (1, 3, 2))
+    state = ((state + one) + three) + two
+    states = [state] + [swapped(state, "x", bits) for bits in (1, 3, 2)]
+    part = f32(CHUNK // 2, 8, LANES)
+    far, near, state_far, state_near = call(
+        carry_kernel, (half, half, part, part), (SLOTS, wave_far, wave_near, *states), name="carry"
+    )
+    beyond_far = lax.ppermute(state_far, "z", other)
+    beyond_near = swapped(state_near, "z", 1)
     edges = call(
         inner_kernel,
         f32(SWEEPS, 2, 4, 8, LANES),
@@ -445,7 +465,7 @@
     done = call(
         outer_kernel,
         f32(FREQS, 16, LANES),
-        (ops, lows, scale, inverse, far, near, beyond_far, beyond_near, edges, done),
+        (SLOTS, ops, lows, scale, inverse, far, near, beyond_wave_far, beyond_far, beyond_wave_near, beyond_near, edges, done),
         (pltpu.VMEM((2, 2 * SWEEPS + 2, 8, LANES), jnp.float32), both),
         name="outer",
     )

time: 108 us -> 108 us (level)
  waiting for transfers between devices: 9.5 us -> 7.93 us
  starting transfers between devices: 8.05 us -> 9.22 us
    ppermute x8 -> x9, waiting for transfers between devices: 8.15 us -> 6.95 us  [swapped(): lax.ppermute(block, axis, [(i, i ^ bits) for i in range(lax.axis_size(axi...]
    ppermute x8 -> x9, starting transfers between devices: 7.95 us -> 9.03 us  [swapped(): lax.ppermute(block, axis, [(i, i ^ bits) for i in range(lax.axis_size(axi...]
  transfers between devices with their start and end apart: 9 -> 11, of which waited for: 7 -> 7; matrix products, arithmetic and copies ran while one was open for 0% -> 0% of each run, Pallas kernels for 2% -> 2%
where the time goes in v12:
time: 108 us; the launch traced here: 107 us
  blocking collectives  79.7 us (74%)
  Pallas kernels  10 us (9%)
  starting transfers between devices  9.22 us (9%)
  waiting for transfers between devices  7.93 us (7%)
    all_to_all x4, blocking collectives, exchange(): return lax.all_to_all(blocks, axes, 0, 0, tiled=True)  79.7 us
    pallas_call x9, Pallas kernels, call(): pl.pallas_call(kernel, out_shape=outs, in_specs=specs or [VMEM] * len(ins...  10 us
    ppermute x9, starting transfers between devices, swapped(): lax.ppermute(block, axis, [(i, i ^ bits) for i in range(lax.axis_size(axi...  9.03 us
    ppermute x9, waiting for transfers between devices, swapped(): lax.ppermute(block, axis, [(i, i ^ bits) for i in range(lax.axis_size(axi...  6.95 us
  transfers between devices with their start and end apart: 11, of which 7 were waited for; matrix products, arithmetic and copies ran while one was open for 0% of the time, Pallas kernels for 2%

profile of v12, /device:TPU:1, one launch (start us, length us, event | category | flops | bytes accessed | tf_op | source)
XLA Modules:
  0.0 107.2 jit_solution(2495304485924595505)
XLA Ops:
  0.0 1.6 %pack.1 = (f32[768,128]{1,0:T(8,128)S(1)}, bf16[256,768]{1,0:T(8,128)(2,1)S(1)}, bf16[128,512]{1,0:T(8,128)(2,1)S(1)}, f32[8,128]{1,0:T(8,128)S(1)}) custom-call(f32[250,2,128]{2,1,0:T(2,128)} %bitcast.17, f32[1,125,2,128]{3,2,1,0:T(2,128)} %bitcast.19, f32[1,2,128]{2,1,0:T(2,128)} %bitcast.21, f32[1,125,125]{2,1,0:T(8,128)} %bitcast.20, f32[125,4,125]{2,1,0:T(4,128)} %bitcast.18), custom_call_target="tpu_custom_call" | custom-call | tf_op jit(solution)/shard_map/pack/pallas_call | solution.py:374
  1.6 0.0 copy-start.2
  1.6 28.0 %all_to_all.20 = f32[64,3,4,128]{3,2,1,0:T(4,128)S(1)} all-to-all(f32[64,3,4,128]{3,2,1,0:T(4,128)S(1)} %bitcast.16), channel_id=1, replica_groups=mesh['z'=8,'x'=4,'core'=2,'y'=4] {'z','x','core'}, dimensions={0} | all-to-all | bytes 786432 | tf_op jit(solution)/shard_map/all_to_all | solution.py:391
  29.6 0.0 copy-done.2
  29.6 0.3 forward.1
  30.0 0.0 copy-start
  30.0 16.8 %all_to_all.21.got = f32[32,24,128]{2,1,0:T(8,128)S(1)} all-to-all(f32[32,24,128]{2,1,0:T(8,128)S(1)} %bitcast.12), channel_id=1, replica_groups=mesh['z'=8,'x'=4,'core'=2,'y'=4] {'core','y','x'}, dimensions={0} | all-to-all | bytes 786432 | tf_op jit(solution)/shard_map/all_to_all | solution.py:391
  46.7 0.0 copy-done
  46.7 2.7 %first.1 = (f32[2,16,8,128]{3,2,1,0:T(8,128)S(1)}, f32[16,8,128]{2,1,0:T(8,128)S(1)}, f32[32,8,128]{2,1,0:T(8,128)S(1)}, f32[3,32,8,128]{3,2,1,0:T(8,128)S(1)}) custom-call(f32[32,8,128]{2,1,0:T(8,128)S(1)} %copy-done, bf16[256,768]{1,0:T(8,128)(2,1)S(1)} %get-tuple-element.20.ops, bf16[128,512]{1,0:T(8,128)(2,1)S(1)} %get-tuple-element.21.lows, ...), custom_call_target="tpu_custom_call" | custom-call | tf_op jit(solution)/shard_map/first/pallas_call | solution.py:374
  49.4 1.3 %collective-permute-start = (f32[16,8,128]{2,1,0:T(8,128)S(1)}, f32[16,8,128]{2,1,0:T(8,128)S(1)}, u32[]{:S(2)}, u32[]{:S(2)}) collective-permute-start(f32[16,8,128]{2,1,0:T(8,128)S(1)} %get-tuple-element.27), channel_id=1, source_target_pairs={{0,4},{4,0},{1,5},{5,1},{2,6},{6,2},{3,7},{7,3},{8,12},{12,8},{9,1... | collective-permute-start | bytes 196616 | tf_op jit(solution)/shard_map/ppermute | solution.py:395
  50.7 0.9 collective-permute-done
  51.6 1.4 %collective-permute-start.3 = (f32[16,8,128]{2,1,0:T(8,128)S(1)}, f32[16,8,128]{2,1,0:T(8,128)S(1)}, u32[]{:S(2)}, u32[]{:S(2)}) collective-permute-start(f32[16,8,128]{2,1,0:T(8,128)S(1)} %add.12.after), channel_id=1, source_target_pairs={{0,2},{1,3},{2,0},{3,1},{4,6},{5,7},{6,4},{7,5},{8,10},{9,11},{10,... | collective-permute-start | bytes 196616 | tf_op jit(solution)/shard_map/ppermute | solution.py:395
  53.0 1.4 %collective-permute-start.2 = (f32[16,8,128]{2,1,0:T(8,128)S(1)}, f32[16,8,128]{2,1,0:T(8,128)S(1)}, u32[]{:S(2)}, u32[]{:S(2)}) collective-permute-start(f32[16,8,128]{2,1,0:T(8,128)S(1)} %add.12.after), channel_id=1, source_target_pairs={{0,3},{1,2},{2,1},{3,0},{4,7},{5,6},{6,5},{7,4},{8,11},{9,10},{10,... | collective-permute-start | bytes 196616 | tf_op jit(solution)/shard_map/ppermute | solution.py:395
  54.5 0.0 collective-permute-start.1
  54.5 1.9 %collective-permute-done.3 = f32[16,8,128]{2,1,0:T(8,128)S(1)} collective-permute-done((f32[16,8,128]{2,1,0:T(8,128)S(1)}, f32[16,8,128]{2,1,0:T(8,128)S(1)}, u32[]{:S(2)}, u32[]{:S(2)}) %collective-permute-start.3) | collective-permute-done | bytes 65568 | tf_op jit(solution)/shard_map/ppermute | solution.py:395
  56.4 1.9 %collective-permute-done.2 = f32[16,8,128]{2,1,0:T(8,128)S(1)} collective-permute-done((f32[16,8,128]{2,1,0:T(8,128)S(1)}, f32[16,8,128]{2,1,0:T(8,128)S(1)}, u32[]{:S(2)}, u32[]{:S(2)}) %collective-permute-start.2) | collective-permute-done | bytes 65568 | tf_op jit(solution)/shard_map/ppermute | solution.py:395
  58.3 0.0 collective-permute-done.1
  58.3 1.3 %collective-permute-start.6 = (f32[16,8,128]{2,1,0:T(8,128)S(1)}, f32[16,8,128]{2,1,0:T(8,128)S(1)}, u32[]{:S(2)}, u32[]{:S(2)}) collective-permute-start(f32[16,8,128]{2,1,0:T(8,128)S(1)} %add_add_fusion.state0), channel_id=1, source_target_pairs={{0,16},{8,24},{16,0},{24,8},{1,17},{9,25},{17,1},{25,9},{2,18},{10... | collective-permute-start | bytes 196616 | tf_op jit(solution)/shard_map/ppermute | solution.py:395
  59.6 0.9 collective-permute-start.5
  60.5 0.5 collective-permute-start.4
  61.0 0.1 between.1
  61.2 0.1 collective-permute-start.7
  61.3 1.1 %collective-permute-start.9 = (f32[2,8,8,128]{3,2,1,0:T(8,128)S(1)}, f32[2,8,8,128]{3,2,1,0:T(8,128)S(1)}, u32[]{:S(2)}, u32[]{:S(2)}) collective-permute-start(f32[2,8,8,128]{3,2,1,0:T(8,128)S(1)} %get-tuple-element.29.wave_near), channel_id=1, source_target_pairs={{0,32},{32,0},{64,96},{96,64},{128,160},{160,128},{192,224},{224,1... | collective-permute-start | bytes 196616 | tf_op jit(solution)/shard_map/ppermute | solution.py:395
  62.3 0.7 collective-permute-done.6.state3
  63.0 1.0 collective-permute-done.5.state2
  64.0 0.6 collective-permute-done.4.state1
  64.6 0.1 collective-permute-start.8
  64.7 1.1 %collective-permute-start.10 = (f32[8,8,128]{2,1,0:T(8,128)S(1)}, f32[8,8,128]{2,1,0:T(8,128)S(1)}, u32[]{:S(2)}, u32[]{:S(2)}) collective-permute-start(f32[8,8,128]{2,1,0:T(8,128)S(1)} %get-tuple-element.33), channel_id=1, source_target_pairs={{0,32},{32,0},{64,96},{96,64},{128,160},{160,128},{192,224},{224,1... | collective-permute-start | bytes 98312 | tf_op jit(solution)/shard_map/ppermute | solution.py:395
  65.8 1.9 %inner.1.edges = f32[8,2,4,8,128]{4,3,2,1,0:T(8,128)S(1)} custom-call(bf16[256,768]{1,0:T(8,128)(2,1)S(1)} %get-tuple-element.20.ops, bf16[128,512]{1,0:T(8,128)(2,1)S(1)} %get-tuple-element.21.lows, f32[32,8,128]{2,1,0:T(8,128)S(1)} %get-tuple-element.24.scale, f32[3,32,8,128]{3,2,1,0:T(8,128)S(1)} %get-tuple-element.25.inverse, ...), custom_call_target="tpu_custom_call" | custom-call | flops 2000000000 | bytes 1000000 | tf_op jit(solution)/shard_map/inner/pallas_call | solution.py:374
  67.7 0.0 collective-permute-done.7.wave_far
  67.7 0.0 collective-permute-done.9.wave_near
  67.7 1.0 collective-permute-done.8.state_far
  68.7 0.0 collective-permute-done.10.state_near
  68.7 2.2 %outer.1 = f32[32,16,128]{2,1,0:T(8,128)S(1)} custom-call(f32[32,8,128]{2,1,0:T(8,128)S(1)} %copy-done, bf16[256,768]{1,0:T(8,128)(2,1)S(1)} %get-tuple-element.20.ops, bf16[128,512]{1,0:T(8,128)(2,1)S(1)} %get-tuple-element.21.lows, f32[32,8,128]{2,1,0:T(8,128)S(1)} %get-tuple-element.24.scale, f32[3,32,8,128]{3,2,1,0:T(8,128)S(1)} %get-tuple-element.25.inverse, ...), custom_call_target="tpu_custom_call" | custom-call | tf_op jit(solution)/shard_map/outer/pallas_call | solution.py:374
  70.9 0.0 copy-start.1
  70.9 15.7 %all_to_all.22 = f32[32,16,128]{2,1,0:T(8,128)S(1)} all-to-all(f32[32,16,128]{2,1,0:T(8,128)S(1)} %outer.1), channel_id=1, replica_groups=mesh['z'=8,'x'=4,'core'=2,'y'=4] {'core','y','x'}, dimensions={0} | all-to-all | bytes 524288 | tf_op jit(solution)/shard_map/all_to_all | solution.py:391
  86.5 0.0 copy-done.1
  86.5 0.3 backward.1
  86.8 19.3 %all_to_all.23 = f32[64,8,128]{2,1,0:T(8,128)S(1)} all-to-all(f32[64,8,128]{2,1,0:T(8,128)S(1)} %bitcast.14), channel_id=1, replica_groups=mesh['z'=8,'x'=4,'core'=2,'y'=4] {'z','x','core'}, dimensions={0} | all-to-all | bytes 524288 | tf_op jit(solution)/shard_map/all_to_all | solution.py:391
  106.1 0.9 unpack.1
  (3 shorter events, 0.1 us)
Async XLA Ops:
  1.6 28.0 %copy-start.2 = (bf16[64,384]{1,0:T(8,128)(2,1)S(1)}, bf16[64,384]{1,0:T(8,128)(2,1)}, u32[]{:S(2)}) copy-start(bf16[64,384]{1,0:T(8,128)(2,1)} %constant.6.clone.table) | copy-start | bytes 147460
  30.0 16.8 %copy-start = (f32[32,8,128]{2,1,0:T(8,128)S(1)}, f32[32,8,128]{2,1,0:T(8,128)}, u32[]{:S(2)}) copy-start(f32[32,8,128]{2,1,0:T(8,128)} %constant.7.clone.slots) | copy-start | bytes 393220
  49.4 2.2 %collective-permute-start = (f32[16,8,128]{2,1,0:T(8,128)S(1)}, f32[16,8,128]{2,1,0:T(8,128)S(1)}, u32[]{:S(2)}, u32[]{:S(2)}) collective-permute-start(f32[16,8,128]{2,1,0:T(8,128)S(1)} %get-tuple-element.27), channel_id=1, source_target_pairs={{0,4},{4,0},{1,5},{5,1},{2,6},{6,2},{3,7},{7,3},{8,12},{12,8},{9,1... | collective-permute-start | bytes 196616 | tf_op jit(solution)/shard_map/ppermute | solution.py:395
  51.6 4.7 %collective-permute-start.3 = (f32[16,8,128]{2,1,0:T(8,128)S(1)}, f32[16,8,128]{2,1,0:T(8,128)S(1)}, u32[]{:S(2)}, u32[]{:S(2)}) collective-permute-start(f32[16,8,128]{2,1,0:T(8,128)S(1)} %add.12.after), channel_id=1, source_target_pairs={{0,2},{1,3},{2,0},{3,1},{4,6},{5,7},{6,4},{7,5},{8,10},{9,11},{10,... | collective-permute-start | bytes 196616 | tf_op jit(solution)/shard_map/ppermute | solution.py:395
  53.0 5.3 %collective-permute-start.2 = (f32[16,8,128]{2,1,0:T(8,128)S(1)}, f32[16,8,128]{2,1,0:T(8,128)S(1)}, u32[]{:S(2)}, u32[]{:S(2)}) collective-permute-start(f32[16,8,128]{2,1,0:T(8,128)S(1)} %add.12.after), channel_id=1, source_target_pairs={{0,3},{1,2},{2,1},{3,0},{4,7},{5,6},{6,5},{7,4},{8,11},{9,10},{10,... | collective-permute-start | bytes 196616 | tf_op jit(solution)/shard_map/ppermute | solution.py:395
  54.5 3.8 %collective-permute-start.1 = (f32[16,8,128]{2,1,0:T(8,128)S(1)}, f32[16,8,128]{2,1,0:T(8,128)S(1)}, u32[]{:S(2)}, u32[]{:S(2)}) collective-permute-start(f32[16,8,128]{2,1,0:T(8,128)S(1)} %add.12.after), channel_id=1, source_target_pairs={{0,1},{1,0},{2,3},{3,2},{4,5},{5,4},{6,7},{7,6},{8,9},{9,8},{10,11... | collective-permute-start | bytes 196616 | tf_op jit(solution)/shard_map/ppermute | solution.py:395
  58.3 4.7 %collective-permute-start.6 = (f32[16,8,128]{2,1,0:T(8,128)S(1)}, f32[16,8,128]{2,1,0:T(8,128)S(1)}, u32[]{:S(2)}, u32[]{:S(2)}) collective-permute-start(f32[16,8,128]{2,1,0:T(8,128)S(1)} %add_add_fusion.state0), channel_id=1, source_target_pairs={{0,16},{8,24},{16,0},{24,8},{1,17},{9,25},{17,1},{25,9},{2,18},{10... | collective-permute-start | bytes 196616 | tf_op jit(solution)/shard_map/ppermute | solution.py:395
  59.6 4.3 %collective-permute-start.5 = (f32[16,8,128]{2,1,0:T(8,128)S(1)}, f32[16,8,128]{2,1,0:T(8,128)S(1)}, u32[]{:S(2)}, u32[]{:S(2)}) collective-permute-start(f32[16,8,128]{2,1,0:T(8,128)S(1)} %add_add_fusion.state0), channel_id=1, source_target_pairs={{0,24},{8,16},{16,8},{24,0},{1,25},{9,17},{17,9},{25,1},{2,26},{10... | collective-permute-start | bytes 196616 | tf_op jit(solution)/shard_map/ppermute | solution.py:395
  60.5 4.1 %collective-permute-start.4 = (f32[16,8,128]{2,1,0:T(8,128)S(1)}, f32[16,8,128]{2,1,0:T(8,128)S(1)}, u32[]{:S(2)}, u32[]{:S(2)}) collective-permute-start(f32[16,8,128]{2,1,0:T(8,128)S(1)} %add_add_fusion.state0), channel_id=1, source_target_pairs={{0,8},{8,0},{16,24},{24,16},{1,9},{9,1},{17,25},{25,17},{2,10},{10... | collective-permute-start | bytes 196616 | tf_op jit(solution)/shard_map/ppermute | solution.py:395
  61.2 6.5 %collective-permute-start.7 = (f32[2,8,8,128]{3,2,1,0:T(8,128)S(1)}, f32[2,8,8,128]{3,2,1,0:T(8,128)S(1)}, u32[]{:S(2)}, u32[]{:S(2)}) collective-permute-start(f32[2,8,8,128]{3,2,1,0:T(8,128)S(1)} %get-tuple-element.28.wave_far), channel_id=1, source_target_pairs={{0,224},{32,64},{64,32},{96,128},{128,96},{160,192},{192,160},{224... | collective-permute-start | bytes 196616 | tf_op jit(solution)/shard_map/ppermute | solution.py:446
  61.3 6.4 %collective-permute-start.9 = (f32[2,8,8,128]{3,2,1,0:T(8,128)S(1)}, f32[2,8,8,128]{3,2,1,0:T(8,128)S(1)}, u32[]{:S(2)}, u32[]{:S(2)}) collective-permute-start(f32[2,8,8,128]{3,2,1,0:T(8,128)S(1)} %get-tuple-element.29.wave_near), channel_id=1, source_target_pairs={{0,32},{32,0},{64,96},{96,64},{128,160},{160,128},{192,224},{224,1... | collective-permute-start | bytes 196616 | tf_op jit(solution)/shard_map/ppermute | solution.py:395
  64.6 4.1 %collective-permute-start.8 = (f32[8,8,128]{2,1,0:T(8,128)S(1)}, f32[8,8,128]{2,1,0:T(8,128)S(1)}, u32[]{:S(2)}, u32[]{:S(2)}) collective-permute-start(f32[8,8,128]{2,1,0:T(8,128)S(1)} %get-tuple-element.32), channel_id=1, source_target_pairs={{0,224},{32,64},{64,32},{96,128},{128,96},{160,192},{192,160},{224... | collective-permute-start | bytes 98312 | tf_op jit(solution)/shard_map/ppermute | solution.py:455
  64.7 4.0 %collective-permute-start.10 = (f32[8,8,128]{2,1,0:T(8,128)S(1)}, f32[8,8,128]{2,1,0:T(8,128)S(1)}, u32[]{:S(2)}, u32[]{:S(2)}) collective-permute-start(f32[8,8,128]{2,1,0:T(8,128)S(1)} %get-tuple-element.33), channel_id=1, source_target_pairs={{0,32},{32,0},{64,96},{96,64},{128,160},{160,128},{192,224},{224,1... | collective-permute-start | bytes 98312 | tf_op jit(solution)/shard_map/ppermute | solution.py:395
  70.9 15.7 %copy-start.1 = (bf16[64,384]{1,0:T(8,128)(2,1)S(1)}, bf16[64,384]{1,0:T(8,128)(2,1)}, u32[]{:S(2)}) copy-start(bf16[64,384]{1,0:T(8,128)(2,1)} %constant.8.clone.table) | copy-start | bytes 147460

commit v13 on v10

--- a/solution.py
+++ b/solution.py
@@ -256,7 +256,7 @@
     state[...] = mine[3:4][None] * middle[0] + mine[4:5][None] * middle[1]
 
 
-def between_kernel(got, solved, after, done, left, right):
+def between_kernel(got, solved, after, done, far, near, left, right):
     del after
     for c in range(2):
         for xc in range(8):
@@ -267,6 +267,7 @@
                     at = c * 4 + col * 2
                     done[seat(xc, yd), at : at + 2, :] = solved[c, 2 * xc + col, rows, :]
                     side[c, 2 * (xc % 4) + col, rows, :] = got[seat(xc, yd), 16 + at : 18 + at, :]
+    far[...], near[...] = by_side(right[...], left[...])
 
 
 def by_side(one, two):
@@ -274,12 +275,13 @@
     return jnp.where(even, two, one), jnp.where(even, one, two)
 
 
-def carry_kernel(slots, left, right, state0, state1, state2, state3, far, near):
+def carry_kernel(slots, wave_far, wave_near, state0, state1, state2, state3, far, near, state_far, state_near):
     state = (state0[...] + state1[...]) + (state2[...] + state3[...])
     mine = slots[slot()]
+    state_far[...], state_near[...] = by_side(state[CHUNK // 2 :], state[: CHUNK // 2])
     for c in range(2):
-        part = mine[5 + c : 6 + c][None] * state
-        far[c], near[c] = by_side(right[c] + part[CHUNK // 2 :], left[c] + part[: CHUNK // 2])
+        far[c] = wave_far[c] + mine[5 + c : 6 + c][None] * state_far[...]
+        near[c] = wave_near[c] + mine[5 + c : 6 + c][None] * state_near[...]
 
 
 def inner_kernel(ops, lows, scale, inverse, far, near, edges, core, iterate, source):
@@ -302,10 +304,16 @@
 
 
 def outer_kernel(
-    ops, lows, scale, inverse, far, near, beyond_far, beyond_near, edges, core, before, out, sides, iterate, source
+    slots, ops, lows, scale, inverse, far, near, wave_far, state_far, wave_near, state_near, edges, core, before,
+    out, sides, iterate, source,
 ):
+    mine = slots[slot()]
+
+    def halo(wave, state):
+        return jnp.stack([wave[c] + mine[5 + c : 6 + c][None] * state[...] for c in range(2)])
+
     left, right = by_side(near[...], far[...])
-    west, east = by_side(beyond_near[...], beyond_far[...])
+    west, east = by_side(halo(wave_near, state_near), halo(wave_far, state_far))
     for i, part in enumerate((west, left, right, east)):
         start(inverse, part, source, slice(i * HALO, (i + 1) * HALO))
     out[:, :8, :] = before[...]
@@ -424,17 +432,27 @@
     )
     half = f32(2, CHUNK // 2, 8, LANES)
     state = state + swapped(state, "core", 1)
-    done, left, right = call(
-        between_kernel, (f32(FREQS, 8, LANES), half, half), (got, solved, state), (), [VMEM, VMEM, ANY], name="between"
-    )
-    near, far, across = (swapped(state, "y", bits) for bits in (1, 3, 2))
-    state = ((state + near) + far) + across
-    states = [state] + [swapped(state, "x", bits) for bits in (1, 3, 2)]
-    far, near = call(carry_kernel, (half, half), (SLOTS, left, right, *states), name="carry")
     planes = lax.axis_size("z")
     other = [(z, (z + 1 if z % 2 else z - 1) % planes) for z in range(planes)]
-    beyond_far = lax.ppermute(far, "z", other)
-    beyond_near = swapped(near, "z", 1)
+    done, wave_far, wave_near = call(
+        between_kernel,
+        (f32(FREQS, 8, LANES), half, half),
+        (got, solved, state),
+        (pltpu.VMEM(half.shape, jnp.float32), pltpu.VMEM(half.shape, jnp.float32)),
+        [VMEM, VMEM, ANY],
+        name="between",
+    )
+    beyond_wave_far = lax.ppermute(wave_far, "z", other)
+    beyond_wave_near = swapped(wave_near, "z", 1)
+    one, three, two = (swapped(state, "y", bits) for bits in (1, 3, 2))
+    state = ((state + one) + three) + two
+    states = [state] + [swapped(state, "x", bits) for bits in (1, 3, 2)]
+    part = f32(CHUNK // 2, 8, LANES)
+    far, near, state_far, state_near = call(
+        carry_kernel, (half, half, part, part), (SLOTS, wave_far, wave_near, *states), name="carry"
+    )
+    beyond_far = lax.ppermute(state_far, "z", other)
+    beyond_near = swapped(state_near, "z", 1)
     edges, core = call(
         inner_kernel,
         (f32(INNER, 2, 4, 8, LANES), f32(2, CHUNK - 2 * INNER, 8, LANES)),
@@ -446,7 +464,7 @@
     done = call(
         outer_kernel,
         f32(FREQS, 16, LANES),
-        (ops, lows, scale, inverse, far, near, beyond_far, beyond_near, edges, core, done),
+        (SLOTS, ops, lows, scale, inverse, far, near, beyond_wave_far, beyond_far, beyond_wave_near, beyond_near, edges, core, done),
         (pltpu.VMEM((2, 2 * HALO + 2, 8, LANES), jnp.float32), both, both),
         name="outer",
     )

time: 108 us -> 108 us (level)
  waiting for transfers between devices: 10.3 us -> 8.67 us
  starting transfers between devices: 8.03 us -> 9.21 us
    ppermute x8 -> x9, waiting for transfers between devices: 8.16 us -> 6.95 us  [swapped(): lax.ppermute(block, axis, [(i, i ^ bits) for i in range(lax.axis_size(axi...]
    ppermute x8 -> x9, starting transfers between devices: 7.94 us -> 9.03 us  [swapped(): lax.ppermute(block, axis, [(i, i ^ bits) for i in range(lax.axis_size(axi...]
  transfers between devices with their start and end apart: 9 -> 11, of which waited for: 7 -> 7; matrix products, arithmetic and copies ran while one was open for 0% -> 0% of each run, Pallas kernels for 1% -> 1%
where the time goes in v13:
time: 108 us; the launch traced here: 107 us
  blocking collectives  79.7 us (74%)
  Pallas kernels  9.34 us (9%)
  starting transfers between devices  9.21 us (9%)
  waiting for transfers between devices  8.67 us (8%)
    all_to_all x4, blocking collectives, exchange(): return lax.all_to_all(blocks, axes, 0, 0, tiled=True)  79.7 us
    pallas_call x9, Pallas kernels, call(): pl.pallas_call(kernel, out_shape=outs, in_specs=specs or [VMEM] * len(ins...  9.34 us
    ppermute x9, starting transfers between devices, swapped(): lax.ppermute(block, axis, [(i, i ^ bits) for i in range(lax.axis_size(axi...  9.03 us
    ppermute x9, waiting for transfers between devices, swapped(): lax.ppermute(block, axis, [(i, i ^ bits) for i in range(lax.axis_size(axi...  6.95 us
  transfers between devices with their start and end apart: 11, of which 7 were waited for; matrix products, arithmetic and copies ran while one was open for 0% of the time, Pallas kernels for 1%

profile of v13, /device:TPU:1, one launch (start us, length us, event | category | flops | bytes accessed | tf_op | source)
XLA Modules:
  0.0 107.2 jit_solution(8610532997207736279)
XLA Ops:
  0.0 1.6 %pack.1 = (f32[768,128]{1,0:T(8,128)S(1)}, bf16[256,768]{1,0:T(8,128)(2,1)S(1)}, bf16[128,512]{1,0:T(8,128)(2,1)S(1)}, f32[8,128]{1,0:T(8,128)S(1)}) custom-call(f32[250,2,128]{2,1,0:T(2,128)} %bitcast.17, f32[1,125,2,128]{3,2,1,0:T(2,128)} %bitcast.19, f32[1,2,128]{2,1,0:T(2,128)} %bitcast.21, f32[1,125,125]{2,1,0:T(8,128)} %bitcast.20, f32[125,4,125]{2,1,0:T(4,128)} %bitcast.18), custom_call_target="tpu_custom_call" | custom-call | tf_op jit(solution)/shard_map/pack/pallas_call | solution.py:373
  1.6 0.0 copy-start.2
  1.6 28.0 %all_to_all.20 = f32[64,3,4,128]{3,2,1,0:T(4,128)S(1)} all-to-all(f32[64,3,4,128]{3,2,1,0:T(4,128)S(1)} %bitcast.16), channel_id=1, replica_groups=mesh['z'=8,'x'=4,'core'=2,'y'=4] {'z','x','core'}, dimensions={0} | all-to-all | bytes 786432 | tf_op jit(solution)/shard_map/all_to_all | solution.py:390
  29.6 0.0 copy-done.2
  29.6 0.3 forward.1
  30.0 0.0 copy-start
  30.0 16.8 %all_to_all.21.got = f32[32,24,128]{2,1,0:T(8,128)S(1)} all-to-all(f32[32,24,128]{2,1,0:T(8,128)S(1)} %bitcast.12), channel_id=1, replica_groups=mesh['z'=8,'x'=4,'core'=2,'y'=4] {'core','y','x'}, dimensions={0} | all-to-all | bytes 786432 | tf_op jit(solution)/shard_map/all_to_all | solution.py:390
  46.7 0.0 copy-done
  46.7 2.7 %first.1 = (f32[2,16,8,128]{3,2,1,0:T(8,128)S(1)}, f32[16,8,128]{2,1,0:T(8,128)S(1)}, f32[32,8,128]{2,1,0:T(8,128)S(1)}, f32[3,32,8,128]{3,2,1,0:T(8,128)S(1)}) custom-call(f32[32,8,128]{2,1,0:T(8,128)S(1)} %copy-done, bf16[256,768]{1,0:T(8,128)(2,1)S(1)} %get-tuple-element.22.ops, bf16[128,512]{1,0:T(8,128)(2,1)S(1)} %get-tuple-element.23.lows, ...), custom_call_target="tpu_custom_call" | custom-call | tf_op jit(solution)/shard_map/first/pallas_call | solution.py:373
  49.4 1.3 %collective-permute-start = (f32[16,8,128]{2,1,0:T(8,128)S(1)}, f32[16,8,128]{2,1,0:T(8,128)S(1)}, u32[]{:S(2)}, u32[]{:S(2)}) collective-permute-start(f32[16,8,128]{2,1,0:T(8,128)S(1)} %get-tuple-element.29), channel_id=1, source_target_pairs={{0,4},{4,0},{1,5},{5,1},{2,6},{6,2},{3,7},{7,3},{8,12},{12,8},{9,1... | collective-permute-start | bytes 196616 | tf_op jit(solution)/shard_map/ppermute | solution.py:394
  50.7 0.9 collective-permute-done
  51.6 1.4 %collective-permute-start.3 = (f32[16,8,128]{2,1,0:T(8,128)S(1)}, f32[16,8,128]{2,1,0:T(8,128)S(1)}, u32[]{:S(2)}, u32[]{:S(2)}) collective-permute-start(f32[16,8,128]{2,1,0:T(8,128)S(1)} %add.12.after), channel_id=1, source_target_pairs={{0,2},{1,3},{2,0},{3,1},{4,6},{5,7},{6,4},{7,5},{8,10},{9,11},{10,... | collective-permute-start | bytes 196616 | tf_op jit(solution)/shard_map/ppermute | solution.py:394
  53.0 1.4 %collective-permute-start.2 = (f32[16,8,128]{2,1,0:T(8,128)S(1)}, f32[16,8,128]{2,1,0:T(8,128)S(1)}, u32[]{:S(2)}, u32[]{:S(2)}) collective-permute-start(f32[16,8,128]{2,1,0:T(8,128)S(1)} %add.12.after), channel_id=1, source_target_pairs={{0,3},{1,2},{2,1},{3,0},{4,7},{5,6},{6,5},{7,4},{8,11},{9,10},{10,... | collective-permute-start | bytes 196616 | tf_op jit(solution)/shard_map/ppermute | solution.py:394
  54.5 0.0 collective-permute-start.1
  54.5 1.9 %collective-permute-done.3 = f32[16,8,128]{2,1,0:T(8,128)S(1)} collective-permute-done((f32[16,8,128]{2,1,0:T(8,128)S(1)}, f32[16,8,128]{2,1,0:T(8,128)S(1)}, u32[]{:S(2)}, u32[]{:S(2)}) %collective-permute-start.3) | collective-permute-done | bytes 65568 | tf_op jit(solution)/shard_map/ppermute | solution.py:394
  56.4 1.9 %collective-permute-done.2 = f32[16,8,128]{2,1,0:T(8,128)S(1)} collective-permute-done((f32[16,8,128]{2,1,0:T(8,128)S(1)}, f32[16,8,128]{2,1,0:T(8,128)S(1)}, u32[]{:S(2)}, u32[]{:S(2)}) %collective-permute-start.2) | collective-permute-done | bytes 65568 | tf_op jit(solution)/shard_map/ppermute | solution.py:394
  58.3 0.0 collective-permute-done.1
  58.3 1.3 %collective-permute-start.6 = (f32[16,8,128]{2,1,0:T(8,128)S(1)}, f32[16,8,128]{2,1,0:T(8,128)S(1)}, u32[]{:S(2)}, u32[]{:S(2)}) collective-permute-start(f32[16,8,128]{2,1,0:T(8,128)S(1)} %add_add_fusion.state0), channel_id=1, source_target_pairs={{0,16},{8,24},{16,0},{24,8},{1,17},{9,25},{17,1},{25,9},{2,18},{10... | collective-permute-start | bytes 196616 | tf_op jit(solution)/shard_map/ppermute | solution.py:394
  59.7 0.9 collective-permute-start.5
  60.5 0.5 collective-permute-start.4
  61.0 0.1 between.1
  61.2 0.1 collective-permute-start.7
  61.3 1.1 %collective-permute-start.9 = (f32[2,8,8,128]{3,2,1,0:T(8,128)S(1)}, f32[2,8,8,128]{3,2,1,0:T(8,128)S(1)}, u32[]{:S(2)}, u32[]{:S(2)}) collective-permute-start(f32[2,8,8,128]{3,2,1,0:T(8,128)S(1)} %get-tuple-element.31.wave_near), channel_id=1, source_target_pairs={{0,32},{32,0},{64,96},{96,64},{128,160},{160,128},{192,224},{224,1... | collective-permute-start | bytes 196616 | tf_op jit(solution)/shard_map/ppermute | solution.py:394
  62.3 0.7 collective-permute-done.6.state3
  63.0 1.0 collective-permute-done.5.state2
  64.0 0.6 collective-permute-done.4.state1
  64.6 0.1 collective-permute-start.8
  64.7 1.1 %collective-permute-start.10 = (f32[8,8,128]{2,1,0:T(8,128)S(1)}, f32[8,8,128]{2,1,0:T(8,128)S(1)}, u32[]{:S(2)}, u32[]{:S(2)}) collective-permute-start(f32[8,8,128]{2,1,0:T(8,128)S(1)} %get-tuple-element.35), channel_id=1, source_target_pairs={{0,32},{32,0},{64,96},{96,64},{128,160},{160,128},{192,224},{224,1... | collective-permute-start | bytes 98312 | tf_op jit(solution)/shard_map/ppermute | solution.py:394
  65.8 1.1 %inner.1 = (f32[4,2,4,8,128]{4,3,2,1,0:T(8,128)S(1)}, f32[2,8,8,128]{3,2,1,0:T(8,128)S(1)}) custom-call(bf16[256,768]{1,0:T(8,128)(2,1)S(1)} %get-tuple-element.22.ops, bf16[128,512]{1,0:T(8,128)(2,1)S(1)} %get-tuple-element.23.lows, f32[32,8,128]{2,1,0:T(8,128)S(1)} %get-tuple-element.26.scale, f32[3,32,8,128]{3,2,1,0:T(8,128)S(1)} %get-tuple-element.27.inverse, ...), custom_call_target="tpu_custom_call" | custom-call | flops 2000000000 | bytes 1000000 | tf_op jit(solution)/shard_map/inner/pallas_call | solution.py:373
  66.9 0.0 collective-permute-done.7.wave_far
  67.0 0.0 collective-permute-done.9.wave_near
  67.0 1.7 %collective-permute-done.8.state_far = f32[8,8,128]{2,1,0:T(8,128)S(1)} collective-permute-done((f32[8,8,128]{2,1,0:T(8,128)S(1)}, f32[8,8,128]{2,1,0:T(8,128)S(1)}, u32[]{:S(2)}, u32[]{:S(2)}) %collective-permute-start.8) | collective-permute-done | bytes 32800 | tf_op jit(solution)/shard_map/ppermute | solution.py:454
  68.7 0.0 collective-permute-done.10.state_near
  68.7 2.2 %outer.1 = f32[32,16,128]{2,1,0:T(8,128)S(1)} custom-call(f32[32,8,128]{2,1,0:T(8,128)S(1)} %copy-done, bf16[256,768]{1,0:T(8,128)(2,1)S(1)} %get-tuple-element.22.ops, bf16[128,512]{1,0:T(8,128)(2,1)S(1)} %get-tuple-element.23.lows, f32[32,8,128]{2,1,0:T(8,128)S(1)} %get-tuple-element.26.scale, f32[3,32,8,128]{3,2,1,0:T(8,128)S(1)} %get-tuple-element.27.inverse, ...), custom_call_target="tpu_custom_call" | custom-call | tf_op jit(solution)/shard_map/outer/pallas_call | solution.py:373
  70.9 0.0 copy-start.1
  70.9 15.7 %all_to_all.22 = f32[32,16,128]{2,1,0:T(8,128)S(1)} all-to-all(f32[32,16,128]{2,1,0:T(8,128)S(1)} %outer.1), channel_id=1, replica_groups=mesh['z'=8,'x'=4,'core'=2,'y'=4] {'core','y','x'}, dimensions={0} | all-to-all | bytes 524288 | tf_op jit(solution)/shard_map/all_to_all | solution.py:390
  86.6 0.0 copy-done.1
  86.6 0.3 backward.1
  86.9 19.3 %all_to_all.23 = f32[64,8,128]{2,1,0:T(8,128)S(1)} all-to-all(f32[64,8,128]{2,1,0:T(8,128)S(1)} %bitcast.14), channel_id=1, replica_groups=mesh['z'=8,'x'=4,'core'=2,'y'=4] {'z','x','core'}, dimensions={0} | all-to-all | bytes 524288 | tf_op jit(solution)/shard_map/all_to_all | solution.py:390
  106.2 0.9 unpack.1
  (3 shorter events, 0.1 us)
Async XLA Ops:
  1.6 28.0 %copy-start.2 = (bf16[64,384]{1,0:T(8,128)(2,1)S(1)}, bf16[64,384]{1,0:T(8,128)(2,1)}, u32[]{:S(2)}) copy-start(bf16[64,384]{1,0:T(8,128)(2,1)} %constant.6.clone.table) | copy-start | bytes 147460
  30.0 16.8 %copy-start = (f32[32,8,128]{2,1,0:T(8,128)S(1)}, f32[32,8,128]{2,1,0:T(8,128)}, u32[]{:S(2)}) copy-start(f32[32,8,128]{2,1,0:T(8,128)} %constant.7.clone.slots) | copy-start | bytes 393220
  49.4 2.2 %collective-permute-start = (f32[16,8,128]{2,1,0:T(8,128)S(1)}, f32[16,8,128]{2,1,0:T(8,128)S(1)}, u32[]{:S(2)}, u32[]{:S(2)}) collective-permute-start(f32[16,8,128]{2,1,0:T(8,128)S(1)} %get-tuple-element.29), channel_id=1, source_target_pairs={{0,4},{4,0},{1,5},{5,1},{2,6},{6,2},{3,7},{7,3},{8,12},{12,8},{9,1... | collective-permute-start | bytes 196616 | tf_op jit(solution)/shard_map/ppermute | solution.py:394
  51.6 4.7 %collective-permute-start.3 = (f32[16,8,128]{2,1,0:T(8,128)S(1)}, f32[16,8,128]{2,1,0:T(8,128)S(1)}, u32[]{:S(2)}, u32[]{:S(2)}) collective-permute-start(f32[16,8,128]{2,1,0:T(8,128)S(1)} %add.12.after), channel_id=1, source_target_pairs={{0,2},{1,3},{2,0},{3,1},{4,6},{5,7},{6,4},{7,5},{8,10},{9,11},{10,... | collective-permute-start | bytes 196616 | tf_op jit(solution)/shard_map/ppermute | solution.py:394
  53.0 5.3 %collective-permute-start.2 = (f32[16,8,128]{2,1,0:T(8,128)S(1)}, f32[16,8,128]{2,1,0:T(8,128)S(1)}, u32[]{:S(2)}, u32[]{:S(2)}) collective-permute-start(f32[16,8,128]{2,1,0:T(8,128)S(1)} %add.12.after), channel_id=1, source_target_pairs={{0,3},{1,2},{2,1},{3,0},{4,7},{5,6},{6,5},{7,4},{8,11},{9,10},{10,... | collective-permute-start | bytes 196616 | tf_op jit(solution)/shard_map/ppermute | solution.py:394
  54.5 3.8 %collective-permute-start.1 = (f32[16,8,128]{2,1,0:T(8,128)S(1)}, f32[16,8,128]{2,1,0:T(8,128)S(1)}, u32[]{:S(2)}, u32[]{:S(2)}) collective-permute-start(f32[16,8,128]{2,1,0:T(8,128)S(1)} %add.12.after), channel_id=1, source_target_pairs={{0,1},{1,0},{2,3},{3,2},{4,5},{5,4},{6,7},{7,6},{8,9},{9,8},{10,11... | collective-permute-start | bytes 196616 | tf_op jit(solution)/shard_map/ppermute | solution.py:394
  58.3 4.7 %collective-permute-start.6 = (f32[16,8,128]{2,1,0:T(8,128)S(1)}, f32[16,8,128]{2,1,0:T(8,128)S(1)}, u32[]{:S(2)}, u32[]{:S(2)}) collective-permute-start(f32[16,8,128]{2,1,0:T(8,128)S(1)} %add_add_fusion.state0), channel_id=1, source_target_pairs={{0,16},{8,24},{16,0},{24,8},{1,17},{9,25},{17,1},{25,9},{2,18},{10... | collective-permute-start | bytes 196616 | tf_op jit(solution)/shard_map/ppermute | solution.py:394
  59.7 4.3 %collective-permute-start.5 = (f32[16,8,128]{2,1,0:T(8,128)S(1)}, f32[16,8,128]{2,1,0:T(8,128)S(1)}, u32[]{:S(2)}, u32[]{:S(2)}) collective-permute-start(f32[16,8,128]{2,1,0:T(8,128)S(1)} %add_add_fusion.state0), channel_id=1, source_target_pairs={{0,24},{8,16},{16,8},{24,0},{1,25},{9,17},{17,9},{25,1},{2,26},{10... | collective-permute-start | bytes 196616 | tf_op jit(solution)/shard_map/ppermute | solution.py:394
  60.5 4.1 %collective-permute-start.4 = (f32[16,8,128]{2,1,0:T(8,128)S(1)}, f32[16,8,128]{2,1,0:T(8,128)S(1)}, u32[]{:S(2)}, u32[]{:S(2)}) collective-permute-start(f32[16,8,128]{2,1,0:T(8,128)S(1)} %add_add_fusion.state0), channel_id=1, source_target_pairs={{0,8},{8,0},{16,24},{24,16},{1,9},{9,1},{17,25},{25,17},{2,10},{10... | collective-permute-start | bytes 196616 | tf_op jit(solution)/shard_map/ppermute | solution.py:394
  61.2 5.8 %collective-permute-start.7 = (f32[2,8,8,128]{3,2,1,0:T(8,128)S(1)}, f32[2,8,8,128]{3,2,1,0:T(8,128)S(1)}, u32[]{:S(2)}, u32[]{:S(2)}) collective-permute-start(f32[2,8,8,128]{3,2,1,0:T(8,128)S(1)} %get-tuple-element.30.wave_far), channel_id=1, source_target_pairs={{0,224},{32,64},{64,32},{96,128},{128,96},{160,192},{192,160},{224... | collective-permute-start | bytes 196616 | tf_op jit(solution)/shard_map/ppermute | solution.py:445
  61.3 5.7 %collective-permute-start.9 = (f32[2,8,8,128]{3,2,1,0:T(8,128)S(1)}, f32[2,8,8,128]{3,2,1,0:T(8,128)S(1)}, u32[]{:S(2)}, u32[]{:S(2)}) collective-permute-start(f32[2,8,8,128]{3,2,1,0:T(8,128)S(1)} %get-tuple-element.31.wave_near), channel_id=1, source_target_pairs={{0,32},{32,0},{64,96},{96,64},{128,160},{160,128},{192,224},{224,1... | collective-permute-start | bytes 196616 | tf_op jit(solution)/shard_map/ppermute | solution.py:394
  64.6 4.1 %collective-permute-start.8 = (f32[8,8,128]{2,1,0:T(8,128)S(1)}, f32[8,8,128]{2,1,0:T(8,128)S(1)}, u32[]{:S(2)}, u32[]{:S(2)}) collective-permute-start(f32[8,8,128]{2,1,0:T(8,128)S(1)} %get-tuple-element.34), channel_id=1, source_target_pairs={{0,224},{32,64},{64,32},{96,128},{128,96},{160,192},{192,160},{224... | collective-permute-start | bytes 98312 | tf_op jit(solution)/shard_map/ppermute | solution.py:454
  64.7 4.0 %collective-permute-start.10 = (f32[8,8,128]{2,1,0:T(8,128)S(1)}, f32[8,8,128]{2,1,0:T(8,128)S(1)}, u32[]{:S(2)}, u32[]{:S(2)}) collective-permute-start(f32[8,8,128]{2,1,0:T(8,128)S(1)} %get-tuple-element.35), channel_id=1, source_target_pairs={{0,32},{32,0},{64,96},{96,64},{128,160},{160,128},{192,224},{224,1... | collective-permute-start | bytes 98312 | tf_op jit(solution)/shard_map/ppermute | solution.py:394
  70.9 15.7 %copy-start.1 = (bf16[64,384]{1,0:T(8,128)(2,1)S(1)}, bf16[64,384]{1,0:T(8,128)(2,1)}, u32[]{:S(2)}) copy-start(bf16[64,384]{1,0:T(8,128)(2,1)} %constant.8.clone.table) | copy-start | bytes 147460

commit v14 on v13

--- a/solution.py
+++ b/solution.py
@@ -275,7 +275,10 @@
     return jnp.where(even, two, one), jnp.where(even, one, two)
 
 
-def carry_kernel(slots, wave_far, wave_near, state0, state1, state2, state3, far, near, state_far, state_near):
+def carry_kernel(
+    slots, wave_far, wave_near, state0, state1, state2, state3, early, far, near, state_far, state_near
+):
+    del early
     state = (state0[...] + state1[...]) + (state2[...] + state3[...])
     mine = slots[slot()]
     state_far[...], state_near[...] = by_side(state[CHUNK // 2 :], state[: CHUNK // 2])
@@ -449,7 +452,12 @@
     states = [state] + [swapped(state, "x", bits) for bits in (1, 3, 2)]
     part = f32(CHUNK // 2, 8, LANES)
     far, near, state_far, state_near = call(
-        carry_kernel, (half, half, part, part), (SLOTS, wave_far, wave_near, *states), name="carry"
+        carry_kernel,
+        (half, half, part, part),
+        (SLOTS, wave_far, wave_near, *states, beyond_wave_far),
+        (),
+        [VMEM] * 7 + [ANY],
+        name="carry",
     )
     beyond_far = lax.ppermute(state_far, "z", other)
     beyond_near = swapped(state_near, "z", 1)

time: 108 us -> 108 us (level)
  no operation moved by 1% of the time
where the time goes in v14:
time: 108 us; the launch traced here: 107 us
  blocking collectives  79.7 us (74%)
  Pallas kernels  9.34 us (9%)
  waiting for transfers between devices  9.19 us (9%)
  starting transfers between devices  8.7 us (8%)
    all_to_all x4, blocking collectives, exchange(): return lax.all_to_all(blocks, axes, 0, 0, tiled=True)  79.7 us
    pallas_call x9, Pallas kernels, call(): pl.pallas_call(kernel, out_shape=outs, in_specs=specs or [VMEM] * len(ins...  9.34 us
    ppermute x9, starting transfers between devices, swapped(): lax.ppermute(block, axis, [(i, i ^ bits) for i in range(lax.axis_size(axi...  8.51 us
    ppermute x9, waiting for transfers between devices, swapped(): lax.ppermute(block, axis, [(i, i ^ bits) for i in range(lax.axis_size(axi...  7.46 us
  transfers between devices with their start and end apart: 11, of which 7 were waited for; matrix products, arithmetic and copies ran while one was open for 0% of the time, Pallas kernels for 1%

profile of v14, /device:TPU:1, one launch (start us, length us, event | category | flops | bytes accessed | tf_op | source)
XLA Modules:
  0.0 107.2 jit_solution(6219135408097216966)
XLA Ops:
  0.0 1.6 %pack.1 = (f32[768,128]{1,0:T(8,128)S(1)}, bf16[256,768]{1,0:T(8,128)(2,1)S(1)}, bf16[128,512]{1,0:T(8,128)(2,1)S(1)}, f32[8,128]{1,0:T(8,128)S(1)}) custom-call(f32[250,2,128]{2,1,0:T(2,128)} %bitcast.17, f32[1,125,2,128]{3,2,1,0:T(2,128)} %bitcast.19, f32[1,2,128]{2,1,0:T(2,128)} %bitcast.21, f32[1,125,125]{2,1,0:T(8,128)} %bitcast.20, f32[125,4,125]{2,1,0:T(4,128)} %bitcast.18), custom_call_target="tpu_custom_call" | custom-call | tf_op jit(solution)/shard_map/pack/pallas_call | solution.py:376
  1.6 0.0 copy-start.2
  1.6 28.0 %all_to_all.20 = f32[64,3,4,128]{3,2,1,0:T(4,128)S(1)} all-to-all(f32[64,3,4,128]{3,2,1,0:T(4,128)S(1)} %bitcast.16), channel_id=1, replica_groups=mesh['z'=8,'x'=4,'core'=2,'y'=4] {'z','x','core'}, dimensions={0} | all-to-all | bytes 786432 | tf_op jit(solution)/shard_map/all_to_all | solution.py:393
  29.6 0.0 copy-done.2
  29.6 0.3 forward.1
  30.0 0.0 copy-start
  30.0 16.8 %all_to_all.21.got = f32[32,24,128]{2,1,0:T(8,128)S(1)} all-to-all(f32[32,24,128]{2,1,0:T(8,128)S(1)} %bitcast.12), channel_id=1, replica_groups=mesh['z'=8,'x'=4,'core'=2,'y'=4] {'core','y','x'}, dimensions={0} | all-to-all | bytes 786432 | tf_op jit(solution)/shard_map/all_to_all | solution.py:393
  46.7 0.0 copy-done
  46.7 2.7 %first.1 = (f32[2,16,8,128]{3,2,1,0:T(8,128)S(1)}, f32[16,8,128]{2,1,0:T(8,128)S(1)}, f32[32,8,128]{2,1,0:T(8,128)S(1)}, f32[3,32,8,128]{3,2,1,0:T(8,128)S(1)}) custom-call(f32[32,8,128]{2,1,0:T(8,128)S(1)} %copy-done, bf16[256,768]{1,0:T(8,128)(2,1)S(1)} %get-tuple-element.22.ops, bf16[128,512]{1,0:T(8,128)(2,1)S(1)} %get-tuple-element.23.lows, ...), custom_call_target="tpu_custom_call" | custom-call | tf_op jit(solution)/shard_map/first/pallas_call | solution.py:376
  49.4 1.3 %collective-permute-start = (f32[16,8,128]{2,1,0:T(8,128)S(1)}, f32[16,8,128]{2,1,0:T(8,128)S(1)}, u32[]{:S(2)}, u32[]{:S(2)}) collective-permute-start(f32[16,8,128]{2,1,0:T(8,128)S(1)} %get-tuple-element.29), channel_id=1, source_target_pairs={{0,4},{4,0},{1,5},{5,1},{2,6},{6,2},{3,7},{7,3},{8,12},{12,8},{9,1... | collective-permute-start | bytes 196616 | tf_op jit(solution)/shard_map/ppermute | solution.py:397
  50.7 0.9 collective-permute-done
  51.6 1.4 %collective-permute-start.3 = (f32[16,8,128]{2,1,0:T(8,128)S(1)}, f32[16,8,128]{2,1,0:T(8,128)S(1)}, u32[]{:S(2)}, u32[]{:S(2)}) collective-permute-start(f32[16,8,128]{2,1,0:T(8,128)S(1)} %add.12.after), channel_id=1, source_target_pairs={{0,2},{1,3},{2,0},{3,1},{4,6},{5,7},{6,4},{7,5},{8,10},{9,11},{10,... | collective-permute-start | bytes 196616 | tf_op jit(solution)/shard_map/ppermute | solution.py:397
  53.0 1.4 %collective-permute-start.2 = (f32[16,8,128]{2,1,0:T(8,128)S(1)}, f32[16,8,128]{2,1,0:T(8,128)S(1)}, u32[]{:S(2)}, u32[]{:S(2)}) collective-permute-start(f32[16,8,128]{2,1,0:T(8,128)S(1)} %add.12.after), channel_id=1, source_target_pairs={{0,3},{1,2},{2,1},{3,0},{4,7},{5,6},{6,5},{7,4},{8,11},{9,10},{10,... | collective-permute-start | bytes 196616 | tf_op jit(solution)/shard_map/ppermute | solution.py:397
  54.5 0.0 collective-permute-start.1
  54.5 0.1 between.1
  54.6 0.1 collective-permute-start.7
  54.7 1.7 %collective-permute-done.3 = f32[16,8,128]{2,1,0:T(8,128)S(1)} collective-permute-done((f32[16,8,128]{2,1,0:T(8,128)S(1)}, f32[16,8,128]{2,1,0:T(8,128)S(1)}, u32[]{:S(2)}, u32[]{:S(2)}) %collective-permute-start.3) | collective-permute-done | bytes 65568 | tf_op jit(solution)/shard_map/ppermute | solution.py:397
  56.4 1.9 %collective-permute-done.2 = f32[16,8,128]{2,1,0:T(8,128)S(1)} collective-permute-done((f32[16,8,128]{2,1,0:T(8,128)S(1)}, f32[16,8,128]{2,1,0:T(8,128)S(1)}, u32[]{:S(2)}, u32[]{:S(2)}) %collective-permute-start.2) | collective-permute-done | bytes 65568 | tf_op jit(solution)/shard_map/ppermute | solution.py:397
  58.3 0.0 collective-permute-done.1
  58.3 1.3 %collective-permute-start.6 = (f32[16,8,128]{2,1,0:T(8,128)S(1)}, f32[16,8,128]{2,1,0:T(8,128)S(1)}, u32[]{:S(2)}, u32[]{:S(2)}) collective-permute-start(f32[16,8,128]{2,1,0:T(8,128)S(1)} %add_add_fusion.state0), channel_id=1, source_target_pairs={{0,16},{8,24},{16,0},{24,8},{1,17},{9,25},{17,1},{25,9},{2,18},{10... | collective-permute-start | bytes 196616 | tf_op jit(solution)/shard_map/ppermute | solution.py:397
  59.7 0.9 collective-permute-start.5
  60.5 0.5 collective-permute-start.4
  61.0 0.6 collective-permute-start.9
  61.6 0.0 collective-permute-done.7.early.wave_far
  61.6 1.4 %collective-permute-done.6.state3 = f32[16,8,128]{2,1,0:T(8,128)S(1)} collective-permute-done((f32[16,8,128]{2,1,0:T(8,128)S(1)}, f32[16,8,128]{2,1,0:T(8,128)S(1)}, u32[]{:S(2)}, u32[]{:S(2)}) %collective-permute-start.6) | collective-permute-done | bytes 65568 | tf_op jit(solution)/shard_map/ppermute | solution.py:397
  63.0 1.0 collective-permute-done.5.state2
  64.0 0.6 collective-permute-done.4.state1
  64.6 0.1 collective-permute-start.8
  64.7 1.1 %collective-permute-start.10 = (f32[8,8,128]{2,1,0:T(8,128)S(1)}, f32[8,8,128]{2,1,0:T(8,128)S(1)}, u32[]{:S(2)}, u32[]{:S(2)}) collective-permute-start(f32[8,8,128]{2,1,0:T(8,128)S(1)} %get-tuple-element.35), channel_id=1, source_target_pairs={{0,32},{32,0},{64,96},{96,64},{128,160},{160,128},{192,224},{224,1... | collective-permute-start | bytes 98312 | tf_op jit(solution)/shard_map/ppermute | solution.py:397
  65.8 1.1 %inner.1 = (f32[4,2,4,8,128]{4,3,2,1,0:T(8,128)S(1)}, f32[2,8,8,128]{3,2,1,0:T(8,128)S(1)}) custom-call(bf16[256,768]{1,0:T(8,128)(2,1)S(1)} %get-tuple-element.22.ops, bf16[128,512]{1,0:T(8,128)(2,1)S(1)} %get-tuple-element.23.lows, f32[32,8,128]{2,1,0:T(8,128)S(1)} %get-tuple-element.26.scale, f32[3,32,8,128]{3,2,1,0:T(8,128)S(1)} %get-tuple-element.27.inverse, ...), custom_call_target="tpu_custom_call" | custom-call | flops 2000000000 | bytes 1000000 | tf_op jit(solution)/shard_map/inner/pallas_call | solution.py:376
  66.9 0.0 collective-permute-done.9.wave_near
  67.0 1.7 %collective-permute-done.8.state_far = f32[8,8,128]{2,1,0:T(8,128)S(1)} collective-permute-done((f32[8,8,128]{2,1,0:T(8,128)S(1)}, f32[8,8,128]{2,1,0:T(8,128)S(1)}, u32[]{:S(2)}, u32[]{:S(2)}) %collective-permute-start.8) | collective-permute-done | bytes 32800 | tf_op jit(solution)/shard_map/ppermute | solution.py:462
  68.7 0.0 collective-permute-done.10.state_near
  68.7 2.2 %outer.1 = f32[32,16,128]{2,1,0:T(8,128)S(1)} custom-call(f32[32,8,128]{2,1,0:T(8,128)S(1)} %copy-done, bf16[256,768]{1,0:T(8,128)(2,1)S(1)} %get-tuple-element.22.ops, bf16[128,512]{1,0:T(8,128)(2,1)S(1)} %get-tuple-element.23.lows, f32[32,8,128]{2,1,0:T(8,128)S(1)} %get-tuple-element.26.scale, f32[3,32,8,128]{3,2,1,0:T(8,128)S(1)} %get-tuple-element.27.inverse, ...), custom_call_target="tpu_custom_call" | custom-call | tf_op jit(solution)/shard_map/outer/pallas_call | solution.py:376
  70.9 0.0 copy-start.1
  70.9 15.7 %all_to_all.22 = f32[32,16,128]{2,1,0:T(8,128)S(1)} all-to-all(f32[32,16,128]{2,1,0:T(8,128)S(1)} %outer.1), channel_id=1, replica_groups=mesh['z'=8,'x'=4,'core'=2,'y'=4] {'core','y','x'}, dimensions={0} | all-to-all | bytes 524288 | tf_op jit(solution)/shard_map/all_to_all | solution.py:393
  86.6 0.0 copy-done.1
  86.6 0.3 backward.1
  86.9 19.3 %all_to_all.23 = f32[64,8,128]{2,1,0:T(8,128)S(1)} all-to-all(f32[64,8,128]{2,1,0:T(8,128)S(1)} %bitcast.14), channel_id=1, replica_groups=mesh['z'=8,'x'=4,'core'=2,'y'=4] {'z','x','core'}, dimensions={0} | all-to-all | bytes 524288 | tf_op jit(solution)/shard_map/all_to_all | solution.py:393
  106.2 0.9 unpack.1
  (3 shorter events, 0.1 us)
Async XLA Ops:
  1.6 28.0 %copy-start.2 = (bf16[64,384]{1,0:T(8,128)(2,1)S(1)}, bf16[64,384]{1,0:T(8,128)(2,1)}, u32[]{:S(2)}) copy-start(bf16[64,384]{1,0:T(8,128)(2,1)} %constant.6.clone.table) | copy-start | bytes 147460
  30.0 16.8 %copy-start = (f32[32,8,128]{2,1,0:T(8,128)S(1)}, f32[32,8,128]{2,1,0:T(8,128)}, u32[]{:S(2)}) copy-start(f32[32,8,128]{2,1,0:T(8,128)} %constant.7.clone.slots) | copy-start | bytes 393220
  49.4 2.2 %collective-permute-start = (f32[16,8,128]{2,1,0:T(8,128)S(1)}, f32[16,8,128]{2,1,0:T(8,128)S(1)}, u32[]{:S(2)}, u32[]{:S(2)}) collective-permute-start(f32[16,8,128]{2,1,0:T(8,128)S(1)} %get-tuple-element.29), channel_id=1, source_target_pairs={{0,4},{4,0},{1,5},{5,1},{2,6},{6,2},{3,7},{7,3},{8,12},{12,8},{9,1... | collective-permute-start | bytes 196616 | tf_op jit(solution)/shard_map/ppermute | solution.py:397
  51.6 4.7 %collective-permute-start.3 = (f32[16,8,128]{2,1,0:T(8,128)S(1)}, f32[16,8,128]{2,1,0:T(8,128)S(1)}, u32[]{:S(2)}, u32[]{:S(2)}) collective-permute-start(f32[16,8,128]{2,1,0:T(8,128)S(1)} %add.12.after), channel_id=1, source_target_pairs={{0,2},{1,3},{2,0},{3,1},{4,6},{5,7},{6,4},{7,5},{8,10},{9,11},{10,... | collective-permute-start | bytes 196616 | tf_op jit(solution)/shard_map/ppermute | solution.py:397
  53.0 5.3 %collective-permute-start.2 = (f32[16,8,128]{2,1,0:T(8,128)S(1)}, f32[16,8,128]{2,1,0:T(8,128)S(1)}, u32[]{:S(2)}, u32[]{:S(2)}) collective-permute-start(f32[16,8,128]{2,1,0:T(8,128)S(1)} %add.12.after), channel_id=1, source_target_pairs={{0,3},{1,2},{2,1},{3,0},{4,7},{5,6},{6,5},{7,4},{8,11},{9,10},{10,... | collective-permute-start | bytes 196616 | tf_op jit(solution)/shard_map/ppermute | solution.py:397
  54.5 3.8 %collective-permute-start.1 = (f32[16,8,128]{2,1,0:T(8,128)S(1)}, f32[16,8,128]{2,1,0:T(8,128)S(1)}, u32[]{:S(2)}, u32[]{:S(2)}) collective-permute-start(f32[16,8,128]{2,1,0:T(8,128)S(1)} %add.12.after), channel_id=1, source_target_pairs={{0,1},{1,0},{2,3},{3,2},{4,5},{5,4},{6,7},{7,6},{8,9},{9,8},{10,11... | collective-permute-start | bytes 196616 | tf_op jit(solution)/shard_map/ppermute | solution.py:397
  54.6 7.0 %collective-permute-start.7 = (f32[2,8,8,128]{3,2,1,0:T(8,128)S(1)}, f32[2,8,8,128]{3,2,1,0:T(8,128)S(1)}, u32[]{:S(2)}, u32[]{:S(2)}) collective-permute-start(f32[2,8,8,128]{3,2,1,0:T(8,128)S(1)} %get-tuple-element.30.wave_far), channel_id=1, source_target_pairs={{0,224},{32,64},{64,32},{96,128},{128,96},{160,192},{192,160},{224... | collective-permute-start | bytes 196616 | tf_op jit(solution)/shard_map/ppermute | solution.py:448
  58.3 4.7 %collective-permute-start.6 = (f32[16,8,128]{2,1,0:T(8,128)S(1)}, f32[16,8,128]{2,1,0:T(8,128)S(1)}, u32[]{:S(2)}, u32[]{:S(2)}) collective-permute-start(f32[16,8,128]{2,1,0:T(8,128)S(1)} %add_add_fusion.state0), channel_id=1, source_target_pairs={{0,16},{8,24},{16,0},{24,8},{1,17},{9,25},{17,1},{25,9},{2,18},{10... | collective-permute-start | bytes 196616 | tf_op jit(solution)/shard_map/ppermute | solution.py:397
  59.7 4.3 %collective-permute-start.5 = (f32[16,8,128]{2,1,0:T(8,128)S(1)}, f32[16,8,128]{2,1,0:T(8,128)S(1)}, u32[]{:S(2)}, u32[]{:S(2)}) collective-permute-start(f32[16,8,128]{2,1,0:T(8,128)S(1)} %add_add_fusion.state0), channel_id=1, source_target_pairs={{0,24},{8,16},{16,8},{24,0},{1,25},{9,17},{17,9},{25,1},{2,26},{10... | collective-permute-start | bytes 196616 | tf_op jit(solution)/shard_map/ppermute | solution.py:397
  60.5 4.1 %collective-permute-start.4 = (f32[16,8,128]{2,1,0:T(8,128)S(1)}, f32[16,8,128]{2,1,0:T(8,128)S(1)}, u32[]{:S(2)}, u32[]{:S(2)}) collective-permute-start(f32[16,8,128]{2,1,0:T(8,128)S(1)} %add_add_fusion.state0), channel_id=1, source_target_pairs={{0,8},{8,0},{16,24},{24,16},{1,9},{9,1},{17,25},{25,17},{2,10},{10... | collective-permute-start | bytes 196616 | tf_op jit(solution)/shard_map/ppermute | solution.py:397
  61.0 5.9 %collective-permute-start.9 = (f32[2,8,8,128]{3,2,1,0:T(8,128)S(1)}, f32[2,8,8,128]{3,2,1,0:T(8,128)S(1)}, u32[]{:S(2)}, u32[]{:S(2)}) collective-permute-start(f32[2,8,8,128]{3,2,1,0:T(8,128)S(1)} %get-tuple-element.31.wave_near), channel_id=1, source_target_pairs={{0,32},{32,0},{64,96},{96,64},{128,160},{160,128},{192,224},{224,1... | collective-permute-start | bytes 196616 | tf_op jit(solution)/shard_map/ppermute | solution.py:397
  64.6 4.1 %collective-permute-start.8 = (f32[8,8,128]{2,1,0:T(8,128)S(1)}, f32[8,8,128]{2,1,0:T(8,128)S(1)}, u32[]{:S(2)}, u32[]{:S(2)}) collective-permute-start(f32[8,8,128]{2,1,0:T(8,128)S(1)} %get-tuple-element.34), channel_id=1, source_target_pairs={{0,224},{32,64},{64,32},{96,128},{128,96},{160,192},{192,160},{224... | collective-permute-start | bytes 98312 | tf_op jit(solution)/shard_map/ppermute | solution.py:462
  64.7 4.0 %collective-permute-start.10 = (f32[8,8,128]{2,1,0:T(8,128)S(1)}, f32[8,8,128]{2,1,0:T(8,128)S(1)}, u32[]{:S(2)}, u32[]{:S(2)}) collective-permute-start(f32[8,8,128]{2,1,0:T(8,128)S(1)} %get-tuple-element.35), channel_id=1, source_target_pairs={{0,32},{32,0},{64,96},{96,64},{128,160},{160,128},{192,224},{224,1... | collective-permute-start | bytes 98312 | tf_op jit(solution)/shard_map/ppermute | solution.py:397
  70.9 15.7 %copy-start.1 = (bf16[64,384]{1,0:T(8,128)(2,1)S(1)}, bf16[64,384]{1,0:T(8,128)(2,1)}, u32[]{:S(2)}) copy-start(bf16[64,384]{1,0:T(8,128)(2,1)} %constant.8.clone.table) | copy-start | bytes 147460

commit v15 on v14

--- a/solution.py
+++ b/solution.py
@@ -18,7 +18,7 @@
 CHUNK = 16
 WINDOW = 32
 HALO = 8
-INNER = 4
+INNER = 3
 ES_LANE = NB
 
 circ_alpha = 0.01

time: 108 us -> 108 us (level)
  no operation moved by 1% of the time
where the time goes in v15:
time: 108 us; the launch traced here: 107 us
  blocking collectives  79.7 us (74%)
  waiting for transfers between devices  9.46 us (9%)
  Pallas kernels  9.13 us (8%)
  starting transfers between devices  8.7 us (8%)
    all_to_all x4, blocking collectives, exchange(): return lax.all_to_all(blocks, axes, 0, 0, tiled=True)  79.7 us
    pallas_call x9, Pallas kernels, call(): pl.pallas_call(kernel, out_shape=outs, in_specs=specs or [VMEM] * len(ins...  9.13 us
    ppermute x9, starting transfers between devices, swapped(): lax.ppermute(block, axis, [(i, i ^ bits) for i in range(lax.axis_size(axi...  8.51 us
    ppermute x9, waiting for transfers between devices, swapped(): lax.ppermute(block, axis, [(i, i ^ bits) for i in range(lax.axis_size(axi...  7.46 us
  transfers between devices with their start and end apart: 11, of which 7 were waited for; matrix products, arithmetic and copies ran while one was open for 0% of the time, Pallas kernels for 1%

profile of v15, /device:TPU:1, one launch (start us, length us, event | category | flops | bytes accessed | tf_op | source)
XLA Modules:
  0.0 107.3 jit_solution(14983610518673046449)
XLA Ops:
  0.0 1.6 %pack.1 = (f32[768,128]{1,0:T(8,128)S(1)}, bf16[256,768]{1,0:T(8,128)(2,1)S(1)}, bf16[128,512]{1,0:T(8,128)(2,1)S(1)}, f32[8,128]{1,0:T(8,128)S(1)}) custom-call(f32[250,2,128]{2,1,0:T(2,128)} %bitcast.17, f32[1,125,2,128]{3,2,1,0:T(2,128)} %bitcast.19, f32[1,2,128]{2,1,0:T(2,128)} %bitcast.21, f32[1,125,125]{2,1,0:T(8,128)} %bitcast.20, f32[125,4,125]{2,1,0:T(4,128)} %bitcast.18), custom_call_target="tpu_custom_call" | custom-call | tf_op jit(solution)/shard_map/pack/pallas_call | solution.py:376
  1.6 0.0 copy-start.2
  1.6 28.0 %all_to_all.20 = f32[64,3,4,128]{3,2,1,0:T(4,128)S(1)} all-to-all(f32[64,3,4,128]{3,2,1,0:T(4,128)S(1)} %bitcast.16), channel_id=1, replica_groups=mesh['z'=8,'x'=4,'core'=2,'y'=4] {'z','x','core'}, dimensions={0} | all-to-all | bytes 786432 | tf_op jit(solution)/shard_map/all_to_all | solution.py:393
  29.6 0.0 copy-done.2
  29.6 0.3 forward.1
  30.0 0.0 copy-start
  30.0 16.8 %all_to_all.21.got = f32[32,24,128]{2,1,0:T(8,128)S(1)} all-to-all(f32[32,24,128]{2,1,0:T(8,128)S(1)} %bitcast.12), channel_id=1, replica_groups=mesh['z'=8,'x'=4,'core'=2,'y'=4] {'core','y','x'}, dimensions={0} | all-to-all | bytes 786432 | tf_op jit(solution)/shard_map/all_to_all | solution.py:393
  46.7 0.0 copy-done
  46.7 2.7 %first.1 = (f32[2,16,8,128]{3,2,1,0:T(8,128)S(1)}, f32[16,8,128]{2,1,0:T(8,128)S(1)}, f32[32,8,128]{2,1,0:T(8,128)S(1)}, f32[3,32,8,128]{3,2,1,0:T(8,128)S(1)}) custom-call(f32[32,8,128]{2,1,0:T(8,128)S(1)} %copy-done, bf16[256,768]{1,0:T(8,128)(2,1)S(1)} %get-tuple-element.22.ops, bf16[128,512]{1,0:T(8,128)(2,1)S(1)} %get-tuple-element.23.lows, ...), custom_call_target="tpu_custom_call" | custom-call | tf_op jit(solution)/shard_map/first/pallas_call | solution.py:376
  49.4 1.3 %collective-permute-start = (f32[16,8,128]{2,1,0:T(8,128)S(1)}, f32[16,8,128]{2,1,0:T(8,128)S(1)}, u32[]{:S(2)}, u32[]{:S(2)}) collective-permute-start(f32[16,8,128]{2,1,0:T(8,128)S(1)} %get-tuple-element.29), channel_id=1, source_target_pairs={{0,4},{4,0},{1,5},{5,1},{2,6},{6,2},{3,7},{7,3},{8,12},{12,8},{9,1... | collective-permute-start | bytes 196616 | tf_op jit(solution)/shard_map/ppermute | solution.py:397
  50.7 0.9 collective-permute-done
  51.6 1.4 %collective-permute-start.3 = (f32[16,8,128]{2,1,0:T(8,128)S(1)}, f32[16,8,128]{2,1,0:T(8,128)S(1)}, u32[]{:S(2)}, u32[]{:S(2)}) collective-permute-start(f32[16,8,128]{2,1,0:T(8,128)S(1)} %add.12.after), channel_id=1, source_target_pairs={{0,2},{1,3},{2,0},{3,1},{4,6},{5,7},{6,4},{7,5},{8,10},{9,11},{10,... | collective-permute-start | bytes 196616 | tf_op jit(solution)/shard_map/ppermute | solution.py:397
  53.0 1.4 %collective-permute-start.2 = (f32[16,8,128]{2,1,0:T(8,128)S(1)}, f32[16,8,128]{2,1,0:T(8,128)S(1)}, u32[]{:S(2)}, u32[]{:S(2)}) collective-permute-start(f32[16,8,128]{2,1,0:T(8,128)S(1)} %add.12.after), channel_id=1, source_target_pairs={{0,3},{1,2},{2,1},{3,0},{4,7},{5,6},{6,5},{7,4},{8,11},{9,10},{10,... | collective-permute-start | bytes 196616 | tf_op jit(solution)/shard_map/ppermute | solution.py:397
  54.5 0.0 collective-permute-start.1
  54.5 0.1 between.1
  54.6 0.1 collective-permute-start.7
  54.7 1.7 %collective-permute-done.3 = f32[16,8,128]{2,1,0:T(8,128)S(1)} collective-permute-done((f32[16,8,128]{2,1,0:T(8,128)S(1)}, f32[16,8,128]{2,1,0:T(8,128)S(1)}, u32[]{:S(2)}, u32[]{:S(2)}) %collective-permute-start.3) | collective-permute-done | bytes 65568 | tf_op jit(solution)/shard_map/ppermute | solution.py:397
  56.4 1.9 %collective-permute-done.2 = f32[16,8,128]{2,1,0:T(8,128)S(1)} collective-permute-done((f32[16,8,128]{2,1,0:T(8,128)S(1)}, f32[16,8,128]{2,1,0:T(8,128)S(1)}, u32[]{:S(2)}, u32[]{:S(2)}) %collective-permute-start.2) | collective-permute-done | bytes 65568 | tf_op jit(solution)/shard_map/ppermute | solution.py:397
  58.3 0.0 collective-permute-done.1
  58.3 1.3 %collective-permute-start.6 = (f32[16,8,128]{2,1,0:T(8,128)S(1)}, f32[16,8,128]{2,1,0:T(8,128)S(1)}, u32[]{:S(2)}, u32[]{:S(2)}) collective-permute-start(f32[16,8,128]{2,1,0:T(8,128)S(1)} %add_add_fusion.state0), channel_id=1, source_target_pairs={{0,16},{8,24},{16,0},{24,8},{1,17},{9,25},{17,1},{25,9},{2,18},{10... | collective-permute-start | bytes 196616 | tf_op jit(solution)/shard_map/ppermute | solution.py:397
  59.7 0.9 collective-permute-start.5
  60.5 0.5 collective-permute-start.4
  61.0 0.6 collective-permute-start.9
  61.6 0.0 collective-permute-done.7.early.wave_far
  61.6 1.4 %collective-permute-done.6.state3 = f32[16,8,128]{2,1,0:T(8,128)S(1)} collective-permute-done((f32[16,8,128]{2,1,0:T(8,128)S(1)}, f32[16,8,128]{2,1,0:T(8,128)S(1)}, u32[]{:S(2)}, u32[]{:S(2)}) %collective-permute-start.6) | collective-permute-done | bytes 65568 | tf_op jit(solution)/shard_map/ppermute | solution.py:397
  63.0 1.0 collective-permute-done.5.state2
  64.0 0.6 collective-permute-done.4.state1
  64.6 0.1 collective-permute-start.8
  64.7 1.1 %collective-permute-start.10 = (f32[8,8,128]{2,1,0:T(8,128)S(1)}, f32[8,8,128]{2,1,0:T(8,128)S(1)}, u32[]{:S(2)}, u32[]{:S(2)}) collective-permute-start(f32[8,8,128]{2,1,0:T(8,128)S(1)} %get-tuple-element.35), channel_id=1, source_target_pairs={{0,32},{32,0},{64,96},{96,64},{128,160},{160,128},{192,224},{224,1... | collective-permute-start | bytes 98312 | tf_op jit(solution)/shard_map/ppermute | solution.py:397
  65.8 0.9 inner.1
  66.7 0.0 collective-permute-done.9.wave_near
  66.7 2.0 %collective-permute-done.8.state_far = f32[8,8,128]{2,1,0:T(8,128)S(1)} collective-permute-done((f32[8,8,128]{2,1,0:T(8,128)S(1)}, f32[8,8,128]{2,1,0:T(8,128)S(1)}, u32[]{:S(2)}, u32[]{:S(2)}) %collective-permute-start.8) | collective-permute-done | bytes 32800 | tf_op jit(solution)/shard_map/ppermute | solution.py:462
  68.7 0.0 collective-permute-done.10.state_near
  68.7 2.3 %outer.1 = f32[32,16,128]{2,1,0:T(8,128)S(1)} custom-call(f32[32,8,128]{2,1,0:T(8,128)S(1)} %copy-done, bf16[256,768]{1,0:T(8,128)(2,1)S(1)} %get-tuple-element.22.ops, bf16[128,512]{1,0:T(8,128)(2,1)S(1)} %get-tuple-element.23.lows, f32[32,8,128]{2,1,0:T(8,128)S(1)} %get-tuple-element.26.scale, f32[3,32,8,128]{3,2,1,0:T(8,128)S(1)} %get-tuple-element.27.inverse, ...), custom_call_target="tpu_custom_call" | custom-call | tf_op jit(solution)/shard_map/outer/pallas_call | solution.py:376
  71.0 0.0 copy-start.1
  71.0 15.7 %all_to_all.22 = f32[32,16,128]{2,1,0:T(8,128)S(1)} all-to-all(f32[32,16,128]{2,1,0:T(8,128)S(1)} %outer.1), channel_id=1, replica_groups=mesh['z'=8,'x'=4,'core'=2,'y'=4] {'core','y','x'}, dimensions={0} | all-to-all | bytes 524288 | tf_op jit(solution)/shard_map/all_to_all | solution.py:393
  86.7 0.0 copy-done.1
  86.7 0.3 backward.1
  87.0 19.3 %all_to_all.23 = f32[64,8,128]{2,1,0:T(8,128)S(1)} all-to-all(f32[64,8,128]{2,1,0:T(8,128)S(1)} %bitcast.14), channel_id=1, replica_groups=mesh['z'=8,'x'=4,'core'=2,'y'=4] {'z','x','core'}, dimensions={0} | all-to-all | bytes 524288 | tf_op jit(solution)/shard_map/all_to_all | solution.py:393
  106.2 0.9 unpack.1
  (3 shorter events, 0.1 us)
Async XLA Ops:
  1.6 28.0 %copy-start.2 = (bf16[64,384]{1,0:T(8,128)(2,1)S(1)}, bf16[64,384]{1,0:T(8,128)(2,1)}, u32[]{:S(2)}) copy-start(bf16[64,384]{1,0:T(8,128)(2,1)} %constant.6.clone.table) | copy-start | bytes 147460
  30.0 16.8 %copy-start = (f32[32,8,128]{2,1,0:T(8,128)S(1)}, f32[32,8,128]{2,1,0:T(8,128)}, u32[]{:S(2)}) copy-start(f32[32,8,128]{2,1,0:T(8,128)} %constant.7.clone.slots) | copy-start | bytes 393220
  49.4 2.2 %collective-permute-start = (f32[16,8,128]{2,1,0:T(8,128)S(1)}, f32[16,8,128]{2,1,0:T(8,128)S(1)}, u32[]{:S(2)}, u32[]{:S(2)}) collective-permute-start(f32[16,8,128]{2,1,0:T(8,128)S(1)} %get-tuple-element.29), channel_id=1, source_target_pairs={{0,4},{4,0},{1,5},{5,1},{2,6},{6,2},{3,7},{7,3},{8,12},{12,8},{9,1... | collective-permute-start | bytes 196616 | tf_op jit(solution)/shard_map/ppermute | solution.py:397
  51.6 4.7 %collective-permute-start.3 = (f32[16,8,128]{2,1,0:T(8,128)S(1)}, f32[16,8,128]{2,1,0:T(8,128)S(1)}, u32[]{:S(2)}, u32[]{:S(2)}) collective-permute-start(f32[16,8,128]{2,1,0:T(8,128)S(1)} %add.12.after), channel_id=1, source_target_pairs={{0,2},{1,3},{2,0},{3,1},{4,6},{5,7},{6,4},{7,5},{8,10},{9,11},{10,... | collective-permute-start | bytes 196616 | tf_op jit(solution)/shard_map/ppermute | solution.py:397
  53.0 5.3 %collective-permute-start.2 = (f32[16,8,128]{2,1,0:T(8,128)S(1)}, f32[16,8,128]{2,1,0:T(8,128)S(1)}, u32[]{:S(2)}, u32[]{:S(2)}) collective-permute-start(f32[16,8,128]{2,1,0:T(8,128)S(1)} %add.12.after), channel_id=1, source_target_pairs={{0,3},{1,2},{2,1},{3,0},{4,7},{5,6},{6,5},{7,4},{8,11},{9,10},{10,... | collective-permute-start | bytes 196616 | tf_op jit(solution)/shard_map/ppermute | solution.py:397
  54.5 3.8 %collective-permute-start.1 = (f32[16,8,128]{2,1,0:T(8,128)S(1)}, f32[16,8,128]{2,1,0:T(8,128)S(1)}, u32[]{:S(2)}, u32[]{:S(2)}) collective-permute-start(f32[16,8,128]{2,1,0:T(8,128)S(1)} %add.12.after), channel_id=1, source_target_pairs={{0,1},{1,0},{2,3},{3,2},{4,5},{5,4},{6,7},{7,6},{8,9},{9,8},{10,11... | collective-permute-start | bytes 196616 | tf_op jit(solution)/shard_map/ppermute | solution.py:397
  54.6 7.0 %collective-permute-start.7 = (f32[2,8,8,128]{3,2,1,0:T(8,128)S(1)}, f32[2,8,8,128]{3,2,1,0:T(8,128)S(1)}, u32[]{:S(2)}, u32[]{:S(2)}) collective-permute-start(f32[2,8,8,128]{3,2,1,0:T(8,128)S(1)} %get-tuple-element.30.wave_far), channel_id=1, source_target_pairs={{0,224},{32,64},{64,32},{96,128},{128,96},{160,192},{192,160},{224... | collective-permute-start | bytes 196616 | tf_op jit(solution)/shard_map/ppermute | solution.py:448
  58.3 4.7 %collective-permute-start.6 = (f32[16,8,128]{2,1,0:T(8,128)S(1)}, f32[16,8,128]{2,1,0:T(8,128)S(1)}, u32[]{:S(2)}, u32[]{:S(2)}) collective-permute-start(f32[16,8,128]{2,1,0:T(8,128)S(1)} %add_add_fusion.state0), channel_id=1, source_target_pairs={{0,16},{8,24},{16,0},{24,8},{1,17},{9,25},{17,1},{25,9},{2,18},{10... | collective-permute-start | bytes 196616 | tf_op jit(solution)/shard_map/ppermute | solution.py:397
  59.7 4.3 %collective-permute-start.5 = (f32[16,8,128]{2,1,0:T(8,128)S(1)}, f32[16,8,128]{2,1,0:T(8,128)S(1)}, u32[]{:S(2)}, u32[]{:S(2)}) collective-permute-start(f32[16,8,128]{2,1,0:T(8,128)S(1)} %add_add_fusion.state0), channel_id=1, source_target_pairs={{0,24},{8,16},{16,8},{24,0},{1,25},{9,17},{17,9},{25,1},{2,26},{10... | collective-permute-start | bytes 196616 | tf_op jit(solution)/shard_map/ppermute | solution.py:397
  60.5 4.1 %collective-permute-start.4 = (f32[16,8,128]{2,1,0:T(8,128)S(1)}, f32[16,8,128]{2,1,0:T(8,128)S(1)}, u32[]{:S(2)}, u32[]{:S(2)}) collective-permute-start(f32[16,8,128]{2,1,0:T(8,128)S(1)} %add_add_fusion.state0), channel_id=1, source_target_pairs={{0,8},{8,0},{16,24},{24,16},{1,9},{9,1},{17,25},{25,17},{2,10},{10... | collective-permute-start | bytes 196616 | tf_op jit(solution)/shard_map/ppermute | solution.py:397
  61.0 5.6 %collective-permute-start.9 = (f32[2,8,8,128]{3,2,1,0:T(8,128)S(1)}, f32[2,8,8,128]{3,2,1,0:T(8,128)S(1)}, u32[]{:S(2)}, u32[]{:S(2)}) collective-permute-start(f32[2,8,8,128]{3,2,1,0:T(8,128)S(1)} %get-tuple-element.31.wave_near), channel_id=1, source_target_pairs={{0,32},{32,0},{64,96},{96,64},{128,160},{160,128},{192,224},{224,1... | collective-permute-start | bytes 196616 | tf_op jit(solution)/shard_map/ppermute | solution.py:397
  64.6 4.1 %collective-permute-start.8 = (f32[8,8,128]{2,1,0:T(8,128)S(1)}, f32[8,8,128]{2,1,0:T(8,128)S(1)}, u32[]{:S(2)}, u32[]{:S(2)}) collective-permute-start(f32[8,8,128]{2,1,0:T(8,128)S(1)} %get-tuple-element.34), channel_id=1, source_target_pairs={{0,224},{32,64},{64,32},{96,128},{128,96},{160,192},{192,160},{224... | collective-permute-start | bytes 98312 | tf_op jit(solution)/shard_map/ppermute | solution.py:462
  64.7 4.0 %collective-permute-start.10 = (f32[8,8,128]{2,1,0:T(8,128)S(1)}, f32[8,8,128]{2,1,0:T(8,128)S(1)}, u32[]{:S(2)}, u32[]{:S(2)}) collective-permute-start(f32[8,8,128]{2,1,0:T(8,128)S(1)} %get-tuple-element.35), channel_id=1, source_target_pairs={{0,32},{32,0},{64,96},{96,64},{128,160},{160,128},{192,224},{224,1... | collective-permute-start | bytes 98312 | tf_op jit(solution)/shard_map/ppermute | solution.py:397
  71.0 15.7 %copy-start.1 = (bf16[64,384]{1,0:T(8,128)(2,1)S(1)}, bf16[64,384]{1,0:T(8,128)(2,1)}, u32[]{:S(2)}) copy-start(bf16[64,384]{1,0:T(8,128)(2,1)} %constant.8.clone.table) | copy-start | bytes 147460

commit v16 on v14

--- a/solution.py
+++ b/solution.py
@@ -447,9 +447,9 @@
     )
     beyond_wave_far = lax.ppermute(wave_far, "z", other)
     beyond_wave_near = swapped(wave_near, "z", 1)
-    one, three, two = (swapped(state, "y", bits) for bits in (1, 3, 2))
+    one, three, two = (swapped(state, "x", bits) for bits in (1, 3, 2))
     state = ((state + one) + three) + two
-    states = [state] + [swapped(state, "x", bits) for bits in (1, 3, 2)]
+    states = [state] + [swapped(state, "y", bits) for bits in (1, 3, 2)]
     part = f32(CHUNK // 2, 8, LANES)
     far, near, state_far, state_near = call(
         carry_kernel,

time: 108 us -> 108 us (level)
  transfers between devices with their start and end apart: 11 -> 11, of which waited for: 7 -> 6; matrix products, arithmetic and copies ran while one was open for 0% -> 0% of each run, Pallas kernels for 1% -> 1%
where the time goes in v16:
time: 108 us; the launch traced here: 107 us
  blocking collectives  79.2 us (73%)
  waiting for transfers between devices  9.5 us (9%)
  Pallas kernels  9.35 us (9%)
  starting transfers between devices  8.86 us (8%)
    all_to_all x4, blocking collectives, exchange(): return lax.all_to_all(blocks, axes, 0, 0, tiled=True)  79.2 us
    pallas_call x9, Pallas kernels, call(): pl.pallas_call(kernel, out_shape=outs, in_specs=specs or [VMEM] * len(ins...  9.35 us
    ppermute x9, starting transfers between devices, swapped(): lax.ppermute(block, axis, [(i, i ^ bits) for i in range(lax.axis_size(axi...  8.67 us
    ppermute x9, waiting for transfers between devices, swapped(): lax.ppermute(block, axis, [(i, i ^ bits) for i in range(lax.axis_size(axi...  7.78 us
  transfers between devices with their start and end apart: 11, of which 6 were waited for; matrix products, arithmetic and copies ran while one was open for 0% of the time, Pallas kernels for 1%

profile of v16, /device:TPU:1, one launch (start us, length us, event | category | flops | bytes accessed | tf_op | source)
XLA Modules:
  0.0 107.2 jit_solution(13240782831511149510)
XLA Ops:
  0.0 1.6 %pack.1 = (f32[768,128]{1,0:T(8,128)S(1)}, bf16[256,768]{1,0:T(8,128)(2,1)S(1)}, bf16[128,512]{1,0:T(8,128)(2,1)S(1)}, f32[8,128]{1,0:T(8,128)S(1)}) custom-call(f32[250,2,128]{2,1,0:T(2,128)} %bitcast.17, f32[1,125,2,128]{3,2,1,0:T(2,128)} %bitcast.19, f32[1,2,128]{2,1,0:T(2,128)} %bitcast.21, f32[1,125,125]{2,1,0:T(8,128)} %bitcast.20, f32[125,4,125]{2,1,0:T(4,128)} %bitcast.18), custom_call_target="tpu_custom_call" | custom-call | tf_op jit(solution)/shard_map/pack/pallas_call | solution.py:376
  1.6 0.0 copy-start.2
  1.6 28.0 %all_to_all.20 = f32[64,3,4,128]{3,2,1,0:T(4,128)S(1)} all-to-all(f32[64,3,4,128]{3,2,1,0:T(4,128)S(1)} %bitcast.16), channel_id=1, replica_groups=mesh['z'=8,'x'=4,'core'=2,'y'=4] {'z','x','core'}, dimensions={0} | all-to-all | bytes 786432 | tf_op jit(solution)/shard_map/all_to_all | solution.py:393
  29.6 0.0 copy-done.2
  29.6 0.3 forward.1
  30.0 0.0 copy-start
  30.0 16.8 %all_to_all.21.got = f32[32,24,128]{2,1,0:T(8,128)S(1)} all-to-all(f32[32,24,128]{2,1,0:T(8,128)S(1)} %bitcast.12), channel_id=1, replica_groups=mesh['z'=8,'x'=4,'core'=2,'y'=4] {'core','y','x'}, dimensions={0} | all-to-all | bytes 786432 | tf_op jit(solution)/shard_map/all_to_all | solution.py:393
  46.7 0.0 copy-done
  46.7 2.7 %first.1 = (f32[2,16,8,128]{3,2,1,0:T(8,128)S(1)}, f32[16,8,128]{2,1,0:T(8,128)S(1)}, f32[32,8,128]{2,1,0:T(8,128)S(1)}, f32[3,32,8,128]{3,2,1,0:T(8,128)S(1)}) custom-call(f32[32,8,128]{2,1,0:T(8,128)S(1)} %copy-done, bf16[256,768]{1,0:T(8,128)(2,1)S(1)} %get-tuple-element.22.ops, bf16[128,512]{1,0:T(8,128)(2,1)S(1)} %get-tuple-element.23.lows, ...), custom_call_target="tpu_custom_call" | custom-call | tf_op jit(solution)/shard_map/first/pallas_call | solution.py:376
  49.4 1.3 %collective-permute-start = (f32[16,8,128]{2,1,0:T(8,128)S(1)}, f32[16,8,128]{2,1,0:T(8,128)S(1)}, u32[]{:S(2)}, u32[]{:S(2)}) collective-permute-start(f32[16,8,128]{2,1,0:T(8,128)S(1)} %get-tuple-element.29), channel_id=1, source_target_pairs={{0,4},{4,0},{1,5},{5,1},{2,6},{6,2},{3,7},{7,3},{8,12},{12,8},{9,1... | collective-permute-start | bytes 196616 | tf_op jit(solution)/shard_map/ppermute | solution.py:397
  50.7 0.9 collective-permute-done
  51.6 1.0 collective-permute-start.3
  52.7 1.6 %collective-permute-start.2 = (f32[16,8,128]{2,1,0:T(8,128)S(1)}, f32[16,8,128]{2,1,0:T(8,128)S(1)}, u32[]{:S(2)}, u32[]{:S(2)}) collective-permute-start(f32[16,8,128]{2,1,0:T(8,128)S(1)} %add.12.after), channel_id=1, source_target_pairs={{0,24},{8,16},{16,8},{24,0},{1,25},{9,17},{17,9},{25,1},{2,26},{10... | collective-permute-start | bytes 196616 | tf_op jit(solution)/shard_map/ppermute | solution.py:397
  54.3 0.1 collective-permute-start.1
  54.4 0.1 between.1
  54.5 0.1 collective-permute-start.7
  54.6 1.8 %collective-permute-done.3 = f32[16,8,128]{2,1,0:T(8,128)S(1)} collective-permute-done((f32[16,8,128]{2,1,0:T(8,128)S(1)}, f32[16,8,128]{2,1,0:T(8,128)S(1)}, u32[]{:S(2)}, u32[]{:S(2)}) %collective-permute-start.3) | collective-permute-done | bytes 65568 | tf_op jit(solution)/shard_map/ppermute | solution.py:397
  56.4 2.1 %collective-permute-done.2 = f32[16,8,128]{2,1,0:T(8,128)S(1)} collective-permute-done((f32[16,8,128]{2,1,0:T(8,128)S(1)}, f32[16,8,128]{2,1,0:T(8,128)S(1)}, u32[]{:S(2)}, u32[]{:S(2)}) %collective-permute-start.2) | collective-permute-done | bytes 65568 | tf_op jit(solution)/shard_map/ppermute | solution.py:397
  58.4 0.0 collective-permute-done.1
  58.4 1.6 %collective-permute-start.6 = (f32[16,8,128]{2,1,0:T(8,128)S(1)}, f32[16,8,128]{2,1,0:T(8,128)S(1)}, u32[]{:S(2)}, u32[]{:S(2)}) collective-permute-start(f32[16,8,128]{2,1,0:T(8,128)S(1)} %add_add_fusion.state0), channel_id=1, source_target_pairs={{0,2},{1,3},{2,0},{3,1},{4,6},{5,7},{6,4},{7,5},{8,10},{9,11},{10,... | collective-permute-start | bytes 196616 | tf_op jit(solution)/shard_map/ppermute | solution.py:397
  60.0 1.4 %collective-permute-start.5 = (f32[16,8,128]{2,1,0:T(8,128)S(1)}, f32[16,8,128]{2,1,0:T(8,128)S(1)}, u32[]{:S(2)}, u32[]{:S(2)}) collective-permute-start(f32[16,8,128]{2,1,0:T(8,128)S(1)} %add_add_fusion.state0), channel_id=1, source_target_pairs={{0,3},{1,2},{2,1},{3,0},{4,7},{5,6},{6,5},{7,4},{8,11},{9,10},{10,... | collective-permute-start | bytes 196616 | tf_op jit(solution)/shard_map/ppermute | solution.py:397
  61.4 0.0 collective-permute-start.4
  61.4 0.5 collective-permute-start.9
  62.0 0.0 collective-permute-done.7.early.wave_far
  62.0 1.2 %collective-permute-done.6.state3 = f32[16,8,128]{2,1,0:T(8,128)S(1)} collective-permute-done((f32[16,8,128]{2,1,0:T(8,128)S(1)}, f32[16,8,128]{2,1,0:T(8,128)S(1)}, u32[]{:S(2)}, u32[]{:S(2)}) %collective-permute-start.6) | collective-permute-done | bytes 65568 | tf_op jit(solution)/shard_map/ppermute | solution.py:397
  63.1 1.9 %collective-permute-done.5.state2 = f32[16,8,128]{2,1,0:T(8,128)S(1)} collective-permute-done((f32[16,8,128]{2,1,0:T(8,128)S(1)}, f32[16,8,128]{2,1,0:T(8,128)S(1)}, u32[]{:S(2)}, u32[]{:S(2)}) %collective-permute-start.5) | collective-permute-done | bytes 65568 | tf_op jit(solution)/shard_map/ppermute | solution.py:397
  65.0 0.0 collective-permute-done.4.state1
  65.1 0.1 collective-permute-start.8
  65.2 1.1 %collective-permute-start.10 = (f32[8,8,128]{2,1,0:T(8,128)S(1)}, f32[8,8,128]{2,1,0:T(8,128)S(1)}, u32[]{:S(2)}, u32[]{:S(2)}) collective-permute-start(f32[8,8,128]{2,1,0:T(8,128)S(1)} %get-tuple-element.35), channel_id=1, source_target_pairs={{0,32},{32,0},{64,96},{96,64},{128,160},{160,128},{192,224},{224,1... | collective-permute-start | bytes 98312 | tf_op jit(solution)/shard_map/ppermute | solution.py:397
  66.3 1.1 %inner.1 = (f32[4,2,4,8,128]{4,3,2,1,0:T(8,128)S(1)}, f32[2,8,8,128]{3,2,1,0:T(8,128)S(1)}) custom-call(bf16[256,768]{1,0:T(8,128)(2,1)S(1)} %get-tuple-element.22.ops, bf16[128,512]{1,0:T(8,128)(2,1)S(1)} %get-tuple-element.23.lows, f32[32,8,128]{2,1,0:T(8,128)S(1)} %get-tuple-element.26.scale, f32[3,32,8,128]{3,2,1,0:T(8,128)S(1)} %get-tuple-element.27.inverse, ...), custom_call_target="tpu_custom_call" | custom-call | flops 2000000000 | bytes 1000000 | tf_op jit(solution)/shard_map/inner/pallas_call | solution.py:376
  67.4 0.0 collective-permute-done.9.wave_near
  67.4 1.7 %collective-permute-done.8.state_far = f32[8,8,128]{2,1,0:T(8,128)S(1)} collective-permute-done((f32[8,8,128]{2,1,0:T(8,128)S(1)}, f32[8,8,128]{2,1,0:T(8,128)S(1)}, u32[]{:S(2)}, u32[]{:S(2)}) %collective-permute-start.8) | collective-permute-done | bytes 32800 | tf_op jit(solution)/shard_map/ppermute | solution.py:462
  69.1 0.0 collective-permute-done.10.state_near
  69.1 2.3 %outer.1 = f32[32,16,128]{2,1,0:T(8,128)S(1)} custom-call(f32[32,8,128]{2,1,0:T(8,128)S(1)} %copy-done, bf16[256,768]{1,0:T(8,128)(2,1)S(1)} %get-tuple-element.22.ops, bf16[128,512]{1,0:T(8,128)(2,1)S(1)} %get-tuple-element.23.lows, f32[32,8,128]{2,1,0:T(8,128)S(1)} %get-tuple-element.26.scale, f32[3,32,8,128]{3,2,1,0:T(8,128)S(1)} %get-tuple-element.27.inverse, ...), custom_call_target="tpu_custom_call" | custom-call | tf_op jit(solution)/shard_map/outer/pallas_call | solution.py:376
  71.4 0.0 copy-start.1
  71.4 15.2 %all_to_all.22 = f32[32,16,128]{2,1,0:T(8,128)S(1)} all-to-all(f32[32,16,128]{2,1,0:T(8,128)S(1)} %outer.1), channel_id=1, replica_groups=mesh['z'=8,'x'=4,'core'=2,'y'=4] {'core','y','x'}, dimensions={0} | all-to-all | bytes 524288 | tf_op jit(solution)/shard_map/all_to_all | solution.py:393
  86.6 0.0 copy-done.1
  86.6 0.3 backward.1
  86.9 19.3 %all_to_all.23 = f32[64,8,128]{2,1,0:T(8,128)S(1)} all-to-all(f32[64,8,128]{2,1,0:T(8,128)S(1)} %bitcast.14), channel_id=1, replica_groups=mesh['z'=8,'x'=4,'core'=2,'y'=4] {'z','x','core'}, dimensions={0} | all-to-all | bytes 524288 | tf_op jit(solution)/shard_map/all_to_all | solution.py:393
  106.2 0.9 unpack.1
  (3 shorter events, 0.1 us)
Async XLA Ops:
  1.6 28.0 %copy-start.2 = (bf16[64,384]{1,0:T(8,128)(2,1)S(1)}, bf16[64,384]{1,0:T(8,128)(2,1)}, u32[]{:S(2)}) copy-start(bf16[64,384]{1,0:T(8,128)(2,1)} %constant.6.clone.table) | copy-start | bytes 147460
  30.0 16.8 %copy-start = (f32[32,8,128]{2,1,0:T(8,128)S(1)}, f32[32,8,128]{2,1,0:T(8,128)}, u32[]{:S(2)}) copy-start(f32[32,8,128]{2,1,0:T(8,128)} %constant.7.clone.slots) | copy-start | bytes 393220
  49.4 2.2 %collective-permute-start = (f32[16,8,128]{2,1,0:T(8,128)S(1)}, f32[16,8,128]{2,1,0:T(8,128)S(1)}, u32[]{:S(2)}, u32[]{:S(2)}) collective-permute-start(f32[16,8,128]{2,1,0:T(8,128)S(1)} %get-tuple-element.29), channel_id=1, source_target_pairs={{0,4},{4,0},{1,5},{5,1},{2,6},{6,2},{3,7},{7,3},{8,12},{12,8},{9,1... | collective-permute-start | bytes 196616 | tf_op jit(solution)/shard_map/ppermute | solution.py:397
  51.6 4.7 %collective-permute-start.3 = (f32[16,8,128]{2,1,0:T(8,128)S(1)}, f32[16,8,128]{2,1,0:T(8,128)S(1)}, u32[]{:S(2)}, u32[]{:S(2)}) collective-permute-start(f32[16,8,128]{2,1,0:T(8,128)S(1)} %add.12.after), channel_id=1, source_target_pairs={{0,16},{8,24},{16,0},{24,8},{1,17},{9,25},{17,1},{25,9},{2,18},{10... | collective-permute-start | bytes 196616 | tf_op jit(solution)/shard_map/ppermute | solution.py:397
  52.7 5.7 %collective-permute-start.2 = (f32[16,8,128]{2,1,0:T(8,128)S(1)}, f32[16,8,128]{2,1,0:T(8,128)S(1)}, u32[]{:S(2)}, u32[]{:S(2)}) collective-permute-start(f32[16,8,128]{2,1,0:T(8,128)S(1)} %add.12.after), channel_id=1, source_target_pairs={{0,24},{8,16},{16,8},{24,0},{1,25},{9,17},{17,9},{25,1},{2,26},{10... | collective-permute-start | bytes 196616 | tf_op jit(solution)/shard_map/ppermute | solution.py:397
  54.3 4.2 %collective-permute-start.1 = (f32[16,8,128]{2,1,0:T(8,128)S(1)}, f32[16,8,128]{2,1,0:T(8,128)S(1)}, u32[]{:S(2)}, u32[]{:S(2)}) collective-permute-start(f32[16,8,128]{2,1,0:T(8,128)S(1)} %add.12.after), channel_id=1, source_target_pairs={{0,8},{8,0},{16,24},{24,16},{1,9},{9,1},{17,25},{25,17},{2,10},{10... | collective-permute-start | bytes 196616 | tf_op jit(solution)/shard_map/ppermute | solution.py:397
  54.5 7.5 %collective-permute-start.7 = (f32[2,8,8,128]{3,2,1,0:T(8,128)S(1)}, f32[2,8,8,128]{3,2,1,0:T(8,128)S(1)}, u32[]{:S(2)}, u32[]{:S(2)}) collective-permute-start(f32[2,8,8,128]{3,2,1,0:T(8,128)S(1)} %get-tuple-element.30.wave_far), channel_id=1, source_target_pairs={{0,224},{32,64},{64,32},{96,128},{128,96},{160,192},{192,160},{224... | collective-permute-start | bytes 196616 | tf_op jit(solution)/shard_map/ppermute | solution.py:448
  58.4 4.7 %collective-permute-start.6 = (f32[16,8,128]{2,1,0:T(8,128)S(1)}, f32[16,8,128]{2,1,0:T(8,128)S(1)}, u32[]{:S(2)}, u32[]{:S(2)}) collective-permute-start(f32[16,8,128]{2,1,0:T(8,128)S(1)} %add_add_fusion.state0), channel_id=1, source_target_pairs={{0,2},{1,3},{2,0},{3,1},{4,6},{5,7},{6,4},{7,5},{8,10},{9,11},{10,... | collective-permute-start | bytes 196616 | tf_op jit(solution)/shard_map/ppermute | solution.py:397
  60.0 5.0 %collective-permute-start.5 = (f32[16,8,128]{2,1,0:T(8,128)S(1)}, f32[16,8,128]{2,1,0:T(8,128)S(1)}, u32[]{:S(2)}, u32[]{:S(2)}) collective-permute-start(f32[16,8,128]{2,1,0:T(8,128)S(1)} %add_add_fusion.state0), channel_id=1, source_target_pairs={{0,3},{1,2},{2,1},{3,0},{4,7},{5,6},{6,5},{7,4},{8,11},{9,10},{10,... | collective-permute-start | bytes 196616 | tf_op jit(solution)/shard_map/ppermute | solution.py:397
  61.4 3.6 %collective-permute-start.4 = (f32[16,8,128]{2,1,0:T(8,128)S(1)}, f32[16,8,128]{2,1,0:T(8,128)S(1)}, u32[]{:S(2)}, u32[]{:S(2)}) collective-permute-start(f32[16,8,128]{2,1,0:T(8,128)S(1)} %add_add_fusion.state0), channel_id=1, source_target_pairs={{0,1},{1,0},{2,3},{3,2},{4,5},{5,4},{6,7},{7,6},{8,9},{9,8},{10,11... | collective-permute-start | bytes 196616 | tf_op jit(solution)/shard_map/ppermute | solution.py:397
  61.4 6.0 %collective-permute-start.9 = (f32[2,8,8,128]{3,2,1,0:T(8,128)S(1)}, f32[2,8,8,128]{3,2,1,0:T(8,128)S(1)}, u32[]{:S(2)}, u32[]{:S(2)}) collective-permute-start(f32[2,8,8,128]{3,2,1,0:T(8,128)S(1)} %get-tuple-element.31.wave_near), channel_id=1, source_target_pairs={{0,32},{32,0},{64,96},{96,64},{128,160},{160,128},{192,224},{224,1... | collective-permute-start | bytes 196616 | tf_op jit(solution)/shard_map/ppermute | solution.py:397
  65.1 4.1 %collective-permute-start.8 = (f32[8,8,128]{2,1,0:T(8,128)S(1)}, f32[8,8,128]{2,1,0:T(8,128)S(1)}, u32[]{:S(2)}, u32[]{:S(2)}) collective-permute-start(f32[8,8,128]{2,1,0:T(8,128)S(1)} %get-tuple-element.34), channel_id=1, source_target_pairs={{0,224},{32,64},{64,32},{96,128},{128,96},{160,192},{192,160},{224... | collective-permute-start | bytes 98312 | tf_op jit(solution)/shard_map/ppermute | solution.py:462
  65.2 4.0 %collective-permute-start.10 = (f32[8,8,128]{2,1,0:T(8,128)S(1)}, f32[8,8,128]{2,1,0:T(8,128)S(1)}, u32[]{:S(2)}, u32[]{:S(2)}) collective-permute-start(f32[8,8,128]{2,1,0:T(8,128)S(1)} %get-tuple-element.35), channel_id=1, source_target_pairs={{0,32},{32,0},{64,96},{96,64},{128,160},{160,128},{192,224},{224,1... | collective-permute-start | bytes 98312 | tf_op jit(solution)/shard_map/ppermute | solution.py:397
  71.4 15.2 %copy-start.1 = (bf16[64,384]{1,0:T(8,128)(2,1)S(1)}, bf16[64,384]{1,0:T(8,128)(2,1)}, u32[]{:S(2)}) copy-start(bf16[64,384]{1,0:T(8,128)(2,1)} %constant.8.clone.table) | copy-start | bytes 147460
